TPU v7x, 32 devices: a whole 2x2x4 slice. The times are simulated.
32 devices in a mesh: tm: 8 (over z, core), space: 4 (over y, x).
Axes of the slice: x: 2, y: 2, z: 4, core: 2. Of those that a mesh axis runs over, the one named last changes fastest.
Arguments:
- initial: float32 [64, 64, 2048], P('tm', 'space'), may hold values from -6 to 6
- source: float32 [64, 64, 2048], P('tm', 'space'), may hold values from -3 to 3.3
- diffusivity: float32 [64, 2048], P('space'), may hold values from 0.3 to 1
- growth: float32 [64, 2048], P('space'), may hold values from 0.5 to 4
Outputs:
- solution: float32 [64, 64, 2048], P('tm', 'space')
All inputs are finite; a program needn't handle non-finite values.
Results may differ from a plain program's by a relative error of at most 0.00002.
Values sent between devices are 32-bit elements; how exact they have to be, the bound alone decides.
No kernel may reach another device: no remote copies, remote signals or barrier semaphores. Data moves between devices by JAX's collectives and lax.ppermute only.
A program may use at most 64 MiB of HBM per device.

v0:
```python
import jax
import jax.numpy as jnp
from jax import lax
from jax.sharding import PartitionSpec as P

LEVELS = 4


diffusion_number = 0.03
time_step = 0.02


def padded_2(block, sides, width):
    for axis, dim in sides:
        count = lax.axis_size(axis)
        forward = [(i, i + 1) for i in range(count - 1)]
        backward = [(target, source) for source, target in forward]
        low = lax.ppermute(
            lax.slice_in_dim(block, block.shape[dim] - width, None, axis=dim), axis, forward
        )
        high = lax.ppermute(lax.slice_in_dim(block, 0, width, axis=dim), axis, backward)
        block = jnp.concatenate([low, block, high], axis=dim)
    return block


def from_behind(array, axis, by):
    peers = lax.axis_size(axis)
    return lax.ppermute(array, axis, [(i, (i + by) % peers) for i in range(peers)])


def stencil_local(fields, factor, diffusivity, growth):
    padded = jnp.pad(fields, ((0, 0), (1, 1), (1, 1)))
    beside_all = (
        padded[:, :-2, 1:-1] + padded[:, 2:, 1:-1] + padded[:, 1:-1, :-2] + padded[:, 1:-1, 2:]
    )
    laplace = beside_all - 4.0 * fields
    return (
        fields
        + diffusion_number * factor * diffusivity * laplace
        + time_step * factor * growth * fields / (1.0 + fields * fields)
    )


def propagate(fields, scales, diffusivity, growth):
    padded = padded_2(fields, (("space", 1),), 1)
    padded = jnp.pad(padded, ((0, 0), (0, 0), (1, 1)))
    beside_all = (
        padded[:, :-2, 1:-1] + padded[:, 2:, 1:-1] + padded[:, 1:-1, :-2] + padded[:, 1:-1, 2:]
    )
    laplace = beside_all - 4.0 * fields
    factor = scales[:, None, None]
    return (
        fields
        + diffusion_number * factor * diffusivity * laplace
        + time_step * factor * growth * fields / (1.0 + fields * fields)
    )


def uniform_scales(count, level_index):
    return jnp.full((count,), 2.0**level_index, jnp.float32)


def previous(points):
    return from_behind(points[-1:], "tm", 1)


def relax_wide(even_points, even_forcing, odd_forcing, level_index, diffusivity, growth):
    half = even_points.shape[0]
    rows = even_points.shape[1]
    stacked = jnp.concatenate(
        [even_points, even_forcing, odd_forcing, diffusivity[None], growth[None]], axis=0
    )
    wide = padded_2(stacked, (("space", 1),), 3)
    even_wide = wide[:half]
    even_terms = wide[half : 2 * half]
    odd_terms = wide[2 * half : 3 * half]
    diff_wide = wide[3 * half]
    grow_wide = wide[3 * half + 1]
    global_rows = lax.axis_index("space") * rows + jnp.arange(rows + 6, dtype=jnp.int32) - 3
    inside = ((global_rows >= 0) & (global_rows < rows * lax.axis_size("space"))).astype(
        jnp.float32
    )[None, :, None]
    factor = 2.0**level_index
    odd_wide = (stencil_local(even_wide, factor, diff_wide, grow_wide) + odd_terms) * inside
    arrived = from_behind(odd_wide[-1:], "tm", 1)
    shifted = jnp.concatenate([arrived, odd_wide[:-1]], axis=0)
    even_wide = (stencil_local(shifted, factor, diff_wide, grow_wide) + even_terms) * inside
    odd_wide = (stencil_local(even_wide, factor, diff_wide, grow_wide) + odd_terms) * inside
    return (even_wide[:, 3:-3], odd_wide[:, 3:-3])


def coarsest(states, forcing, diffusivity, growth):
    unit = uniform_scales(1, LEVELS - 1)
    position = lax.axis_index("tm")
    arriving = previous(states)

    def section(index, carry):
        waiting, result = carry
        prior = waiting
        prior = propagate(prior, unit, diffusivity, growth) + forcing
        outputs = [prior]
        fresh = jnp.concatenate(outputs, axis=0)
        result = jnp.where(position == index, fresh, result)
        passed = previous(result)
        waiting = jnp.where(position == index + 1, passed, waiting)
        return (waiting, result)

    arriving, result = lax.fori_loop(0, lax.axis_size("tm"), section, (arriving, states))
    return result


def cycle(level_index, states, forcing, diffusivity, growth):
    if level_index == LEVELS - 1:
        return coarsest(states, forcing, diffusivity, growth)
    half = states.shape[0] // 2
    scales = uniform_scales(half, level_index)
    even_forcing = forcing[0::2]
    odd_forcing = forcing[1::2]
    even_points = states[0::2]
    even_points, odd_points = relax_wide(
        even_points, even_forcing, odd_forcing, level_index, diffusivity, growth
    )
    both_scales = jnp.concatenate([scales, uniform_scales(half, level_index + 1)])
    images = propagate(
        jnp.concatenate([odd_points, even_points], axis=0), both_scales, diffusivity, growth
    )
    pair_terms = images[:half] - images[half:]
    reduced_forcing = even_forcing + jnp.concatenate(
        [previous(pair_terms), pair_terms[:-1]], axis=0
    )
    coarse_points = cycle(level_index + 1, even_points, reduced_forcing, diffusivity, growth)
    odd_points = propagate(coarse_points, scales, diffusivity, growth) + odd_forcing
    return jnp.stack([coarse_points, odd_points], axis=1).reshape(states.shape)


def body(initial, source, diffusivity, growth):
    return cycle(0, initial, source, diffusivity, growth)


def solution(mesh):
    placed = (P("tm", "space", None), P("tm", "space", None), P("space", None), P("space", None))
    return jax.shard_map(
        body, mesh=mesh, in_specs=placed, out_specs=P("tm", "space", None), check_vma=False
    )
```

profile of v0, /device:TPU:0, one launch (start us, length us, event | category | flops | bytes accessed | tf_op | source)
XLA Modules:
  0.0 272.3 jit_solution(9537858527738246663)
XLA Ops:
  4.6 5.5 %collective-permute-start.3 = (f32[14,3,2048]{2,1,0:T(4,128)S(1)}, f32[14,3,2048]{2,1,0:T(4,128)S(1)}, u32[]{:S(2)}, u32[]{:S(2)}) collective-permute-start(f32[14,3,2048]{2,1,0:T(4,128)S(1)} %get-tuple-element.210), channel_id=1, source_target_pairs={{0,1},{1,2},{2,3},{4,5},{5,6},{6,7},{8,9},{9,10},{10,11},{12,13},{... | collective-permute-start | bytes 1032200 | tf_op jit(solution)/shard_map/ppermute | solution.py:18
  10.2 9.6 %collective-permute-done.4 = f32[14,3,2048]{2,1,0:T(4,128)S(1)} collective-permute-done((f32[14,3,2048]{2,1,0:T(4,128)}, f32[14,3,2048]{2,1,0:T(4,128)S(1)}, u32[]{:S(2)}, u32[]{:S(2)}) %collective-permute-start.4) | collective-permute-done | bytes 344096 | tf_op jit(solution)/shard_map/ppermute | solution.py:21
  21.5 6.7 %collective-permute-done.5 = f32[1,22,2048]{2,1,0:T(8,128)S(1)} collective-permute-done((f32[1,22,2048]{2,1,0:T(8,128)S(1)}, f32[1,22,2048]{2,1,0:T(8,128)S(1)}, u32[]{:S(2)}, u32[]{:S(2)}) %collective-permute-start.5) | collective-permute-done | bytes 180256 | tf_op jit(solution)/shard_map/ppermute | solution.py:28
  30.0 1.3 collective-permute-start.7
  31.3 10.9 %collective-permute-start.6 = (f32[8,1,2048]{2,1,0:T(1,128)S(1)}, f32[8,1,2048]{2,1,0:T(1,128)S(1)}, u32[]{:S(2)}, u32[]{:S(2)}) collective-permute-start(f32[8,1,2048]{2,1,0:T(1,128)S(1)} %get-tuple-element.216), channel_id=1, source_target_pairs={{0,1},{1,2},{2,3},{4,5},{5,6},{6,7},{8,9},{9,10},{10,11},{12,13},{... | collective-permute-start | bytes 196616 | tf_op jit(solution)/shard_map/ppermute | solution.py:18
  42.5 1.6 collective-permute-done.6
  46.2 6.1 %collective-permute-done.8 = f32[1,16,2048]{2,1,0:T(8,128)S(1)} collective-permute-done((f32[1,16,2048]{2,1,0:T(8,128)S(1)}, f32[1,16,2048]{2,1,0:T(8,128)S(1)}, u32[]{:S(2)}, u32[]{:S(2)}) %collective-permute-start.8) | collective-permute-done | bytes 131104 | tf_op jit(solution)/shard_map/ppermute | solution.py:28
  52.6 1.3 collective-permute-start.10
  53.9 5.9 %collective-permute-start.9 = (f32[8,3,2048]{2,1,0:T(4,128)S(1)}, f32[8,3,2048]{2,1,0:T(4,128)S(1)}, u32[]{:S(2)}, u32[]{:S(2)}) collective-permute-start(f32[8,3,2048]{2,1,0:T(4,128)S(1)} %get-tuple-element.214), channel_id=1, source_target_pairs={{0,1},{1,2},{2,3},{4,5},{5,6},{6,7},{8,9},{9,10},{10,11},{12,13},{... | collective-permute-start | bytes 589832 | tf_op jit(solution)/shard_map/ppermute | solution.py:18
  59.8 5.1 %collective-permute-done.10 = f32[8,3,2048]{2,1,0:T(4,128)S(1)} collective-permute-done((f32[8,3,2048]{2,1,0:T(4,128)S(1)}, f32[8,3,2048]{2,1,0:T(4,128)S(1)}, u32[]{:S(2)}, u32[]{:S(2)}) %collective-permute-start.10) | collective-permute-done | bytes 196640 | tf_op jit(solution)/shard_map/ppermute | solution.py:21
  65.9 6.8 %collective-permute-done.11 = f32[1,22,2048]{2,1,0:T(8,128)S(1)} collective-permute-done((f32[1,22,2048]{2,1,0:T(8,128)S(1)}, f32[1,22,2048]{2,1,0:T(8,128)S(1)}, u32[]{:S(2)}, u32[]{:S(2)}) %collective-permute-start.11) | collective-permute-done | bytes 180256 | tf_op jit(solution)/shard_map/ppermute | solution.py:28
  73.7 1.3 collective-permute-start.13
  75.0 5.0 %collective-permute-start.12 = (f32[4,1,2048]{2,1,0:T(1,128)S(1)}, f32[4,1,2048]{2,1,0:T(1,128)S(1)}, u32[]{:S(2)}, u32[]{:S(2)}) collective-permute-start(f32[4,1,2048]{2,1,0:T(1,128)S(1)} %get-tuple-element.228), channel_id=1, source_target_pairs={{0,1},{1,2},{2,3},{4,5},{5,6},{6,7},{8,9},{9,10},{10,11},{12,13},{... | collective-permute-start | bytes 98312 | tf_op jit(solution)/shard_map/ppermute | solution.py:18
  80.0 1.5 collective-permute-done.12
  82.7 6.2 %collective-permute-done.14 = f32[1,16,2048]{2,1,0:T(8,128)S(1)} collective-permute-done((f32[1,16,2048]{2,1,0:T(8,128)S(1)}, f32[1,16,2048]{2,1,0:T(8,128)S(1)}, u32[]{:S(2)}, u32[]{:S(2)}) %collective-permute-start.14) | collective-permute-done | bytes 131104 | tf_op jit(solution)/shard_map/ppermute | solution.py:28
  88.9 1.3 collective-permute-start.16
  90.2 5.9 %collective-permute-start.15 = (f32[5,3,2048]{2,1,0:T(4,128)S(1)}, f32[5,3,2048]{2,1,0:T(4,128)S(1)}, u32[]{:S(2)}, u32[]{:S(2)}) collective-permute-start(f32[5,3,2048]{2,1,0:T(4,128)S(1)} %get-tuple-element.224), channel_id=1, source_target_pairs={{0,1},{1,2},{2,3},{4,5},{5,6},{6,7},{8,9},{9,10},{10,11},{12,13},{... | collective-permute-start | bytes 368648 | tf_op jit(solution)/shard_map/ppermute | solution.py:18
  96.2 2.4 collective-permute-done.16
  99.4 6.9 %collective-permute-done.17 = f32[1,22,2048]{2,1,0:T(8,128)S(1)} collective-permute-done((f32[1,22,2048]{2,1,0:T(8,128)S(1)}, f32[1,22,2048]{2,1,0:T(8,128)S(1)}, u32[]{:S(2)}, u32[]{:S(2)}) %collective-permute-start.17) | collective-permute-done | bytes 180256 | tf_op jit(solution)/shard_map/ppermute | solution.py:28
  106.9 1.3 collective-permute-start.20
  108.2 5.7 %collective-permute-start.19 = (f32[2,1,2048]{2,1,0:T(1,128)S(1)}, f32[2,1,2048]{2,1,0:T(1,128)S(1)}, u32[]{:S(2)}, u32[]{:S(2)}) collective-permute-start(f32[2,1,2048]{2,1,0:T(1,128)S(1)} %get-tuple-element.238), channel_id=1, source_target_pairs={{0,1},{1,2},{2,3},{4,5},{5,6},{6,7},{8,9},{9,10},{10,11},{12,13},{... | collective-permute-start | bytes 49160 | tf_op jit(solution)/shard_map/ppermute | solution.py:18
  113.9 1.4 collective-permute-done.19
  116.2 5.9 %collective-permute-done.21 = f32[1,16,2048]{2,1,0:T(8,128)S(1)} collective-permute-done((f32[1,16,2048]{2,1,0:T(8,128)S(1)}, f32[1,16,2048]{2,1,0:T(8,128)S(1)}, u32[]{:S(2)}, u32[]{:S(2)}) %collective-permute-start.21) | collective-permute-done | bytes 131104 | tf_op jit(solution)/shard_map/ppermute | solution.py:28
  122.2 1.4 collective-permute-done.18
  123.5 120.3 %while.17 = (s32[]{:T(128)}, f32[1,16,2048]{2,1,0:T(8,128)S(1)}, f32[1,16,2048]{2,1,0:T(8,128)S(1)}, s32[]{:T(128)}, f32[16,2048]{1,0:T(8,128)S(1)}, /*index=5*/...) while((s32[]{:T(128)}, f32[1,16,2048]{2,1,0:T(8,128)S(1)}, f32[1,16,2048]{2,1,0:T(8,128)S(1)}, ...), condition=%wide.region_1.2_spmd, body=%wide.region_0.1_spmd.sunk | while | flops 917796 | bytes 2376049 | solution.py:108
  123.6 1.3 collective-permute-start
  124.9 5.9 %collective-permute-start.1 = (f32[1,1,2048]{2,1,0:T(1,128)S(1)}, f32[1,1,2048]{2,1,0:T(1,128)S(1)}, u32[]{:S(2)}, u32[]{:S(2)}) collective-permute-start(f32[1,1,2048]{2,1,0:T(1,128)S(1)} %get-tuple-element.296), channel_id=1, source_target_pairs={{0,1},{1,2},{2,3},{4,5},{5,6},{6,7},{8,9},{9,10},{10,11},{12,13},{... | collective-permute-start | bytes 24584 | tf_op jit(solution)/shard_map/while/body/eval_jaxpr/ppermute | solution.py:18
  130.8 1.3 collective-permute-done.1
  132.5 6.2 %collective-permute-done.2 = f32[1,16,2048]{2,1,0:T(8,128)S(1)} collective-permute-done((f32[1,16,2048]{2,1,0:T(8,128)S(1)}, f32[1,16,2048]{2,1,0:T(8,128)S(1)}, u32[]{:S(2)}, u32[]{:S(2)}) %collective-permute-start.2) | collective-permute-done | bytes 131104 | tf_op jit(solution)/shard_map/while/body/eval_jaxpr/ppermute | solution.py:28
  138.8 1.3 collective-permute-start
  140.1 5.7 %collective-permute-start.1 = (f32[1,1,2048]{2,1,0:T(1,128)S(1)}, f32[1,1,2048]{2,1,0:T(1,128)S(1)}, u32[]{:S(2)}, u32[]{:S(2)}) collective-permute-start(f32[1,1,2048]{2,1,0:T(1,128)S(1)} %get-tuple-element.296), channel_id=1, source_target_pairs={{0,1},{1,2},{2,3},{4,5},{5,6},{6,7},{8,9},{9,10},{10,11},{12,13},{... | collective-permute-start | bytes 24584 | tf_op jit(solution)/shard_map/while/body/eval_jaxpr/ppermute | solution.py:18
  145.8 1.3 collective-permute-done.1
  147.5 6.2 %collective-permute-done.2 = f32[1,16,2048]{2,1,0:T(8,128)S(1)} collective-permute-done((f32[1,16,2048]{2,1,0:T(8,128)S(1)}, f32[1,16,2048]{2,1,0:T(8,128)S(1)}, u32[]{:S(2)}, u32[]{:S(2)}) %collective-permute-start.2) | collective-permute-done | bytes 131104 | tf_op jit(solution)/shard_map/while/body/eval_jaxpr/ppermute | solution.py:28
  153.8 1.3 collective-permute-start
  155.1 5.7 %collective-permute-start.1 = (f32[1,1,2048]{2,1,0:T(1,128)S(1)}, f32[1,1,2048]{2,1,0:T(1,128)S(1)}, u32[]{:S(2)}, u32[]{:S(2)}) collective-permute-start(f32[1,1,2048]{2,1,0:T(1,128)S(1)} %get-tuple-element.296), channel_id=1, source_target_pairs={{0,1},{1,2},{2,3},{4,5},{5,6},{6,7},{8,9},{9,10},{10,11},{12,13},{... | collective-permute-start | bytes 24584 | tf_op jit(solution)/shard_map/while/body/eval_jaxpr/ppermute | solution.py:18
  160.8 1.3 collective-permute-done.1
  162.6 6.2 %collective-permute-done.2 = f32[1,16,2048]{2,1,0:T(8,128)S(1)} collective-permute-done((f32[1,16,2048]{2,1,0:T(8,128)S(1)}, f32[1,16,2048]{2,1,0:T(8,128)S(1)}, u32[]{:S(2)}, u32[]{:S(2)}) %collective-permute-start.2) | collective-permute-done | bytes 131104 | tf_op jit(solution)/shard_map/while/body/eval_jaxpr/ppermute | solution.py:28
  168.8 1.3 collective-permute-start
  170.1 5.7 %collective-permute-start.1 = (f32[1,1,2048]{2,1,0:T(1,128)S(1)}, f32[1,1,2048]{2,1,0:T(1,128)S(1)}, u32[]{:S(2)}, u32[]{:S(2)}) collective-permute-start(f32[1,1,2048]{2,1,0:T(1,128)S(1)} %get-tuple-element.296), channel_id=1, source_target_pairs={{0,1},{1,2},{2,3},{4,5},{5,6},{6,7},{8,9},{9,10},{10,11},{12,13},{... | collective-permute-start | bytes 24584 | tf_op jit(solution)/shard_map/while/body/eval_jaxpr/ppermute | solution.py:18
  175.8 1.3 collective-permute-done.1
  177.6 6.2 %collective-permute-done.2 = f32[1,16,2048]{2,1,0:T(8,128)S(1)} collective-permute-done((f32[1,16,2048]{2,1,0:T(8,128)S(1)}, f32[1,16,2048]{2,1,0:T(8,128)S(1)}, u32[]{:S(2)}, u32[]{:S(2)}) %collective-permute-start.2) | collective-permute-done | bytes 131104 | tf_op jit(solution)/shard_map/while/body/eval_jaxpr/ppermute | solution.py:28
  183.8 1.3 collective-permute-start
  185.1 5.7 %collective-permute-start.1 = (f32[1,1,2048]{2,1,0:T(1,128)S(1)}, f32[1,1,2048]{2,1,0:T(1,128)S(1)}, u32[]{:S(2)}, u32[]{:S(2)}) collective-permute-start(f32[1,1,2048]{2,1,0:T(1,128)S(1)} %get-tuple-element.296), channel_id=1, source_target_pairs={{0,1},{1,2},{2,3},{4,5},{5,6},{6,7},{8,9},{9,10},{10,11},{12,13},{... | collective-permute-start | bytes 24584 | tf_op jit(solution)/shard_map/while/body/eval_jaxpr/ppermute | solution.py:18
  190.8 1.3 collective-permute-done.1
  192.6 6.2 %collective-permute-done.2 = f32[1,16,2048]{2,1,0:T(8,128)S(1)} collective-permute-done((f32[1,16,2048]{2,1,0:T(8,128)S(1)}, f32[1,16,2048]{2,1,0:T(8,128)S(1)}, u32[]{:S(2)}, u32[]{:S(2)}) %collective-permute-start.2) | collective-permute-done | bytes 131104 | tf_op jit(solution)/shard_map/while/body/eval_jaxpr/ppermute | solution.py:28
  198.8 1.3 collective-permute-start
  200.1 5.7 %collective-permute-start.1 = (f32[1,1,2048]{2,1,0:T(1,128)S(1)}, f32[1,1,2048]{2,1,0:T(1,128)S(1)}, u32[]{:S(2)}, u32[]{:S(2)}) collective-permute-start(f32[1,1,2048]{2,1,0:T(1,128)S(1)} %get-tuple-element.296), channel_id=1, source_target_pairs={{0,1},{1,2},{2,3},{4,5},{5,6},{6,7},{8,9},{9,10},{10,11},{12,13},{... | collective-permute-start | bytes 24584 | tf_op jit(solution)/shard_map/while/body/eval_jaxpr/ppermute | solution.py:18
  205.9 1.3 collective-permute-done.1
  207.6 6.2 %collective-permute-done.2 = f32[1,16,2048]{2,1,0:T(8,128)S(1)} collective-permute-done((f32[1,16,2048]{2,1,0:T(8,128)S(1)}, f32[1,16,2048]{2,1,0:T(8,128)S(1)}, u32[]{:S(2)}, u32[]{:S(2)}) %collective-permute-start.2) | collective-permute-done | bytes 131104 | tf_op jit(solution)/shard_map/while/body/eval_jaxpr/ppermute | solution.py:28
  215.1 5.7 %collective-permute-start.1 = (f32[1,1,2048]{2,1,0:T(1,128)S(1)}, f32[1,1,2048]{2,1,0:T(1,128)S(1)}, u32[]{:S(2)}, u32[]{:S(2)}) collective-permute-start(f32[1,1,2048]{2,1,0:T(1,128)S(1)} %get-tuple-element.296), channel_id=1, source_target_pairs={{0,1},{1,2},{2,3},{4,5},{5,6},{6,7},{8,9},{9,10},{10,11},{12,13},{... | collective-permute-start | bytes 24584 | tf_op jit(solution)/shard_map/while/body/eval_jaxpr/ppermute | solution.py:18
  220.9 1.3 collective-permute-done.1
  222.6 6.2 %collective-permute-done.2 = f32[1,16,2048]{2,1,0:T(8,128)S(1)} collective-permute-done((f32[1,16,2048]{2,1,0:T(8,128)S(1)}, f32[1,16,2048]{2,1,0:T(8,128)S(1)}, u32[]{:S(2)}, u32[]{:S(2)}) %collective-permute-start.2) | collective-permute-done | bytes 131104 | tf_op jit(solution)/shard_map/while/body/eval_jaxpr/ppermute | solution.py:28
  228.8 1.3 collective-permute-start
  230.1 5.7 %collective-permute-start.1 = (f32[1,1,2048]{2,1,0:T(1,128)S(1)}, f32[1,1,2048]{2,1,0:T(1,128)S(1)}, u32[]{:S(2)}, u32[]{:S(2)}) collective-permute-start(f32[1,1,2048]{2,1,0:T(1,128)S(1)} %get-tuple-element.296), channel_id=1, source_target_pairs={{0,1},{1,2},{2,3},{4,5},{5,6},{6,7},{8,9},{9,10},{10,11},{12,13},{... | collective-permute-start | bytes 24584 | tf_op jit(solution)/shard_map/while/body/eval_jaxpr/ppermute | solution.py:18
  235.9 1.3 collective-permute-done.1
  237.6 6.2 %collective-permute-done.2 = f32[1,16,2048]{2,1,0:T(8,128)S(1)} collective-permute-done((f32[1,16,2048]{2,1,0:T(8,128)S(1)}, f32[1,16,2048]{2,1,0:T(8,128)S(1)}, u32[]{:S(2)}, u32[]{:S(2)}) %collective-permute-start.2) | collective-permute-done | bytes 131104 | tf_op jit(solution)/shard_map/while/body/eval_jaxpr/ppermute | solution.py:28
  243.8 1.3 collective-permute-start.23
  245.1 5.7 %collective-permute-start.22 = (f32[1,1,2048]{2,1,0:T(1,128)S(1)}, f32[1,1,2048]{2,1,0:T(1,128)S(1)}, u32[]{:S(2)}, u32[]{:S(2)}) collective-permute-start(f32[1,1,2048]{2,1,0:T(1,128)S(1)} %get-tuple-element.248), channel_id=1, source_target_pairs={{0,1},{1,2},{2,3},{4,5},{5,6},{6,7},{8,9},{9,10},{10,11},{12,13},{... | collective-permute-start | bytes 24584 | tf_op jit(solution)/shard_map/ppermute | solution.py:18
  250.9 1.3 collective-permute-done.22
  252.6 1.3 collective-permute-start.25
  253.9 5.7 %collective-permute-start.24 = (f32[2,1,2048]{2,1,0:T(1,128)S(1)}, f32[2,1,2048]{2,1,0:T(1,128)S(1)}, u32[]{:S(2)}, u32[]{:S(2)}) collective-permute-start(f32[2,1,2048]{2,1,0:T(1,128)S(1)} %get-tuple-element.236), channel_id=1, source_target_pairs={{0,1},{1,2},{2,3},{4,5},{5,6},{6,7},{8,9},{9,10},{10,11},{12,13},{... | collective-permute-start | bytes 49160 | tf_op jit(solution)/shard_map/ppermute | solution.py:18
  259.7 1.4 collective-permute-done.24
  263.0 5.7 %collective-permute-start.26 = (f32[4,1,2048]{2,1,0:T(1,128)S(1)}, f32[4,1,2048]{2,1,0:T(1,128)S(1)}, u32[]{:S(2)}, u32[]{:S(2)}) collective-permute-start(f32[4,1,2048]{2,1,0:T(1,128)S(1)} %get-tuple-element.226), channel_id=1, source_target_pairs={{0,1},{1,2},{2,3},{4,5},{5,6},{6,7},{8,9},{9,10},{10,11},{12,13},{... | collective-permute-start | bytes 98312 | tf_op jit(solution)/shard_map/ppermute | solution.py:18
  268.7 1.6 collective-permute-done.26
  (166 shorter events, 24.7 us)
Async XLA Ops:
  0.0 2.3 copy-start.2
  0.0 2.3 copy-start.1
  0.0 2.4 copy-start
  3.3 16.4 %collective-permute-start.4 = (f32[14,3,2048]{2,1,0:T(4,128)}, f32[14,3,2048]{2,1,0:T(4,128)S(1)}, u32[]{:S(2)}, u32[]{:S(2)}) collective-permute-start(f32[14,3,2048]{2,1,0:T(4,128)} %get-tuple-element.211), channel_id=1, source_target_pairs={{1,0},{2,1},{3,2},{5,4},{6,5},{7,6},{9,8},{10,9},{11,10},{13,12},{... | collective-permute-start | bytes 1032200 | tf_op jit(solution)/shard_map/ppermute | solution.py:21
  4.6 15.2 %collective-permute-start.3 = (f32[14,3,2048]{2,1,0:T(4,128)S(1)}, f32[14,3,2048]{2,1,0:T(4,128)S(1)}, u32[]{:S(2)}, u32[]{:S(2)}) collective-permute-start(f32[14,3,2048]{2,1,0:T(4,128)S(1)} %get-tuple-element.210), channel_id=1, source_target_pairs={{0,1},{1,2},{2,3},{4,5},{5,6},{6,7},{8,9},{9,10},{10,11},{12,13},{... | collective-permute-start | bytes 1032200 | tf_op jit(solution)/shard_map/ppermute | solution.py:18
  21.2 6.9 %collective-permute-start.5 = (f32[1,22,2048]{2,1,0:T(8,128)S(1)}, f32[1,22,2048]{2,1,0:T(8,128)S(1)}, u32[]{:S(2)}, u32[]{:S(2)}) collective-permute-start(f32[1,22,2048]{2,1,0:T(8,128)S(1)} %slice.586), channel_id=1, source_target_pairs={{0,4},{4,8},{8,12},{12,16},{16,20},{20,24},{24,28},{28,0},{1,5},{5... | collective-permute-start | bytes 540680 | tf_op jit(solution)/shard_map/ppermute | solution.py:28
  29.8 15.1 %copy-start.8 = (f32[8]{0:T(128)S(1)}, f32[8]{0:T(128)}, u32[]{:S(2)}) copy-start(f32[8]{0:T(128)} %constant.123.clone.1) | copy-start | bytes 100
  29.9 15.1 %copy-start.9 = (f32[8]{0:T(128)S(1)}, f32[8]{0:T(128)}, u32[]{:S(2)}) copy-start(f32[8]{0:T(128)} %constant.122.clone.1) | copy-start | bytes 100
  30.0 12.6 %collective-permute-start.7 = (f32[8,1,2048]{2,1,0:T(1,128)S(1)}, f32[8,1,2048]{2,1,0:T(1,128)S(1)}, u32[]{:S(2)}, u32[]{:S(2)}) collective-permute-start(f32[8,1,2048]{2,1,0:T(1,128)S(1)} %get-tuple-element.217), channel_id=1, source_target_pairs={{1,0},{2,1},{3,2},{5,4},{6,5},{7,6},{9,8},{10,9},{11,10},{13,12},{... | collective-permute-start | bytes 196616 | tf_op jit(solution)/shard_map/ppermute | solution.py:21
  31.3 12.8 %collective-permute-start.6 = (f32[8,1,2048]{2,1,0:T(1,128)S(1)}, f32[8,1,2048]{2,1,0:T(1,128)S(1)}, u32[]{:S(2)}, u32[]{:S(2)}) collective-permute-start(f32[8,1,2048]{2,1,0:T(1,128)S(1)} %get-tuple-element.216), channel_id=1, source_target_pairs={{0,1},{1,2},{2,3},{4,5},{5,6},{6,7},{8,9},{9,10},{10,11},{12,13},{... | collective-permute-start | bytes 196616 | tf_op jit(solution)/shard_map/ppermute | solution.py:18
  46.0 6.3 %copy-start.3 = (f32[8,16,2048]{2,1,0:T(8,128)S(1)}, f32[8,16,2048]{2,1,0:T(8,128)}, u32[]{:S(2)}) copy-start(f32[8,16,2048]{2,1,0:T(8,128)} %param.7) | copy-start | bytes 3145732
  46.1 6.2 %collective-permute-start.8 = (f32[1,16,2048]{2,1,0:T(8,128)S(1)}, f32[1,16,2048]{2,1,0:T(8,128)S(1)}, u32[]{:S(2)}, u32[]{:S(2)}) collective-permute-start(f32[1,16,2048]{2,1,0:T(8,128)S(1)} %slice.604), channel_id=1, source_target_pairs={{0,4},{4,8},{8,12},{12,16},{16,20},{20,24},{24,28},{28,0},{1,5},{5... | collective-permute-start | bytes 393224 | tf_op jit(solution)/shard_map/ppermute | solution.py:28
  52.6 12.3 %collective-permute-start.10 = (f32[8,3,2048]{2,1,0:T(4,128)S(1)}, f32[8,3,2048]{2,1,0:T(4,128)S(1)}, u32[]{:S(2)}, u32[]{:S(2)}) collective-permute-start(f32[8,3,2048]{2,1,0:T(4,128)S(1)} %get-tuple-element.215), channel_id=1, source_target_pairs={{1,0},{2,1},{3,2},{5,4},{6,5},{7,6},{9,8},{10,9},{11,10},{13,12},{... | collective-permute-start | bytes 589832 | tf_op jit(solution)/shard_map/ppermute | solution.py:21
  53.9 11.0 %collective-permute-start.9 = (f32[8,3,2048]{2,1,0:T(4,128)S(1)}, f32[8,3,2048]{2,1,0:T(4,128)S(1)}, u32[]{:S(2)}, u32[]{:S(2)}) collective-permute-start(f32[8,3,2048]{2,1,0:T(4,128)S(1)} %get-tuple-element.214), channel_id=1, source_target_pairs={{0,1},{1,2},{2,3},{4,5},{5,6},{6,7},{8,9},{9,10},{10,11},{12,13},{... | collective-permute-start | bytes 589832 | tf_op jit(solution)/shard_map/ppermute | solution.py:18
  65.8 6.9 %collective-permute-start.11 = (f32[1,22,2048]{2,1,0:T(8,128)S(1)}, f32[1,22,2048]{2,1,0:T(8,128)S(1)}, u32[]{:S(2)}, u32[]{:S(2)}) collective-permute-start(f32[1,22,2048]{2,1,0:T(8,128)S(1)} %get-tuple-element.232), channel_id=1, source_target_pairs={{0,4},{4,8},{8,12},{12,16},{16,20},{20,24},{24,28},{28,0},{1,5},{5... | collective-permute-start | bytes 540680 | tf_op jit(solution)/shard_map/ppermute | solution.py:28
  73.4 8.6 %copy-start.6 = (f32[4]{0:T(128)S(1)}, f32[4]{0:T(128)}, u32[]{:S(2)}) copy-start(f32[4]{0:T(128)} %constant.127.clone.1) | copy-start | bytes 52
  73.4 8.6 %copy-start.7 = (f32[4]{0:T(128)S(1)}, f32[4]{0:T(128)}, u32[]{:S(2)}) copy-start(f32[4]{0:T(128)} %constant.126.clone.1) | copy-start | bytes 52
  73.7 6.3 %collective-permute-start.13 = (f32[4,1,2048]{2,1,0:T(1,128)S(1)}, f32[4,1,2048]{2,1,0:T(1,128)S(1)}, u32[]{:S(2)}, u32[]{:S(2)}) collective-permute-start(f32[4,1,2048]{2,1,0:T(1,128)S(1)} %get-tuple-element.229), channel_id=1, source_target_pairs={{1,0},{2,1},{3,2},{5,4},{6,5},{7,6},{9,8},{10,9},{11,10},{13,12},{... | collective-permute-start | bytes 98312 | tf_op jit(solution)/shard_map/ppermute | solution.py:21
  75.0 6.6 %collective-permute-start.12 = (f32[4,1,2048]{2,1,0:T(1,128)S(1)}, f32[4,1,2048]{2,1,0:T(1,128)S(1)}, u32[]{:S(2)}, u32[]{:S(2)}) collective-permute-start(f32[4,1,2048]{2,1,0:T(1,128)S(1)} %get-tuple-element.228), channel_id=1, source_target_pairs={{0,1},{1,2},{2,3},{4,5},{5,6},{6,7},{8,9},{9,10},{10,11},{12,13},{... | collective-permute-start | bytes 98312 | tf_op jit(solution)/shard_map/ppermute | solution.py:18
  82.6 6.2 %collective-permute-start.14 = (f32[1,16,2048]{2,1,0:T(8,128)S(1)}, f32[1,16,2048]{2,1,0:T(8,128)S(1)}, u32[]{:S(2)}, u32[]{:S(2)}) collective-permute-start(f32[1,16,2048]{2,1,0:T(8,128)S(1)} %get-tuple-element.240), channel_id=1, source_target_pairs={{0,4},{4,8},{8,12},{12,16},{16,20},{20,24},{24,28},{28,0},{1,5},{5... | collective-permute-start | bytes 393224 | tf_op jit(solution)/shard_map/ppermute | solution.py:28
  88.9 9.7 %collective-permute-start.16 = (f32[5,3,2048]{2,1,0:T(4,128)S(1)}, f32[5,3,2048]{2,1,0:T(4,128)S(1)}, u32[]{:S(2)}, u32[]{:S(2)}) collective-permute-start(f32[5,3,2048]{2,1,0:T(4,128)S(1)} %get-tuple-element.225), channel_id=1, source_target_pairs={{1,0},{2,1},{3,2},{5,4},{6,5},{7,6},{9,8},{10,9},{11,10},{13,12},{... | collective-permute-start | bytes 368648 | tf_op jit(solution)/shard_map/ppermute | solution.py:21
  90.2 8.7 %collective-permute-start.15 = (f32[5,3,2048]{2,1,0:T(4,128)S(1)}, f32[5,3,2048]{2,1,0:T(4,128)S(1)}, u32[]{:S(2)}, u32[]{:S(2)}) collective-permute-start(f32[5,3,2048]{2,1,0:T(4,128)S(1)} %get-tuple-element.224), channel_id=1, source_target_pairs={{0,1},{1,2},{2,3},{4,5},{5,6},{6,7},{8,9},{9,10},{10,11},{12,13},{... | collective-permute-start | bytes 368648 | tf_op jit(solution)/shard_map/ppermute | solution.py:18
  99.4 16.2 %copy-start.4 = (f32[2]{0:T(128)S(1)}, f32[2]{0:T(128)}, u32[]{:S(2)}) copy-start(f32[2]{0:T(128)} %constant.131.clone.1) | copy-start | bytes 28
  99.4 16.2 %copy-start.5 = (f32[2]{0:T(128)S(1)}, f32[2]{0:T(128)}, u32[]{:S(2)}) copy-start(f32[2]{0:T(128)} %constant.130.clone.1) | copy-start | bytes 28
  99.4 6.9 %collective-permute-start.17 = (f32[1,22,2048]{2,1,0:T(8,128)S(1)}, f32[1,22,2048]{2,1,0:T(8,128)S(1)}, u32[]{:S(2)}, u32[]{:S(2)}) collective-permute-start(f32[1,22,2048]{2,1,0:T(8,128)S(1)} %get-tuple-element.219), channel_id=1, source_target_pairs={{0,4},{4,8},{8,12},{12,16},{16,20},{20,24},{24,28},{28,0},{1,5},{5... | collective-permute-start | bytes 540680 | tf_op jit(solution)/shard_map/ppermute | solution.py:28
  106.9 7.1 %collective-permute-start.20 = (f32[2,1,2048]{2,1,0:T(1,128)S(1)}, f32[2,1,2048]{2,1,0:T(1,128)S(1)}, u32[]{:S(2)}, u32[]{:S(2)}) collective-permute-start(f32[2,1,2048]{2,1,0:T(1,128)S(1)} %get-tuple-element.239), channel_id=1, source_target_pairs={{1,0},{2,1},{3,2},{5,4},{6,5},{7,6},{9,8},{10,9},{11,10},{13,12},{... | collective-permute-start | bytes 49160 | tf_op jit(solution)/shard_map/ppermute | solution.py:21
  108.2 7.2 %collective-permute-start.19 = (f32[2,1,2048]{2,1,0:T(1,128)S(1)}, f32[2,1,2048]{2,1,0:T(1,128)S(1)}, u32[]{:S(2)}, u32[]{:S(2)}) collective-permute-start(f32[2,1,2048]{2,1,0:T(1,128)S(1)} %get-tuple-element.238), channel_id=1, source_target_pairs={{0,1},{1,2},{2,3},{4,5},{5,6},{6,7},{8,9},{9,10},{10,11},{12,13},{... | collective-permute-start | bytes 49160 | tf_op jit(solution)/shard_map/ppermute | solution.py:18
  115.9 6.2 %collective-permute-start.21 = (f32[1,16,2048]{2,1,0:T(8,128)S(1)}, f32[1,16,2048]{2,1,0:T(8,128)S(1)}, u32[]{:S(2)}, u32[]{:S(2)}) collective-permute-start(f32[1,16,2048]{2,1,0:T(8,128)S(1)} %slice_subtract_fusion.4), channel_id=1, source_target_pairs={{0,4},{4,8},{8,12},{12,16},{16,20},{20,24},{24,28},{28,0},{1,5},{5... | collective-permute-start | bytes 393224 | tf_op jit(solution)/shard_map/ppermute | solution.py:28
  116.0 7.6 %collective-permute-start.18 = (f32[1,16,2048]{2,1,0:T(8,128)S(1)}, f32[1,16,2048]{2,1,0:T(8,128)S(1)}, u32[]{:S(2)}, u32[]{:S(2)}) collective-permute-start(f32[1,16,2048]{2,1,0:T(8,128)S(1)} %get-tuple-element.299), channel_id=1, source_target_pairs={{0,4},{4,8},{8,12},{12,16},{16,20},{20,24},{24,28},{28,0},{1,5},{5... | collective-permute-start | bytes 393224 | tf_op jit(solution)/shard_map/ppermute | solution.py:28
  123.6 7.2 %collective-permute-start = (f32[1,1,2048]{2,1,0:T(1,128)S(1)}, f32[1,1,2048]{2,1,0:T(1,128)S(1)}, u32[]{:S(2)}, u32[]{:S(2)}) collective-permute-start(f32[1,1,2048]{2,1,0:T(1,128)S(1)} %get-tuple-element.295), channel_id=1, source_target_pairs={{1,0},{2,1},{3,2},{5,4},{6,5},{7,6},{9,8},{10,9},{11,10},{13,12},{... | collective-permute-start | bytes 24584 | tf_op jit(solution)/shard_map/while/body/eval_jaxpr/ppermute | solution.py:21
  124.9 7.3 %collective-permute-start.1 = (f32[1,1,2048]{2,1,0:T(1,128)S(1)}, f32[1,1,2048]{2,1,0:T(1,128)S(1)}, u32[]{:S(2)}, u32[]{:S(2)}) collective-permute-start(f32[1,1,2048]{2,1,0:T(1,128)S(1)} %get-tuple-element.296), channel_id=1, source_target_pairs={{0,1},{1,2},{2,3},{4,5},{5,6},{6,7},{8,9},{9,10},{10,11},{12,13},{... | collective-permute-start | bytes 24584 | tf_op jit(solution)/shard_map/while/body/eval_jaxpr/ppermute | solution.py:18
  132.5 6.2 %collective-permute-start.2 = (f32[1,16,2048]{2,1,0:T(8,128)S(1)}, f32[1,16,2048]{2,1,0:T(8,128)S(1)}, u32[]{:S(2)}, u32[]{:S(2)}) collective-permute-start(f32[1,16,2048]{2,1,0:T(8,128)S(1)} %fusion.103), channel_id=1, source_target_pairs={{0,4},{4,8},{8,12},{12,16},{16,20},{20,24},{24,28},{28,0},{1,5},{5... | collective-permute-start | bytes 393224 | tf_op jit(solution)/shard_map/while/body/eval_jaxpr/ppermute | solution.py:28
  138.8 7.0 %collective-permute-start = (f32[1,1,2048]{2,1,0:T(1,128)S(1)}, f32[1,1,2048]{2,1,0:T(1,128)S(1)}, u32[]{:S(2)}, u32[]{:S(2)}) collective-permute-start(f32[1,1,2048]{2,1,0:T(1,128)S(1)} %get-tuple-element.295), channel_id=1, source_target_pairs={{1,0},{2,1},{3,2},{5,4},{6,5},{7,6},{9,8},{10,9},{11,10},{13,12},{... | collective-permute-start | bytes 24584 | tf_op jit(solution)/shard_map/while/body/eval_jaxpr/ppermute | solution.py:21
  140.1 7.1 %collective-permute-start.1 = (f32[1,1,2048]{2,1,0:T(1,128)S(1)}, f32[1,1,2048]{2,1,0:T(1,128)S(1)}, u32[]{:S(2)}, u32[]{:S(2)}) collective-permute-start(f32[1,1,2048]{2,1,0:T(1,128)S(1)} %get-tuple-element.296), channel_id=1, source_target_pairs={{0,1},{1,2},{2,3},{4,5},{5,6},{6,7},{8,9},{9,10},{10,11},{12,13},{... | collective-permute-start | bytes 24584 | tf_op jit(solution)/shard_map/while/body/eval_jaxpr/ppermute | solution.py:18
  147.5 6.2 %collective-permute-start.2 = (f32[1,16,2048]{2,1,0:T(8,128)S(1)}, f32[1,16,2048]{2,1,0:T(8,128)S(1)}, u32[]{:S(2)}, u32[]{:S(2)}) collective-permute-start(f32[1,16,2048]{2,1,0:T(8,128)S(1)} %fusion.103), channel_id=1, source_target_pairs={{0,4},{4,8},{8,12},{12,16},{16,20},{20,24},{24,28},{28,0},{1,5},{5... | collective-permute-start | bytes 393224 | tf_op jit(solution)/shard_map/while/body/eval_jaxpr/ppermute | solution.py:28
  153.8 7.0 %collective-permute-start = (f32[1,1,2048]{2,1,0:T(1,128)S(1)}, f32[1,1,2048]{2,1,0:T(1,128)S(1)}, u32[]{:S(2)}, u32[]{:S(2)}) collective-permute-start(f32[1,1,2048]{2,1,0:T(1,128)S(1)} %get-tuple-element.295), channel_id=1, source_target_pairs={{1,0},{2,1},{3,2},{5,4},{6,5},{7,6},{9,8},{10,9},{11,10},{13,12},{... | collective-permute-start | bytes 24584 | tf_op jit(solution)/shard_map/while/body/eval_jaxpr/ppermute | solution.py:21
  155.1 7.1 %collective-permute-start.1 = (f32[1,1,2048]{2,1,0:T(1,128)S(1)}, f32[1,1,2048]{2,1,0:T(1,128)S(1)}, u32[]{:S(2)}, u32[]{:S(2)}) collective-permute-start(f32[1,1,2048]{2,1,0:T(1,128)S(1)} %get-tuple-element.296), channel_id=1, source_target_pairs={{0,1},{1,2},{2,3},{4,5},{5,6},{6,7},{8,9},{9,10},{10,11},{12,13},{... | collective-permute-start | bytes 24584 | tf_op jit(solution)/shard_map/while/body/eval_jaxpr/ppermute | solution.py:18
  162.5 6.2 %collective-permute-start.2 = (f32[1,16,2048]{2,1,0:T(8,128)S(1)}, f32[1,16,2048]{2,1,0:T(8,128)S(1)}, u32[]{:S(2)}, u32[]{:S(2)}) collective-permute-start(f32[1,16,2048]{2,1,0:T(8,128)S(1)} %fusion.103), channel_id=1, source_target_pairs={{0,4},{4,8},{8,12},{12,16},{16,20},{20,24},{24,28},{28,0},{1,5},{5... | collective-permute-start | bytes 393224 | tf_op jit(solution)/shard_map/while/body/eval_jaxpr/ppermute | solution.py:28
  168.8 7.0 %collective-permute-start = (f32[1,1,2048]{2,1,0:T(1,128)S(1)}, f32[1,1,2048]{2,1,0:T(1,128)S(1)}, u32[]{:S(2)}, u32[]{:S(2)}) collective-permute-start(f32[1,1,2048]{2,1,0:T(1,128)S(1)} %get-tuple-element.295), channel_id=1, source_target_pairs={{1,0},{2,1},{3,2},{5,4},{6,5},{7,6},{9,8},{10,9},{11,10},{13,12},{... | collective-permute-start | bytes 24584 | tf_op jit(solution)/shard_map/while/body/eval_jaxpr/ppermute | solution.py:21
  170.1 7.1 %collective-permute-start.1 = (f32[1,1,2048]{2,1,0:T(1,128)S(1)}, f32[1,1,2048]{2,1,0:T(1,128)S(1)}, u32[]{:S(2)}, u32[]{:S(2)}) collective-permute-start(f32[1,1,2048]{2,1,0:T(1,128)S(1)} %get-tuple-element.296), channel_id=1, source_target_pairs={{0,1},{1,2},{2,3},{4,5},{5,6},{6,7},{8,9},{9,10},{10,11},{12,13},{... | collective-permute-start | bytes 24584 | tf_op jit(solution)/shard_map/while/body/eval_jaxpr/ppermute | solution.py:18
  177.5 6.2 %collective-permute-start.2 = (f32[1,16,2048]{2,1,0:T(8,128)S(1)}, f32[1,16,2048]{2,1,0:T(8,128)S(1)}, u32[]{:S(2)}, u32[]{:S(2)}) collective-permute-start(f32[1,16,2048]{2,1,0:T(8,128)S(1)} %fusion.103), channel_id=1, source_target_pairs={{0,4},{4,8},{8,12},{12,16},{16,20},{20,24},{24,28},{28,0},{1,5},{5... | collective-permute-start | bytes 393224 | tf_op jit(solution)/shard_map/while/body/eval_jaxpr/ppermute | solution.py:28
  183.8 7.0 %collective-permute-start = (f32[1,1,2048]{2,1,0:T(1,128)S(1)}, f32[1,1,2048]{2,1,0:T(1,128)S(1)}, u32[]{:S(2)}, u32[]{:S(2)}) collective-permute-start(f32[1,1,2048]{2,1,0:T(1,128)S(1)} %get-tuple-element.295), channel_id=1, source_target_pairs={{1,0},{2,1},{3,2},{5,4},{6,5},{7,6},{9,8},{10,9},{11,10},{13,12},{... | collective-permute-start | bytes 24584 | tf_op jit(solution)/shard_map/while/body/eval_jaxpr/ppermute | solution.py:21
  185.1 7.1 %collective-permute-start.1 = (f32[1,1,2048]{2,1,0:T(1,128)S(1)}, f32[1,1,2048]{2,1,0:T(1,128)S(1)}, u32[]{:S(2)}, u32[]{:S(2)}) collective-permute-start(f32[1,1,2048]{2,1,0:T(1,128)S(1)} %get-tuple-element.296), channel_id=1, source_target_pairs={{0,1},{1,2},{2,3},{4,5},{5,6},{6,7},{8,9},{9,10},{10,11},{12,13},{... | collective-permute-start | bytes 24584 | tf_op jit(solution)/shard_map/while/body/eval_jaxpr/ppermute | solution.py:18
  192.5 6.2 %collective-permute-start.2 = (f32[1,16,2048]{2,1,0:T(8,128)S(1)}, f32[1,16,2048]{2,1,0:T(8,128)S(1)}, u32[]{:S(2)}, u32[]{:S(2)}) collective-permute-start(f32[1,16,2048]{2,1,0:T(8,128)S(1)} %fusion.103), channel_id=1, source_target_pairs={{0,4},{4,8},{8,12},{12,16},{16,20},{20,24},{24,28},{28,0},{1,5},{5... | collective-permute-start | bytes 393224 | tf_op jit(solution)/shard_map/while/body/eval_jaxpr/ppermute | solution.py:28
  198.8 7.0 %collective-permute-start = (f32[1,1,2048]{2,1,0:T(1,128)S(1)}, f32[1,1,2048]{2,1,0:T(1,128)S(1)}, u32[]{:S(2)}, u32[]{:S(2)}) collective-permute-start(f32[1,1,2048]{2,1,0:T(1,128)S(1)} %get-tuple-element.295), channel_id=1, source_target_pairs={{1,0},{2,1},{3,2},{5,4},{6,5},{7,6},{9,8},{10,9},{11,10},{13,12},{... | collective-permute-start | bytes 24584 | tf_op jit(solution)/shard_map/while/body/eval_jaxpr/ppermute | solution.py:21
  200.1 7.1 %collective-permute-start.1 = (f32[1,1,2048]{2,1,0:T(1,128)S(1)}, f32[1,1,2048]{2,1,0:T(1,128)S(1)}, u32[]{:S(2)}, u32[]{:S(2)}) collective-permute-start(f32[1,1,2048]{2,1,0:T(1,128)S(1)} %get-tuple-element.296), channel_id=1, source_target_pairs={{0,1},{1,2},{2,3},{4,5},{5,6},{6,7},{8,9},{9,10},{10,11},{12,13},{... | collective-permute-start | bytes 24584 | tf_op jit(solution)/shard_map/while/body/eval_jaxpr/ppermute | solution.py:18
  207.5 6.2 %collective-permute-start.2 = (f32[1,16,2048]{2,1,0:T(8,128)S(1)}, f32[1,16,2048]{2,1,0:T(8,128)S(1)}, u32[]{:S(2)}, u32[]{:S(2)}) collective-permute-start(f32[1,16,2048]{2,1,0:T(8,128)S(1)} %fusion.103), channel_id=1, source_target_pairs={{0,4},{4,8},{8,12},{12,16},{16,20},{20,24},{24,28},{28,0},{1,5},{5... | collective-permute-start | bytes 393224 | tf_op jit(solution)/shard_map/while/body/eval_jaxpr/ppermute | solution.py:28
  213.8 7.0 %collective-permute-start = (f32[1,1,2048]{2,1,0:T(1,128)S(1)}, f32[1,1,2048]{2,1,0:T(1,128)S(1)}, u32[]{:S(2)}, u32[]{:S(2)}) collective-permute-start(f32[1,1,2048]{2,1,0:T(1,128)S(1)} %get-tuple-element.295), channel_id=1, source_target_pairs={{1,0},{2,1},{3,2},{5,4},{6,5},{7,6},{9,8},{10,9},{11,10},{13,12},{... | collective-permute-start | bytes 24584 | tf_op jit(solution)/shard_map/while/body/eval_jaxpr/ppermute | solution.py:21
  215.1 7.1 %collective-permute-start.1 = (f32[1,1,2048]{2,1,0:T(1,128)S(1)}, f32[1,1,2048]{2,1,0:T(1,128)S(1)}, u32[]{:S(2)}, u32[]{:S(2)}) collective-permute-start(f32[1,1,2048]{2,1,0:T(1,128)S(1)} %get-tuple-element.296), channel_id=1, source_target_pairs={{0,1},{1,2},{2,3},{4,5},{5,6},{6,7},{8,9},{9,10},{10,11},{12,13},{... | collective-permute-start | bytes 24584 | tf_op jit(solution)/shard_map/while/body/eval_jaxpr/ppermute | solution.py:18
  222.5 6.2 %collective-permute-start.2 = (f32[1,16,2048]{2,1,0:T(8,128)S(1)}, f32[1,16,2048]{2,1,0:T(8,128)S(1)}, u32[]{:S(2)}, u32[]{:S(2)}) collective-permute-start(f32[1,16,2048]{2,1,0:T(8,128)S(1)} %fusion.103), channel_id=1, source_target_pairs={{0,4},{4,8},{8,12},{12,16},{16,20},{20,24},{24,28},{28,0},{1,5},{5... | collective-permute-start | bytes 393224 | tf_op jit(solution)/shard_map/while/body/eval_jaxpr/ppermute | solution.py:28
  228.8 7.0 %collective-permute-start = (f32[1,1,2048]{2,1,0:T(1,128)S(1)}, f32[1,1,2048]{2,1,0:T(1,128)S(1)}, u32[]{:S(2)}, u32[]{:S(2)}) collective-permute-start(f32[1,1,2048]{2,1,0:T(1,128)S(1)} %get-tuple-element.295), channel_id=1, source_target_pairs={{1,0},{2,1},{3,2},{5,4},{6,5},{7,6},{9,8},{10,9},{11,10},{13,12},{... | collective-permute-start | bytes 24584 | tf_op jit(solution)/shard_map/while/body/eval_jaxpr/ppermute | solution.py:21
  230.1 7.1 %collective-permute-start.1 = (f32[1,1,2048]{2,1,0:T(1,128)S(1)}, f32[1,1,2048]{2,1,0:T(1,128)S(1)}, u32[]{:S(2)}, u32[]{:S(2)}) collective-permute-start(f32[1,1,2048]{2,1,0:T(1,128)S(1)} %get-tuple-element.296), channel_id=1, source_target_pairs={{0,1},{1,2},{2,3},{4,5},{5,6},{6,7},{8,9},{9,10},{10,11},{12,13},{... | collective-permute-start | bytes 24584 | tf_op jit(solution)/shard_map/while/body/eval_jaxpr/ppermute | solution.py:18
  237.5 6.2 %collective-permute-start.2 = (f32[1,16,2048]{2,1,0:T(8,128)S(1)}, f32[1,16,2048]{2,1,0:T(8,128)S(1)}, u32[]{:S(2)}, u32[]{:S(2)}) collective-permute-start(f32[1,16,2048]{2,1,0:T(8,128)S(1)} %fusion.103), channel_id=1, source_target_pairs={{0,4},{4,8},{8,12},{12,16},{16,20},{20,24},{24,28},{28,0},{1,5},{5... | collective-permute-start | bytes 393224 | tf_op jit(solution)/shard_map/while/body/eval_jaxpr/ppermute | solution.py:28
  243.8 7.1 %collective-permute-start.23 = (f32[1,1,2048]{2,1,0:T(1,128)S(1)}, f32[1,1,2048]{2,1,0:T(1,128)S(1)}, u32[]{:S(2)}, u32[]{:S(2)}) collective-permute-start(f32[1,1,2048]{2,1,0:T(1,128)S(1)} %get-tuple-element.249), channel_id=1, source_target_pairs={{1,0},{2,1},{3,2},{5,4},{6,5},{7,6},{9,8},{10,9},{11,10},{13,12},{... | collective-permute-start | bytes 24584 | tf_op jit(solution)/shard_map/ppermute | solution.py:21
  245.1 7.1 %collective-permute-start.22 = (f32[1,1,2048]{2,1,0:T(1,128)S(1)}, f32[1,1,2048]{2,1,0:T(1,128)S(1)}, u32[]{:S(2)}, u32[]{:S(2)}) collective-permute-start(f32[1,1,2048]{2,1,0:T(1,128)S(1)} %get-tuple-element.248), channel_id=1, source_target_pairs={{0,1},{1,2},{2,3},{4,5},{5,6},{6,7},{8,9},{9,10},{10,11},{12,13},{... | collective-permute-start | bytes 24584 | tf_op jit(solution)/shard_map/ppermute | solution.py:18
  252.6 7.1 %collective-permute-start.25 = (f32[2,1,2048]{2,1,0:T(1,128)S(1)}, f32[2,1,2048]{2,1,0:T(1,128)S(1)}, u32[]{:S(2)}, u32[]{:S(2)}) collective-permute-start(f32[2,1,2048]{2,1,0:T(1,128)S(1)} %get-tuple-element.237), channel_id=1, source_target_pairs={{1,0},{2,1},{3,2},{5,4},{6,5},{7,6},{9,8},{10,9},{11,10},{13,12},{... | collective-permute-start | bytes 49160 | tf_op jit(solution)/shard_map/ppermute | solution.py:21
  253.9 7.1 %collective-permute-start.24 = (f32[2,1,2048]{2,1,0:T(1,128)S(1)}, f32[2,1,2048]{2,1,0:T(1,128)S(1)}, u32[]{:S(2)}, u32[]{:S(2)}) collective-permute-start(f32[2,1,2048]{2,1,0:T(1,128)S(1)} %get-tuple-element.236), channel_id=1, source_target_pairs={{0,1},{1,2},{2,3},{4,5},{5,6},{6,7},{8,9},{9,10},{10,11},{12,13},{... | collective-permute-start | bytes 49160 | tf_op jit(solution)/shard_map/ppermute | solution.py:18
  261.7 7.0 %collective-permute-start.27 = (f32[4,1,2048]{2,1,0:T(1,128)S(1)}, f32[4,1,2048]{2,1,0:T(1,128)S(1)}, u32[]{:S(2)}, u32[]{:S(2)}) collective-permute-start(f32[4,1,2048]{2,1,0:T(1,128)S(1)} %get-tuple-element.227), channel_id=1, source_target_pairs={{1,0},{2,1},{3,2},{5,4},{6,5},{7,6},{9,8},{10,9},{11,10},{13,12},{... | collective-permute-start | bytes 98312 | tf_op jit(solution)/shard_map/ppermute | solution.py:21
  263.0 7.3 %collective-permute-start.26 = (f32[4,1,2048]{2,1,0:T(1,128)S(1)}, f32[4,1,2048]{2,1,0:T(1,128)S(1)}, u32[]{:S(2)}, u32[]{:S(2)}) collective-permute-start(f32[4,1,2048]{2,1,0:T(1,128)S(1)} %get-tuple-element.226), channel_id=1, source_target_pairs={{0,1},{1,2},{2,3},{4,5},{5,6},{6,7},{8,9},{9,10},{10,11},{12,13},{... | collective-permute-start | bytes 98312 | tf_op jit(solution)/shard_map/ppermute | solution.py:18
where the time goes:
time: 275 us; the launch traced here: 272 us
  waiting for transfers between devices  127 us (46%)
  starting transfers between devices  125 us (45%)
  other arithmetic  13.7 us (5%)
  local copies, waits for them, and re-layouts  5.2 us (2%)
    ppermute x17, starting transfers between devices, padded_2(): lax.ppermute(lax.slice_in_dim(block, block.shape[dim] - width, None, axis...  102 us
    ppermute x15, waiting for transfers between devices, from_behind(): lax.ppermute(array, axis, [(i, (i + by) % peers) for i in range(peers)])  89.4 us
    ppermute x17, starting transfers between devices, padded_2(): lax.ppermute(lax.slice_in_dim(block, 0, width, axis=dim), axis, backward)  22 us
    ppermute x17, waiting for transfers between devices, padded_2(): lax.ppermute(lax.slice_in_dim(block, block.shape[dim] - width, None, axis...  20 us
    ppermute x17, waiting for transfers between devices, padded_2(): lax.ppermute(lax.slice_in_dim(block, 0, width, axis=dim), axis, backward)  17.5 us
  transfers between devices with their start and end apart: 49, of which 36 were waited for; matrix products, arithmetic and copies ran while one was open for 0% of the time, Pallas kernels for 0%

commit v1 on v0

v1 whole, which is shorter than its diff:
```python
import functools

import jax
import jax.numpy as jnp
from jax import lax
from jax.experimental import pallas as pl
from jax.experimental.pallas import tpu as pltpu
from jax.sharding import PartitionSpec as P

LANES = 128
MARGIN = 4
REACH = 32
UP_RIM = 3
POINTS = 8
diffusion_number = 0.03
time_step = 0.02

RIMS_0 = (
    ("e0", 4), ("e1", 4), ("e2", 4),
    ("o0", 3), ("o1", 3), ("o2", 3), ("o3", 1),
    ("s0", 2), ("s1", 2), ("s2", 2), ("s3", 2),
    ("d", 3), ("g", 3),
)
CORES = ("e0", "e1", "e2", "o0", "o1", "o2", "o3", "s0", "s1", "s2", "s3", "d", "g")
BEHIND_0 = (("ep", 4), ("op", 3))
BEHIND = (("pair", 2), ("odd", 3))


def count(rims):
    return sum(rows for _, rows in rims)


def params(mib=16):
    return pltpu.CompilerParams(vmem_limit_bytes=mib * 2**20)


def call(kernel, outs, scratch, *args, mib=16):
    return pl.pallas_call(
        kernel,
        out_shape=tuple(jax.ShapeDtypeStruct(shape, jnp.float32) for shape in outs),
        in_specs=[pl.BlockSpec(memory_space=pltpu.VMEM)] * len(args),
        out_specs=tuple(pl.BlockSpec(memory_space=pltpu.VMEM) for _ in outs),
        scratch_shapes=[pltpu.VMEM(shape, jnp.float32) for shape in scratch],
        compiler_params=params(mib),
    )(*args)


def beside(mid):
    depth = mid.shape[1]
    lane = lax.broadcasted_iota(jnp.int32, mid.shape, 2)
    line = lax.broadcasted_iota(jnp.int32, mid.shape, 1)
    left = pltpu.roll(mid, 1, 2)
    left_turn = pltpu.roll(left, 1, 1)
    right = pltpu.roll(mid, LANES - 1, 2)
    right_turn = pltpu.roll(right, depth - 1, 1)
    left = jnp.where(lane == 0, jnp.where(line == 0, 0.0, left_turn), left)
    right = jnp.where(lane == LANES - 1, jnp.where(line == depth - 1, 0.0, right_turn), right)
    return left + right


def growth_of(ref, at, rows, diff, grow):
    wide = ref[pl.ds(at - 1, rows + 2)]
    mid = wide[1:-1]
    laplace = wide[:-2] + wide[2:] + beside(mid) - 4.0 * mid
    return mid, diff * laplace + grow * mid / (1.0 + mid * mid)


def over_rows(rows, rim, body, step=2):
    lax.fori_loop(
        0, (rows + 2 * rim) // step, lambda i, _: (body(MARGIN - rim + i * step), 0)[1], 0
    )


def flags():
    slab = lax.axis_index("space")
    low = jnp.where(slab > 0, 1.0, 0.0).astype(jnp.float32)
    high = jnp.where(slab < lax.axis_size("space") - 1, 1.0, 0.0).astype(jnp.float32)
    return low, high


def set_rims(buffer, rows, rim, low_rows, high_rows, low, high, inner=0):
    width = rim - inner
    buffer[pl.ds(MARGIN - rim, width)] = low_rows * low
    buffer[pl.ds(MARGIN + rows + inner, width)] = high_rows * high


def pieces(name, initial, source, diffusivity, growth):
    if name == "d":
        return lambda rows, cols: diffusivity[rows, cols] * diffusion_number
    if name == "g":
        return lambda rows, cols: growth[rows, cols] * time_step
    if name == "ep":
        return lambda rows, cols: initial[POINTS - 2, rows, cols]
    if name == "op":
        return lambda rows, cols: source[POINTS - 1, rows, cols]
    which = int(name[1])
    if name[0] == "e":
        return lambda rows, cols: initial[2 * which, rows, cols]
    return lambda rows, cols: source[2 * which + (name[0] == "o"), rows, cols]


def pack_kernel(initial, source, diffusivity, growth, down, up, turn, slant_down, slant_up):
    rows, cols = diffusivity.shape
    depth = cols // LANES
    for rims, low, high in ((RIMS_0, down, up), (BEHIND_0, slant_down, slant_up)):
        at = 0
        for name, rim in rims:
            get = pieces(name, initial, source, diffusivity, growth)
            for c in range(depth):
                lanes = pl.ds(c * LANES, LANES)
                place = pl.ds(at * depth + c, rim, stride=depth)
                low[place, :] = get(pl.ds(rows - rim, rim), lanes)
                high[place, :] = get(pl.ds(0, rim), lanes)
            at += rim
    for index, (name, _) in enumerate(BEHIND_0):
        get = pieces(name, initial, source, diffusivity, growth)
        for c in range(depth):
            for r in range(0, rows, 8):
                place = pl.ds((index * rows + r) * depth + c, 8, stride=depth)
                turn[place, :] = get(pl.ds(r, 8), pl.ds(c * LANES, LANES))


def window(get, first, depth):
    line, offset = first // LANES, first % LANES
    shape = get(0).shape
    source = lax.broadcasted_iota(jnp.int32, shape, 1) + (offset - REACH)
    shift = (REACH - offset) % LANES
    before = jnp.where(line > 0, pltpu.roll(get(jnp.maximum(line - 1, 0)), shift, 1), 0.0)
    here = pltpu.roll(get(line), shift, 1)
    after = jnp.where(
        line < depth - 1, pltpu.roll(get(jnp.minimum(line + 1, depth - 1)), shift, 1), 0.0
    )
    return jnp.where(source < 0, before, jnp.where(source >= LANES, after, here))


def core_kernel(share, initial, source, diffusivity, growth, core, back, windows):
    rows, cols = diffusivity.shape
    depth = cols // LANES
    for index, name in enumerate(CORES):
        get = pieces(name, initial, source, diffusivity, growth)
        for c in range(depth):
            for r in range(0, rows, 8):
                value = get(pl.ds(r, 8), pl.ds(c * LANES, LANES))
                core[pl.ds((index * rows + r) * depth + c, 8, stride=depth), :] = value
                if name == "s0":
                    back[pl.ds(r * depth + c, 8, stride=depth), :] = value
    block = lax.axis_index("tm") * lax.axis_size("space")
    for target in range(windows.shape[0]):
        first = (block + target) * share
        for which, name in enumerate(("d", "g")):
            start = CORES.index(name) * rows * depth
            get = lambda line: core[pl.ds(start + line, rows, stride=depth), :]
            windows[target, which] = window(get, first, depth)


def split(ref, rims):
    at, out = 0, {}
    for name, rim in rims:
        out[name] = ref[pl.ds(at, rim)]
        at += rim
    return out


def level0_kernel(
    core, above, below, behind, behind_above, behind_below,
    turn, down, up, slant_down, slant_up, state, forcing, first_forcing, coefs,
    fields, diff, grow,
):
    rows = core.shape[0] // len(CORES)
    low, high = flags()
    names = list(CORES) + ["ep", "op"]
    spots = {name: index for index, name in enumerate(names)}
    for rims, from_low, from_high in (
        (RIMS_0, above, below),
        (BEHIND_0, behind_above, behind_below),
    ):
        lows, highs = split(from_low, rims), split(from_high, rims)
        for name, rim in rims:
            if name in ("d", "g"):
                buffer = diff if name == "d" else grow
            else:
                buffer = fields.at[spots[name]]
            set_rims(buffer, rows, rim, lows[name], highs[name], low, high)
    for name in CORES:
        if name in ("d", "g"):
            buffer = diff if name == "d" else grow
        else:
            buffer = fields.at[spots[name]]
        buffer[pl.ds(MARGIN, rows)] = core[pl.ds(CORES.index(name) * rows, rows)]
    for index, (name, _) in enumerate(BEHIND_0):
        fields[spots[name], pl.ds(MARGIN, rows)] = behind[pl.ds(index * rows, rows)]
    extra = len(names)
    halves = POINTS // 2
    odd = [extra + i for i in range(halves)]
    even = [extra + halves + i for i in range(halves)]
    image = [extra + 2 * halves + i for i in range(halves)]

    def first(at):
        d, g = diff[pl.ds(at, 2)], grow[pl.ds(at, 2)]
        for i in range(halves):
            start, term = ("ep", "op") if i == 0 else (f"e{i - 1}", f"o{i - 1}")
            mid, slope = growth_of(fields.at[spots[start]], at, 2, d, g)
            fields[odd[i], pl.ds(at, 2)] = mid + slope + fields[spots[term], pl.ds(at, 2)]

    def second(at):
        d, g = diff[pl.ds(at, 2)], grow[pl.ds(at, 2)]
        for i in range(halves):
            mid, slope = growth_of(fields.at[odd[i]], at, 2, d, g)
            fields[even[i], pl.ds(at, 2)] = mid + slope + fields[spots[f"s{i}"], pl.ds(at, 2)]

    def third(at):
        d, g = diff[pl.ds(at, 2)], grow[pl.ds(at, 2)]
        for i in range(halves):
            mid, slope = growth_of(fields.at[even[i]], at, 2, d, g)
            fields[odd[i], pl.ds(at, 2)] = mid + slope + fields[spots[f"o{i}"], pl.ds(at, 2)]
            fields[image[i], pl.ds(at, 2)] = mid + 2.0 * slope

    def fourth(at):
        d, g = diff[pl.ds(at, 2)], grow[pl.ds(at, 2)]
        here = at - MARGIN
        for i in range(halves):
            mid, slope = growth_of(fields.at[odd[i]], at, 2, d, g)
            pair = mid + slope - fields[image[i], pl.ds(at, 2)]
            if i == halves - 1:
                turn[pl.ds(here, 2)] = pair
            else:
                term = fields[spots[f"s{i + 1}"], pl.ds(at, 2)] + pair
                forcing[pl.ds(i * rows + here, 2)] = term
                if i == halves - 2:
                    turn[pl.ds(rows + here, 2)] = fields[image[i], pl.ds(at, 2)] + term

    over_rows(rows, 3, first)
    over_rows(rows, 2, second)
    over_rows(rows, 1, third)
    over_rows(rows, 0, fourth)
    state[...] = fields[even[0], pl.ds(MARGIN - 2, rows + 4)]
    first_forcing[...] = fields[spots["s0"], pl.ds(MARGIN - 2, rows + 4)]
    coefs[pl.ds(0, rows + 6)] = diff[pl.ds(MARGIN - 3, rows + 6)]
    coefs[pl.ds(rows + 6, rows + 6)] = grow[pl.ds(MARGIN - 3, rows + 6)]
    send_behind(turn, slant_down, slant_up, rows)
    down[pl.ds(0, 2)] = fields[even[0], pl.ds(MARGIN + rows - 4, 2)]
    up[pl.ds(0, 2)] = fields[even[0], pl.ds(MARGIN + 2, 2)]
    at = 2
    for which, rim in ((0, 3), (2, 1), (1, 2)):
        down[pl.ds(at, rim)] = forcing[pl.ds((which + 1) * rows - rim, rim)]
        up[pl.ds(at, rim)] = forcing[pl.ds(which * rows, rim)]
        at += rim


RIMS_1 = (("state", 2), ("g1", 3), ("g3", 1), ("g2", 2))


def send_behind(turn, slant_down, slant_up, rows):
    at = 0
    for index, (_, rim) in enumerate(BEHIND):
        slant_down[pl.ds(at, rim)] = turn[pl.ds((index + 1) * rows - rim, rim)]
        slant_up[pl.ds(at, rim)] = turn[pl.ds(index * rows, rim)]
        at += rim


def take_behind(rows, buffers, behind, behind_above, behind_below, low, high):
    lows, highs = split(behind_above, BEHIND), split(behind_below, BEHIND)
    for index, (name, rim) in enumerate(BEHIND):
        buffer = buffers[index]
        set_rims(buffer, rows, rim, lows[name], highs[name], low, high)
        buffer[pl.ds(MARGIN, rows)] = behind[pl.ds(index * rows, rows)]


def take_coefs(rows, coefs, diff, grow):
    diff[pl.ds(MARGIN - 3, rows + 6)] = coefs[pl.ds(0, rows + 6)]
    grow[pl.ds(MARGIN - 3, rows + 6)] = coefs[pl.ds(rows + 6, rows + 6)]


def level1_kernel(
    state, forcing, first_forcing, coefs, above, below, behind, behind_above, behind_below,
    turn, down, up, slant_down, slant_up, next_first, next_forcing, late_a, late_b,
    fields, diff, grow,
):
    rows = forcing.shape[0] // 3
    low, high = flags()
    take_coefs(rows, coefs, diff, grow)
    v, g1, g3, g2, g0, pair, before, after, even0, even1, image0, image1, odd0, odd1 = range(14)
    lows, highs = split(above, RIMS_1), split(below, RIMS_1)
    for name, spot, rim, inner in (
        ("state", v, 4, 2), ("g1", g1, 3, 0), ("g3", g3, 1, 0), ("g2", g2, 2, 0),
    ):
        set_rims(fields.at[spot], rows, rim, lows[name], highs[name], low, high, inner)
    fields[v, pl.ds(MARGIN - 2, rows + 4)] = state[...]
    for which, spot in enumerate((g1, g2, g3)):
        fields[spot, pl.ds(MARGIN, rows)] = forcing[pl.ds(which * rows, rows)]
    take_behind(
        rows, (fields.at[pair], fields.at[before]), behind, behind_above, behind_below, low, high
    )
    fields[g0, pl.ds(MARGIN - 2, rows + 4)] = (
        first_forcing[...] + fields[pair, pl.ds(MARGIN - 2, rows + 4)]
    )

    def first(at):
        mid, slope = growth_of(fields.at[v], at, 2, diff[pl.ds(at, 2)], grow[pl.ds(at, 2)])
        fields[after, pl.ds(at, 2)] = mid + 2.0 * slope + fields[g1, pl.ds(at, 2)]

    def second(at):
        d, g = diff[pl.ds(at, 2)], grow[pl.ds(at, 2)]
        for start, term, end in ((before, g0, even0), (after, g2, even1)):
            mid, slope = growth_of(fields.at[start], at, 2, d, g)
            fields[end, pl.ds(at, 2)] = mid + 2.0 * slope + fields[term, pl.ds(at, 2)]

    def third(at):
        d, g = diff[pl.ds(at, 2)], grow[pl.ds(at, 2)]
        for start, term, end, image in ((even0, g1, odd0, image0), (even1, g3, odd1, image1)):
            mid, slope = growth_of(fields.at[start], at, 2, d, g)
            fields[end, pl.ds(at, 2)] = mid + 2.0 * slope + fields[term, pl.ds(at, 2)]
            fields[image, pl.ds(at, 2)] = mid + 4.0 * slope

    def fourth(at):
        d, g = diff[pl.ds(at, 2)], grow[pl.ds(at, 2)]
        here = at - MARGIN
        mid, slope = growth_of(fields.at[odd1], at, 2, d, g)
        turn[pl.ds(here, 2)] = mid + 2.0 * slope - fields[image1, pl.ds(at, 2)]
        mid, slope = growth_of(fields.at[odd0], at, 2, d, g)
        image = fields[image0, pl.ds(at, 2)]
        term = fields[g2, pl.ds(at, 2)] + (mid + 2.0 * slope - image)
        next_forcing[pl.ds(here, 2)] = term
        turn[pl.ds(rows + here, 2)] = image + term

    over_rows(rows, 3, first)
    over_rows(rows, 2, second)
    over_rows(rows, 1, third)
    over_rows(rows, 0, fourth)
    next_first[...] = fields[g0, pl.ds(MARGIN - 2, rows + 4)]
    late_a[...] = fields[g1, pl.ds(MARGIN - 1, rows + 2)]
    late_b[...] = fields[g3, pl.ds(MARGIN - 1, rows + 2)]
    send_behind(turn, slant_down, slant_up, rows)
    down[...] = next_forcing[pl.ds(rows - 2, 2)]
    up[...] = next_forcing[pl.ds(0, 2)]


def level2_kernel(
    share, next_first, next_forcing, coefs, above, below, behind, behind_above, behind_below,
    ahead, pair0, pair1, slots, wide_forcing, fields, diff, grow, flat,
):
    rows = next_forcing.shape[0]
    depth = next_forcing.shape[1]
    low, high = flags()
    take_coefs(rows, coefs, diff, grow)
    g1, g0, pair, before, even, image, odd = range(7)
    set_rims(fields.at[g1], rows, 2, above[...], below[...], low, high)
    fields[g1, pl.ds(MARGIN, rows)] = next_forcing[...]
    take_behind(
        rows, (fields.at[pair], fields.at[before]), behind, behind_above, behind_below, low, high
    )
    fields[g0, pl.ds(MARGIN - 2, rows + 4)] = (
        next_first[...] + fields[pair, pl.ds(MARGIN - 2, rows + 4)]
    )
    wide_forcing[...] = fields[g1, pl.ds(MARGIN - 2, rows + 4)]
    last = lax.axis_index("tm") == lax.axis_size("tm") - 1

    def second(at):
        mid, slope = growth_of(fields.at[before], at, 2, diff[pl.ds(at, 2)], grow[pl.ds(at, 2)])
        fields[even, pl.ds(at, 2)] = mid + 4.0 * slope + fields[g0, pl.ds(at, 2)]

    def third(at):
        mid, slope = growth_of(fields.at[even], at, 2, diff[pl.ds(at, 2)], grow[pl.ds(at, 2)])
        fields[odd, pl.ds(at, 2)] = mid + 4.0 * slope + fields[g1, pl.ds(at, 2)]
        fields[image, pl.ds(at, 2)] = mid + 8.0 * slope

    def fourth(at):
        here = at - MARGIN
        mid, slope = growth_of(fields.at[odd], at, 2, diff[pl.ds(at, 2)], grow[pl.ds(at, 2)])
        stepped = fields[image, pl.ds(at, 2)]
        term = (
            ahead[pl.ds(here, 2)]
            + pair0[pl.ds(here, 2)]
            + pair1[pl.ds(here, 2)]
            + (mid + 4.0 * slope - stepped)
        )
        term = term + jnp.where(last, stepped, 0.0)
        for i in range(2):
            flat[pl.ds(pl.multiple_of((here + i) * depth, depth), depth), :] = term[i]

    over_rows(rows, 2, second)
    over_rows(rows, 1, third)
    over_rows(rows, 0, fourth)
    lines = [flat[pl.ds(line, rows, stride=depth), :] for line in range(depth)]
    lane = lax.broadcasted_iota(jnp.int32, (rows, LANES), 1)
    for target in range(slots.shape[0]):
        line, offset = target * share // LANES, target * share % LANES
        shift = (REACH - offset) % LANES
        place = lane + (offset - REACH)
        value = pltpu.roll(lines[line], shift, 1)
        if offset < REACH:
            before_line = pltpu.roll(lines[line - 1], shift, 1) if line > 0 else 0.0
            value = jnp.where(place < 0, before_line, value)
        if offset - REACH + LANES > LANES:
            after_line = pltpu.roll(lines[line + 1], shift, 1) if line < depth - 1 else 0.0
            value = jnp.where(place >= LANES, after_line, value)
        slots[target] = value


def packing(rows, share):
    groups = LANES // share
    each = -(-(rows + 2 * UP_RIM) // groups)
    return groups, each, -(-each // 8) * 8


def sweep_kernel(share, slabs, arrived, windows, slots, padded):
    devices, rows, _ = arrived.shape
    blocks = devices // slabs
    total = slabs * rows
    groups, each, held = packing(rows, share)
    diff = jnp.concatenate([windows[slab, 0] for slab in range(slabs)], axis=0)
    grow = jnp.concatenate([windows[slab, 1] for slab in range(slabs)], axis=0)
    line = lax.broadcasted_iota(jnp.int32, (total, LANES), 0)
    lane = lax.broadcasted_iota(jnp.int32, (held, LANES), 1)
    padded[...] = jnp.zeros(padded.shape, jnp.float32)

    def block(index):
        return jnp.concatenate([arrived[index * slabs + slab] for slab in range(slabs)], axis=0)

    field = block(blocks - 1)
    for index in range(blocks):
        for group in range(groups):
            padded[group, pl.ds(8, total), :] = pltpu.roll(
                field, (group * share - REACH) % LANES, 1
            )
        for slab in range(slabs):
            start = 8 + slab * rows - UP_RIM
            value = padded[0, pl.ds(start, held), :]
            for group in range(1, groups):
                piece = padded[group, pl.ds(start + group * each, held), :]
                value = jnp.where(lane >= group * share, piece, value)
            slots[index * slabs + slab] = value
        if index < blocks - 1:
            north = jnp.where(line == 0, 0.0, pltpu.roll(field, 1, 0))
            south = jnp.where(line == total - 1, 0.0, pltpu.roll(field, total - 1, 0))
            sides = pltpu.roll(field, 1, 1) + pltpu.roll(field, LANES - 1, 1)
            laplace = north + south + sides - 4.0 * field
            slope = diff * laplace + grow * field / (1.0 + field * field)
            field = field + 8.0 * slope + block(index)


def up_kernel(
    share, arrived, wide_forcing, late_a, late_b, core, coefs, out, fields, diff, grow, flat
):
    rows = wide_forcing.shape[0] - 4
    depth = wide_forcing.shape[1]
    groups, each, held = packing(rows, share)
    take_coefs(rows, coefs, diff, grow)
    lane = lax.broadcasted_iota(jnp.int32, (depth, LANES), 1)
    for row in range(rows + 2 * UP_RIM):
        group, line = row // each, row % each
        value = None
        for part in range(groups):
            piece = arrived[pl.ds(part * held + line, depth, stride=groups * held), :]
            piece = pltpu.roll(piece, ((part - group) * share) % LANES, 1) if part != group else piece
            value = piece if value is None else jnp.where(lane >= part * share, piece, value)
        fields[0, MARGIN - UP_RIM + row] = value
    odd_first = CORES.index("o0") * rows

    def put(spot, here, value):
        for i in range(2):
            place = (spot * rows + here + i) * depth
            flat[pl.ds(pl.multiple_of(place, depth), depth), :] = value[i]

    def first(at):
        mid, slope = growth_of(fields.at[0], at, 2, diff[pl.ds(at, 2)], grow[pl.ds(at, 2)])
        fields[2, pl.ds(at, 2)] = mid + 4.0 * slope + wide_forcing[pl.ds(at - MARGIN + 2, 2)]

    def second(at):
        d, g = diff[pl.ds(at, 2)], grow[pl.ds(at, 2)]
        for start, late in ((0, late_a), (2, late_b)):
            mid, slope = growth_of(fields.at[start], at, 2, d, g)
            fields[start + 1, pl.ds(at, 2)] = mid + 2.0 * slope + late[pl.ds(at - MARGIN + 1, 2)]

    def third(at):
        d, g = diff[pl.ds(at, 2)], grow[pl.ds(at, 2)]
        here = at - MARGIN
        for i in range(POINTS // 2):
            mid, slope = growth_of(fields.at[i], at, 2, d, g)
            put(2 * i, here, mid)
            put(2 * i + 1, here, mid + slope + core[pl.ds(odd_first + i * rows + here, 2)])

    over_rows(rows, 2, first)
    over_rows(rows, 1, second)
    over_rows(rows, 0, third)
    for point in range(POINTS):
        for r in range(0, rows, 8):
            for c in range(depth):
                start = (point * rows + r) * depth + c
                out[point, pl.ds(r, 8), pl.ds(c * LANES, LANES)] = flat[
                    pl.ds(start, 8, stride=depth), :
                ]


def moved(array, blocks, slabs):
    tm, space = lax.axis_size("tm"), lax.axis_size("space")
    pairs = [
        (t * space + s, (t + blocks) % tm * space + (s + slabs) % space)
        for t in range(tm)
        for s in range(space)
    ]
    return lax.ppermute(array, ("tm", "space"), pairs)


def exchange(down, up, turn, slant_down, slant_up):
    return (
        moved(down, 0, 1), moved(up, 0, -1), moved(turn, 1, 0),
        moved(slant_down, 1, 1), moved(slant_up, 1, -1),
    )


def body(initial, source, diffusivity, growth):
    points, rows, cols = initial.shape
    assert points == POINTS and rows % 8 == 0 and cols % LANES == 0
    depth = cols // LANES
    tm, space = lax.axis_size("tm"), lax.axis_size("space")
    devices = tm * space
    share = cols // devices
    assert share * devices == cols and LANES % share == 0
    assert tm - 1 <= REACH and REACH + share + tm - 1 <= LANES
    groups, each, held = packing(rows, share)
    wide = rows + 2 * MARGIN

    def lines(n):
        return (n * depth, LANES)

    def field(n):
        return (n, depth, LANES)

    def as_rows(array):
        return array.reshape(-1, depth, LANES)

    sides, behind = count(RIMS_0), count(BEHIND_0)
    sends = call(
        pack_kernel,
        [lines(sides), lines(sides), lines(2 * rows), lines(behind), lines(behind)],
        [],
        initial, source, diffusivity, growth,
    )
    core, back, windows = call(
        functools.partial(core_kernel, share),
        [lines(len(CORES) * rows), lines(rows), (space, 2, rows, LANES)],
        [],
        initial, source, diffusivity, growth,
    )
    arrived = exchange(*(as_rows(part) for part in sends))
    ahead = as_rows(moved(back, -1, 0))
    core = as_rows(core)
    slab = lax.axis_index("space")
    kept = [lax.dynamic_index_in_dim(windows, slab, 0, keepdims=False)]
    for by in range(1, space):
        piece = lax.dynamic_index_in_dim(windows, (slab + by) % space, 0, keepdims=False)
        kept.append(moved(piece, 0, by))
    order = (slab - jnp.arange(space)) % space
    coef_windows = jnp.take(jnp.stack(kept), order, axis=0)

    buffers = [(wide, depth, LANES), (wide, depth, LANES)]
    rim1, rimb = count(RIMS_1), count(BEHIND)
    turn, down, up, slant_down, slant_up, state, forcing, first_forcing, coefs = call(
        level0_kernel,
        [
            field(2 * rows), field(rim1), field(rim1), field(rimb), field(rimb),
            field(rows + 4), field(3 * rows), field(rows + 4), field(2 * (rows + 6)),
        ],
        [(len(CORES) + 2 + 3 * (POINTS // 2), wide, depth, LANES)] + buffers,
        core, *arrived,
    )
    pair0 = turn[:rows]
    arrived = exchange(down, up, turn, slant_down, slant_up)
    turn, down, up, slant_down, slant_up, next_first, next_forcing, late_a, late_b = call(
        level1_kernel,
        [
            field(2 * rows), field(2), field(2), field(rimb), field(rimb),
            field(rows + 4), field(rows), field(rows + 2), field(rows + 2),
        ],
        [(14, wide, depth, LANES)] + buffers,
        state, forcing, first_forcing, coefs, *arrived,
    )
    pair1 = turn[:rows]
    arrived = exchange(down, up, turn, slant_down, slant_up)
    slots, wide_forcing = call(
        functools.partial(level2_kernel, share),
        [(devices, rows, LANES), field(rows + 4)],
        [(7, wide, depth, LANES)] + buffers + [(rows * depth, LANES)],
        next_first, next_forcing, coefs, *arrived, ahead, pair0, pair1,
    )
    slots = lax.all_to_all(slots, ("tm", "space"), 0, 0, tiled=True)
    (slots,) = call(
        functools.partial(sweep_kernel, share, space),
        [(devices, held, LANES)],
        [(groups, 8 + space * rows + 2 * rows + held, LANES)],
        slots, coef_windows,
    )
    slots = lax.all_to_all(slots, ("tm", "space"), 0, 0, tiled=True)
    (out,) = call(
        functools.partial(up_kernel, share),
        [(points, rows, cols)],
        [(4, wide, depth, LANES)] + buffers + [(points * rows * depth, LANES)],
        slots.reshape(devices * held, LANES), wide_forcing, late_a, late_b, core, coefs,
    )
    return out


def solution(mesh):
    placed = (P("tm", "space", None), P("tm", "space", None), P("space", None), P("space", None))
    return jax.shard_map(
        body, mesh=mesh, in_specs=placed, out_specs=P("tm", "space", None), check_vma=False
    )
```

time: 275 us -> 95.6 us (0.35)
  waiting for transfers between devices: 127 us -> 25.3 us
  starting transfers between devices: 125 us -> 30.4 us
  Pallas kernels: 0 us -> 18.9 us
  other arithmetic: 13.7 us -> 0.7 us
  blocking collectives: 0 us -> 12.8 us
    ppermute x49 -> x19, waiting for transfers between devices: 127 us -> 15.1 us  [moved(): return lax.ppermute(array, ('tm', 'space'), pairs)]
    ppermute x49 -> x19, starting transfers between devices: 125 us -> 25.4 us  [moved(): return lax.ppermute(array, ('tm', 'space'), pairs)]
    pallas_call x0 -> x7, Pallas kernels: none -> 18.9 us  [call(): pl.pallas_call(kernel, out_shape=tuple((jax.ShapeDtypeStruct(shape, jnp.f...]
    all_to_all x0 -> x1, blocking collectives: none -> 12.8 us  [body(): slots = lax.all_to_all(slots, ('tm', 'space'), 0, 0, tiled=True)]
    all_to_all x0 -> x1, waiting for transfers between devices: none -> 10.2 us  [body(): slots = lax.all_to_all(slots, ('tm', 'space'), 0, 0, tiled=True)]
    all_to_all x0 -> x1, starting transfers between devices: none -> 5.02 us  [body(): slots = lax.all_to_all(slots, ('tm', 'space'), 0, 0, tiled=True)]
    concatenate x22 -> x0, other arithmetic: 4.63 us -> none  [the longest x17 4.38 us: padded_2(): block = jnp.concatenate([low, block, high], axis=dim)]
    mul x12 -> x0, other arithmetic: 3.38 us -> none  [the longest x4 1.62 us: relax_wide(): (stencil_local(even_wide, factor, diff_wide, grow_wide) + odd_terms) * in...]
  transfers between devices with their start and end apart: 49 -> 20, of which waited for: 36 -> 6; matrix products, arithmetic and copies ran while one was open for 0% -> 3% of each run, Pallas kernels for 0% -> 5%
where the time goes in v1:
time: 95.6 us; the launch traced here: 95.2 us
  starting transfers between devices  30.4 us (32%)
  waiting for transfers between devices  25.3 us (26%)
  Pallas kernels  18.9 us (20%)
  blocking collectives  12.8 us (13%)
  local copies, waits for them, and re-layouts  6.97 us (7%)
    ppermute x19, starting transfers between devices, moved(): return lax.ppermute(array, ('tm', 'space'), pairs)  25.4 us
    pallas_call x7, Pallas kernels, call(): pl.pallas_call(kernel, out_shape=tuple((jax.ShapeDtypeStruct(shape, jnp.f...  18.9 us
    ppermute x19, waiting for transfers between devices, moved(): return lax.ppermute(array, ('tm', 'space'), pairs)  15.1 us
    all_to_all x1, blocking collectives, body(): slots = lax.all_to_all(slots, ('tm', 'space'), 0, 0, tiled=True)  12.8 us
    all_to_all x1, waiting for transfers between devices, body(): slots = lax.all_to_all(slots, ('tm', 'space'), 0, 0, tiled=True)  10.2 us
    all_to_all x1, starting transfers between devices, body(): slots = lax.all_to_all(slots, ('tm', 'space'), 0, 0, tiled=True)  5.02 us
    unnamed x14, local copies, waits for them, and re-layouts  4.86 us
  transfers between devices with their start and end apart: 20, of which 6 were waited for; matrix products, arithmetic and copies ran while one was open for 3% of the time, Pallas kernels for 5%

profile of v1, /device:TPU:0, one launch (start us, length us, event | category | flops | bytes accessed | tf_op | source)
XLA Modules:
  0.0 95.2 jit_solution(9579335264021273723)
XLA Ops:
  0.0 1.2 %copy-done = f32[8,16,2048]{2,1,0:T(8,128)S(1)} copy-done((f32[8,16,2048]{2,1,0:T(8,128)S(1)}, f32[8,16,2048]{2,1,0:T(8,128)}, u32[]{:S(2)}) %copy-start) | copy-done | bytes 1048600
  1.2 0.0 copy-start.1
  1.2 1.2 %copy-done.1 = f32[8,16,2048]{2,1,0:T(8,128)S(1)} copy-done((f32[8,16,2048]{2,1,0:T(8,128)S(1)}, f32[8,16,2048]{2,1,0:T(8,128)}, u32[]{:S(2)}) %copy-start.1) | copy-done | bytes 1048600
  2.5 0.0 copy-start.2
  2.5 0.9 copy-done.2
  3.4 0.9 copy-done.3
  4.3 0.4 shard_map.47
  4.7 3.9 %collective-permute-start.1 = (f32[36,16,128]{2,1,0:T(8,128)S(1)}, f32[36,16,128]{2,1,0:T(8,128)S(1)}, u32[]{:S(2)}, u32[]{:S(2)}) collective-permute-start(f32[36,16,128]{2,1,0:T(8,128)S(1)} %bitcast.24), channel_id=1, source_target_pairs={{0,3},{1,0},{2,1},{3,2},{4,7},{5,4},{6,5},{7,6},{8,11},{9,8},{10,9... | collective-permute-start | bytes 884744 | tf_op jit(solution)/shard_map/ppermute | solution.py:502
  8.6 0.0 collective-permute-start
  8.6 0.0 collective-permute-start.2
  8.6 3.3 %collective-permute-start.3 = (f32[7,16,128]{2,1,0:T(8,128)S(1)}, f32[7,16,128]{2,1,0:T(8,128)S(1)}, u32[]{:S(2)}, u32[]{:S(2)}) collective-permute-start(f32[7,16,128]{2,1,0:T(8,128)S(1)} %bitcast.27), channel_id=1, source_target_pairs={{0,5},{1,6},{2,7},{3,4},{4,9},{5,10},{6,11},{7,8},{8,13},{9,14},{1... | collective-permute-start | bytes 172040 | tf_op jit(solution)/shard_map/ppermute | solution.py:502
  11.9 1.0 %collective-permute-start.4 = (f32[7,16,128]{2,1,0:T(8,128)S(1)}, f32[7,16,128]{2,1,0:T(8,128)S(1)}, u32[]{:S(2)}, u32[]{:S(2)}) collective-permute-start(f32[7,16,128]{2,1,0:T(8,128)S(1)} %bitcast.26), channel_id=1, source_target_pairs={{0,7},{1,4},{2,5},{3,6},{4,11},{5,8},{6,9},{7,10},{8,15},{9,12},{1... | collective-permute-start | bytes 172040 | tf_op jit(solution)/shard_map/ppermute | solution.py:502
  12.9 1.4 %shard_map.46 = (f32[3328,128]{1,0:T(8,128)S(1)}, f32[256,128]{1,0:T(8,128)}, f32[4,2,16,128]{3,2,1,0:T(8,128)S(1)}) custom-call(f32[8,16,2048]{2,1,0:T(8,128)S(1)} %copy-done, f32[8,16,2048]{2,1,0:T(8,128)S(1)} %copy-done.1, f32[16,2048]{1,0:T(8,128)S(1)} %copy-done.2, f32[16,2048]{1,0:T(8,128)S(1)} %copy-done.3), custom_call_target="tpu_custom_call" | custom-call | tf_op jit(solution)/shard_map/pallas_call | solution.py:38
  14.2 8.8 %collective-permute-done.3.behind_above = f32[7,16,128]{2,1,0:T(8,128)S(1)} collective-permute-done((f32[7,16,128]{2,1,0:T(8,128)S(1)}, f32[7,16,128]{2,1,0:T(8,128)S(1)}, u32[]{:S(2)}, u32[]{:S(2)}) %collective-permute-start.3) | collective-permute-done | bytes 57376 | tf_op jit(solution)/shard_map/ppermute | solution.py:502
  23.1 0.6 collective-permute-done.4.behind_below
  23.7 0.0 collective-permute-done.2.behind
  23.7 0.0 collective-permute-done.1.below
  23.7 0.0 collective-permute-done.above
  23.7 4.6 %shard_map.48 = (f32[32,16,128]{2,1,0:T(8,128)S(1)}, f32[8,16,128]{2,1,0:T(8,128)S(1)}, f32[8,16,128]{2,1,0:T(8,128)S(1)}, f32[5,16,128]{2,1,0:T(8,128)S(1)}, f3...) custom-call(f32[208,16,128]{2,1,0:T(8,128)S(1)} %bitcast.19, ...), custom_call_target="tpu_custom_call" | custom-call | tf_op jit(solution)/shard_map/pallas_call | solution.py:38
  28.3 0.3 collective-permute-start.7
  28.5 2.0 %collective-permute-start.5 = (f32[8,16,128]{2,1,0:T(8,128)S(1)}, f32[8,16,128]{2,1,0:T(8,128)S(1)}, u32[]{:S(2)}, u32[]{:S(2)}) collective-permute-start(f32[8,16,128]{2,1,0:T(8,128)S(1)} %get-tuple-element.43), channel_id=1, source_target_pairs={{0,1},{1,2},{2,3},{3,0},{4,5},{5,6},{6,7},{7,4},{8,9},{9,10},{10,1... | collective-permute-start | bytes 196616 | tf_op jit(solution)/shard_map/ppermute | solution.py:502
  30.6 1.0 %collective-permute-start.6 = (f32[8,16,128]{2,1,0:T(8,128)S(1)}, f32[8,16,128]{2,1,0:T(8,128)S(1)}, u32[]{:S(2)}, u32[]{:S(2)}) collective-permute-start(f32[8,16,128]{2,1,0:T(8,128)S(1)} %get-tuple-element.44), channel_id=1, source_target_pairs={{0,3},{1,0},{2,1},{3,2},{4,7},{5,4},{6,5},{7,6},{8,11},{9,8},{10,9... | collective-permute-start | bytes 196616 | tf_op jit(solution)/shard_map/ppermute | solution.py:502
  31.5 0.8 collective-permute-start.8
  32.3 2.8 %collective-permute-start.9 = (f32[5,16,128]{2,1,0:T(8,128)S(1)}, f32[5,16,128]{2,1,0:T(8,128)S(1)}, u32[]{:S(2)}, u32[]{:S(2)}) collective-permute-start(f32[5,16,128]{2,1,0:T(8,128)S(1)} %get-tuple-element.47), channel_id=1, source_target_pairs={{0,7},{1,4},{2,5},{3,6},{4,11},{5,8},{6,9},{7,10},{8,15},{9,12},{1... | collective-permute-start | bytes 122888 | tf_op jit(solution)/shard_map/ppermute | solution.py:502
  35.2 3.5 %collective-permute-done.8.behind_above = f32[5,16,128]{2,1,0:T(8,128)S(1)} collective-permute-done((f32[5,16,128]{2,1,0:T(8,128)S(1)}, f32[5,16,128]{2,1,0:T(8,128)S(1)}, u32[]{:S(2)}, u32[]{:S(2)}) %collective-permute-start.8) | collective-permute-done | bytes 40992 | tf_op jit(solution)/shard_map/ppermute | solution.py:502
  38.7 0.0 collective-permute-done.9.behind_below
  38.7 0.0 collective-permute-done.5.above
  38.7 0.0 collective-permute-done.6.below
  38.7 0.0 collective-permute-done.7.behind
  38.7 4.4 %shard_map.49 = (f32[32,16,128]{2,1,0:T(8,128)}, f32[2,16,128]{2,1,0:T(8,128)S(1)}, f32[2,16,128]{2,1,0:T(8,128)S(1)}, f32[5,16,128]{2,1,0:T(8,128)S(1)}, f32[5,...) custom-call(f32[20,16,128]{2,1,0:T(8,128)S(1)} %get-tuple-element.39, ...), custom_call_target="tpu_custom_call" | custom-call | tf_op jit(solution)/shard_map/pallas_call | solution.py:38
  43.1 0.6 copy-done.4
  43.7 0.0 collective-permute-start.12
  43.7 3.5 %collective-permute-start.15 = (f32[256,128]{1,0:T(8,128)}, f32[256,128]{1,0:T(8,128)S(1)}, u32[]{:S(2)}, u32[]{:S(2)}) collective-permute-start(f32[256,128]{1,0:T(8,128)} %get-tuple-element.55), channel_id=1, source_target_pairs={{0,28},{1,29},{2,30},{3,31},{4,0},{5,1},{6,2},{7,3},{8,4},{9,5},{1... | collective-permute-start | bytes 393224 | tf_op jit(solution)/shard_map/ppermute | solution.py:502
  47.3 0.6 constant_dynamic-slice_fusion
  47.9 2.2 %collective-permute-start.10 = (f32[2,16,128]{2,1,0:T(8,128)}, f32[2,16,128]{2,1,0:T(8,128)S(1)}, u32[]{:S(2)}, u32[]{:S(2)}) collective-permute-start(f32[2,16,128]{2,1,0:T(8,128)} %copy-done.4), channel_id=1, source_target_pairs={{0,1},{1,2},{2,3},{3,0},{4,5},{5,6},{6,7},{7,4},{8,9},{9,10},{10,1... | collective-permute-start | bytes 49160 | tf_op jit(solution)/shard_map/ppermute | solution.py:502
  50.1 1.0 %collective-permute-start.11 = (f32[2,16,128]{2,1,0:T(8,128)S(1)}, f32[2,16,128]{2,1,0:T(8,128)S(1)}, u32[]{:S(2)}, u32[]{:S(2)}) collective-permute-start(f32[2,16,128]{2,1,0:T(8,128)S(1)} %get-tuple-element.51), channel_id=1, source_target_pairs={{0,3},{1,0},{2,1},{3,2},{4,7},{5,4},{6,5},{7,6},{8,11},{9,8},{10,9... | collective-permute-start | bytes 49160 | tf_op jit(solution)/shard_map/ppermute | solution.py:502
  51.1 0.0 collective-permute-start.13
  51.1 0.0 collective-permute-done.15
  51.1 0.2 collective-permute-start.14
  51.3 0.6 fusion.2
  51.9 0.0 copy-start.6
  51.9 0.0 copy-start.5
  51.9 0.9 slice.7.pair1
  52.8 0.2 collective-permute-done.10.above
  53.0 2.7 %collective-permute-start.18 = (f32[2,16,128]{2,1,0:T(8,128)}, f32[2,16,128]{2,1,0:T(8,128)S(1)}, u32[]{:S(2)}, u32[]{:S(2)}) collective-permute-start(f32[2,16,128]{2,1,0:T(8,128)} %get-tuple-element.62), channel_id=1, source_target_pairs={{0,3},{1,0},{2,1},{3,2},{4,7},{5,4},{6,5},{7,6},{8,11},{9,8},{10,9... | collective-permute-start | bytes 49160 | tf_op jit(solution)/shard_map/ppermute | solution.py:502
  55.8 0.0 collective-permute-done.11.below
  55.8 0.5 collective-permute-start.17
  56.3 1.9 %collective-permute-done.13.behind_above = f32[5,16,128]{2,1,0:T(8,128)S(1)} collective-permute-done((f32[5,16,128]{2,1,0:T(8,128)S(1)}, f32[5,16,128]{2,1,0:T(8,128)S(1)}, u32[]{:S(2)}, u32[]{:S(2)}) %collective-permute-start.13) | collective-permute-done | bytes 40992 | tf_op jit(solution)/shard_map/ppermute | solution.py:502
  58.1 0.2 collective-permute-start.16
  58.3 0.0 collective-permute-done.14.behind_below
  58.3 0.0 collective-permute-done.12.behind
  58.3 3.3 %shard_map.50 = (f32[32,16,128]{2,1,0:T(8,128)}, f32[20,16,128]{2,1,0:T(8,128)S(1)}) custom-call(f32[20,16,128]{2,1,0:T(8,128)S(1)} %get-tuple-element.48.next_first, f32[16,16,128]{2,1,0:T(8,128)S(1)} %get-tuple-element.49.next_forcing, f32[44,16,128]{2,1,0:T(8,128)S(1)} %get-tuple-element.42.coefs, f32[2,16,128]{2,1,0:T(8,128)S(1)} %collective-permute-done.10.above, ...), custom_call_target="tpu_custom_call" | custom-call | tf_op jit(solution)/shard_map/pallas_call | solution.py:38
  61.6 5.0 %all-to-all-start = ((f32[32,16,128]{2,1,0:T(8,128)}), f32[32,16,128]{2,1,0:T(8,128)S(1)}, u32[]{:S(2)}, u32[]{:S(2)}) async-start(f32[32,16,128]{2,1,0:T(8,128)} %get-tuple-element.56), calls=%async_computation | async-start | bytes 524288 | tf_op jit(solution)/shard_map/all_to_all | solution.py:587
  66.6 0.0 copy-done.6
  66.7 0.0 collective-permute-done.18
  66.7 0.0 collective-permute-done.17
  66.7 0.0 collective-permute-done.16
  66.7 0.0 copy-done.5
  66.7 0.6 gather_fusion
  67.3 0.1 broadcast_select_fusion.windows
  67.4 10.2 %all-to-all-done.arrived = f32[32,16,128]{2,1,0:T(8,128)S(1)} async-done(((f32[32,16,128]{2,1,0:T(8,128)}), f32[32,16,128]{2,1,0:T(8,128)S(1)}, u32[]{:S(2)}, u32[]{:S(2)}) %all-to-all-start) | async-done | bytes 262176 | tf_op jit(solution)/shard_map/all_to_all | solution.py:587
  77.6 0.7 shard_map.51
  78.3 12.8 %all_to_all.10 = f32[32,16,128]{2,1,0:T(8,128)S(1)} all-to-all(f32[32,16,128]{2,1,0:T(8,128)S(1)} %shard_map.51), channel_id=1, replica_groups=mesh['tm'=8,'space'=4] {'tm','space'}, dimensions={0} | all-to-all | bytes 524288 | tf_op jit(solution)/shard_map/all_to_all | solution.py:594
  91.1 4.1 %shard_map.52 = f32[8,16,2048]{2,1,0:T(8,128)} custom-call(f32[512,128]{1,0:T(8,128)S(1)} %bitcast.21, f32[20,16,128]{2,1,0:T(8,128)S(1)} %get-tuple-element.58.wide_forcing, f32[18,16,128]{2,1,0:T(8,128)S(1)} %get-tuple-element.59.late_a, f32[18,16,128]{2,1,0:T(8,128)S(1)} %get-tuple-element.60.late_b, f32[208,16,128]{2,1,0:T(8,128)S(1)} %bitcast.20, ...), custom_call_target="tpu_custom_call" | custom-call | tf_op jit(solution)/shard_map/pallas_call | solution.py:38
  (7 shorter events, 0.0 us)
Async XLA Ops:
  0.0 1.2 %copy-start = (f32[8,16,2048]{2,1,0:T(8,128)S(1)}, f32[8,16,2048]{2,1,0:T(8,128)}, u32[]{:S(2)}) copy-start(f32[8,16,2048]{2,1,0:T(8,128)} %initial.3) | copy-start | bytes 3145732
  1.2 1.2 %copy-start.1 = (f32[8,16,2048]{2,1,0:T(8,128)S(1)}, f32[8,16,2048]{2,1,0:T(8,128)}, u32[]{:S(2)}) copy-start(f32[8,16,2048]{2,1,0:T(8,128)} %source.3) | copy-start | bytes 3145732
  2.5 0.9 copy-start.2
  3.4 0.9 copy-start.3
  4.7 19.0 %collective-permute-start.1 = (f32[36,16,128]{2,1,0:T(8,128)S(1)}, f32[36,16,128]{2,1,0:T(8,128)S(1)}, u32[]{:S(2)}, u32[]{:S(2)}) collective-permute-start(f32[36,16,128]{2,1,0:T(8,128)S(1)} %bitcast.24), channel_id=1, source_target_pairs={{0,3},{1,0},{2,1},{3,2},{4,7},{5,4},{6,5},{7,6},{8,11},{9,8},{10,9... | collective-permute-start | bytes 884744 | tf_op jit(solution)/shard_map/ppermute | solution.py:502
  8.6 15.1 %collective-permute-start = (f32[36,16,128]{2,1,0:T(8,128)S(1)}, f32[36,16,128]{2,1,0:T(8,128)S(1)}, u32[]{:S(2)}, u32[]{:S(2)}) collective-permute-start(f32[36,16,128]{2,1,0:T(8,128)S(1)} %bitcast.23), channel_id=1, source_target_pairs={{0,1},{1,2},{2,3},{3,0},{4,5},{5,6},{6,7},{7,4},{8,9},{9,10},{10,1... | collective-permute-start | bytes 884744 | tf_op jit(solution)/shard_map/ppermute | solution.py:502
  8.6 15.0 %collective-permute-start.2 = (f32[32,16,128]{2,1,0:T(8,128)S(1)}, f32[32,16,128]{2,1,0:T(8,128)S(1)}, u32[]{:S(2)}, u32[]{:S(2)}) collective-permute-start(f32[32,16,128]{2,1,0:T(8,128)S(1)} %bitcast.25), channel_id=1, source_target_pairs={{0,4},{1,5},{2,6},{3,7},{4,8},{5,9},{6,10},{7,11},{8,12},{9,13},{1... | collective-permute-start | bytes 786440 | tf_op jit(solution)/shard_map/ppermute | solution.py:502
  8.6 14.4 %collective-permute-start.3 = (f32[7,16,128]{2,1,0:T(8,128)S(1)}, f32[7,16,128]{2,1,0:T(8,128)S(1)}, u32[]{:S(2)}, u32[]{:S(2)}) collective-permute-start(f32[7,16,128]{2,1,0:T(8,128)S(1)} %bitcast.27), channel_id=1, source_target_pairs={{0,5},{1,6},{2,7},{3,4},{4,9},{5,10},{6,11},{7,8},{8,13},{9,14},{1... | collective-permute-start | bytes 172040 | tf_op jit(solution)/shard_map/ppermute | solution.py:502
  11.9 11.8 %collective-permute-start.4 = (f32[7,16,128]{2,1,0:T(8,128)S(1)}, f32[7,16,128]{2,1,0:T(8,128)S(1)}, u32[]{:S(2)}, u32[]{:S(2)}) collective-permute-start(f32[7,16,128]{2,1,0:T(8,128)S(1)} %bitcast.26), channel_id=1, source_target_pairs={{0,7},{1,4},{2,5},{3,6},{4,11},{5,8},{6,9},{7,10},{8,15},{9,12},{1... | collective-permute-start | bytes 172040 | tf_op jit(solution)/shard_map/ppermute | solution.py:502
  28.3 10.5 %collective-permute-start.7 = (f32[32,16,128]{2,1,0:T(8,128)S(1)}, f32[32,16,128]{2,1,0:T(8,128)S(1)}, u32[]{:S(2)}, u32[]{:S(2)}) collective-permute-start(f32[32,16,128]{2,1,0:T(8,128)S(1)} %get-tuple-element.45), channel_id=1, source_target_pairs={{0,4},{1,5},{2,6},{3,7},{4,8},{5,9},{6,10},{7,11},{8,12},{9,13},{1... | collective-permute-start | bytes 786440 | tf_op jit(solution)/shard_map/ppermute | solution.py:502
  28.5 10.2 %collective-permute-start.5 = (f32[8,16,128]{2,1,0:T(8,128)S(1)}, f32[8,16,128]{2,1,0:T(8,128)S(1)}, u32[]{:S(2)}, u32[]{:S(2)}) collective-permute-start(f32[8,16,128]{2,1,0:T(8,128)S(1)} %get-tuple-element.43), channel_id=1, source_target_pairs={{0,1},{1,2},{2,3},{3,0},{4,5},{5,6},{6,7},{7,4},{8,9},{9,10},{10,1... | collective-permute-start | bytes 196616 | tf_op jit(solution)/shard_map/ppermute | solution.py:502
  30.6 8.2 %collective-permute-start.6 = (f32[8,16,128]{2,1,0:T(8,128)S(1)}, f32[8,16,128]{2,1,0:T(8,128)S(1)}, u32[]{:S(2)}, u32[]{:S(2)}) collective-permute-start(f32[8,16,128]{2,1,0:T(8,128)S(1)} %get-tuple-element.44), channel_id=1, source_target_pairs={{0,3},{1,0},{2,1},{3,2},{4,7},{5,4},{6,5},{7,6},{8,11},{9,8},{10,9... | collective-permute-start | bytes 196616 | tf_op jit(solution)/shard_map/ppermute | solution.py:502
  31.5 7.2 %collective-permute-start.8 = (f32[5,16,128]{2,1,0:T(8,128)S(1)}, f32[5,16,128]{2,1,0:T(8,128)S(1)}, u32[]{:S(2)}, u32[]{:S(2)}) collective-permute-start(f32[5,16,128]{2,1,0:T(8,128)S(1)} %get-tuple-element.46), channel_id=1, source_target_pairs={{0,5},{1,6},{2,7},{3,4},{4,9},{5,10},{6,11},{7,8},{8,13},{9,14},{1... | collective-permute-start | bytes 122888 | tf_op jit(solution)/shard_map/ppermute | solution.py:502
  32.3 6.4 %collective-permute-start.9 = (f32[5,16,128]{2,1,0:T(8,128)S(1)}, f32[5,16,128]{2,1,0:T(8,128)S(1)}, u32[]{:S(2)}, u32[]{:S(2)}) collective-permute-start(f32[5,16,128]{2,1,0:T(8,128)S(1)} %get-tuple-element.47), channel_id=1, source_target_pairs={{0,7},{1,4},{2,5},{3,6},{4,11},{5,8},{6,9},{7,10},{8,15},{9,12},{1... | collective-permute-start | bytes 122888 | tf_op jit(solution)/shard_map/ppermute | solution.py:502
  43.1 0.6 copy-start.4
  43.7 14.6 %collective-permute-start.12 = (f32[32,16,128]{2,1,0:T(8,128)}, f32[32,16,128]{2,1,0:T(8,128)S(1)}, u32[]{:S(2)}, u32[]{:S(2)}) collective-permute-start(f32[32,16,128]{2,1,0:T(8,128)} %get-tuple-element.52), channel_id=1, source_target_pairs={{0,4},{1,5},{2,6},{3,7},{4,8},{5,9},{6,10},{7,11},{8,12},{9,13},{1... | collective-permute-start | bytes 786440 | tf_op jit(solution)/shard_map/ppermute | solution.py:502
  43.7 7.4 %collective-permute-start.15 = (f32[256,128]{1,0:T(8,128)}, f32[256,128]{1,0:T(8,128)S(1)}, u32[]{:S(2)}, u32[]{:S(2)}) collective-permute-start(f32[256,128]{1,0:T(8,128)} %get-tuple-element.55), channel_id=1, source_target_pairs={{0,28},{1,29},{2,30},{3,31},{4,0},{5,1},{6,2},{7,3},{8,4},{9,5},{1... | collective-permute-start | bytes 393224 | tf_op jit(solution)/shard_map/ppermute | solution.py:502
  47.9 5.1 %collective-permute-start.10 = (f32[2,16,128]{2,1,0:T(8,128)}, f32[2,16,128]{2,1,0:T(8,128)S(1)}, u32[]{:S(2)}, u32[]{:S(2)}) collective-permute-start(f32[2,16,128]{2,1,0:T(8,128)} %copy-done.4), channel_id=1, source_target_pairs={{0,1},{1,2},{2,3},{3,0},{4,5},{5,6},{6,7},{7,4},{8,9},{9,10},{10,1... | collective-permute-start | bytes 49160 | tf_op jit(solution)/shard_map/ppermute | solution.py:502
  50.1 5.6 %collective-permute-start.11 = (f32[2,16,128]{2,1,0:T(8,128)S(1)}, f32[2,16,128]{2,1,0:T(8,128)S(1)}, u32[]{:S(2)}, u32[]{:S(2)}) collective-permute-start(f32[2,16,128]{2,1,0:T(8,128)S(1)} %get-tuple-element.51), channel_id=1, source_target_pairs={{0,3},{1,0},{2,1},{3,2},{4,7},{5,4},{6,5},{7,6},{8,11},{9,8},{10,9... | collective-permute-start | bytes 49160 | tf_op jit(solution)/shard_map/ppermute | solution.py:502
  51.1 7.0 %collective-permute-start.13 = (f32[5,16,128]{2,1,0:T(8,128)S(1)}, f32[5,16,128]{2,1,0:T(8,128)S(1)}, u32[]{:S(2)}, u32[]{:S(2)}) collective-permute-start(f32[5,16,128]{2,1,0:T(8,128)S(1)} %get-tuple-element.53), channel_id=1, source_target_pairs={{0,5},{1,6},{2,7},{3,4},{4,9},{5,10},{6,11},{7,8},{8,13},{9,14},{1... | collective-permute-start | bytes 122888 | tf_op jit(solution)/shard_map/ppermute | solution.py:502
  51.1 7.2 %collective-permute-start.14 = (f32[5,16,128]{2,1,0:T(8,128)S(1)}, f32[5,16,128]{2,1,0:T(8,128)S(1)}, u32[]{:S(2)}, u32[]{:S(2)}) collective-permute-start(f32[5,16,128]{2,1,0:T(8,128)S(1)} %get-tuple-element.54), channel_id=1, source_target_pairs={{0,7},{1,4},{2,5},{3,6},{4,11},{5,8},{6,9},{7,10},{8,15},{9,12},{1... | collective-permute-start | bytes 122888 | tf_op jit(solution)/shard_map/ppermute | solution.py:502
  51.9 14.8 %copy-start.6 = (s32[4]{0:T(128)S(1)}, s32[4]{0:T(128)}, u32[]{:S(2)}) copy-start(s32[4]{0:T(128)} %fusion.2) | copy-start | bytes 52
  51.9 14.8 %copy-start.5 = (f32[1,2,16,128]{3,2,1,0:T(8,128)S(1)}, f32[1,2,16,128]{3,2,1,0:T(8,128)}, u32[]{:S(2)}) copy-start(f32[1,2,16,128]{3,2,1,0:T(8,128)} %get-tuple-element.61) | copy-start | bytes 49156
  53.0 13.7 %collective-permute-start.18 = (f32[2,16,128]{2,1,0:T(8,128)}, f32[2,16,128]{2,1,0:T(8,128)S(1)}, u32[]{:S(2)}, u32[]{:S(2)}) collective-permute-start(f32[2,16,128]{2,1,0:T(8,128)} %get-tuple-element.62), channel_id=1, source_target_pairs={{0,3},{1,0},{2,1},{3,2},{4,7},{5,4},{6,5},{7,6},{8,11},{9,8},{10,9... | collective-permute-start | bytes 49160 | tf_op jit(solution)/shard_map/ppermute | solution.py:502
  55.8 10.9 %collective-permute-start.17 = (f32[2,16,128]{2,1,0:T(8,128)}, f32[2,16,128]{2,1,0:T(8,128)S(1)}, u32[]{:S(2)}, u32[]{:S(2)}) collective-permute-start(f32[2,16,128]{2,1,0:T(8,128)} %get-tuple-element.63), channel_id=1, source_target_pairs={{0,2},{1,3},{2,0},{3,1},{4,6},{5,7},{6,4},{7,5},{8,10},{9,11},{10,... | collective-permute-start | bytes 49160 | tf_op jit(solution)/shard_map/ppermute | solution.py:502
  58.1 8.6 %collective-permute-start.16 = (f32[2,16,128]{2,1,0:T(8,128)}, f32[2,16,128]{2,1,0:T(8,128)S(1)}, u32[]{:S(2)}, u32[]{:S(2)}) collective-permute-start(f32[2,16,128]{2,1,0:T(8,128)} %get-tuple-element.64), channel_id=1, source_target_pairs={{0,1},{1,2},{2,3},{3,0},{4,5},{5,6},{6,7},{7,4},{8,9},{9,10},{10,1... | collective-permute-start | bytes 49160 | tf_op jit(solution)/shard_map/ppermute | solution.py:502
  61.6 16.0 %all-to-all-start = ((f32[32,16,128]{2,1,0:T(8,128)}), f32[32,16,128]{2,1,0:T(8,128)S(1)}, u32[]{:S(2)}, u32[]{:S(2)}) async-start(f32[32,16,128]{2,1,0:T(8,128)} %get-tuple-element.56), calls=%async_computation | async-start | bytes 524288 | tf_op jit(solution)/shard_map/all_to_all | solution.py:587

commit v2 on v1

v2 whole, which is shorter than its diff:
```python
import functools

import jax
import jax.numpy as jnp
from jax import lax
from jax.experimental import pallas as pl
from jax.experimental.pallas import tpu as pltpu
from jax.sharding import PartitionSpec as P

LANES = 128
MARGIN = 4
REACH = 32
UP_RIM = 3
FIELDS = 3
POINTS = 8
diffusion_number = 0.03
time_step = 0.02

RIMS_0 = (
    ("e0", 4), ("e1", 4), ("e2", 4),
    ("o0", 3), ("o1", 3), ("o2", 3), ("o3", 1),
    ("s0", 2), ("s1", 2), ("s2", 2), ("s3", 2),
    ("d", 3), ("g", 3),
)
CORES = ("e0", "e1", "e2", "o0", "o1", "o2", "o3", "s0", "s1", "s2", "s3", "d", "g")
BEHIND_0 = (("ep", 4), ("op", 3))
BEHIND = (("pair", 2), ("odd", 3))


def count(rims):
    return sum(rows for _, rows in rims)


def params(mib=16):
    return pltpu.CompilerParams(vmem_limit_bytes=mib * 2**20)


def call(kernel, outs, scratch, *args, mib=16, place=pltpu.VMEM, sems=0):
    return pl.pallas_call(
        kernel,
        out_shape=tuple(jax.ShapeDtypeStruct(shape, jnp.float32) for shape in outs),
        in_specs=[pl.BlockSpec(memory_space=place)] * len(args),
        out_specs=tuple(pl.BlockSpec(memory_space=pltpu.VMEM) for _ in outs),
        scratch_shapes=[pltpu.VMEM(shape, jnp.float32) for shape in scratch]
        + ([pltpu.SemaphoreType.DMA((sems,))] if sems else []),
        compiler_params=params(mib),
    )(*args)


def beside(mid):
    depth = mid.shape[1]
    lane = lax.broadcasted_iota(jnp.int32, mid.shape, 2)
    line = lax.broadcasted_iota(jnp.int32, mid.shape, 1)
    left = pltpu.roll(mid, 1, 2)
    left_turn = pltpu.roll(left, 1, 1)
    right = pltpu.roll(mid, LANES - 1, 2)
    right_turn = pltpu.roll(right, depth - 1, 1)
    left = jnp.where(lane == 0, jnp.where(line == 0, 0.0, left_turn), left)
    right = jnp.where(lane == LANES - 1, jnp.where(line == depth - 1, 0.0, right_turn), right)
    return left + right


def growth_of(ref, at, rows, diff, grow):
    wide = ref[pl.ds(at - 1, rows + 2)]
    mid = wide[1:-1]
    laplace = wide[:-2] + wide[2:] + beside(mid) - 4.0 * mid
    return mid, diff * laplace + grow * mid / (1.0 + mid * mid)


def over_rows(rows, rim, body):
    body(MARGIN - rim, rows + 2 * rim)


def flags():
    slab = lax.axis_index("space")
    low = jnp.where(slab > 0, 1.0, 0.0).astype(jnp.float32)
    high = jnp.where(slab < lax.axis_size("space") - 1, 1.0, 0.0).astype(jnp.float32)
    return low, high


def set_rims(buffer, rows, rim, low_rows, high_rows, low, high, inner=0):
    width = rim - inner
    buffer[pl.ds(MARGIN - rim, width)] = low_rows * low
    buffer[pl.ds(MARGIN + rows + inner, width)] = high_rows * high


def pieces(name, evens, source, diffusivity, growth):
    if name == "d":
        return lambda rows, cols: diffusivity[rows, cols] * diffusion_number
    if name == "g":
        return lambda rows, cols: growth[rows, cols] * time_step
    if name == "ep":
        return lambda rows, cols: evens[POINTS // 2 - 1, rows, cols]
    if name == "op":
        return lambda rows, cols: source[POINTS - 1, rows, cols]
    which = int(name[1])
    if name[0] == "e":
        return lambda rows, cols: evens[which, rows, cols]
    return lambda rows, cols: source[2 * which + (name[0] == "o"), rows, cols]


def pack_kernel(
    initial_all, source_all, diffusivity_all, growth_all,
    down, up, turn, slant_down, slant_up, evens, source, diffusivity, growth, sems,
):
    pairs = [(initial_all.at[2 * i], evens.at[i]) for i in range(POINTS // 2)]
    pairs += [(source_all, source), (diffusivity_all, diffusivity), (growth_all, growth)]
    copies = [pltpu.make_async_copy(*pair, sems.at[i]) for i, pair in enumerate(pairs)]
    for copy in copies:
        copy.start()
    for copy in copies:
        copy.wait()
    rows, cols = diffusivity.shape
    depth = cols // LANES
    for rims, low, high in ((RIMS_0, down, up), (BEHIND_0, slant_down, slant_up)):
        at = 0
        for name, rim in rims:
            get = pieces(name, evens, source, diffusivity, growth)
            for c in range(depth):
                lanes = pl.ds(c * LANES, LANES)
                place = pl.ds(at * depth + c, rim, stride=depth)
                low[place, :] = get(pl.ds(rows - rim, rim), lanes)
                high[place, :] = get(pl.ds(0, rim), lanes)
            at += rim
    for index, (name, _) in enumerate(BEHIND_0):
        get = pieces(name, evens, source, diffusivity, growth)
        for c in range(depth):
            for r in range(0, rows, 8):
                place = pl.ds((index * rows + r) * depth + c, 8, stride=depth)
                turn[place, :] = get(pl.ds(r, 8), pl.ds(c * LANES, LANES))


def window(get, first, depth):
    line, offset = first // LANES, first % LANES
    shape = get(0).shape
    source = lax.broadcasted_iota(jnp.int32, shape, 1) + (offset - REACH)
    shift = (REACH - offset) % LANES
    before = jnp.where(line > 0, pltpu.roll(get(jnp.maximum(line - 1, 0)), shift, 1), 0.0)
    here = pltpu.roll(get(line), shift, 1)
    after = jnp.where(
        line < depth - 1, pltpu.roll(get(jnp.minimum(line + 1, depth - 1)), shift, 1), 0.0
    )
    return jnp.where(source < 0, before, jnp.where(source >= LANES, after, here))


def core_kernel(share, evens, source, diffusivity, growth, core, back, *windows):
    rows, cols = diffusivity.shape
    depth = cols // LANES
    for index, name in enumerate(CORES):
        get = pieces(name, evens, source, diffusivity, growth)
        for c in range(depth):
            for r in range(0, rows, 8):
                value = get(pl.ds(r, 8), pl.ds(c * LANES, LANES))
                core[pl.ds((index * rows + r) * depth + c, 8, stride=depth), :] = value
                if name == "s0":
                    back[pl.ds(r * depth + c, 8, stride=depth), :] = value
    slabs = lax.axis_size("space")
    for by, out in enumerate(windows):
        target = lax.axis_index("tm") * slabs + (lax.axis_index("space") + by) % slabs
        for which, name in enumerate(("d", "g")):
            start = CORES.index(name) * rows * depth
            get = lambda line: core[pl.ds(start + line, rows, stride=depth), :]
            out[which] = window(get, target * share, depth)


def split(ref, rims):
    at, out = 0, {}
    for name, rim in rims:
        out[name] = ref[pl.ds(at, rim)]
        at += rim
    return out


def level0_kernel(
    core, above, below, behind, behind_above, behind_below,
    turn, down, up, slant_down, slant_up, state, forcing, first_forcing, coefs,
    fields, diff, grow,
):
    rows = core.shape[0] // len(CORES)
    low, high = flags()
    names = list(CORES) + ["ep", "op"]
    spots = {name: index for index, name in enumerate(names)}
    for rims, from_low, from_high in (
        (RIMS_0, above, below),
        (BEHIND_0, behind_above, behind_below),
    ):
        lows, highs = split(from_low, rims), split(from_high, rims)
        for name, rim in rims:
            if name in ("d", "g"):
                buffer = diff if name == "d" else grow
            else:
                buffer = fields.at[spots[name]]
            set_rims(buffer, rows, rim, lows[name], highs[name], low, high)
    for name in CORES:
        if name in ("d", "g"):
            buffer = diff if name == "d" else grow
        else:
            buffer = fields.at[spots[name]]
        buffer[pl.ds(MARGIN, rows)] = core[pl.ds(CORES.index(name) * rows, rows)]
    for index, (name, _) in enumerate(BEHIND_0):
        fields[spots[name], pl.ds(MARGIN, rows)] = behind[pl.ds(index * rows, rows)]
    extra = len(names)
    halves = POINTS // 2
    odd = [extra + i for i in range(halves)]
    even = [extra + halves + i for i in range(halves)]
    image = [extra + 2 * halves + i for i in range(halves)]

    def first(at, n):
        d, g = diff[pl.ds(at, n)], grow[pl.ds(at, n)]
        for i in range(halves):
            start, term = ("ep", "op") if i == 0 else (f"e{i - 1}", f"o{i - 1}")
            mid, slope = growth_of(fields.at[spots[start]], at, n, d, g)
            fields[odd[i], pl.ds(at, n)] = mid + slope + fields[spots[term], pl.ds(at, n)]

    def second(at, n):
        d, g = diff[pl.ds(at, n)], grow[pl.ds(at, n)]
        for i in range(halves):
            mid, slope = growth_of(fields.at[odd[i]], at, n, d, g)
            fields[even[i], pl.ds(at, n)] = mid + slope + fields[spots[f"s{i}"], pl.ds(at, n)]

    def third(at, n):
        d, g = diff[pl.ds(at, n)], grow[pl.ds(at, n)]
        for i in range(halves):
            mid, slope = growth_of(fields.at[even[i]], at, n, d, g)
            fields[odd[i], pl.ds(at, n)] = mid + slope + fields[spots[f"o{i}"], pl.ds(at, n)]
            fields[image[i], pl.ds(at, n)] = mid + 2.0 * slope

    def fourth(at, n):
        d, g = diff[pl.ds(at, n)], grow[pl.ds(at, n)]
        here = at - MARGIN
        for i in range(halves):
            mid, slope = growth_of(fields.at[odd[i]], at, n, d, g)
            pair = mid + slope - fields[image[i], pl.ds(at, n)]
            if i == halves - 1:
                turn[pl.ds(here, n)] = pair
            else:
                term = fields[spots[f"s{i + 1}"], pl.ds(at, n)] + pair
                forcing[pl.ds(i * rows + here, n)] = term
                if i == halves - 2:
                    turn[pl.ds(rows + here, n)] = fields[image[i], pl.ds(at, n)] + term

    over_rows(rows, 3, first)
    over_rows(rows, 2, second)
    over_rows(rows, 1, third)
    over_rows(rows, 0, fourth)
    state[...] = fields[even[0], pl.ds(MARGIN - 2, rows + 4)]
    first_forcing[...] = fields[spots["s0"], pl.ds(MARGIN - 2, rows + 4)]
    coefs[pl.ds(0, rows + 6)] = diff[pl.ds(MARGIN - 3, rows + 6)]
    coefs[pl.ds(rows + 6, rows + 6)] = grow[pl.ds(MARGIN - 3, rows + 6)]
    send_behind(turn, slant_down, slant_up, rows)
    down[pl.ds(0, 2)] = fields[even[0], pl.ds(MARGIN + rows - 4, 2)]
    up[pl.ds(0, 2)] = fields[even[0], pl.ds(MARGIN + 2, 2)]
    at = 2
    for which, rim in ((0, 3), (2, 1), (1, 2)):
        down[pl.ds(at, rim)] = forcing[pl.ds((which + 1) * rows - rim, rim)]
        up[pl.ds(at, rim)] = forcing[pl.ds(which * rows, rim)]
        at += rim


RIMS_1 = (("state", 2), ("g1", 3), ("g3", 1), ("g2", 2))


def send_behind(turn, slant_down, slant_up, rows):
    at = 0
    for index, (_, rim) in enumerate(BEHIND):
        slant_down[pl.ds(at, rim)] = turn[pl.ds((index + 1) * rows - rim, rim)]
        slant_up[pl.ds(at, rim)] = turn[pl.ds(index * rows, rim)]
        at += rim


def take_behind(rows, buffers, behind, behind_above, behind_below, low, high):
    lows, highs = split(behind_above, BEHIND), split(behind_below, BEHIND)
    for index, (name, rim) in enumerate(BEHIND):
        buffer = buffers[index]
        set_rims(buffer, rows, rim, lows[name], highs[name], low, high)
        buffer[pl.ds(MARGIN, rows)] = behind[pl.ds(index * rows, rows)]


def take_coefs(rows, coefs, diff, grow):
    diff[pl.ds(MARGIN - 3, rows + 6)] = coefs[pl.ds(0, rows + 6)]
    grow[pl.ds(MARGIN - 3, rows + 6)] = coefs[pl.ds(rows + 6, rows + 6)]


def level1_kernel(
    share, state, forcing, first_forcing, coefs, last_pair, ahead,
    above, below, behind, behind_above, behind_below,
    slots, down, up, next_forcing, late_a, late_b,
    fields, diff, grow, flat,
):
    rows = forcing.shape[0] // 3
    low, high = flags()
    take_coefs(rows, coefs, diff, grow)
    v, g1, g3, g2, g0, pair, before, after, even0, even1, image0, image1, odd0, odd1 = range(14)
    lows, highs = split(above, RIMS_1), split(below, RIMS_1)
    for name, spot, rim, inner in (
        ("state", v, 4, 2), ("g1", g1, 3, 0), ("g3", g3, 1, 0), ("g2", g2, 2, 0),
    ):
        set_rims(fields.at[spot], rows, rim, lows[name], highs[name], low, high, inner)
    fields[v, pl.ds(MARGIN - 2, rows + 4)] = state[...]
    for which, spot in enumerate((g1, g2, g3)):
        fields[spot, pl.ds(MARGIN, rows)] = forcing[pl.ds(which * rows, rows)]
    take_behind(
        rows, (fields.at[pair], fields.at[before]), behind, behind_above, behind_below, low, high
    )
    fields[g0, pl.ds(MARGIN - 2, rows + 4)] = (
        first_forcing[...] + fields[pair, pl.ds(MARGIN - 2, rows + 4)]
    )

    def first(at, n):
        mid, slope = growth_of(fields.at[v], at, n, diff[pl.ds(at, n)], grow[pl.ds(at, n)])
        fields[after, pl.ds(at, n)] = mid + 2.0 * slope + fields[g1, pl.ds(at, n)]

    def second(at, n):
        d, g = diff[pl.ds(at, n)], grow[pl.ds(at, n)]
        for start, term, end in ((before, g0, even0), (after, g2, even1)):
            mid, slope = growth_of(fields.at[start], at, n, d, g)
            fields[end, pl.ds(at, n)] = mid + 2.0 * slope + fields[term, pl.ds(at, n)]

    def third(at, n):
        d, g = diff[pl.ds(at, n)], grow[pl.ds(at, n)]
        for start, term, end, image in ((even0, g1, odd0, image0), (even1, g3, odd1, image1)):
            mid, slope = growth_of(fields.at[start], at, n, d, g)
            fields[end, pl.ds(at, n)] = mid + 2.0 * slope + fields[term, pl.ds(at, n)]
            fields[image, pl.ds(at, n)] = mid + 4.0 * slope

    def fourth(at, n):
        d, g = diff[pl.ds(at, n)], grow[pl.ds(at, n)]
        here = at - MARGIN
        mid, slope = growth_of(fields.at[odd1], at, n, d, g)
        pair1 = mid + 2.0 * slope - fields[image1, pl.ds(at, n)]
        put_rows(flat, rows, ahead[...] + last_pair[pl.ds(0, rows)] + pair1)
        mid, slope = growth_of(fields.at[odd0], at, n, d, g)
        image = fields[image0, pl.ds(at, n)]
        term = fields[g2, pl.ds(at, n)] + (mid + 2.0 * slope - image)
        next_forcing[pl.ds(here, n)] = term
        put_rows(flat, 2 * rows, term)
        put_rows(flat, 0, image + term)

    over_rows(rows, 3, first)
    over_rows(rows, 2, second)
    over_rows(rows, 1, third)
    over_rows(rows, 0, fourth)
    late_a[...] = fields[g1, pl.ds(MARGIN - 1, rows + 2)]
    late_b[...] = fields[g3, pl.ds(MARGIN - 1, rows + 2)]
    down[...] = next_forcing[pl.ds(rows - 2, 2)]
    up[...] = next_forcing[pl.ds(0, 2)]
    depth = forcing.shape[1]
    if folded(rows, share, reach_of()):
        pack_folded(slots, flat, rows, depth, reach_of())
    else:
        pack_windows(slots, flat, rows, depth, share)


def put_rows(flat, first, value):
    depth = value.shape[1]
    for i in range(value.shape[0]):
        flat[pl.ds((first + i) * depth, depth), :] = value[i]


def reach_of():
    return lax.axis_size("tm") + 2


def folded(rows, share, reach):
    return rows == 16 and 2 * share == LANES and FIELDS * 2 * reach <= share


def pack_folded(slots, flat, rows, depth, reach):
    devices = slots.shape[0]
    lane = lax.broadcasted_iota(jnp.int32, (8, LANES), 1)
    place = lane % (LANES // 2)
    rims = [None] * devices
    for field in range(FIELDS):
        first = field * rows * depth
        cells = []
        for line in range(depth):
            top = flat[pl.ds(first + line, 8, stride=depth), :]
            low = flat[pl.ds(first + 8 * depth + line, 8, stride=depth), :]
            cells.append(jnp.where(lane < LANES // 2, top, pltpu.roll(low, LANES // 2, 1)))
            cells.append(jnp.where(lane < LANES // 2, pltpu.roll(top, LANES // 2, 1), low))
        for target in range(devices):
            slots[target, pl.ds(field * 8, 8)] = cells[target]
            left = cells[target - 1] if target > 0 else 0.0
            right = cells[target + 1] if target < devices - 1 else 0.0
            rim = jnp.where(
                place >= LANES // 2 - reach, left, jnp.where(place < reach, right, 0.0)
            )
            if field == 0:
                rims[target] = rim
            else:
                rims[target] = rims[target] + pltpu.roll(rim, 2 * reach * field, 1)
    for target in range(devices):
        slots[target, pl.ds(FIELDS * 8, 8)] = rims[target]


def unfold(slot, field, reach):
    cells, rims = slot[pl.ds(field * 8, 8)], slot[pl.ds(FIELDS * 8, 8)]
    lane = lax.broadcasted_iota(jnp.int32, (8, LANES), 1)
    half = LANES // 2
    near = pltpu.roll(rims, (REACH - 2 * reach * field) % LANES, 1)
    far = pltpu.roll(rims, (-REACH - 2 * reach * field) % LANES, 1)
    parts = []
    for shift, rim in ((REACH, far), (-REACH, near)):
        own = pltpu.roll(cells, shift % LANES, 1)
        value = jnp.where((lane >= REACH - reach) & (lane < REACH + half + reach), rim, 0.0)
        parts.append(jnp.where((lane >= REACH) & (lane < REACH + half), own, value))
    return jnp.concatenate(parts, axis=0)


def pack_windows(slots, flat, rows, depth, share):
    lane = lax.broadcasted_iota(jnp.int32, (rows, LANES), 1)
    for field in range(FIELDS):
        first = field * rows * depth
        lines = [flat[pl.ds(first + line, rows, stride=depth), :] for line in range(depth)]
        for target in range(slots.shape[0]):
            line, offset = target * share // LANES, target * share % LANES
            shift = (REACH - offset) % LANES
            place = lane + (offset - REACH)
            value = pltpu.roll(lines[line], shift, 1)
            if offset < REACH:
                before = pltpu.roll(lines[line - 1], shift, 1) if line > 0 else 0.0
                value = jnp.where(place < 0, before, value)
            if offset > REACH:
                after = pltpu.roll(lines[line + 1], shift, 1) if line < depth - 1 else 0.0
                value = jnp.where(place >= LANES, after, value)
            slots[target, pl.ds(field * rows, rows)] = value


def packing(rows, share):
    groups = LANES // share
    each = -(-(rows + 2 * UP_RIM) // groups)
    return groups, each, -(-each // 8) * 8


def sweep_kernel(share, rows, arrived, *refs):
    slabs = lax.axis_size("space")
    windows, (slots, diff, grow, terms, padded) = refs[:slabs], refs[slabs:]
    devices = arrived.shape[0]
    blocks = devices // slabs
    total = slabs * rows
    reach = reach_of()
    groups, each, held = packing(rows, share)
    for by, part in enumerate(windows):
        slab = (lax.axis_index("space") - by) % slabs
        start = pl.multiple_of(slab * rows, rows)
        diff[pl.ds(start, rows), :] = part[0]
        grow[pl.ds(start, rows), :] = part[1]
    line = lax.broadcasted_iota(jnp.int32, (total, LANES), 0)
    lane = lax.broadcasted_iota(jnp.int32, (held, LANES), 1)
    padded[...] = jnp.zeros(padded.shape, jnp.float32)

    def block(field, index):
        parts = []
        for slab in range(slabs):
            slot = arrived.at[index * slabs + slab]
            if folded(rows, share, reach):
                parts.append(unfold(slot, field, reach))
            else:
                parts.append(slot[pl.ds(field * rows, rows)])
        return jnp.concatenate(parts, axis=0)

    def slope_of(field):
        north = jnp.where(line == 0, 0.0, pltpu.roll(field, 1, 0))
        south = jnp.where(line == total - 1, 0.0, pltpu.roll(field, total - 1, 0))
        sides = pltpu.roll(field, 1, 1) + pltpu.roll(field, LANES - 1, 1)
        laplace = north + south + sides - 4.0 * field
        return diff[...] * laplace + grow[...] * field / (1.0 + field * field)

    field = None
    for index in range(blocks):
        behind = (index - 1) % blocks
        odd, term = block(0, behind), block(1, behind)
        even = odd + 4.0 * slope_of(odd) + term
        slope = slope_of(even)
        odd = even + 4.0 * slope + block(2, index)
        stepped = even + 8.0 * slope
        pair = odd + 4.0 * slope_of(odd) - stepped
        terms[index] = block(1, index) + pair
        if index == blocks - 1:
            field = stepped + terms[index]
    for index in range(blocks):
        for group in range(groups):
            padded[group, pl.ds(8, total), :] = pltpu.roll(
                field, (group * share - REACH) % LANES, 1
            )
        for slab in range(slabs):
            start = 8 + slab * rows - UP_RIM
            value = padded[0, pl.ds(start, held), :]
            for group in range(1, groups):
                piece = padded[group, pl.ds(start + group * each, held), :]
                value = jnp.where(lane >= group * share, piece, value)
            slots[index * slabs + slab] = value
        if index < blocks - 1:
            field = field + 8.0 * slope_of(field) + terms[index]


def up_kernel(
    share, arrived, next_forcing, above, below, late_a, late_b, core, coefs,
    out, fields, diff, grow, flat,
):
    rows = next_forcing.shape[0]
    depth = next_forcing.shape[1]
    low, high = flags()
    set_rims(fields.at[5], rows, 2, above[...], below[...], low, high)
    fields[5, pl.ds(MARGIN, rows)] = next_forcing[...]
    groups, each, held = packing(rows, share)
    take_coefs(rows, coefs, diff, grow)
    lane = lax.broadcasted_iota(jnp.int32, (depth, LANES), 1)
    for row in range(rows + 2 * UP_RIM):
        group, line = row // each, row % each
        value = None
        for part in range(groups):
            piece = arrived[pl.ds(part * held + line, depth, stride=groups * held), :]
            piece = pltpu.roll(piece, ((part - group) * share) % LANES, 1) if part != group else piece
            value = piece if value is None else jnp.where(lane >= part * share, piece, value)
        fields[0, MARGIN - UP_RIM + row] = value
    odd_first = CORES.index("o0") * rows

    def first(at, n):
        mid, slope = growth_of(fields.at[0], at, n, diff[pl.ds(at, n)], grow[pl.ds(at, n)])
        fields[2, pl.ds(at, n)] = mid + 4.0 * slope + fields[5, pl.ds(at, n)]

    def second(at, n):
        d, g = diff[pl.ds(at, n)], grow[pl.ds(at, n)]
        for start, late in ((0, late_a), (2, late_b)):
            mid, slope = growth_of(fields.at[start], at, n, d, g)
            fields[start + 1, pl.ds(at, n)] = mid + 2.0 * slope + late[pl.ds(at - MARGIN + 1, n)]

    def third(at, n):
        d, g = diff[pl.ds(at, n)], grow[pl.ds(at, n)]
        here = at - MARGIN
        for i in range(POINTS // 2):
            mid, slope = growth_of(fields.at[i], at, n, d, g)
            put_rows(flat, 2 * i * rows, mid)
            put_rows(flat, (2 * i + 1) * rows, mid + slope + core[pl.ds(odd_first + i * rows + here, n)])

    over_rows(rows, 2, first)
    over_rows(rows, 1, second)
    over_rows(rows, 0, third)
    for point in range(POINTS):
        for r in range(0, rows, 8):
            for c in range(depth):
                start = (point * rows + r) * depth + c
                out[point, pl.ds(r, 8), pl.ds(c * LANES, LANES)] = flat[
                    pl.ds(start, 8, stride=depth), :
                ]


def moved(array, blocks, slabs):
    tm, space = lax.axis_size("tm"), lax.axis_size("space")
    pairs = [
        (t * space + s, (t + blocks) % tm * space + (s + slabs) % space)
        for t in range(tm)
        for s in range(space)
    ]
    return lax.ppermute(array, ("tm", "space"), pairs)


def exchange(down, up, turn, slant_down, slant_up):
    return (
        moved(down, 0, 1), moved(up, 0, -1), moved(turn, 1, 0),
        moved(slant_down, 1, 1), moved(slant_up, 1, -1),
    )


def body(initial, source, diffusivity, growth):
    points, rows, cols = initial.shape
    assert points == POINTS and rows % 8 == 0 and cols % LANES == 0
    depth = cols // LANES
    tm, space = lax.axis_size("tm"), lax.axis_size("space")
    devices = tm * space
    share = cols // devices
    assert share * devices == cols and LANES % share == 0
    assert reach_of() <= REACH and REACH + share + reach_of() <= LANES
    _, _, held = packing(rows, share)
    wide = rows + 2 * MARGIN

    def lines(n):
        return (n * depth, LANES)

    def field(n):
        return (n, depth, LANES)

    def as_rows(array):
        return array.reshape(-1, depth, LANES)

    sides, behind = count(RIMS_0), count(BEHIND_0)
    *sends, evens, terms, diff, grow = call(
        pack_kernel,
        [lines(sides), lines(sides), lines(2 * rows), lines(behind), lines(behind)]
        + [(points // 2, rows, cols), source.shape, diffusivity.shape, growth.shape],
        [],
        initial, source, diffusivity, growth,
        place=pltpu.HBM, sems=points // 2 + 3,
    )
    core, back, *windows = call(
        functools.partial(core_kernel, share),
        [lines(len(CORES) * rows), lines(rows)] + [(2, rows, LANES)] * space,
        [],
        evens, terms, diff, grow,
    )
    arrived = exchange(*(as_rows(part) for part in sends))
    ahead = as_rows(moved(back, -1, 0))
    windows = [windows[0]] + [moved(windows[by], 0, by) for by in range(1, space)]
    core = as_rows(core)

    buffers = [(wide, depth, LANES), (wide, depth, LANES)]
    rim1, rimb = count(RIMS_1), count(BEHIND)
    turn, down, up, slant_down, slant_up, state, forcing, first_forcing, coefs = call(
        level0_kernel,
        [
            field(2 * rows), field(rim1), field(rim1), field(rimb), field(rimb),
            field(rows + 4), field(3 * rows), field(rows + 4), field(2 * (rows + 6)),
        ],
        [(len(CORES) + 2 + 3 * (POINTS // 2), wide, depth, LANES)] + buffers,
        core, *arrived,
    )
    arrived = exchange(down, up, turn, slant_down, slant_up)
    arrived, ahead, windows = lax.optimization_barrier((arrived, ahead, windows))
    held_rows = FIELDS * 8 + 8 if folded(rows, share, reach_of()) else FIELDS * rows
    slots, down, up, next_forcing, late_a, late_b = call(
        functools.partial(level1_kernel, share),
        [
            (devices, held_rows, LANES), field(2), field(2),
            field(rows), field(rows + 2), field(rows + 2),
        ],
        [(14, wide, depth, LANES)] + buffers + [(FIELDS * rows * depth, LANES)],
        state, forcing, first_forcing, coefs, turn, ahead, *arrived,
    )
    above, below = moved(down, 0, 1), moved(up, 0, -1)
    slots = lax.all_to_all(slots, ("tm", "space"), 0, 0, tiled=True)
    (slots,) = call(
        functools.partial(sweep_kernel, share, rows),
        [(devices, held, LANES)],
        [(space * rows, LANES), (space * rows, LANES), (tm, space * rows, LANES)]
        + [(LANES // share, 8 + space * rows + 2 * rows + held, LANES)],
        slots, *windows,
    )
    slots = lax.all_to_all(slots, ("tm", "space"), 0, 0, tiled=True)
    (out,) = call(
        functools.partial(up_kernel, share),
        [(points, rows, cols)],
        [(6, wide, depth, LANES)] + buffers + [(points * rows * depth, LANES)],
        slots.reshape(devices * held, LANES), next_forcing, above, below,
        late_a, late_b, core, coefs,
    )
    return out


def solution(mesh):
    placed = (P("tm", "space", None), P("tm", "space", None), P("space", None), P("space", None))
    return jax.shard_map(
        body, mesh=mesh, in_specs=placed, out_specs=P("tm", "space", None), check_vma=False
    )
```

time: 95.6 us -> 86.5 us (0.905)
  Pallas kernels: 18.9 us -> 10.9 us
  blocking collectives: 12.8 us -> 18.8 us
  starting transfers between devices: 30.4 us -> 25.4 us
  local copies, waits for them, and re-layouts: 6.97 us -> 4.26 us
  waiting for transfers between devices: 25.3 us -> 26.9 us
    pallas_call x7 -> x6, Pallas kernels: 18.9 us -> 10.9 us  [call(): pl.pallas_call(kernel, out_shape=tuple((jax.ShapeDtypeStruct(shape, jnp.f...]
    ppermute x19 -> x16, waiting for transfers between devices: 15.1 us -> 21.4 us  [moved(): return lax.ppermute(array, ('tm', 'space'), pairs)]
    all_to_all x1, blocking collectives: 12.8 us -> 18.8 us  [body(): slots = lax.all_to_all(slots, ('tm', 'space'), 0, 0, tiled=True)]
    all_to_all x1, waiting for transfers between devices: 10.2 us -> 5.48 us  [body(): slots = lax.all_to_all(slots, ('tm', 'space'), 0, 0, tiled=True)]
    ppermute x19 -> x16, starting transfers between devices: 25.4 us -> 22.8 us  [moved(): return lax.ppermute(array, ('tm', 'space'), pairs)]
    all_to_all x1, starting transfers between devices: 5.02 us -> 2.59 us  [body(): slots = lax.all_to_all(slots, ('tm', 'space'), 0, 0, tiled=True)]
    unnamed x14 -> x8, local copies, waits for them, and re-layouts: 4.86 us -> 4.26 us
  transfers between devices with their start and end apart: 20 -> 17, of which waited for: 6 -> 10; matrix products, arithmetic and copies ran while one was open for 3% -> 0% of each run, Pallas kernels for 5% -> 1%
where the time goes in v2:
time: 86.5 us; the launch traced here: 86.2 us
  waiting for transfers between devices  26.9 us (31%)
  starting transfers between devices  25.4 us (29%)
  blocking collectives  18.8 us (22%)
  Pallas kernels  10.9 us (13%)
  local copies, waits for them, and re-layouts  4.26 us (5%)
    ppermute x16, starting transfers between devices, moved(): return lax.ppermute(array, ('tm', 'space'), pairs)  22.8 us
    ppermute x16, waiting for transfers between devices, moved(): return lax.ppermute(array, ('tm', 'space'), pairs)  21.4 us
    all_to_all x1, blocking collectives, body(): slots = lax.all_to_all(slots, ('tm', 'space'), 0, 0, tiled=True)  18.8 us
    pallas_call x6, Pallas kernels, call(): pl.pallas_call(kernel, out_shape=tuple((jax.ShapeDtypeStruct(shape, jnp.f...  10.9 us
    all_to_all x1, waiting for transfers between devices, body(): slots = lax.all_to_all(slots, ('tm', 'space'), 0, 0, tiled=True)  5.48 us
    unnamed x8, local copies, waits for them, and re-layouts  4.26 us
    all_to_all x1, starting transfers between devices, body(): slots = lax.all_to_all(slots, ('tm', 'space'), 0, 0, tiled=True)  2.59 us
  transfers between devices with their start and end apart: 17, of which 10 were waited for; matrix products, arithmetic and copies ran while one was open for 0% of the time, Pallas kernels for 1%

profile of v2, /device:TPU:0, one launch (start us, length us, event | category | flops | bytes accessed | tf_op | source)
XLA Modules:
  0.0 86.2 jit_solution(1279819173561858632)
XLA Ops:
  0.0 0.0 copy-start
  0.0 1.2 %copy-done = f32[8,16,2048]{2,1,0:T(8,128)S(1)} copy-done((f32[8,16,2048]{2,1,0:T(8,128)S(1)}, f32[8,16,2048]{2,1,0:T(8,128)}, u32[]{:S(2)}) %copy-start) | copy-done | bytes 1048600
  1.2 0.0 copy-start.1
  1.2 1.2 %copy-done.1 = f32[8,16,2048]{2,1,0:T(8,128)S(1)} copy-done((f32[8,16,2048]{2,1,0:T(8,128)S(1)}, f32[8,16,2048]{2,1,0:T(8,128)}, u32[]{:S(2)}) %copy-start.1) | copy-done | bytes 1048600
  2.5 0.0 copy-start.2
  2.5 0.9 %copy-done.2 = f32[16,2048]{1,0:T(8,128)S(1)} copy-done((f32[16,2048]{1,0:T(8,128)S(1)}, f32[16,2048]{1,0:T(8,128)}, u32[]{:S(2)}) %copy-start.2) | copy-done | bytes 131096
  3.4 0.0 copy-start.3
  3.4 0.9 %copy-done.3 = f32[16,2048]{1,0:T(8,128)S(1)} copy-done((f32[16,2048]{1,0:T(8,128)S(1)}, f32[16,2048]{1,0:T(8,128)}, u32[]{:S(2)}) %copy-start.3) | copy-done | bytes 131096
  4.3 1.5 %shard_map.46 = (f32[576,128]{1,0:T(8,128)S(1)}, f32[576,128]{1,0:T(8,128)S(1)}, f32[512,128]{1,0:T(8,128)S(1)}, f32[112,128]{1,0:T(8,128)S(1)}, f32[112,128]{1,...) custom-call(f32[8,16,2048]{2,1,0:T(8,128)S(1)} %copy-done, ...), custom_call_target="tpu_custom_call" | custom-call | tf_op jit(solution)/shard_map/pallas_call | solution.py:39
  5.8 3.0 %collective-permute-start = (f32[36,16,128]{2,1,0:T(8,128)S(1)}, f32[36,16,128]{2,1,0:T(8,128)S(1)}, u32[]{:S(2)}, u32[]{:S(2)}) collective-permute-start(f32[36,16,128]{2,1,0:T(8,128)S(1)} %bitcast.13), channel_id=1, source_target_pairs={{0,1},{1,2},{2,3},{3,0},{4,5},{5,6},{6,7},{7,4},{8,9},{9,10},{10,1... | collective-permute-start | bytes 884744 | tf_op jit(solution)/shard_map/ppermute | solution.py:556
  8.8 1.0 %collective-permute-start.1 = (f32[36,16,128]{2,1,0:T(8,128)S(1)}, f32[36,16,128]{2,1,0:T(8,128)S(1)}, u32[]{:S(2)}, u32[]{:S(2)}) collective-permute-start(f32[36,16,128]{2,1,0:T(8,128)S(1)} %bitcast.12), channel_id=1, source_target_pairs={{0,3},{1,0},{2,1},{3,2},{4,7},{5,4},{6,5},{7,6},{8,11},{9,8},{10,9... | collective-permute-start | bytes 884744 | tf_op jit(solution)/shard_map/ppermute | solution.py:556
  9.8 0.0 collective-permute-start.2
  9.8 2.3 %collective-permute-start.3 = (f32[7,16,128]{2,1,0:T(8,128)S(1)}, f32[7,16,128]{2,1,0:T(8,128)S(1)}, u32[]{:S(2)}, u32[]{:S(2)}) collective-permute-start(f32[7,16,128]{2,1,0:T(8,128)S(1)} %bitcast.16), channel_id=1, source_target_pairs={{0,5},{1,6},{2,7},{3,4},{4,9},{5,10},{6,11},{7,8},{8,13},{9,14},{1... | collective-permute-start | bytes 172040 | tf_op jit(solution)/shard_map/ppermute | solution.py:556
  12.1 1.8 %collective-permute-start.4 = (f32[7,16,128]{2,1,0:T(8,128)S(1)}, f32[7,16,128]{2,1,0:T(8,128)S(1)}, u32[]{:S(2)}, u32[]{:S(2)}) collective-permute-start(f32[7,16,128]{2,1,0:T(8,128)S(1)} %bitcast.15), channel_id=1, source_target_pairs={{0,7},{1,4},{2,5},{3,6},{4,11},{5,8},{6,9},{7,10},{8,15},{9,12},{1... | collective-permute-start | bytes 172040 | tf_op jit(solution)/shard_map/ppermute | solution.py:556
  13.9 0.8 shard_map.47
  14.7 8.5 %collective-permute-done.3.behind_above = f32[7,16,128]{2,1,0:T(8,128)S(1)} collective-permute-done((f32[7,16,128]{2,1,0:T(8,128)S(1)}, f32[7,16,128]{2,1,0:T(8,128)S(1)}, u32[]{:S(2)}, u32[]{:S(2)}) %collective-permute-start.3) | collective-permute-done | bytes 57376 | tf_op jit(solution)/shard_map/ppermute | solution.py:556
  23.2 0.6 collective-permute-done.4.behind_below
  23.8 0.0 collective-permute-done.2.behind
  23.9 0.0 collective-permute-done.above
  23.9 0.7 collective-permute-done.1.below
  24.6 1.8 %shard_map.48 = (f32[32,16,128]{2,1,0:T(8,128)S(1)}, f32[8,16,128]{2,1,0:T(8,128)S(1)}, f32[8,16,128]{2,1,0:T(8,128)S(1)}, f32[5,16,128]{2,1,0:T(8,128)S(1)}, f3...) custom-call(f32[208,16,128]{2,1,0:T(8,128)S(1)} %bitcast.8, ...), custom_call_target="tpu_custom_call" | custom-call | tf_op jit(solution)/shard_map/pallas_call | solution.py:39
  26.4 1.1 %collective-permute-start.7 = (f32[32,16,128]{2,1,0:T(8,128)S(1)}, f32[32,16,128]{2,1,0:T(8,128)S(1)}, u32[]{:S(2)}, u32[]{:S(2)}) collective-permute-start(f32[32,16,128]{2,1,0:T(8,128)S(1)} %get-tuple-element.59.last_pair), channel_id=1, source_target_pairs={{0,4},{1,5},{2,6},{3,7},{4,8},{5,9},{6,10},{7,11},{8,12},{9,13},{1... | collective-permute-start | bytes 786440 | tf_op jit(solution)/shard_map/ppermute | solution.py:556
  27.5 3.3 %collective-permute-start.10 = (f32[256,128]{1,0:T(8,128)S(1)}, f32[256,128]{1,0:T(8,128)S(1)}, u32[]{:S(2)}, u32[]{:S(2)}) collective-permute-start(f32[256,128]{1,0:T(8,128)S(1)} %get-tuple-element.64), channel_id=1, source_target_pairs={{0,28},{1,29},{2,30},{3,31},{4,0},{5,1},{6,2},{7,3},{8,4},{9,5},{1... | collective-permute-start | bytes 393224 | tf_op jit(solution)/shard_map/ppermute | solution.py:556
  30.8 1.5 %collective-permute-start.11 = (f32[2,16,128]{2,1,0:T(8,128)S(1)}, f32[2,16,128]{2,1,0:T(8,128)S(1)}, u32[]{:S(2)}, u32[]{:S(2)}) collective-permute-start(f32[2,16,128]{2,1,0:T(8,128)S(1)} %get-tuple-element.66), channel_id=1, source_target_pairs={{0,1},{1,2},{2,3},{3,0},{4,5},{5,6},{6,7},{7,4},{8,9},{9,10},{10,1... | collective-permute-start | bytes 49160 | tf_op jit(solution)/shard_map/ppermute | solution.py:556
  32.3 0.5 collective-permute-start.12
  32.8 1.5 %collective-permute-start.5 = (f32[8,16,128]{2,1,0:T(8,128)S(1)}, f32[8,16,128]{2,1,0:T(8,128)S(1)}, u32[]{:S(2)}, u32[]{:S(2)}) collective-permute-start(f32[8,16,128]{2,1,0:T(8,128)S(1)} %get-tuple-element.60), channel_id=1, source_target_pairs={{0,1},{1,2},{2,3},{3,0},{4,5},{5,6},{6,7},{7,4},{8,9},{9,10},{10,1... | collective-permute-start | bytes 196616 | tf_op jit(solution)/shard_map/ppermute | solution.py:556
  34.3 1.1 %collective-permute-done.11.refs_1_ = f32[2,16,128]{2,1,0:T(8,128)S(1)} collective-permute-done((f32[2,16,128]{2,1,0:T(8,128)S(1)}, f32[2,16,128]{2,1,0:T(8,128)S(1)}, u32[]{:S(2)}, u32[]{:S(2)}) %collective-permute-start.11) | collective-permute-done | bytes 16416 | tf_op jit(solution)/shard_map/ppermute | solution.py:556
  35.4 0.7 collective-permute-start.6
  36.1 0.0 collective-permute-done.12.refs_2_
  36.2 1.7 %collective-permute-start.13 = (f32[2,16,128]{2,1,0:T(8,128)S(1)}, f32[2,16,128]{2,1,0:T(8,128)S(1)}, u32[]{:S(2)}, u32[]{:S(2)}) collective-permute-start(f32[2,16,128]{2,1,0:T(8,128)S(1)} %get-tuple-element.68), channel_id=1, source_target_pairs={{0,3},{1,0},{2,1},{3,2},{4,7},{5,4},{6,5},{7,6},{8,11},{9,8},{10,9... | collective-permute-start | bytes 49160 | tf_op jit(solution)/shard_map/ppermute | solution.py:556
  37.9 2.0 %collective-permute-done.13.refs_3_ = f32[2,16,128]{2,1,0:T(8,128)S(1)} collective-permute-done((f32[2,16,128]{2,1,0:T(8,128)S(1)}, f32[2,16,128]{2,1,0:T(8,128)S(1)}, u32[]{:S(2)}, u32[]{:S(2)}) %collective-permute-start.13) | collective-permute-done | bytes 16416 | tf_op jit(solution)/shard_map/ppermute | solution.py:556
  39.9 0.0 collective-permute-start.8
  39.9 0.0 collective-permute-done.10
  39.9 1.5 %collective-permute-start.9 = (f32[5,16,128]{2,1,0:T(8,128)S(1)}, f32[5,16,128]{2,1,0:T(8,128)S(1)}, u32[]{:S(2)}, u32[]{:S(2)}) collective-permute-start(f32[5,16,128]{2,1,0:T(8,128)S(1)} %get-tuple-element.63), channel_id=1, source_target_pairs={{0,7},{1,4},{2,5},{3,6},{4,11},{5,8},{6,9},{7,10},{8,15},{9,12},{1... | collective-permute-start | bytes 122888 | tf_op jit(solution)/shard_map/ppermute | solution.py:556
  41.4 5.5 %collective-permute-done.8.behind_above = f32[5,16,128]{2,1,0:T(8,128)S(1)} collective-permute-done((f32[5,16,128]{2,1,0:T(8,128)S(1)}, f32[5,16,128]{2,1,0:T(8,128)S(1)}, u32[]{:S(2)}, u32[]{:S(2)}) %collective-permute-start.8) | collective-permute-done | bytes 40992 | tf_op jit(solution)/shard_map/ppermute | solution.py:556
  46.9 0.3 collective-permute-done.9.behind_below
  47.2 0.0 collective-permute-done.5.above
  47.2 0.0 collective-permute-done.6.below
  47.2 0.0 collective-permute-done.7.behind
  47.2 1.2 %shard_map.49 = (f32[32,32,128]{2,1,0:T(8,128)S(1)}, f32[2,16,128]{2,1,0:T(8,128)S(1)}, f32[2,16,128]{2,1,0:T(8,128)S(1)}, f32[16,16,128]{2,1,0:T(8,128)S(1)}, f...) custom-call(f32[20,16,128]{2,1,0:T(8,128)S(1)} %get-tuple-element.55.state, ...), custom_call_target="tpu_custom_call" | custom-call | tf_op jit(solution)/shard_map/pallas_call | solution.py:39
  48.5 18.8 %all_to_all.10.arrived = f32[32,32,128]{2,1,0:T(8,128)S(1)} all-to-all(f32[32,32,128]{2,1,0:T(8,128)S(1)} %get-tuple-element.75), channel_id=1, replica_groups=mesh['tm'=8,'space'=4] {'tm','space'}, dimensions={0} | all-to-all | bytes 1048576 | tf_op jit(solution)/shard_map/all_to_all | solution.py:631
  67.2 3.3 %shard_map.50 = f32[32,16,128]{2,1,0:T(8,128)} custom-call(f32[32,32,128]{2,1,0:T(8,128)S(1)} %all_to_all.10.arrived, f32[2,16,128]{2,1,0:T(8,128)S(1)} %get-tuple-element.76.refs_0_, f32[2,16,128]{2,1,0:T(8,128)S(1)} %collective-permute-done.11.refs_1_, f32[2,16,128]{2,1,0:T(8,128)S(1)} %collective-permute-done.12.refs_2_, ...), custom_call_target="tpu_custom_call" | custom-call | tf_op jit(solution)/shard_map/pallas_call | solution.py:39
  70.6 2.6 %all-to-all-start.1 = ((f32[32,16,128]{2,1,0:T(8,128)}), f32[32,16,128]{2,1,0:T(8,128)S(1)}, u32[]{:S(2)}, u32[]{:S(2)}) async-start(f32[32,16,128]{2,1,0:T(8,128)} %shard_map.50), calls=%async_computation.1 | async-start | bytes 524288 | tf_op jit(solution)/shard_map/all_to_all | solution.py:639
  73.2 1.7 %collective-permute-start.14 = (f32[2,16,128]{2,1,0:T(8,128)S(1)}, f32[2,16,128]{2,1,0:T(8,128)S(1)}, u32[]{:S(2)}, u32[]{:S(2)}) collective-permute-start(f32[2,16,128]{2,1,0:T(8,128)S(1)} %get-tuple-element.81), channel_id=1, source_target_pairs={{0,1},{1,2},{2,3},{3,0},{4,5},{5,6},{6,7},{7,4},{8,9},{9,10},{10,1... | collective-permute-start | bytes 49160 | tf_op jit(solution)/shard_map/ppermute | solution.py:556
  74.9 1.3 %collective-permute-start.15 = (f32[2,16,128]{2,1,0:T(8,128)S(1)}, f32[2,16,128]{2,1,0:T(8,128)S(1)}, u32[]{:S(2)}, u32[]{:S(2)}) collective-permute-start(f32[2,16,128]{2,1,0:T(8,128)S(1)} %get-tuple-element.82), channel_id=1, source_target_pairs={{0,3},{1,0},{2,1},{3,2},{4,7},{5,4},{6,5},{7,6},{8,11},{9,8},{10,9... | collective-permute-start | bytes 49160 | tf_op jit(solution)/shard_map/ppermute | solution.py:556
  76.2 1.8 %collective-permute-done.14.above = f32[2,16,128]{2,1,0:T(8,128)S(1)} collective-permute-done((f32[2,16,128]{2,1,0:T(8,128)S(1)}, f32[2,16,128]{2,1,0:T(8,128)S(1)}, u32[]{:S(2)}, u32[]{:S(2)}) %collective-permute-start.14) | collective-permute-done | bytes 16416 | tf_op jit(solution)/shard_map/ppermute | solution.py:556
  78.0 0.7 collective-permute-done.15.below
  78.7 5.5 %all-to-all-done.1 = f32[32,16,128]{2,1,0:T(8,128)S(1)} async-done(((f32[32,16,128]{2,1,0:T(8,128)}), f32[32,16,128]{2,1,0:T(8,128)S(1)}, u32[]{:S(2)}, u32[]{:S(2)}) %all-to-all-start.1) | async-done | bytes 262176 | tf_op jit(solution)/shard_map/all_to_all | solution.py:639
  84.1 2.1 %shard_map.51 = f32[8,16,2048]{2,1,0:T(8,128)} custom-call(f32[512,128]{1,0:T(8,128)S(1)} %bitcast.10, f32[16,16,128]{2,1,0:T(8,128)S(1)} %get-tuple-element.80.next_forcing, f32[2,16,128]{2,1,0:T(8,128)S(1)} %collective-permute-done.14.above, f32[2,16,128]{2,1,0:T(8,128)S(1)} %collective-permute-done.15.below, f32[18,16,128]{2,1,0:T(8,128)S(1)} %get-tuple-element.83.late_a, ...), custom_call_target="tpu_custom_call" | custom-call | tf_op jit(solution)/shard_map/pallas_call | solution.py:39
Async XLA Ops:
  0.0 1.2 %copy-start = (f32[8,16,2048]{2,1,0:T(8,128)S(1)}, f32[8,16,2048]{2,1,0:T(8,128)}, u32[]{:S(2)}) copy-start(f32[8,16,2048]{2,1,0:T(8,128)} %initial_all.1) | copy-start | bytes 3145732
  1.2 1.2 %copy-start.1 = (f32[8,16,2048]{2,1,0:T(8,128)S(1)}, f32[8,16,2048]{2,1,0:T(8,128)}, u32[]{:S(2)}) copy-start(f32[8,16,2048]{2,1,0:T(8,128)} %source_all.1) | copy-start | bytes 3145732
  2.5 0.9 %copy-start.2 = (f32[16,2048]{1,0:T(8,128)S(1)}, f32[16,2048]{1,0:T(8,128)}, u32[]{:S(2)}) copy-start(f32[16,2048]{1,0:T(8,128)} %diffusivity_all.1) | copy-start | bytes 393220
  3.4 0.9 %copy-start.3 = (f32[16,2048]{1,0:T(8,128)S(1)}, f32[16,2048]{1,0:T(8,128)}, u32[]{:S(2)}) copy-start(f32[16,2048]{1,0:T(8,128)} %growth_all.1) | copy-start | bytes 393220
  5.8 18.0 %collective-permute-start = (f32[36,16,128]{2,1,0:T(8,128)S(1)}, f32[36,16,128]{2,1,0:T(8,128)S(1)}, u32[]{:S(2)}, u32[]{:S(2)}) collective-permute-start(f32[36,16,128]{2,1,0:T(8,128)S(1)} %bitcast.13), channel_id=1, source_target_pairs={{0,1},{1,2},{2,3},{3,0},{4,5},{5,6},{6,7},{7,4},{8,9},{9,10},{10,1... | collective-permute-start | bytes 884744 | tf_op jit(solution)/shard_map/ppermute | solution.py:556
  8.8 15.8 %collective-permute-start.1 = (f32[36,16,128]{2,1,0:T(8,128)S(1)}, f32[36,16,128]{2,1,0:T(8,128)S(1)}, u32[]{:S(2)}, u32[]{:S(2)}) collective-permute-start(f32[36,16,128]{2,1,0:T(8,128)S(1)} %bitcast.12), channel_id=1, source_target_pairs={{0,3},{1,0},{2,1},{3,2},{4,7},{5,4},{6,5},{7,6},{8,11},{9,8},{10,9... | collective-permute-start | bytes 884744 | tf_op jit(solution)/shard_map/ppermute | solution.py:556
  9.8 14.0 %collective-permute-start.2 = (f32[32,16,128]{2,1,0:T(8,128)S(1)}, f32[32,16,128]{2,1,0:T(8,128)S(1)}, u32[]{:S(2)}, u32[]{:S(2)}) collective-permute-start(f32[32,16,128]{2,1,0:T(8,128)S(1)} %bitcast.14), channel_id=1, source_target_pairs={{0,4},{1,5},{2,6},{3,7},{4,8},{5,9},{6,10},{7,11},{8,12},{9,13},{1... | collective-permute-start | bytes 786440 | tf_op jit(solution)/shard_map/ppermute | solution.py:556
  9.8 13.4 %collective-permute-start.3 = (f32[7,16,128]{2,1,0:T(8,128)S(1)}, f32[7,16,128]{2,1,0:T(8,128)S(1)}, u32[]{:S(2)}, u32[]{:S(2)}) collective-permute-start(f32[7,16,128]{2,1,0:T(8,128)S(1)} %bitcast.16), channel_id=1, source_target_pairs={{0,5},{1,6},{2,7},{3,4},{4,9},{5,10},{6,11},{7,8},{8,13},{9,14},{1... | collective-permute-start | bytes 172040 | tf_op jit(solution)/shard_map/ppermute | solution.py:556
  12.1 11.7 %collective-permute-start.4 = (f32[7,16,128]{2,1,0:T(8,128)S(1)}, f32[7,16,128]{2,1,0:T(8,128)S(1)}, u32[]{:S(2)}, u32[]{:S(2)}) collective-permute-start(f32[7,16,128]{2,1,0:T(8,128)S(1)} %bitcast.15), channel_id=1, source_target_pairs={{0,7},{1,4},{2,5},{3,6},{4,11},{5,8},{6,9},{7,10},{8,15},{9,12},{1... | collective-permute-start | bytes 172040 | tf_op jit(solution)/shard_map/ppermute | solution.py:556
  26.4 20.8 %collective-permute-start.7 = (f32[32,16,128]{2,1,0:T(8,128)S(1)}, f32[32,16,128]{2,1,0:T(8,128)S(1)}, u32[]{:S(2)}, u32[]{:S(2)}) collective-permute-start(f32[32,16,128]{2,1,0:T(8,128)S(1)} %get-tuple-element.59.last_pair), channel_id=1, source_target_pairs={{0,4},{1,5},{2,6},{3,7},{4,8},{5,9},{6,10},{7,11},{8,12},{9,13},{1... | collective-permute-start | bytes 786440 | tf_op jit(solution)/shard_map/ppermute | solution.py:556
  27.5 12.4 %collective-permute-start.10 = (f32[256,128]{1,0:T(8,128)S(1)}, f32[256,128]{1,0:T(8,128)S(1)}, u32[]{:S(2)}, u32[]{:S(2)}) collective-permute-start(f32[256,128]{1,0:T(8,128)S(1)} %get-tuple-element.64), channel_id=1, source_target_pairs={{0,28},{1,29},{2,30},{3,31},{4,0},{5,1},{6,2},{7,3},{8,4},{9,5},{1... | collective-permute-start | bytes 393224 | tf_op jit(solution)/shard_map/ppermute | solution.py:556
  30.8 4.6 %collective-permute-start.11 = (f32[2,16,128]{2,1,0:T(8,128)S(1)}, f32[2,16,128]{2,1,0:T(8,128)S(1)}, u32[]{:S(2)}, u32[]{:S(2)}) collective-permute-start(f32[2,16,128]{2,1,0:T(8,128)S(1)} %get-tuple-element.66), channel_id=1, source_target_pairs={{0,1},{1,2},{2,3},{3,0},{4,5},{5,6},{6,7},{7,4},{8,9},{9,10},{10,1... | collective-permute-start | bytes 49160 | tf_op jit(solution)/shard_map/ppermute | solution.py:556
  32.3 3.9 %collective-permute-start.12 = (f32[2,16,128]{2,1,0:T(8,128)S(1)}, f32[2,16,128]{2,1,0:T(8,128)S(1)}, u32[]{:S(2)}, u32[]{:S(2)}) collective-permute-start(f32[2,16,128]{2,1,0:T(8,128)S(1)} %get-tuple-element.67), channel_id=1, source_target_pairs={{0,2},{1,3},{2,0},{3,1},{4,6},{5,7},{6,4},{7,5},{8,10},{9,11},{10,... | collective-permute-start | bytes 49160 | tf_op jit(solution)/shard_map/ppermute | solution.py:556
  32.8 14.4 %collective-permute-start.5 = (f32[8,16,128]{2,1,0:T(8,128)S(1)}, f32[8,16,128]{2,1,0:T(8,128)S(1)}, u32[]{:S(2)}, u32[]{:S(2)}) collective-permute-start(f32[8,16,128]{2,1,0:T(8,128)S(1)} %get-tuple-element.60), channel_id=1, source_target_pairs={{0,1},{1,2},{2,3},{3,0},{4,5},{5,6},{6,7},{7,4},{8,9},{9,10},{10,1... | collective-permute-start | bytes 196616 | tf_op jit(solution)/shard_map/ppermute | solution.py:556
  35.4 11.8 %collective-permute-start.6 = (f32[8,16,128]{2,1,0:T(8,128)S(1)}, f32[8,16,128]{2,1,0:T(8,128)S(1)}, u32[]{:S(2)}, u32[]{:S(2)}) collective-permute-start(f32[8,16,128]{2,1,0:T(8,128)S(1)} %get-tuple-element.61), channel_id=1, source_target_pairs={{0,3},{1,0},{2,1},{3,2},{4,7},{5,4},{6,5},{7,6},{8,11},{9,8},{10,9... | collective-permute-start | bytes 196616 | tf_op jit(solution)/shard_map/ppermute | solution.py:556
  36.2 3.7 %collective-permute-start.13 = (f32[2,16,128]{2,1,0:T(8,128)S(1)}, f32[2,16,128]{2,1,0:T(8,128)S(1)}, u32[]{:S(2)}, u32[]{:S(2)}) collective-permute-start(f32[2,16,128]{2,1,0:T(8,128)S(1)} %get-tuple-element.68), channel_id=1, source_target_pairs={{0,3},{1,0},{2,1},{3,2},{4,7},{5,4},{6,5},{7,6},{8,11},{9,8},{10,9... | collective-permute-start | bytes 49160 | tf_op jit(solution)/shard_map/ppermute | solution.py:556
  39.9 7.0 %collective-permute-start.8 = (f32[5,16,128]{2,1,0:T(8,128)S(1)}, f32[5,16,128]{2,1,0:T(8,128)S(1)}, u32[]{:S(2)}, u32[]{:S(2)}) collective-permute-start(f32[5,16,128]{2,1,0:T(8,128)S(1)} %get-tuple-element.62), channel_id=1, source_target_pairs={{0,5},{1,6},{2,7},{3,4},{4,9},{5,10},{6,11},{7,8},{8,13},{9,14},{1... | collective-permute-start | bytes 122888 | tf_op jit(solution)/shard_map/ppermute | solution.py:556
  39.9 7.3 %collective-permute-start.9 = (f32[5,16,128]{2,1,0:T(8,128)S(1)}, f32[5,16,128]{2,1,0:T(8,128)S(1)}, u32[]{:S(2)}, u32[]{:S(2)}) collective-permute-start(f32[5,16,128]{2,1,0:T(8,128)S(1)} %get-tuple-element.63), channel_id=1, source_target_pairs={{0,7},{1,4},{2,5},{3,6},{4,11},{5,8},{6,9},{7,10},{8,15},{9,12},{1... | collective-permute-start | bytes 122888 | tf_op jit(solution)/shard_map/ppermute | solution.py:556
  70.6 13.5 %all-to-all-start.1 = ((f32[32,16,128]{2,1,0:T(8,128)}), f32[32,16,128]{2,1,0:T(8,128)S(1)}, u32[]{:S(2)}, u32[]{:S(2)}) async-start(f32[32,16,128]{2,1,0:T(8,128)} %shard_map.50), calls=%async_computation.1 | async-start | bytes 524288 | tf_op jit(solution)/shard_map/all_to_all | solution.py:639
  73.2 4.8 %collective-permute-start.14 = (f32[2,16,128]{2,1,0:T(8,128)S(1)}, f32[2,16,128]{2,1,0:T(8,128)S(1)}, u32[]{:S(2)}, u32[]{:S(2)}) collective-permute-start(f32[2,16,128]{2,1,0:T(8,128)S(1)} %get-tuple-element.81), channel_id=1, source_target_pairs={{0,1},{1,2},{2,3},{3,0},{4,5},{5,6},{6,7},{7,4},{8,9},{9,10},{10,1... | collective-permute-start | bytes 49160 | tf_op jit(solution)/shard_map/ppermute | solution.py:556
  74.9 3.8 %collective-permute-start.15 = (f32[2,16,128]{2,1,0:T(8,128)S(1)}, f32[2,16,128]{2,1,0:T(8,128)S(1)}, u32[]{:S(2)}, u32[]{:S(2)}) collective-permute-start(f32[2,16,128]{2,1,0:T(8,128)S(1)} %get-tuple-element.82), channel_id=1, source_target_pairs={{0,3},{1,0},{2,1},{3,2},{4,7},{5,4},{6,5},{7,6},{8,11},{9,8},{10,9... | collective-permute-start | bytes 49160 | tf_op jit(solution)/shard_map/ppermute | solution.py:556

commit v3 on v2

--- a/solution.py
+++ b/solution.py
@@ -17,13 +17,16 @@
 time_step = 0.02
 
 RIMS_0 = (
-    ("e0", 4), ("e1", 4), ("e2", 4),
-    ("o0", 3), ("o1", 3), ("o2", 3), ("o3", 1),
+    ("e0", 2), ("e1", 2), ("e2", 2),
+    ("o0", 1), ("o1", 1), ("o2", 1), ("o3", 1),
     ("s0", 2), ("s1", 2), ("s2", 2), ("s3", 2),
     ("d", 3), ("g", 3),
 )
+BEHIND_0 = (("ep", 2), ("op", 1))
+STEPS_0 = (("e0", "o0"), ("e1", "o1"), ("e2", "o2"))
+STEPS_BEHIND_0 = (("ep", "op"),)
 CORES = ("e0", "e1", "e2", "o0", "o1", "o2", "o3", "s0", "s1", "s2", "s3", "d", "g")
-BEHIND_0 = (("ep", 4), ("op", 3))
+RIMS_1 = (("next", 3), ("g1", 1), ("g3", 1), ("g2", 2))
 BEHIND = (("pair", 2), ("odd", 3))
 
 
@@ -60,11 +63,14 @@
     return left + right
 
 
-def growth_of(ref, at, rows, diff, grow):
-    wide = ref[pl.ds(at - 1, rows + 2)]
+def slope_of_rows(wide, diff, grow):
     mid = wide[1:-1]
     laplace = wide[:-2] + wide[2:] + beside(mid) - 4.0 * mid
     return mid, diff * laplace + grow * mid / (1.0 + mid * mid)
+
+
+def growth_of(ref, at, rows, diff, grow):
+    return slope_of_rows(ref[pl.ds(at - 1, rows + 2)], diff, grow)
 
 
 def over_rows(rows, rim, body):
@@ -101,7 +107,7 @@
 
 def pack_kernel(
     initial_all, source_all, diffusivity_all, growth_all,
-    down, up, turn, slant_down, slant_up, evens, source, diffusivity, growth, sems,
+    down, up, turn, slant_down, slant_up, evens, source, diffusivity, growth, edge, sems,
 ):
     pairs = [(initial_all.at[2 * i], evens.at[i]) for i in range(POINTS // 2)]
     pairs += [(source_all, source), (diffusivity_all, diffusivity), (growth_all, growth)]
@@ -112,22 +118,37 @@
         copy.wait()
     rows, cols = diffusivity.shape
     depth = cols // LANES
-    for rims, low, high in ((RIMS_0, down, up), (BEHIND_0, slant_down, slant_up)):
-        at = 0
-        for name, rim in rims:
-            get = pieces(name, evens, source, diffusivity, growth)
-            for c in range(depth):
-                lanes = pl.ds(c * LANES, LANES)
-                place = pl.ds(at * depth + c, rim, stride=depth)
-                low[place, :] = get(pl.ds(rows - rim, rim), lanes)
-                high[place, :] = get(pl.ds(0, rim), lanes)
-            at += rim
-    for index, (name, _) in enumerate(BEHIND_0):
+
+    def put(ref, at, name, first, count):
         get = pieces(name, evens, source, diffusivity, growth)
         for c in range(depth):
-            for r in range(0, rows, 8):
-                place = pl.ds((index * rows + r) * depth + c, 8, stride=depth)
-                turn[place, :] = get(pl.ds(r, 8), pl.ds(c * LANES, LANES))
+            place = pl.ds(at * depth + c, count, stride=depth)
+            ref[place, :] = get(pl.ds(first, count), pl.ds(c * LANES, LANES))
+
+    def rows_of(at, count):
+        return edge[pl.ds(at * depth, count * depth), :].reshape(count, depth, LANES)
+
+    for rims, steps, low, high in (
+        (RIMS_0, STEPS_0, down, up),
+        (BEHIND_0, STEPS_BEHIND_0, slant_down, slant_up),
+    ):
+        for ref, outer, inner in ((low, rows - 4, rows - 3), (high, 0, 1)):
+            at = 0
+            for name, rim in rims:
+                put(ref, at, name, rows - rim if ref is low else 0, rim)
+                at += rim
+            put(edge, 0, "d", inner, 2)
+            put(edge, 2, "g", inner, 2)
+            for start, term in steps:
+                put(edge, 4, start, outer, 4)
+                put(edge, 8, term, inner, 2)
+                wide = rows_of(4, 4)
+                mid, slope = slope_of_rows(wide, rows_of(0, 2), rows_of(2, 2))
+                put_rows(ref, at, mid + slope + rows_of(8, 2))
+                at += 2
+    for index, (name, _) in enumerate(BEHIND_0):
+        for r in range(0, rows, 8):
+            put(turn, index * rows + r, name, r, 8)
 
 
 def window(get, first, depth):
@@ -173,16 +194,21 @@
 
 def level0_kernel(
     core, above, below, behind, behind_above, behind_below,
-    turn, down, up, slant_down, slant_up, state, forcing, first_forcing, coefs,
+    turn, down, up, slant_down, slant_up, next_odd, forcing, first_forcing, coefs,
     fields, diff, grow,
 ):
     rows = core.shape[0] // len(CORES)
     low, high = flags()
     names = list(CORES) + ["ep", "op"]
     spots = {name: index for index, name in enumerate(names)}
-    for rims, from_low, from_high in (
-        (RIMS_0, above, below),
-        (BEHIND_0, behind_above, behind_below),
+    extra = len(names)
+    halves = POINTS // 2
+    odd = [extra + i for i in range(halves)]
+    even = [extra + halves + i for i in range(halves)]
+    image = [extra + 2 * halves + i for i in range(halves)]
+    for rims, steps, from_low, from_high in (
+        (RIMS_0, STEPS_0, above, below),
+        (BEHIND_0, STEPS_BEHIND_0, behind_above, behind_below),
     ):
         lows, highs = split(from_low, rims), split(from_high, rims)
         for name, rim in rims:
@@ -191,6 +217,13 @@
             else:
                 buffer = fields.at[spots[name]]
             set_rims(buffer, rows, rim, lows[name], highs[name], low, high)
+        at = count(rims)
+        for start, _ in steps:
+            buffer = fields.at[odd[0 if start == "ep" else int(start[1]) + 1]]
+            set_rims(
+                buffer, rows, 3, from_low[pl.ds(at, 2)], from_high[pl.ds(at, 2)], low, high, 1
+            )
+            at += 2
     for name in CORES:
         if name in ("d", "g"):
             buffer = diff if name == "d" else grow
@@ -199,11 +232,6 @@
         buffer[pl.ds(MARGIN, rows)] = core[pl.ds(CORES.index(name) * rows, rows)]
     for index, (name, _) in enumerate(BEHIND_0):
         fields[spots[name], pl.ds(MARGIN, rows)] = behind[pl.ds(index * rows, rows)]
-    extra = len(names)
-    halves = POINTS // 2
-    odd = [extra + i for i in range(halves)]
-    even = [extra + halves + i for i in range(halves)]
-    image = [extra + 2 * halves + i for i in range(halves)]
 
     def first(at, n):
         d, g = diff[pl.ds(at, n)], grow[pl.ds(at, n)]
@@ -236,28 +264,26 @@
             else:
                 term = fields[spots[f"s{i + 1}"], pl.ds(at, n)] + pair
                 forcing[pl.ds(i * rows + here, n)] = term
+                if i == 0:
+                    next_odd[...] = fields[image[0], pl.ds(at, n)] + term
                 if i == halves - 2:
                     turn[pl.ds(rows + here, n)] = fields[image[i], pl.ds(at, n)] + term
 
-    over_rows(rows, 3, first)
+    over_rows(rows, 1, first)
     over_rows(rows, 2, second)
     over_rows(rows, 1, third)
     over_rows(rows, 0, fourth)
-    state[...] = fields[even[0], pl.ds(MARGIN - 2, rows + 4)]
     first_forcing[...] = fields[spots["s0"], pl.ds(MARGIN - 2, rows + 4)]
     coefs[pl.ds(0, rows + 6)] = diff[pl.ds(MARGIN - 3, rows + 6)]
     coefs[pl.ds(rows + 6, rows + 6)] = grow[pl.ds(MARGIN - 3, rows + 6)]
     send_behind(turn, slant_down, slant_up, rows)
-    down[pl.ds(0, 2)] = fields[even[0], pl.ds(MARGIN + rows - 4, 2)]
-    up[pl.ds(0, 2)] = fields[even[0], pl.ds(MARGIN + 2, 2)]
-    at = 2
-    for which, rim in ((0, 3), (2, 1), (1, 2)):
-        down[pl.ds(at, rim)] = forcing[pl.ds((which + 1) * rows - rim, rim)]
-        up[pl.ds(at, rim)] = forcing[pl.ds(which * rows, rim)]
+    at = 0
+    for (name, rim), (ref, first_row) in zip(
+        RIMS_1, ((next_odd, 0), (forcing, 0), (forcing, 2 * rows), (forcing, rows)), strict=True
+    ):
+        down[pl.ds(at, rim)] = ref[pl.ds(first_row + rows - rim, rim)]
+        up[pl.ds(at, rim)] = ref[pl.ds(first_row, rim)]
         at += rim
-
-
-RIMS_1 = (("state", 2), ("g1", 3), ("g3", 1), ("g2", 2))
 
 
 def send_behind(turn, slant_down, slant_up, rows):
@@ -282,21 +308,19 @@
 
 
 def level1_kernel(
-    share, state, forcing, first_forcing, coefs, last_pair, ahead,
+    share, next_odd, forcing, first_forcing, coefs, last_pair, ahead,
     above, below, behind, behind_above, behind_below,
-    slots, down, up, next_forcing, late_a, late_b,
+    slots, next_forcing, late_a, late_b,
     fields, diff, grow, flat,
 ):
     rows = forcing.shape[0] // 3
     low, high = flags()
     take_coefs(rows, coefs, diff, grow)
-    v, g1, g3, g2, g0, pair, before, after, even0, even1, image0, image1, odd0, odd1 = range(14)
+    g1, g3, g2, g0, pair, before, after, even0, even1, image0, image1, odd0, odd1 = range(13)
     lows, highs = split(above, RIMS_1), split(below, RIMS_1)
-    for name, spot, rim, inner in (
-        ("state", v, 4, 2), ("g1", g1, 3, 0), ("g3", g3, 1, 0), ("g2", g2, 2, 0),
-    ):
-        set_rims(fields.at[spot], rows, rim, lows[name], highs[name], low, high, inner)
-    fields[v, pl.ds(MARGIN - 2, rows + 4)] = state[...]
+    for (name, rim), spot in zip(RIMS_1, (after, g1, g3, g2), strict=True):
+        set_rims(fields.at[spot], rows, rim, lows[name], highs[name], low, high)
+    fields[after, pl.ds(MARGIN, rows)] = next_odd[...]
     for which, spot in enumerate((g1, g2, g3)):
         fields[spot, pl.ds(MARGIN, rows)] = forcing[pl.ds(which * rows, rows)]
     take_behind(
@@ -305,10 +329,6 @@
     fields[g0, pl.ds(MARGIN - 2, rows + 4)] = (
         first_forcing[...] + fields[pair, pl.ds(MARGIN - 2, rows + 4)]
     )
-
-    def first(at, n):
-        mid, slope = growth_of(fields.at[v], at, n, diff[pl.ds(at, n)], grow[pl.ds(at, n)])
-        fields[after, pl.ds(at, n)] = mid + 2.0 * slope + fields[g1, pl.ds(at, n)]
 
     def second(at, n):
         d, g = diff[pl.ds(at, n)], grow[pl.ds(at, n)]
@@ -336,14 +356,11 @@
         put_rows(flat, 2 * rows, term)
         put_rows(flat, 0, image + term)
 
-    over_rows(rows, 3, first)
     over_rows(rows, 2, second)
     over_rows(rows, 1, third)
     over_rows(rows, 0, fourth)
     late_a[...] = fields[g1, pl.ds(MARGIN - 1, rows + 2)]
     late_b[...] = fields[g3, pl.ds(MARGIN - 1, rows + 2)]
-    down[...] = next_forcing[pl.ds(rows - 2, 2)]
-    up[...] = next_forcing[pl.ds(0, 2)]
     depth = forcing.shape[1]
     if folded(rows, share, reach_of()):
         pack_folded(slots, flat, rows, depth, reach_of())
@@ -426,15 +443,19 @@
             slots[target, pl.ds(field * rows, rows)] = value
 
 
+def late_rows(rows):
+    return (-2, -1, rows, rows + 1)
+
+
 def packing(rows, share):
     groups = LANES // share
     each = -(-(rows + 2 * UP_RIM) // groups)
-    return groups, each, -(-each // 8) * 8
+    return groups, each, -(-(each + -(-4 // groups)) // 8) * 8
 
 
 def sweep_kernel(share, rows, arrived, *refs):
     slabs = lax.axis_size("space")
-    windows, (slots, diff, grow, terms, padded) = refs[:slabs], refs[slabs:]
+    windows, (slots, diff, grow, terms, padded, kept) = refs[:slabs], refs[slabs:]
     devices = arrived.shape[0]
     blocks = devices // slabs
     total = slabs * rows
@@ -448,6 +469,7 @@
     line = lax.broadcasted_iota(jnp.int32, (total, LANES), 0)
     lane = lax.broadcasted_iota(jnp.int32, (held, LANES), 1)
     padded[...] = jnp.zeros(padded.shape, jnp.float32)
+    kept[...] = jnp.zeros(kept.shape, jnp.float32)
 
     def block(field, index):
         parts = []
@@ -472,7 +494,9 @@
         odd, term = block(0, behind), block(1, behind)
         even = odd + 4.0 * slope_of(odd) + term
         slope = slope_of(even)
-        odd = even + 4.0 * slope + block(2, index)
+        own_term = block(2, index)
+        kept[index, pl.ds(8, total), :] = own_term
+        odd = even + 4.0 * slope + own_term
         stepped = even + 8.0 * slope
         pair = odd + 4.0 * slope_of(odd) - stepped
         terms[index] = block(1, index) + pair
@@ -490,30 +514,41 @@
                 piece = padded[group, pl.ds(start + group * each, held), :]
                 value = jnp.where(lane >= group * share, piece, value)
             slots[index * slabs + slab] = value
+            start = 8 + slab * rows
+            for i, row in enumerate(late_rows(rows)):
+                line_at, group = each + i // groups, i % groups
+                piece = kept[index, pl.ds(start + row, 1), :]
+                piece = pltpu.roll(piece, (group * share - REACH) % LANES, 1)
+                if group > 0:
+                    before = slots[index * slabs + slab, pl.ds(line_at, 1)]
+                    piece = jnp.where(lane[:1] >= group * share, piece, before)
+                slots[index * slabs + slab, pl.ds(line_at, 1)] = piece
         if index < blocks - 1:
             field = field + 8.0 * slope_of(field) + terms[index]
 
 
 def up_kernel(
-    share, arrived, next_forcing, above, below, late_a, late_b, core, coefs,
-    out, fields, diff, grow, flat,
+    share, arrived, next_forcing, late_a, late_b, core, coefs, out, fields, diff, grow, flat
 ):
-    rows = next_forcing.shape[0]
-    depth = next_forcing.shape[1]
-    low, high = flags()
-    set_rims(fields.at[5], rows, 2, above[...], below[...], low, high)
-    fields[5, pl.ds(MARGIN, rows)] = next_forcing[...]
+    rows, depth, _ = next_forcing.shape
     groups, each, held = packing(rows, share)
     take_coefs(rows, coefs, diff, grow)
     lane = lax.broadcasted_iota(jnp.int32, (depth, LANES), 1)
-    for row in range(rows + 2 * UP_RIM):
-        group, line = row // each, row % each
+
+    def whole(line, group):
         value = None
         for part in range(groups):
             piece = arrived[pl.ds(part * held + line, depth, stride=groups * held), :]
-            piece = pltpu.roll(piece, ((part - group) * share) % LANES, 1) if part != group else piece
+            if part != group:
+                piece = pltpu.roll(piece, ((part - group) * share) % LANES, 1)
             value = piece if value is None else jnp.where(lane >= part * share, piece, value)
-        fields[0, MARGIN - UP_RIM + row] = value
+        return value
+
+    for row in range(rows + 2 * UP_RIM):
+        fields[0, MARGIN - UP_RIM + row] = whole(row % each, row // each)
+    for i, row in enumerate(late_rows(rows)):
+        fields[5, MARGIN + row] = whole(each + i // groups, i % groups)
+    fields[5, pl.ds(MARGIN, rows)] = next_forcing[...]
     odd_first = CORES.index("o0") * rows
 
     def first(at, n):
@@ -584,14 +619,15 @@
     def as_rows(array):
         return array.reshape(-1, depth, LANES)
 
-    sides, behind = count(RIMS_0), count(BEHIND_0)
+    sides = count(RIMS_0) + 2 * len(STEPS_0)
+    behind = count(BEHIND_0) + 2 * len(STEPS_BEHIND_0)
     *sends, evens, terms, diff, grow = call(
         pack_kernel,
         [lines(sides), lines(sides), lines(2 * rows), lines(behind), lines(behind)]
         + [(points // 2, rows, cols), source.shape, diffusivity.shape, growth.shape],
-        [],
+        [lines(10)],
         initial, source, diffusivity, growth,
-        place=pltpu.HBM, sems=points // 2 + 3,
+        place=pltpu.HBM, sems=points // 2 + 3, mib=56,
     )
     core, back, *windows = call(
         functools.partial(core_kernel, share),
@@ -606,34 +642,34 @@
 
     buffers = [(wide, depth, LANES), (wide, depth, LANES)]
     rim1, rimb = count(RIMS_1), count(BEHIND)
-    turn, down, up, slant_down, slant_up, state, forcing, first_forcing, coefs = call(
+    arrived, ahead, windows = lax.optimization_barrier((arrived, ahead, windows))
+    turn, down, up, slant_down, slant_up, next_odd, forcing, first_forcing, coefs = call(
         level0_kernel,
         [
             field(2 * rows), field(rim1), field(rim1), field(rimb), field(rimb),
-            field(rows + 4), field(3 * rows), field(rows + 4), field(2 * (rows + 6)),
+            field(rows), field(3 * rows), field(rows + 4), field(2 * (rows + 6)),
         ],
         [(len(CORES) + 2 + 3 * (POINTS // 2), wide, depth, LANES)] + buffers,
         core, *arrived,
     )
     arrived = exchange(down, up, turn, slant_down, slant_up)
-    arrived, ahead, windows = lax.optimization_barrier((arrived, ahead, windows))
     held_rows = FIELDS * 8 + 8 if folded(rows, share, reach_of()) else FIELDS * rows
-    slots, down, up, next_forcing, late_a, late_b = call(
+    slots, next_forcing, late_a, late_b = call(
         functools.partial(level1_kernel, share),
         [
-            (devices, held_rows, LANES), field(2), field(2),
+            (devices, held_rows, LANES),
             field(rows), field(rows + 2), field(rows + 2),
         ],
-        [(14, wide, depth, LANES)] + buffers + [(FIELDS * rows * depth, LANES)],
-        state, forcing, first_forcing, coefs, turn, ahead, *arrived,
-    )
-    above, below = moved(down, 0, 1), moved(up, 0, -1)
+        [(13, wide, depth, LANES)] + buffers + [(FIELDS * rows * depth, LANES)],
+        next_odd, forcing, first_forcing, coefs, turn, ahead, *arrived,
+    )
     slots = lax.all_to_all(slots, ("tm", "space"), 0, 0, tiled=True)
     (slots,) = call(
         functools.partial(sweep_kernel, share, rows),
         [(devices, held, LANES)],
         [(space * rows, LANES), (space * rows, LANES), (tm, space * rows, LANES)]
-        + [(LANES // share, 8 + space * rows + 2 * rows + held, LANES)],
+        + [(LANES // share, 8 + space * rows + 2 * rows + held, LANES)]
+        + [(tm, 16 + space * rows, LANES)],
         slots, *windows,
     )
     slots = lax.all_to_all(slots, ("tm", "space"), 0, 0, tiled=True)
@@ -641,8 +677,7 @@
         functools.partial(up_kernel, share),
         [(points, rows, cols)],
         [(6, wide, depth, LANES)] + buffers + [(points * rows * depth, LANES)],
-        slots.reshape(devices * held, LANES), next_forcing, above, below,
-        late_a, late_b, core, coefs,
+        slots.reshape(devices * held, LANES), next_forcing, late_a, late_b, core, coefs,
     )
     return out
 

time: 86.5 us -> 92 us (1.064)
  blocking collectives: 18.8 us -> 32.7 us
  starting transfers between devices: 25.4 us -> 16 us
  Pallas kernels: 10.9 us -> 12 us
    all_to_all x1 -> x2, blocking collectives: 18.8 us -> 32.7 us  [body(): slots = lax.all_to_all(slots, ('tm', 'space'), 0, 0, tiled=True)]
    ppermute x16 -> x14, starting transfers between devices: 22.8 us -> 16 us  [moved(): return lax.ppermute(array, ('tm', 'space'), pairs)]
    all_to_all x1 -> x0, waiting for transfers between devices: 5.48 us -> none  [body(): slots = lax.all_to_all(slots, ('tm', 'space'), 0, 0, tiled=True)]
    ppermute x16 -> x14, waiting for transfers between devices: 21.4 us -> 26.8 us  [moved(): return lax.ppermute(array, ('tm', 'space'), pairs)]
    all_to_all x1 -> x0, starting transfers between devices: 2.59 us -> none  [body(): slots = lax.all_to_all(slots, ('tm', 'space'), 0, 0, tiled=True)]
    pallas_call x6, Pallas kernels: 10.9 us -> 12 us  [call(): pl.pallas_call(kernel, out_shape=tuple((jax.ShapeDtypeStruct(shape, jnp.f...]
    unnamed x8 -> x12, local copies, waits for them, and re-layouts: 4.26 us -> 4.08 us
  transfers between devices with their start and end apart: 17 -> 14, of which waited for: 10 -> 7; matrix products, arithmetic and copies ran while one was open for 0% -> 0% of each run, Pallas kernels for 1% -> 1%
where the time goes in v3:
time: 92 us; the launch traced here: 91.7 us
  blocking collectives  32.7 us (36%)
  waiting for transfers between devices  26.8 us (29%)
  starting transfers between devices  16 us (17%)
  Pallas kernels  12 us (13%)
  local copies, waits for them, and re-layouts  4.08 us (4%)
    all_to_all x2, blocking collectives, body(): slots = lax.all_to_all(slots, ('tm', 'space'), 0, 0, tiled=True)  32.7 us
    ppermute x14, waiting for transfers between devices, moved(): return lax.ppermute(array, ('tm', 'space'), pairs)  26.8 us
    ppermute x14, starting transfers between devices, moved(): return lax.ppermute(array, ('tm', 'space'), pairs)  16 us
    pallas_call x6, Pallas kernels, call(): pl.pallas_call(kernel, out_shape=tuple((jax.ShapeDtypeStruct(shape, jnp.f...  12 us
    unnamed x12, local copies, waits for them, and re-layouts  4.08 us
  transfers between devices with their start and end apart: 14, of which 7 were waited for; matrix products, arithmetic and copies ran while one was open for 0% of the time, Pallas kernels for 1%

profile of v3, /device:TPU:0, one launch (start us, length us, event | category | flops | bytes accessed | tf_op | source)
XLA Modules:
  0.0 91.7 jit_solution(15885653432221762981)
XLA Ops:
  0.0 3.1 %shard_map.46 = (f32[480,128]{1,0:T(8,128)}, f32[480,128]{1,0:T(8,128)}, f32[512,128]{1,0:T(8,128)}, f32[80,128]{1,0:T(8,128)}, f32[80,128]{1,0:T(8,128)}, /*ind...) custom-call(f32[8,16,2048]{2,1,0:T(8,128)} %initial_all.1, ...), custom_call_target="tpu_custom_call" | custom-call | tf_op jit(solution)/shard_map/pallas_call | solution.py:42
  3.1 0.5 collective-permute-start.2
  3.6 2.6 %collective-permute-start = (f32[30,16,128]{2,1,0:T(8,128)}, f32[30,16,128]{2,1,0:T(8,128)S(1)}, u32[]{:S(2)}, u32[]{:S(2)}) collective-permute-start(f32[30,16,128]{2,1,0:T(8,128)} %bitcast.14), channel_id=1, source_target_pairs={{0,1},{1,2},{2,3},{3,0},{4,5},{5,6},{6,7},{7,4},{8,9},{9,10},{10,1... | collective-permute-start | bytes 737288 | tf_op jit(solution)/shard_map/ppermute | solution.py:591
  6.2 1.0 %collective-permute-start.1 = (f32[30,16,128]{2,1,0:T(8,128)}, f32[30,16,128]{2,1,0:T(8,128)S(1)}, u32[]{:S(2)}, u32[]{:S(2)}) collective-permute-start(f32[30,16,128]{2,1,0:T(8,128)} %bitcast.13), channel_id=1, source_target_pairs={{0,3},{1,0},{2,1},{3,2},{4,7},{5,4},{6,5},{7,6},{8,11},{9,8},{10,9... | collective-permute-start | bytes 737288 | tf_op jit(solution)/shard_map/ppermute | solution.py:591
  7.2 0.0 copy-start
  7.2 1.2 %copy-done = f32[8,16,2048]{2,1,0:T(8,128)S(1)} copy-done((f32[8,16,2048]{2,1,0:T(8,128)S(1)}, f32[8,16,2048]{2,1,0:T(8,128)}, u32[]{:S(2)}) %copy-start) | copy-done | bytes 1048600
  8.4 0.0 copy-start.1
  8.4 1.0 %copy-done.1 = f32[4,16,2048]{2,1,0:T(8,128)S(1)} copy-done((f32[4,16,2048]{2,1,0:T(8,128)S(1)}, f32[4,16,2048]{2,1,0:T(8,128)}, u32[]{:S(2)}) %copy-start.1) | copy-done | bytes 524312
  9.5 0.0 copy-start.2
  9.5 0.9 copy-done.2
  10.4 0.0 copy-start.3
  10.4 0.9 copy-done.3
  11.3 0.0 copy-start.5
  11.3 0.0 copy-start.4
  11.3 0.8 shard_map.47
  12.1 1.1 %collective-permute-start.6 = (f32[2,16,128]{2,1,0:T(8,128)S(1)}, f32[2,16,128]{2,1,0:T(8,128)S(1)}, u32[]{:S(2)}, u32[]{:S(2)}) collective-permute-start(f32[2,16,128]{2,1,0:T(8,128)S(1)} %get-tuple-element.55), channel_id=1, source_target_pairs={{0,1},{1,2},{2,3},{3,0},{4,5},{5,6},{6,7},{7,4},{8,9},{9,10},{10,1... | collective-permute-start | bytes 49160 | tf_op jit(solution)/shard_map/ppermute | solution.py:591
  13.2 2.6 %collective-permute-start.5 = (f32[256,128]{1,0:T(8,128)S(1)}, f32[256,128]{1,0:T(8,128)S(1)}, u32[]{:S(2)}, u32[]{:S(2)}) collective-permute-start(f32[256,128]{1,0:T(8,128)S(1)} %get-tuple-element.53), channel_id=1, source_target_pairs={{0,28},{1,29},{2,30},{3,31},{4,0},{5,1},{6,2},{7,3},{8,4},{9,5},{1... | collective-permute-start | bytes 393224 | tf_op jit(solution)/shard_map/ppermute | solution.py:591
  15.8 2.8 %collective-permute-done.6.refs_1_ = f32[2,16,128]{2,1,0:T(8,128)S(1)} collective-permute-done((f32[2,16,128]{2,1,0:T(8,128)S(1)}, f32[2,16,128]{2,1,0:T(8,128)S(1)}, u32[]{:S(2)}, u32[]{:S(2)}) %collective-permute-start.6) | collective-permute-done | bytes 16416 | tf_op jit(solution)/shard_map/ppermute | solution.py:591
  18.6 2.5 %collective-permute-start.7 = (f32[2,16,128]{2,1,0:T(8,128)S(1)}, f32[2,16,128]{2,1,0:T(8,128)S(1)}, u32[]{:S(2)}, u32[]{:S(2)}) collective-permute-start(f32[2,16,128]{2,1,0:T(8,128)S(1)} %get-tuple-element.56), channel_id=1, source_target_pairs={{0,2},{1,3},{2,0},{3,1},{4,6},{5,7},{6,4},{7,5},{8,10},{9,11},{10,... | collective-permute-start | bytes 49160 | tf_op jit(solution)/shard_map/ppermute | solution.py:591
  21.2 1.7 %collective-permute-done.7.refs_2_ = f32[2,16,128]{2,1,0:T(8,128)S(1)} collective-permute-done((f32[2,16,128]{2,1,0:T(8,128)S(1)}, f32[2,16,128]{2,1,0:T(8,128)S(1)}, u32[]{:S(2)}, u32[]{:S(2)}) %collective-permute-start.7) | collective-permute-done | bytes 16416 | tf_op jit(solution)/shard_map/ppermute | solution.py:591
  22.9 2.1 %collective-permute-start.8 = (f32[2,16,128]{2,1,0:T(8,128)S(1)}, f32[2,16,128]{2,1,0:T(8,128)S(1)}, u32[]{:S(2)}, u32[]{:S(2)}) collective-permute-start(f32[2,16,128]{2,1,0:T(8,128)S(1)} %get-tuple-element.57), channel_id=1, source_target_pairs={{0,3},{1,0},{2,1},{3,2},{4,7},{5,4},{6,5},{7,6},{8,11},{9,8},{10,9... | collective-permute-start | bytes 49160 | tf_op jit(solution)/shard_map/ppermute | solution.py:591
  24.9 1.7 %collective-permute-done.8.refs_3_ = f32[2,16,128]{2,1,0:T(8,128)S(1)} collective-permute-done((f32[2,16,128]{2,1,0:T(8,128)S(1)}, f32[2,16,128]{2,1,0:T(8,128)S(1)}, u32[]{:S(2)}, u32[]{:S(2)}) %collective-permute-start.8) | collective-permute-done | bytes 16416 | tf_op jit(solution)/shard_map/ppermute | solution.py:591
  26.6 0.0 copy-done.5
  26.6 0.0 collective-permute-start.3
  26.6 7.0 %collective-permute-done.3.behind_above = f32[5,16,128]{2,1,0:T(8,128)S(1)} collective-permute-done((f32[5,16,128]{2,1,0:T(8,128)S(1)}, f32[5,16,128]{2,1,0:T(8,128)S(1)}, u32[]{:S(2)}, u32[]{:S(2)}) %collective-permute-start.3) | collective-permute-done | bytes 40992 | tf_op jit(solution)/shard_map/ppermute | solution.py:591
  33.6 0.0 copy-done.4
  33.6 0.0 collective-permute-start.4
  33.6 6.1 %collective-permute-done.4.behind_below = f32[5,16,128]{2,1,0:T(8,128)S(1)} collective-permute-done((f32[5,16,128]{2,1,0:T(8,128)S(1)}, f32[5,16,128]{2,1,0:T(8,128)S(1)}, u32[]{:S(2)}, u32[]{:S(2)}) %collective-permute-start.4) | collective-permute-done | bytes 40992 | tf_op jit(solution)/shard_map/ppermute | solution.py:591
  39.8 0.0 collective-permute-done.5
  39.8 0.0 collective-permute-done.above
  39.8 0.0 collective-permute-done.1.below
  39.8 0.0 collective-permute-done.2.behind
  39.8 1.7 %shard_map.48 = (f32[32,16,128]{2,1,0:T(8,128)S(1)}, f32[7,16,128]{2,1,0:T(8,128)S(1)}, f32[7,16,128]{2,1,0:T(8,128)S(1)}, f32[5,16,128]{2,1,0:T(8,128)S(1)}, f3...) custom-call(f32[208,16,128]{2,1,0:T(8,128)S(1)} %bitcast.8, ...), custom_call_target="tpu_custom_call" | custom-call | tf_op jit(solution)/shard_map/pallas_call | solution.py:42
  41.5 0.1 collective-permute-start.11
  41.6 2.0 %collective-permute-start.9 = (f32[7,16,128]{2,1,0:T(8,128)S(1)}, f32[7,16,128]{2,1,0:T(8,128)S(1)}, u32[]{:S(2)}, u32[]{:S(2)}) collective-permute-start(f32[7,16,128]{2,1,0:T(8,128)S(1)} %get-tuple-element.69), channel_id=1, source_target_pairs={{0,1},{1,2},{2,3},{3,0},{4,5},{5,6},{6,7},{7,4},{8,9},{9,10},{10,1... | collective-permute-start | bytes 172040 | tf_op jit(solution)/shard_map/ppermute | solution.py:591
  43.7 1.0 %collective-permute-start.10 = (f32[7,16,128]{2,1,0:T(8,128)S(1)}, f32[7,16,128]{2,1,0:T(8,128)S(1)}, u32[]{:S(2)}, u32[]{:S(2)}) collective-permute-start(f32[7,16,128]{2,1,0:T(8,128)S(1)} %get-tuple-element.70), channel_id=1, source_target_pairs={{0,3},{1,0},{2,1},{3,2},{4,7},{5,4},{6,5},{7,6},{8,11},{9,8},{10,9... | collective-permute-start | bytes 172040 | tf_op jit(solution)/shard_map/ppermute | solution.py:591
  44.7 0.0 collective-permute-start.12
  44.7 0.5 collective-permute-start.13
  45.2 6.9 %collective-permute-done.12.behind_above = f32[5,16,128]{2,1,0:T(8,128)S(1)} collective-permute-done((f32[5,16,128]{2,1,0:T(8,128)S(1)}, f32[5,16,128]{2,1,0:T(8,128)S(1)}, u32[]{:S(2)}, u32[]{:S(2)}) %collective-permute-start.12) | collective-permute-done | bytes 40992 | tf_op jit(solution)/shard_map/ppermute | solution.py:591
  52.0 0.6 collective-permute-done.13.behind_below
  52.6 0.0 collective-permute-done.9.above
  52.6 0.0 collective-permute-done.10.below
  52.6 0.0 collective-permute-done.11.behind
  52.6 1.1 %shard_map.49 = (f32[32,32,128]{2,1,0:T(8,128)S(1)}, f32[16,16,128]{2,1,0:T(8,128)S(1)}, f32[18,16,128]{2,1,0:T(8,128)S(1)}, f32[18,16,128]{2,1,0:T(8,128)S(1)}) custom-call(f32[16,16,128]{2,1,0:T(8,128)S(1)} %get-tuple-element.63.next_odd, f32[48,16,128]{2,1,0:T(8,128)S(1)} %get-tuple-element.64.forcing, ...), custom_call_target="tpu_custom_call" | custom-call | tf_op jit(solution)/shard_map/pallas_call | solution.py:42
  53.7 19.6 %all_to_all.10.arrived = f32[32,32,128]{2,1,0:T(8,128)S(1)} all-to-all(f32[32,32,128]{2,1,0:T(8,128)S(1)} %get-tuple-element.73), channel_id=1, replica_groups=mesh['tm'=8,'space'=4] {'tm','space'}, dimensions={0} | all-to-all | bytes 1048576 | tf_op jit(solution)/shard_map/all_to_all | solution.py:666
  73.3 3.1 %shard_map.50 = f32[32,16,128]{2,1,0:T(8,128)S(1)} custom-call(f32[32,32,128]{2,1,0:T(8,128)S(1)} %all_to_all.10.arrived, f32[2,16,128]{2,1,0:T(8,128)S(1)} %get-tuple-element.74.refs_0_, f32[2,16,128]{2,1,0:T(8,128)S(1)} %collective-permute-done.6.refs_1_, f32[2,16,128]{2,1,0:T(8,128)S(1)} %collective-permute-done.7.refs_2_, ...), custom_call_target="tpu_custom_call" | custom-call | tf_op jit(solution)/shard_map/pallas_call | solution.py:42
  76.4 13.1 %all_to_all.11 = f32[32,16,128]{2,1,0:T(8,128)S(1)} all-to-all(f32[32,16,128]{2,1,0:T(8,128)S(1)} %shard_map.50), channel_id=1, replica_groups=mesh['tm'=8,'space'=4] {'tm','space'}, dimensions={0} | all-to-all | bytes 524288 | tf_op jit(solution)/shard_map/all_to_all | solution.py:675
  89.5 2.1 %shard_map.51 = f32[8,16,2048]{2,1,0:T(8,128)} custom-call(f32[512,128]{1,0:T(8,128)S(1)} %bitcast.10, f32[16,16,128]{2,1,0:T(8,128)S(1)} %get-tuple-element.78.next_forcing, f32[18,16,128]{2,1,0:T(8,128)S(1)} %get-tuple-element.79.late_a, f32[18,16,128]{2,1,0:T(8,128)S(1)} %get-tuple-element.80.late_b, f32[208,16,128]{2,1,0:T(8,128)S(1)} %bitcast.9, ...), custom_call_target="tpu_custom_call" | custom-call | tf_op jit(solution)/shard_map/pallas_call | solution.py:42
Async XLA Ops:
  3.1 36.7 %collective-permute-start.2 = (f32[32,16,128]{2,1,0:T(8,128)}, f32[32,16,128]{2,1,0:T(8,128)S(1)}, u32[]{:S(2)}, u32[]{:S(2)}) collective-permute-start(f32[32,16,128]{2,1,0:T(8,128)} %bitcast.12), channel_id=1, source_target_pairs={{0,4},{1,5},{2,6},{3,7},{4,8},{5,9},{6,10},{7,11},{8,12},{9,13},{1... | collective-permute-start | bytes 786440 | tf_op jit(solution)/shard_map/ppermute | solution.py:591
  3.6 36.1 %collective-permute-start = (f32[30,16,128]{2,1,0:T(8,128)}, f32[30,16,128]{2,1,0:T(8,128)S(1)}, u32[]{:S(2)}, u32[]{:S(2)}) collective-permute-start(f32[30,16,128]{2,1,0:T(8,128)} %bitcast.14), channel_id=1, source_target_pairs={{0,1},{1,2},{2,3},{3,0},{4,5},{5,6},{6,7},{7,4},{8,9},{9,10},{10,1... | collective-permute-start | bytes 737288 | tf_op jit(solution)/shard_map/ppermute | solution.py:591
  6.2 33.6 %collective-permute-start.1 = (f32[30,16,128]{2,1,0:T(8,128)}, f32[30,16,128]{2,1,0:T(8,128)S(1)}, u32[]{:S(2)}, u32[]{:S(2)}) collective-permute-start(f32[30,16,128]{2,1,0:T(8,128)} %bitcast.13), channel_id=1, source_target_pairs={{0,3},{1,0},{2,1},{3,2},{4,7},{5,4},{6,5},{7,6},{8,11},{9,8},{10,9... | collective-permute-start | bytes 737288 | tf_op jit(solution)/shard_map/ppermute | solution.py:591
  7.2 1.2 %copy-start = (f32[8,16,2048]{2,1,0:T(8,128)S(1)}, f32[8,16,2048]{2,1,0:T(8,128)}, u32[]{:S(2)}) copy-start(f32[8,16,2048]{2,1,0:T(8,128)} %get-tuple-element.44.source) | copy-start | bytes 3145732
  8.4 1.0 %copy-start.1 = (f32[4,16,2048]{2,1,0:T(8,128)S(1)}, f32[4,16,2048]{2,1,0:T(8,128)}, u32[]{:S(2)}) copy-start(f32[4,16,2048]{2,1,0:T(8,128)} %get-tuple-element.43.evens) | copy-start | bytes 1572868
  9.5 0.9 copy-start.2
  10.4 0.9 copy-start.3
  11.3 15.3 %copy-start.5 = (f32[80,128]{1,0:T(8,128)S(1)}, f32[80,128]{1,0:T(8,128)}, u32[]{:S(2)}) copy-start(f32[80,128]{1,0:T(8,128)} %get-tuple-element.51) | copy-start | bytes 122884
  11.3 22.4 %copy-start.4 = (f32[80,128]{1,0:T(8,128)S(1)}, f32[80,128]{1,0:T(8,128)}, u32[]{:S(2)}) copy-start(f32[80,128]{1,0:T(8,128)} %get-tuple-element.52) | copy-start | bytes 122884
  12.1 6.5 %collective-permute-start.6 = (f32[2,16,128]{2,1,0:T(8,128)S(1)}, f32[2,16,128]{2,1,0:T(8,128)S(1)}, u32[]{:S(2)}, u32[]{:S(2)}) collective-permute-start(f32[2,16,128]{2,1,0:T(8,128)S(1)} %get-tuple-element.55), channel_id=1, source_target_pairs={{0,1},{1,2},{2,3},{3,0},{4,5},{5,6},{6,7},{7,4},{8,9},{9,10},{10,1... | collective-permute-start | bytes 49160 | tf_op jit(solution)/shard_map/ppermute | solution.py:591
  13.2 26.6 %collective-permute-start.5 = (f32[256,128]{1,0:T(8,128)S(1)}, f32[256,128]{1,0:T(8,128)S(1)}, u32[]{:S(2)}, u32[]{:S(2)}) collective-permute-start(f32[256,128]{1,0:T(8,128)S(1)} %get-tuple-element.53), channel_id=1, source_target_pairs={{0,28},{1,29},{2,30},{3,31},{4,0},{5,1},{6,2},{7,3},{8,4},{9,5},{1... | collective-permute-start | bytes 393224 | tf_op jit(solution)/shard_map/ppermute | solution.py:591
  18.6 4.2 %collective-permute-start.7 = (f32[2,16,128]{2,1,0:T(8,128)S(1)}, f32[2,16,128]{2,1,0:T(8,128)S(1)}, u32[]{:S(2)}, u32[]{:S(2)}) collective-permute-start(f32[2,16,128]{2,1,0:T(8,128)S(1)} %get-tuple-element.56), channel_id=1, source_target_pairs={{0,2},{1,3},{2,0},{3,1},{4,6},{5,7},{6,4},{7,5},{8,10},{9,11},{10,... | collective-permute-start | bytes 49160 | tf_op jit(solution)/shard_map/ppermute | solution.py:591
  22.9 3.7 %collective-permute-start.8 = (f32[2,16,128]{2,1,0:T(8,128)S(1)}, f32[2,16,128]{2,1,0:T(8,128)S(1)}, u32[]{:S(2)}, u32[]{:S(2)}) collective-permute-start(f32[2,16,128]{2,1,0:T(8,128)S(1)} %get-tuple-element.57), channel_id=1, source_target_pairs={{0,3},{1,0},{2,1},{3,2},{4,7},{5,4},{6,5},{7,6},{8,11},{9,8},{10,9... | collective-permute-start | bytes 49160 | tf_op jit(solution)/shard_map/ppermute | solution.py:591
  26.6 7.0 %collective-permute-start.3 = (f32[5,16,128]{2,1,0:T(8,128)S(1)}, f32[5,16,128]{2,1,0:T(8,128)S(1)}, u32[]{:S(2)}, u32[]{:S(2)}) collective-permute-start(f32[5,16,128]{2,1,0:T(8,128)S(1)} %bitcast.16), channel_id=1, source_target_pairs={{0,5},{1,6},{2,7},{3,4},{4,9},{5,10},{6,11},{7,8},{8,13},{9,14},{1... | collective-permute-start | bytes 122888 | tf_op jit(solution)/shard_map/ppermute | solution.py:591
  33.6 6.1 %collective-permute-start.4 = (f32[5,16,128]{2,1,0:T(8,128)S(1)}, f32[5,16,128]{2,1,0:T(8,128)S(1)}, u32[]{:S(2)}, u32[]{:S(2)}) collective-permute-start(f32[5,16,128]{2,1,0:T(8,128)S(1)} %bitcast.15), channel_id=1, source_target_pairs={{0,7},{1,4},{2,5},{3,6},{4,11},{5,8},{6,9},{7,10},{8,15},{9,12},{1... | collective-permute-start | bytes 122888 | tf_op jit(solution)/shard_map/ppermute | solution.py:591
  41.5 11.1 %collective-permute-start.11 = (f32[32,16,128]{2,1,0:T(8,128)S(1)}, f32[32,16,128]{2,1,0:T(8,128)S(1)}, u32[]{:S(2)}, u32[]{:S(2)}) collective-permute-start(f32[32,16,128]{2,1,0:T(8,128)S(1)} %get-tuple-element.67.last_pair), channel_id=1, source_target_pairs={{0,4},{1,5},{2,6},{3,7},{4,8},{5,9},{6,10},{7,11},{8,12},{9,13},{1... | collective-permute-start | bytes 786440 | tf_op jit(solution)/shard_map/ppermute | solution.py:591
  41.6 11.0 %collective-permute-start.9 = (f32[7,16,128]{2,1,0:T(8,128)S(1)}, f32[7,16,128]{2,1,0:T(8,128)S(1)}, u32[]{:S(2)}, u32[]{:S(2)}) collective-permute-start(f32[7,16,128]{2,1,0:T(8,128)S(1)} %get-tuple-element.69), channel_id=1, source_target_pairs={{0,1},{1,2},{2,3},{3,0},{4,5},{5,6},{6,7},{7,4},{8,9},{9,10},{10,1... | collective-permute-start | bytes 172040 | tf_op jit(solution)/shard_map/ppermute | solution.py:591
  43.7 9.0 %collective-permute-start.10 = (f32[7,16,128]{2,1,0:T(8,128)S(1)}, f32[7,16,128]{2,1,0:T(8,128)S(1)}, u32[]{:S(2)}, u32[]{:S(2)}) collective-permute-start(f32[7,16,128]{2,1,0:T(8,128)S(1)} %get-tuple-element.70), channel_id=1, source_target_pairs={{0,3},{1,0},{2,1},{3,2},{4,7},{5,4},{6,5},{7,6},{8,11},{9,8},{10,9... | collective-permute-start | bytes 172040 | tf_op jit(solution)/shard_map/ppermute | solution.py:591
  44.7 7.3 %collective-permute-start.12 = (f32[5,16,128]{2,1,0:T(8,128)S(1)}, f32[5,16,128]{2,1,0:T(8,128)S(1)}, u32[]{:S(2)}, u32[]{:S(2)}) collective-permute-start(f32[5,16,128]{2,1,0:T(8,128)S(1)} %get-tuple-element.71), channel_id=1, source_target_pairs={{0,5},{1,6},{2,7},{3,4},{4,9},{5,10},{6,11},{7,8},{8,13},{9,14},{1... | collective-permute-start | bytes 122888 | tf_op jit(solution)/shard_map/ppermute | solution.py:591
  44.7 7.9 %collective-permute-start.13 = (f32[5,16,128]{2,1,0:T(8,128)S(1)}, f32[5,16,128]{2,1,0:T(8,128)S(1)}, u32[]{:S(2)}, u32[]{:S(2)}) collective-permute-start(f32[5,16,128]{2,1,0:T(8,128)S(1)} %get-tuple-element.72), channel_id=1, source_target_pairs={{0,7},{1,4},{2,5},{3,6},{4,11},{5,8},{6,9},{7,10},{8,15},{9,12},{1... | collective-permute-start | bytes 122888 | tf_op jit(solution)/shard_map/ppermute | solution.py:591

commit v4 on v3

--- a/solution.py
+++ b/solution.py
@@ -12,6 +12,8 @@
 REACH = 32
 UP_RIM = 3
 FIELDS = 3
+PACK_MIB = 62
+CORE_COST = 30_000_000
 POINTS = 8
 diffusion_number = 0.03
 time_step = 0.02
@@ -34,11 +36,11 @@
     return sum(rows for _, rows in rims)
 
 
-def params(mib=16):
-    return pltpu.CompilerParams(vmem_limit_bytes=mib * 2**20)
-
-
-def call(kernel, outs, scratch, *args, mib=16, place=pltpu.VMEM, sems=0):
+def params(mib):
+    return pltpu.CompilerParams(vmem_limit_bytes=int(mib * 2**20))
+
+
+def call(kernel, outs, scratch, *args, mib=16, place=pltpu.VMEM, sems=0, cost=None):
     return pl.pallas_call(
         kernel,
         out_shape=tuple(jax.ShapeDtypeStruct(shape, jnp.float32) for shape in outs),
@@ -47,6 +49,7 @@
         scratch_shapes=[pltpu.VMEM(shape, jnp.float32) for shape in scratch]
         + ([pltpu.SemaphoreType.DMA((sems,))] if sems else []),
         compiler_params=params(mib),
+        cost_estimate=cost,
     )(*args)
 
 
@@ -105,19 +108,33 @@
     return lambda rows, cols: source[2 * which + (name[0] == "o"), rows, cols]
 
 
-def pack_kernel(
-    initial_all, source_all, diffusivity_all, growth_all,
-    down, up, turn, slant_down, slant_up, evens, source, diffusivity, growth, edge, sems,
-):
+def fetch(initial_all, source_all, diffusivity_all, growth_all, evens, source, coefs, sems):
     pairs = [(initial_all.at[2 * i], evens.at[i]) for i in range(POINTS // 2)]
-    pairs += [(source_all, source), (diffusivity_all, diffusivity), (growth_all, growth)]
+    pairs += [(diffusivity_all, coefs.at[0]), (growth_all, coefs.at[1]), (source_all, source)]
     copies = [pltpu.make_async_copy(*pair, sems.at[i]) for i, pair in enumerate(pairs)]
     for copy in copies:
         copy.start()
-    for copy in copies:
-        copy.wait()
-    rows, cols = diffusivity.shape
+    return copies[:-1], copies[-1]
+
+
+def target_of(by):
+    slabs = lax.axis_size("space")
+    return lax.axis_index("tm") * slabs + (lax.axis_index("space") + by) % slabs
+
+
+EDGE = 8
+
+
+def pack_kernel(
+    share, initial_all, source_all, diffusivity_all, growth_all,
+    down, up, turn, slant_down, slant_up, back, evens, source, coefs, edge, cells, sems,
+):
+    waits, last = fetch(
+        initial_all, source_all, diffusivity_all, growth_all, evens, source, coefs, sems
+    )
+    _, rows, cols = coefs.shape
     depth = cols // LANES
+    diffusivity, growth = coefs.at[0], coefs.at[1]
 
     def put(ref, at, name, first, count):
         get = pieces(name, evens, source, diffusivity, growth)
@@ -128,27 +145,59 @@
     def rows_of(at, count):
         return edge[pl.ds(at * depth, count * depth), :].reshape(count, depth, LANES)
 
-    for rims, steps, low, high in (
-        (RIMS_0, STEPS_0, down, up),
-        (BEHIND_0, STEPS_BEHIND_0, slant_down, slant_up),
-    ):
-        for ref, outer, inner in ((low, rows - 4, rows - 3), (high, 0, 1)):
+    def put_sides(early):
+        for rims, low, high in ((RIMS_0, down, up), (BEHIND_0, slant_down, slant_up)):
             at = 0
             for name, rim in rims:
-                put(ref, at, name, rows - rim if ref is low else 0, rim)
+                if early == (name[0] not in "os"):
+                    put(low, at, name, rows - rim, rim)
+                    put(high, at, name, 0, rim)
                 at += rim
-            put(edge, 0, "d", inner, 2)
-            put(edge, 2, "g", inner, 2)
-            for start, term in steps:
-                put(edge, 4, start, outer, 4)
-                put(edge, 8, term, inner, 2)
-                wide = rows_of(4, 4)
-                mid, slope = slope_of_rows(wide, rows_of(0, 2), rows_of(2, 2))
-                put_rows(ref, at, mid + slope + rows_of(8, 2))
-                at += 2
-    for index, (name, _) in enumerate(BEHIND_0):
+
+    for wait in waits:
+        wait.wait()
+    put_sides(True)
+    for index, name in enumerate(("d", "g")):
         for r in range(0, rows, 8):
-            put(turn, index * rows + r, name, r, 8)
+            put(cells, index * rows + r, name, r, 8)
+    end = (count(RIMS_0) + 2 * len(STEPS_0)) * depth
+    for ref, by, at in ((down, 1, end), (up, -1, end), (down, 2, end + 2 * rows)):
+        if at < ref.shape[0]:
+            for index in range(2):
+                get = lambda line: cells[pl.ds(index * rows * depth + line, rows, stride=depth), :]
+                ref[pl.ds(at + index * rows, rows), :] = window(
+                    get, target_of(by) * share, depth
+                )
+    steps = [
+        (start, term, sides, at + 2 * i)
+        for group, sides, at in (
+            (STEPS_0, (down, up), count(RIMS_0)),
+            (STEPS_BEHIND_0, (slant_down, slant_up), count(BEHIND_0)),
+        )
+        for i, (start, term) in enumerate(group)
+    ]
+    for i, (start, _, _, _) in enumerate(steps):
+        put(edge, 2 * EDGE * i, start, rows - 4, 4)
+        put(edge, 2 * EDGE * i + EDGE, start, 0, 4)
+    put(turn, 0, "ep", 0, 8)
+    put(turn, 8, "ep", 8, 8)
+    last.wait()
+    put_sides(False)
+    for i, (_, term, _, _) in enumerate(steps):
+        put(edge, 2 * EDGE * i + 4, term, rows - 3, 2)
+        put(edge, 2 * EDGE * i + EDGE + 4, term, 1, 2)
+    for r in range(0, rows, 8):
+        put(turn, rows + r, "op", r, 8)
+        put(back, r, "s0", r, 8)
+    for side, first in enumerate((rows - 3, 1)):
+        diff, grow = (
+            cells[pl.ds((index * rows + first) * depth, 2 * depth), :].reshape(2, depth, LANES)
+            for index in range(2)
+        )
+        for i, (_, _, sides, at) in enumerate(steps):
+            spot = (2 * i + side) * EDGE
+            mid, slope = slope_of_rows(rows_of(spot, 4), diff, grow)
+            put_rows(sides[side], at, mid + slope + rows_of(spot + 4, 2))
 
 
 def window(get, first, depth):
@@ -164,24 +213,36 @@
     return jnp.where(source < 0, before, jnp.where(source >= LANES, after, here))
 
 
-def core_kernel(share, evens, source, diffusivity, growth, core, back, *windows):
-    rows, cols = diffusivity.shape
+def core_kernel(
+    share, initial_all, source_all, diffusivity_all, growth_all, core, *refs
+):
+    *windows, evens, source, coefs, sems = refs
+    waits, last = fetch(
+        initial_all, source_all, diffusivity_all, growth_all, evens, source, coefs, sems
+    )
+    for wait in (*waits, last):
+        wait.wait()
+    _, rows, cols = coefs.shape
     depth = cols // LANES
     for index, name in enumerate(CORES):
-        get = pieces(name, evens, source, diffusivity, growth)
+        get = pieces(name, evens, source, coefs.at[0], coefs.at[1])
         for c in range(depth):
             for r in range(0, rows, 8):
                 value = get(pl.ds(r, 8), pl.ds(c * LANES, LANES))
                 core[pl.ds((index * rows + r) * depth + c, 8, stride=depth), :] = value
-                if name == "s0":
-                    back[pl.ds(r * depth + c, 8, stride=depth), :] = value
-    slabs = lax.axis_size("space")
-    for by, out in enumerate(windows):
-        target = lax.axis_index("tm") * slabs + (lax.axis_index("space") + by) % slabs
+    for by, out in zip(direct_windows(lax.axis_size("space")), windows, strict=True):
         for which, name in enumerate(("d", "g")):
             start = CORES.index(name) * rows * depth
             get = lambda line: core[pl.ds(start + line, rows, stride=depth), :]
-            out[which] = window(get, target * share, depth)
+            out[pl.ds(which * rows, rows)] = window(get, target_of(by) * share, depth)
+
+
+def handed_on(slabs):
+    return slabs == 4
+
+
+def direct_windows(slabs):
+    return [0] if handed_on(slabs) else [0] + list(range(2, slabs - 1))
 
 
 def split(ref, rims):
@@ -193,12 +254,16 @@
 
 
 def level0_kernel(
-    core, above, below, behind, behind_above, behind_below,
-    turn, down, up, slant_down, slant_up, next_odd, forcing, first_forcing, coefs,
-    fields, diff, grow,
+    apart, core, above, below, behind, behind_above, behind_below, *refs
 ):
+    windows, refs = refs[: len(apart)], refs[len(apart) :]
+    (
+        turn, down, up, slant_down, slant_up, next_odd, forcing, first_forcing, coefs, held,
+        fields, diff, grow,
+    ) = refs
     rows = core.shape[0] // len(CORES)
     low, high = flags()
+    depth = core.shape[1]
     names = list(CORES) + ["ep", "op"]
     spots = {name: index for index, name in enumerate(names)}
     extra = len(names)
@@ -284,6 +349,18 @@
         down[pl.ds(at, rim)] = ref[pl.ds(first_row + rows - rim, rim)]
         up[pl.ds(at, rim)] = ref[pl.ds(first_row, rim)]
         at += rim
+    extra_rows = down.shape[0] - at
+    if extra_rows:
+        down[pl.ds(at, extra_rows)] = above[pl.ds(above.shape[0] - extra_rows, extra_rows)]
+    slab, slabs = lax.axis_index("space"), lax.axis_size("space")
+    size = 2 * rows // depth
+    at = count(RIMS_0) + 2 * len(STEPS_0)
+    for by, part in (
+        *zip(apart, windows, strict=True),
+        (1, above.at[pl.ds(at, size)]),
+        (slabs - 1, below.at[pl.ds(at, size)]),
+    ):
+        held[pl.ds((slab - by) % slabs * size, size)] = part[...]
 
 
 def send_behind(turn, slant_down, slant_up, rows):
@@ -308,14 +385,20 @@
 
 
 def level1_kernel(
-    share, next_odd, forcing, first_forcing, coefs, last_pair, ahead,
+    share, next_odd, forcing, first_forcing, coefs, last_pair, held, ahead,
     above, below, behind, behind_above, behind_below,
-    slots, next_forcing, late_a, late_b,
+    slots, next_forcing, late_a, late_b, windows,
     fields, diff, grow, flat,
 ):
     rows = forcing.shape[0] // 3
     low, high = flags()
     take_coefs(rows, coefs, diff, grow)
+    windows[...] = held[...]
+    size = above.shape[0] - count(RIMS_1)
+    if size:
+        slabs = lax.axis_size("space")
+        slab = (lax.axis_index("space") - 2) % slabs
+        windows[pl.ds(slab * size, size)] = above[pl.ds(count(RIMS_1), size)]
     g1, g3, g2, g0, pair, before, after, even0, even1, image0, image1, odd0, odd1 = range(13)
     lows, highs = split(above, RIMS_1), split(below, RIMS_1)
     for (name, rim), spot in zip(RIMS_1, (after, g1, g3, g2), strict=True):
@@ -453,19 +536,16 @@
     return groups, each, -(-(each + -(-4 // groups)) // 8) * 8
 
 
-def sweep_kernel(share, rows, arrived, *refs):
+def sweep_kernel(share, rows, arrived, windows, slots, diff, grow, terms, padded, kept):
     slabs = lax.axis_size("space")
-    windows, (slots, diff, grow, terms, padded, kept) = refs[:slabs], refs[slabs:]
     devices = arrived.shape[0]
     blocks = devices // slabs
     total = slabs * rows
     reach = reach_of()
     groups, each, held = packing(rows, share)
-    for by, part in enumerate(windows):
-        slab = (lax.axis_index("space") - by) % slabs
-        start = pl.multiple_of(slab * rows, rows)
-        diff[pl.ds(start, rows), :] = part[0]
-        grow[pl.ds(start, rows), :] = part[1]
+    for slab in range(slabs):
+        diff[pl.ds(slab * rows, rows), :] = windows[pl.ds(2 * slab * rows, rows), :]
+        grow[pl.ds(slab * rows, rows), :] = windows[pl.ds((2 * slab + 1) * rows, rows), :]
     line = lax.broadcasted_iota(jnp.int32, (total, LANES), 0)
     lane = lax.broadcasted_iota(jnp.int32, (held, LANES), 1)
     padded[...] = jnp.zeros(padded.shape, jnp.float32)
@@ -592,10 +672,8 @@
 
 
 def exchange(down, up, turn, slant_down, slant_up):
-    return (
-        moved(down, 0, 1), moved(up, 0, -1), moved(turn, 1, 0),
-        moved(slant_down, 1, 1), moved(slant_up, 1, -1),
-    )
+    slanted = moved(slant_down, 1, 1), moved(slant_up, 1, -1)
+    return moved(down, 0, 1), moved(up, 0, -1), moved(turn, 1, 0), *slanted
 
 
 def body(initial, source, diffusivity, growth):
@@ -619,49 +697,61 @@
     def as_rows(array):
         return array.reshape(-1, depth, LANES)
 
-    sides = count(RIMS_0) + 2 * len(STEPS_0)
+    window_rows = 2 * rows // depth
+    assert window_rows * depth == 2 * rows
+    raw = [(points // 2, rows, cols), source.shape, (2, rows, cols)]
+    sides = count(RIMS_0) + 2 * len(STEPS_0) + window_rows
     behind = count(BEHIND_0) + 2 * len(STEPS_BEHIND_0)
-    *sends, evens, terms, diff, grow = call(
-        pack_kernel,
-        [lines(sides), lines(sides), lines(2 * rows), lines(behind), lines(behind)]
-        + [(points // 2, rows, cols), source.shape, diffusivity.shape, growth.shape],
-        [lines(10)],
+    extra = window_rows if handed_on(space) else 0
+    *sends, back = call(
+        functools.partial(pack_kernel, share),
+        [lines(sides + extra), lines(sides), lines(2 * rows), lines(behind), lines(behind)]
+        + [lines(rows)],
+        raw + [lines(2 * EDGE * (len(STEPS_0) + len(STEPS_BEHIND_0))), lines(2 * rows)],
         initial, source, diffusivity, growth,
-        place=pltpu.HBM, sems=points // 2 + 3, mib=56,
-    )
-    core, back, *windows = call(
+        place=pltpu.HBM, sems=points // 2 + 3, mib=PACK_MIB,
+    )
+    apart = direct_windows(space)
+    core, *windows = call(
         functools.partial(core_kernel, share),
-        [lines(len(CORES) * rows), lines(rows)] + [(2, rows, LANES)] * space,
-        [],
-        evens, terms, diff, grow,
-    )
-    arrived = exchange(*(as_rows(part) for part in sends))
+        [lines(len(CORES) * rows)] + [(2 * rows, LANES)] * len(apart),
+        raw,
+        initial, source, diffusivity, growth,
+        place=pltpu.HBM, sems=points // 2 + 3,
+        cost=pl.CostEstimate(flops=0, transcendentals=0, bytes_accessed=CORE_COST),
+    )
+    above, below, turned, *slanted = exchange(*(as_rows(part) for part in sends))
+    turned, back = lax.optimization_barrier((turned, back))
     ahead = as_rows(moved(back, -1, 0))
-    windows = [windows[0]] + [moved(windows[by], 0, by) for by in range(1, space)]
+    windows = [moved(part, 0, by) if by else part for by, part in zip(apart, windows, strict=True)]
+    windows = [as_rows(part) for part in windows]
     core = as_rows(core)
+    above, below, turned, slanted, ahead, windows = lax.optimization_barrier(
+        (above, below, turned, slanted, ahead, windows)
+    )
 
     buffers = [(wide, depth, LANES), (wide, depth, LANES)]
     rim1, rimb = count(RIMS_1), count(BEHIND)
-    arrived, ahead, windows = lax.optimization_barrier((arrived, ahead, windows))
-    turn, down, up, slant_down, slant_up, next_odd, forcing, first_forcing, coefs = call(
-        level0_kernel,
+    turn, down, up, slant_down, slant_up, next_odd, forcing, first_forcing, coefs, held_windows = call(
+        functools.partial(level0_kernel, tuple(apart)),
         [
-            field(2 * rows), field(rim1), field(rim1), field(rimb), field(rimb),
+            field(2 * rows), field(rim1 + extra), field(rim1), field(rimb), field(rimb),
             field(rows), field(3 * rows), field(rows + 4), field(2 * (rows + 6)),
+            field(window_rows * space),
         ],
         [(len(CORES) + 2 + 3 * (POINTS // 2), wide, depth, LANES)] + buffers,
-        core, *arrived,
+        core, above, below, turned, *slanted, *windows,
     )
     arrived = exchange(down, up, turn, slant_down, slant_up)
     held_rows = FIELDS * 8 + 8 if folded(rows, share, reach_of()) else FIELDS * rows
-    slots, next_forcing, late_a, late_b = call(
+    slots, next_forcing, late_a, late_b, windows = call(
         functools.partial(level1_kernel, share),
         [
             (devices, held_rows, LANES),
-            field(rows), field(rows + 2), field(rows + 2),
+            field(rows), field(rows + 2), field(rows + 2), field(window_rows * space),
         ],
         [(13, wide, depth, LANES)] + buffers + [(FIELDS * rows * depth, LANES)],
-        next_odd, forcing, first_forcing, coefs, turn, ahead, *arrived,
+        next_odd, forcing, first_forcing, coefs, turn, held_windows, ahead, *arrived,
     )
     slots = lax.all_to_all(slots, ("tm", "space"), 0, 0, tiled=True)
     (slots,) = call(
@@ -670,7 +760,7 @@
         [(space * rows, LANES), (space * rows, LANES), (tm, space * rows, LANES)]
         + [(LANES // share, 8 + space * rows + 2 * rows + held, LANES)]
         + [(tm, 16 + space * rows, LANES)],
-        slots, *windows,
+        slots, windows.reshape(-1, LANES),
     )
     slots = lax.all_to_all(slots, ("tm", "space"), 0, 0, tiled=True)
     (out,) = call(

time: 92 us -> 73.1 us (0.79)
  waiting for transfers between devices: 26.8 us -> 11.4 us
  local copies, waits for them, and re-layouts: 4.08 us -> 1.23 us
    ppermute x14 -> x11, waiting for transfers between devices: 26.8 us -> 11.4 us  [moved(): return lax.ppermute(array, ('tm', 'space'), pairs)]
    unnamed x12 -> x8, local copies, waits for them, and re-layouts: 4.08 us -> 1.23 us
    ppermute x14 -> x11, starting transfers between devices: 16 us -> 15.1 us  [moved(): return lax.ppermute(array, ('tm', 'space'), pairs)]
  transfers between devices with their start and end apart: 14 -> 11, of which waited for: 7 -> 5; matrix products, arithmetic and copies ran while one was open for 0% -> 0% of each run, Pallas kernels for 1% -> 2%
where the time goes in v4:
time: 73.1 us; the launch traced here: 72.9 us
  blocking collectives  32.2 us (44%)
  starting transfers between devices  15.1 us (21%)
  Pallas kernels  12.9 us (18%)
  waiting for transfers between devices  11.4 us (16%)
  local copies, waits for them, and re-layouts  1.23 us (2%)
    all_to_all x2, blocking collectives, body(): slots = lax.all_to_all(slots, ('tm', 'space'), 0, 0, tiled=True)  32.2 us
    ppermute x11, starting transfers between devices, moved(): return lax.ppermute(array, ('tm', 'space'), pairs)  15.1 us
    pallas_call x6, Pallas kernels, call(): pl.pallas_call(kernel, out_shape=tuple((jax.ShapeDtypeStruct(shape, jnp.f...  12.9 us
    ppermute x11, waiting for transfers between devices, moved(): return lax.ppermute(array, ('tm', 'space'), pairs)  11.4 us
  transfers between devices with their start and end apart: 11, of which 5 were waited for; matrix products, arithmetic and copies ran while one was open for 0% of the time, Pallas kernels for 2%

profile of v4, /device:TPU:0, one launch (start us, length us, event | category | flops | bytes accessed | tf_op | source)
XLA Modules:
  0.0 72.9 jit_solution(5978923768624708140)
XLA Ops:
  0.0 0.0 copy-start.3
  0.0 0.0 copy-start.2
  0.0 0.0 copy-start
  0.0 3.1 %shard_map.47 = (f32[544,128]{1,0:T(8,128)}, f32[512,128]{1,0:T(8,128)}, f32[512,128]{1,0:T(8,128)}, f32[80,128]{1,0:T(8,128)}, f32[80,128]{1,0:T(8,128)}, /*index=5*/f32[256,128]{1,0:T(8,128)}) custom-call(f32[8,16,2048]{2,1,0:T(8,128)} %initial_all.3, f32[8,16,2048]{2,1,0:T(8,128)} %source_all.3, f32[16,2048]{1,0:T(8,128)} %diffusivity_all.3, ...), custom_call_target="tpu_custom_call" | custom-call | tf_op jit(solution)/shard_map/pallas_call | solution.py:44
  3.1 0.5 collective-permute-start.2
  3.6 2.6 %collective-permute-start = (f32[34,16,128]{2,1,0:T(8,128)}, f32[34,16,128]{2,1,0:T(8,128)S(1)}, u32[]{:S(2)}, u32[]{:S(2)}) collective-permute-start(f32[34,16,128]{2,1,0:T(8,128)} %bitcast.16), channel_id=1, source_target_pairs={{0,1},{1,2},{2,3},{3,0},{4,5},{5,6},{6,7},{7,4},{8,9},{9,10},{10,1... | collective-permute-start | bytes 835592 | tf_op jit(solution)/shard_map/ppermute | solution.py:671
  6.1 1.0 %collective-permute-start.1 = (f32[32,16,128]{2,1,0:T(8,128)}, f32[32,16,128]{2,1,0:T(8,128)S(1)}, u32[]{:S(2)}, u32[]{:S(2)}) collective-permute-start(f32[32,16,128]{2,1,0:T(8,128)} %bitcast.17), channel_id=1, source_target_pairs={{0,3},{1,0},{2,1},{3,2},{4,7},{5,4},{6,5},{7,6},{8,11},{9,8},{10,9... | collective-permute-start | bytes 786440 | tf_op jit(solution)/shard_map/ppermute | solution.py:671
  7.1 4.7 %collective-permute-done.2.behind = f32[32,16,128]{2,1,0:T(8,128)S(1)} collective-permute-done((f32[32,16,128]{2,1,0:T(8,128)}, f32[32,16,128]{2,1,0:T(8,128)S(1)}, u32[]{:S(2)}, u32[]{:S(2)}) %collective-permute-start.2) | collective-permute-done | bytes 262176 | tf_op jit(solution)/shard_map/ppermute | solution.py:671
  11.9 0.0 collective-permute-start.5
  11.9 2.1 %collective-permute-start.3 = (f32[5,16,128]{2,1,0:T(8,128)}, f32[5,16,128]{2,1,0:T(8,128)S(1)}, u32[]{:S(2)}, u32[]{:S(2)}) collective-permute-start(f32[5,16,128]{2,1,0:T(8,128)} %bitcast.20), channel_id=1, source_target_pairs={{0,5},{1,6},{2,7},{3,4},{4,9},{5,10},{6,11},{7,8},{8,13},{9,14},{1... | collective-permute-start | bytes 122888 | tf_op jit(solution)/shard_map/ppermute | solution.py:671
  14.0 1.0 %collective-permute-start.4 = (f32[5,16,128]{2,1,0:T(8,128)}, f32[5,16,128]{2,1,0:T(8,128)S(1)}, u32[]{:S(2)}, u32[]{:S(2)}) collective-permute-start(f32[5,16,128]{2,1,0:T(8,128)} %bitcast.19), channel_id=1, source_target_pairs={{0,7},{1,4},{2,5},{3,6},{4,11},{5,8},{6,9},{7,10},{8,15},{9,12},{1... | collective-permute-start | bytes 122888 | tf_op jit(solution)/shard_map/ppermute | solution.py:671
  14.9 0.0 copy-done.3
  14.9 0.0 copy-done.2
  14.9 0.0 copy-done
  14.9 0.0 copy-start.1
  15.0 1.2 %copy-done.1 = f32[8,16,2048]{2,1,0:T(8,128)S(1)} copy-done((f32[8,16,2048]{2,1,0:T(8,128)S(1)}, f32[8,16,2048]{2,1,0:T(8,128)}, u32[]{:S(2)}) %copy-start.1) | copy-done | bytes 1048600
  16.2 1.8 %shard_map.46 = (f32[3328,128]{1,0:T(8,128)S(1)}, f32[32,128]{1,0:T(8,128)S(1)}) custom-call(f32[8,16,2048]{2,1,0:T(8,128)S(1)} %copy-done, f32[8,16,2048]{2,1,0:T(8,128)S(1)} %copy-done.1, f32[16,2048]{1,0:T(8,128)S(1)} %copy-done.2, f32[16,2048]{1,0:T(8,128)S(1)} %copy-done.3), custom_call_target="tpu_custom_call" | custom-call | bytes 30000000 | tf_op jit(solution)/shard_map/pallas_call | solution.py:44
  18.0 2.3 %collective-permute-done.3.behind_above = f32[5,16,128]{2,1,0:T(8,128)S(1)} collective-permute-done((f32[5,16,128]{2,1,0:T(8,128)}, f32[5,16,128]{2,1,0:T(8,128)S(1)}, u32[]{:S(2)}, u32[]{:S(2)}) %collective-permute-start.3) | collective-permute-done | bytes 40992 | tf_op jit(solution)/shard_map/ppermute | solution.py:671
  20.3 0.6 collective-permute-done.4.behind_below
  20.9 0.4 collective-permute-done.1.below
  21.2 0.0 collective-permute-done.above
  21.2 0.0 collective-permute-done.5
  21.2 1.7 %shard_map.48 = (f32[32,16,128]{2,1,0:T(8,128)S(1)}, f32[9,16,128]{2,1,0:T(8,128)S(1)}, f32[7,16,128]{2,1,0:T(8,128)S(1)}, f32[5,16,128]{2,1,0:T(8,128)S(1)}, f3...) custom-call(f32[208,16,128]{2,1,0:T(8,128)S(1)} %bitcast.10, ...), custom_call_target="tpu_custom_call" | custom-call | tf_op jit(solution)/shard_map/pallas_call | solution.py:44
  23.0 1.4 %collective-permute-start.8 = (f32[32,16,128]{2,1,0:T(8,128)S(1)}, f32[32,16,128]{2,1,0:T(8,128)S(1)}, u32[]{:S(2)}, u32[]{:S(2)}) collective-permute-start(f32[32,16,128]{2,1,0:T(8,128)S(1)} %get-tuple-element.57.last_pair), channel_id=1, source_target_pairs={{0,4},{1,5},{2,6},{3,7},{4,8},{5,9},{6,10},{7,11},{8,12},{9,13},{1... | collective-permute-start | bytes 786440 | tf_op jit(solution)/shard_map/ppermute | solution.py:671
  24.4 1.5 %collective-permute-start.6 = (f32[9,16,128]{2,1,0:T(8,128)S(1)}, f32[9,16,128]{2,1,0:T(8,128)S(1)}, u32[]{:S(2)}, u32[]{:S(2)}) collective-permute-start(f32[9,16,128]{2,1,0:T(8,128)S(1)} %get-tuple-element.60), channel_id=1, source_target_pairs={{0,1},{1,2},{2,3},{3,0},{4,5},{5,6},{6,7},{7,4},{8,9},{9,10},{10,1... | collective-permute-start | bytes 221192 | tf_op jit(solution)/shard_map/ppermute | solution.py:671
  25.9 1.4 %collective-permute-start.7 = (f32[7,16,128]{2,1,0:T(8,128)S(1)}, f32[7,16,128]{2,1,0:T(8,128)S(1)}, u32[]{:S(2)}, u32[]{:S(2)}) collective-permute-start(f32[7,16,128]{2,1,0:T(8,128)S(1)} %get-tuple-element.61), channel_id=1, source_target_pairs={{0,3},{1,0},{2,1},{3,2},{4,7},{5,4},{6,5},{7,6},{8,11},{9,8},{10,9... | collective-permute-start | bytes 172040 | tf_op jit(solution)/shard_map/ppermute | solution.py:671
  27.3 0.0 collective-permute-start.9
  27.3 3.7 %collective-permute-start.10 = (f32[5,16,128]{2,1,0:T(8,128)S(1)}, f32[5,16,128]{2,1,0:T(8,128)S(1)}, u32[]{:S(2)}, u32[]{:S(2)}) collective-permute-start(f32[5,16,128]{2,1,0:T(8,128)S(1)} %get-tuple-element.63), channel_id=1, source_target_pairs={{0,7},{1,4},{2,5},{3,6},{4,11},{5,8},{6,9},{7,10},{8,15},{9,12},{1... | collective-permute-start | bytes 122888 | tf_op jit(solution)/shard_map/ppermute | solution.py:671
  31.0 3.4 %collective-permute-done.9.behind_above = f32[5,16,128]{2,1,0:T(8,128)S(1)} collective-permute-done((f32[5,16,128]{2,1,0:T(8,128)S(1)}, f32[5,16,128]{2,1,0:T(8,128)S(1)}, u32[]{:S(2)}, u32[]{:S(2)}) %collective-permute-start.9) | collective-permute-done | bytes 40992 | tf_op jit(solution)/shard_map/ppermute | solution.py:671
  34.3 0.0 collective-permute-done.10.behind_below
  34.3 0.0 collective-permute-done.7.below
  34.3 0.0 collective-permute-done.6.above
  34.3 0.0 collective-permute-done.8.behind
  34.3 1.1 %shard_map.49 = (f32[32,32,128]{2,1,0:T(8,128)S(1)}, f32[16,16,128]{2,1,0:T(8,128)S(1)}, f32[18,16,128]{2,1,0:T(8,128)S(1)}, f32[18,16,128]{2,1,0:T(8,128)S(1)}, f32[8,16,128]{2,1,0:T(8,128)S(1)}) custom-call(f32[16,16,128]{2,1,0:T(8,128)S(1)} %get-tuple-element.53.next_odd, f32[48,16,128]{2,1,0:T(8,128)S(1)} %get-tuple-element.54.forcing, ...), custom_call_target="tpu_custom_call" | custom-call | tf_op jit(solution)/shard_map/pallas_call | solution.py:44
  35.4 19.1 %all_to_all.10.arrived = f32[32,32,128]{2,1,0:T(8,128)S(1)} all-to-all(f32[32,32,128]{2,1,0:T(8,128)S(1)} %get-tuple-element.64), channel_id=1, replica_groups=mesh['tm'=8,'space'=4] {'tm','space'}, dimensions={0} | all-to-all | bytes 1048576 | tf_op jit(solution)/shard_map/all_to_all | solution.py:756
  54.5 3.1 %shard_map.50 = f32[32,16,128]{2,1,0:T(8,128)S(1)} custom-call(f32[32,32,128]{2,1,0:T(8,128)S(1)} %all_to_all.10.arrived, f32[128,128]{1,0:T(8,128)S(1)} %bitcast.14), custom_call_target="tpu_custom_call" | custom-call | tf_op jit(solution)/shard_map/pallas_call | solution.py:44
  57.6 13.1 %all_to_all.11 = f32[32,16,128]{2,1,0:T(8,128)S(1)} all-to-all(f32[32,16,128]{2,1,0:T(8,128)S(1)} %shard_map.50), channel_id=1, replica_groups=mesh['tm'=8,'space'=4] {'tm','space'}, dimensions={0} | all-to-all | bytes 524288 | tf_op jit(solution)/shard_map/all_to_all | solution.py:765
  70.7 2.1 %shard_map.51 = f32[8,16,2048]{2,1,0:T(8,128)} custom-call(f32[512,128]{1,0:T(8,128)S(1)} %bitcast.12, f32[16,16,128]{2,1,0:T(8,128)S(1)} %get-tuple-element.66.next_forcing, f32[18,16,128]{2,1,0:T(8,128)S(1)} %get-tuple-element.67.late_a, f32[18,16,128]{2,1,0:T(8,128)S(1)} %get-tuple-element.68.late_b, f32[208,16,128]{2,1,0:T(8,128)S(1)} %bitcast.11, ...), custom_call_target="tpu_custom_call" | custom-call | tf_op jit(solution)/shard_map/pallas_call | solution.py:44
Async XLA Ops:
  0.0 14.9 %copy-start.3 = (f32[16,2048]{1,0:T(8,128)S(1)}, f32[16,2048]{1,0:T(8,128)}, u32[]{:S(2)}) copy-start(f32[16,2048]{1,0:T(8,128)} %growth_all.3) | copy-start | bytes 393220
  0.0 14.9 %copy-start.2 = (f32[16,2048]{1,0:T(8,128)S(1)}, f32[16,2048]{1,0:T(8,128)}, u32[]{:S(2)}) copy-start(f32[16,2048]{1,0:T(8,128)} %diffusivity_all.3) | copy-start | bytes 393220
  0.0 14.9 %copy-start = (f32[8,16,2048]{2,1,0:T(8,128)S(1)}, f32[8,16,2048]{2,1,0:T(8,128)}, u32[]{:S(2)}) copy-start(f32[8,16,2048]{2,1,0:T(8,128)} %initial_all.3) | copy-start | bytes 3145732
  3.1 8.8 %collective-permute-start.2 = (f32[32,16,128]{2,1,0:T(8,128)}, f32[32,16,128]{2,1,0:T(8,128)S(1)}, u32[]{:S(2)}, u32[]{:S(2)}) collective-permute-start(f32[32,16,128]{2,1,0:T(8,128)} %bitcast.18), channel_id=1, source_target_pairs={{0,4},{1,5},{2,6},{3,7},{4,8},{5,9},{6,10},{7,11},{8,12},{9,13},{1... | collective-permute-start | bytes 786440 | tf_op jit(solution)/shard_map/ppermute | solution.py:671
  3.6 17.6 %collective-permute-start = (f32[34,16,128]{2,1,0:T(8,128)}, f32[34,16,128]{2,1,0:T(8,128)S(1)}, u32[]{:S(2)}, u32[]{:S(2)}) collective-permute-start(f32[34,16,128]{2,1,0:T(8,128)} %bitcast.16), channel_id=1, source_target_pairs={{0,1},{1,2},{2,3},{3,0},{4,5},{5,6},{6,7},{7,4},{8,9},{9,10},{10,1... | collective-permute-start | bytes 835592 | tf_op jit(solution)/shard_map/ppermute | solution.py:671
  6.1 15.1 %collective-permute-start.1 = (f32[32,16,128]{2,1,0:T(8,128)}, f32[32,16,128]{2,1,0:T(8,128)S(1)}, u32[]{:S(2)}, u32[]{:S(2)}) collective-permute-start(f32[32,16,128]{2,1,0:T(8,128)} %bitcast.17), channel_id=1, source_target_pairs={{0,3},{1,0},{2,1},{3,2},{4,7},{5,4},{6,5},{7,6},{8,11},{9,8},{10,9... | collective-permute-start | bytes 786440 | tf_op jit(solution)/shard_map/ppermute | solution.py:671
  11.9 9.3 %collective-permute-start.5 = (f32[256,128]{1,0:T(8,128)}, f32[256,128]{1,0:T(8,128)S(1)}, u32[]{:S(2)}, u32[]{:S(2)}) collective-permute-start(f32[256,128]{1,0:T(8,128)} %get-tuple-element.45), channel_id=1, source_target_pairs={{0,28},{1,29},{2,30},{3,31},{4,0},{5,1},{6,2},{7,3},{8,4},{9,5},{1... | collective-permute-start | bytes 393224 | tf_op jit(solution)/shard_map/ppermute | solution.py:671
  11.9 8.4 %collective-permute-start.3 = (f32[5,16,128]{2,1,0:T(8,128)}, f32[5,16,128]{2,1,0:T(8,128)S(1)}, u32[]{:S(2)}, u32[]{:S(2)}) collective-permute-start(f32[5,16,128]{2,1,0:T(8,128)} %bitcast.20), channel_id=1, source_target_pairs={{0,5},{1,6},{2,7},{3,4},{4,9},{5,10},{6,11},{7,8},{8,13},{9,14},{1... | collective-permute-start | bytes 122888 | tf_op jit(solution)/shard_map/ppermute | solution.py:671
  14.0 6.9 %collective-permute-start.4 = (f32[5,16,128]{2,1,0:T(8,128)}, f32[5,16,128]{2,1,0:T(8,128)S(1)}, u32[]{:S(2)}, u32[]{:S(2)}) collective-permute-start(f32[5,16,128]{2,1,0:T(8,128)} %bitcast.19), channel_id=1, source_target_pairs={{0,7},{1,4},{2,5},{3,6},{4,11},{5,8},{6,9},{7,10},{8,15},{9,12},{1... | collective-permute-start | bytes 122888 | tf_op jit(solution)/shard_map/ppermute | solution.py:671
  14.9 1.2 %copy-start.1 = (f32[8,16,2048]{2,1,0:T(8,128)S(1)}, f32[8,16,2048]{2,1,0:T(8,128)}, u32[]{:S(2)}) copy-start(f32[8,16,2048]{2,1,0:T(8,128)} %source_all.3) | copy-start | bytes 3145732
  23.0 11.3 %collective-permute-start.8 = (f32[32,16,128]{2,1,0:T(8,128)S(1)}, f32[32,16,128]{2,1,0:T(8,128)S(1)}, u32[]{:S(2)}, u32[]{:S(2)}) collective-permute-start(f32[32,16,128]{2,1,0:T(8,128)S(1)} %get-tuple-element.57.last_pair), channel_id=1, source_target_pairs={{0,4},{1,5},{2,6},{3,7},{4,8},{5,9},{6,10},{7,11},{8,12},{9,13},{1... | collective-permute-start | bytes 786440 | tf_op jit(solution)/shard_map/ppermute | solution.py:671
  24.4 10.0 %collective-permute-start.6 = (f32[9,16,128]{2,1,0:T(8,128)S(1)}, f32[9,16,128]{2,1,0:T(8,128)S(1)}, u32[]{:S(2)}, u32[]{:S(2)}) collective-permute-start(f32[9,16,128]{2,1,0:T(8,128)S(1)} %get-tuple-element.60), channel_id=1, source_target_pairs={{0,1},{1,2},{2,3},{3,0},{4,5},{5,6},{6,7},{7,4},{8,9},{9,10},{10,1... | collective-permute-start | bytes 221192 | tf_op jit(solution)/shard_map/ppermute | solution.py:671
  25.9 8.5 %collective-permute-start.7 = (f32[7,16,128]{2,1,0:T(8,128)S(1)}, f32[7,16,128]{2,1,0:T(8,128)S(1)}, u32[]{:S(2)}, u32[]{:S(2)}) collective-permute-start(f32[7,16,128]{2,1,0:T(8,128)S(1)} %get-tuple-element.61), channel_id=1, source_target_pairs={{0,3},{1,0},{2,1},{3,2},{4,7},{5,4},{6,5},{7,6},{8,11},{9,8},{10,9... | collective-permute-start | bytes 172040 | tf_op jit(solution)/shard_map/ppermute | solution.py:671
  27.3 7.0 %collective-permute-start.9 = (f32[5,16,128]{2,1,0:T(8,128)S(1)}, f32[5,16,128]{2,1,0:T(8,128)S(1)}, u32[]{:S(2)}, u32[]{:S(2)}) collective-permute-start(f32[5,16,128]{2,1,0:T(8,128)S(1)} %get-tuple-element.62), channel_id=1, source_target_pairs={{0,5},{1,6},{2,7},{3,4},{4,9},{5,10},{6,11},{7,8},{8,13},{9,14},{1... | collective-permute-start | bytes 122888 | tf_op jit(solution)/shard_map/ppermute | solution.py:671
  27.3 7.0 %collective-permute-start.10 = (f32[5,16,128]{2,1,0:T(8,128)S(1)}, f32[5,16,128]{2,1,0:T(8,128)S(1)}, u32[]{:S(2)}, u32[]{:S(2)}) collective-permute-start(f32[5,16,128]{2,1,0:T(8,128)S(1)} %get-tuple-element.63), channel_id=1, source_target_pairs={{0,7},{1,4},{2,5},{3,6},{4,11},{5,8},{6,9},{7,10},{8,15},{9,12},{1... | collective-permute-start | bytes 122888 | tf_op jit(solution)/shard_map/ppermute | solution.py:671

commit v5 on v4

--- a/solution.py
+++ b/solution.py
@@ -12,7 +12,6 @@
 REACH = 32
 UP_RIM = 3
 FIELDS = 3
-PACK_MIB = 62
 CORE_COST = 30_000_000
 POINTS = 8
 diffusion_number = 0.03
@@ -22,7 +21,7 @@
     ("e0", 2), ("e1", 2), ("e2", 2),
     ("o0", 1), ("o1", 1), ("o2", 1), ("o3", 1),
     ("s0", 2), ("s1", 2), ("s2", 2), ("s3", 2),
-    ("d", 3), ("g", 3),
+    ("d", 2), ("g", 2),
 )
 BEHIND_0 = (("ep", 2), ("op", 1))
 STEPS_0 = (("e0", "o0"), ("e1", "o1"), ("e2", "o2"))
@@ -40,12 +39,16 @@
     return pltpu.CompilerParams(vmem_limit_bytes=int(mib * 2**20))
 
 
-def call(kernel, outs, scratch, *args, mib=16, place=pltpu.VMEM, sems=0, cost=None):
+def call(
+    kernel, outs, scratch, *args, mib=16, place=pltpu.VMEM, to=pltpu.VMEM, sems=0, cost=None
+):
+    if place == pltpu.HBM:
+        args = [pltpu.with_memory_space_constraint(arg, place) for arg in args]
     return pl.pallas_call(
         kernel,
         out_shape=tuple(jax.ShapeDtypeStruct(shape, jnp.float32) for shape in outs),
         in_specs=[pl.BlockSpec(memory_space=place)] * len(args),
-        out_specs=tuple(pl.BlockSpec(memory_space=pltpu.VMEM) for _ in outs),
+        out_specs=tuple(pl.BlockSpec(memory_space=to) for _ in outs),
         scratch_shapes=[pltpu.VMEM(shape, jnp.float32) for shape in scratch]
         + ([pltpu.SemaphoreType.DMA((sems,))] if sems else []),
         compiler_params=params(mib),
@@ -200,11 +203,15 @@
             put_rows(sides[side], at, mid + slope + rows_of(spot + 4, 2))
 
 
+def column_of(shape, offset):
+    lane = lax.broadcasted_iota(jnp.int32, shape, len(shape) - 1)
+    return jnp.where(lane < LANES - REACH, lane, lane - LANES) + offset
+
+
 def window(get, first, depth):
     line, offset = first // LANES, first % LANES
-    shape = get(0).shape
-    source = lax.broadcasted_iota(jnp.int32, shape, 1) + (offset - REACH)
-    shift = (REACH - offset) % LANES
+    source = column_of(get(0).shape, offset)
+    shift = (LANES - offset) % LANES
     before = jnp.where(line > 0, pltpu.roll(get(jnp.maximum(line - 1, 0)), shift, 1), 0.0)
     here = pltpu.roll(get(line), shift, 1)
     after = jnp.where(
@@ -339,8 +346,8 @@
     over_rows(rows, 1, third)
     over_rows(rows, 0, fourth)
     first_forcing[...] = fields[spots["s0"], pl.ds(MARGIN - 2, rows + 4)]
-    coefs[pl.ds(0, rows + 6)] = diff[pl.ds(MARGIN - 3, rows + 6)]
-    coefs[pl.ds(rows + 6, rows + 6)] = grow[pl.ds(MARGIN - 3, rows + 6)]
+    coefs[pl.ds(0, rows + 4)] = diff[pl.ds(MARGIN - 2, rows + 4)]
+    coefs[pl.ds(rows + 4, rows + 4)] = grow[pl.ds(MARGIN - 2, rows + 4)]
     send_behind(turn, slant_down, slant_up, rows)
     at = 0
     for (name, rim), (ref, first_row) in zip(
@@ -380,8 +387,8 @@
 
 
 def take_coefs(rows, coefs, diff, grow):
-    diff[pl.ds(MARGIN - 3, rows + 6)] = coefs[pl.ds(0, rows + 6)]
-    grow[pl.ds(MARGIN - 3, rows + 6)] = coefs[pl.ds(rows + 6, rows + 6)]
+    diff[pl.ds(MARGIN - 2, rows + 4)] = coefs[pl.ds(0, rows + 4)]
+    grow[pl.ds(MARGIN - 2, rows + 4)] = coefs[pl.ds(rows + 4, rows + 4)]
 
 
 def level1_kernel(
@@ -497,25 +504,26 @@
     cells, rims = slot[pl.ds(field * 8, 8)], slot[pl.ds(FIELDS * 8, 8)]
     lane = lax.broadcasted_iota(jnp.int32, (8, LANES), 1)
     half = LANES // 2
-    near = pltpu.roll(rims, (REACH - 2 * reach * field) % LANES, 1)
-    far = pltpu.roll(rims, (-REACH - 2 * reach * field) % LANES, 1)
-    parts = []
-    for shift, rim in ((REACH, far), (-REACH, near)):
-        own = pltpu.roll(cells, shift % LANES, 1)
-        value = jnp.where((lane >= REACH - reach) & (lane < REACH + half + reach), rim, 0.0)
-        parts.append(jnp.where((lane >= REACH) & (lane < REACH + half), own, value))
-    return jnp.concatenate(parts, axis=0)
+    back = 2 * reach * field
+    top = pltpu.roll(rims, (half - back) % LANES, 1)
+    low = pltpu.roll(rims, (-back) % LANES, 1) if back else rims
+    return jnp.concatenate(
+        [
+            jnp.where(lane < half, cells, top),
+            jnp.where(lane < half, pltpu.roll(cells, half, 1), low),
+        ],
+        axis=0,
+    )
 
 
 def pack_windows(slots, flat, rows, depth, share):
-    lane = lax.broadcasted_iota(jnp.int32, (rows, LANES), 1)
     for field in range(FIELDS):
         first = field * rows * depth
         lines = [flat[pl.ds(first + line, rows, stride=depth), :] for line in range(depth)]
         for target in range(slots.shape[0]):
             line, offset = target * share // LANES, target * share % LANES
-            shift = (REACH - offset) % LANES
-            place = lane + (offset - REACH)
+            shift = (LANES - offset) % LANES
+            place = column_of((rows, LANES), offset)
             value = pltpu.roll(lines[line], shift, 1)
             if offset < REACH:
                 before = pltpu.roll(lines[line - 1], shift, 1) if line > 0 else 0.0
@@ -527,7 +535,7 @@
 
 
 def late_rows(rows):
-    return (-2, -1, rows, rows + 1)
+    return (rows, -2, rows + 1, -1)
 
 
 def packing(rows, share):
@@ -536,7 +544,7 @@
     return groups, each, -(-(each + -(-4 // groups)) // 8) * 8
 
 
-def sweep_kernel(share, rows, arrived, windows, slots, diff, grow, terms, padded, kept):
+def sweep_kernel(share, rows, arrived, windows, slots, diff, grow, terms, padded):
     slabs = lax.axis_size("space")
     devices = arrived.shape[0]
     blocks = devices // slabs
@@ -549,7 +557,6 @@
     line = lax.broadcasted_iota(jnp.int32, (total, LANES), 0)
     lane = lax.broadcasted_iota(jnp.int32, (held, LANES), 1)
     padded[...] = jnp.zeros(padded.shape, jnp.float32)
-    kept[...] = jnp.zeros(kept.shape, jnp.float32)
 
     def block(field, index):
         parts = []
@@ -568,15 +575,34 @@
         laplace = north + south + sides - 4.0 * field
         return diff[...] * laplace + grow[...] * field / (1.0 + field * field)
 
+    def put_late(index, slab):
+        to = slots.at[index * slabs + slab]
+        if folded(rows, share, reach):
+            zero = jnp.zeros((2, LANES), jnp.float32)
+            low = arrived[index * slabs + slab + 1, pl.ds(16, 2)] if slab < slabs - 1 else zero
+            high = arrived[index * slabs + slab - 1, pl.ds(22, 2)] if slab > 0 else zero
+            to[pl.ds(each, 2)] = jnp.where(lane[:2] < share, low, high)
+            return
+        for i, row in enumerate(late_rows(rows)):
+            at, group = each + i // groups, i % groups
+            beside_slab = slab + row // rows
+            if 0 <= beside_slab < slabs:
+                place = pl.ds(2 * rows + row % rows, 1)
+                piece = arrived[index * slabs + beside_slab, place]
+                piece = pltpu.roll(piece, group * share, 1)
+            else:
+                piece = jnp.zeros((1, LANES), jnp.float32)
+            if group:
+                piece = jnp.where(lane[:1] >= group * share, piece, to[pl.ds(at, 1)])
+            to[pl.ds(at, 1)] = piece
+
     field = None
     for index in range(blocks):
         behind = (index - 1) % blocks
         odd, term = block(0, behind), block(1, behind)
         even = odd + 4.0 * slope_of(odd) + term
         slope = slope_of(even)
-        own_term = block(2, index)
-        kept[index, pl.ds(8, total), :] = own_term
-        odd = even + 4.0 * slope + own_term
+        odd = even + 4.0 * slope + block(2, index)
         stepped = even + 8.0 * slope
         pair = odd + 4.0 * slope_of(odd) - stepped
         terms[index] = block(1, index) + pair
@@ -584,8 +610,8 @@
             field = stepped + terms[index]
     for index in range(blocks):
         for group in range(groups):
-            padded[group, pl.ds(8, total), :] = pltpu.roll(
-                field, (group * share - REACH) % LANES, 1
+            padded[group, pl.ds(8, total), :] = (
+                pltpu.roll(field, group * share, 1) if group else field
             )
         for slab in range(slabs):
             start = 8 + slab * rows - UP_RIM
@@ -594,21 +620,14 @@
                 piece = padded[group, pl.ds(start + group * each, held), :]
                 value = jnp.where(lane >= group * share, piece, value)
             slots[index * slabs + slab] = value
-            start = 8 + slab * rows
-            for i, row in enumerate(late_rows(rows)):
-                line_at, group = each + i // groups, i % groups
-                piece = kept[index, pl.ds(start + row, 1), :]
-                piece = pltpu.roll(piece, (group * share - REACH) % LANES, 1)
-                if group > 0:
-                    before = slots[index * slabs + slab, pl.ds(line_at, 1)]
-                    piece = jnp.where(lane[:1] >= group * share, piece, before)
-                slots[index * slabs + slab, pl.ds(line_at, 1)] = piece
+            put_late(index, slab)
         if index < blocks - 1:
             field = field + 8.0 * slope_of(field) + terms[index]
 
 
 def up_kernel(
-    share, arrived, next_forcing, late_a, late_b, core, coefs, out, fields, diff, grow, flat
+    share, arrived, next_forcing, late_a, late_b, core, coefs,
+    out, fields, diff, grow, flat, ready, sems,
 ):
     rows, depth, _ = next_forcing.shape
     groups, each, held = packing(rows, share)
@@ -641,24 +660,36 @@
             mid, slope = growth_of(fields.at[start], at, n, d, g)
             fields[start + 1, pl.ds(at, n)] = mid + 2.0 * slope + late[pl.ds(at - MARGIN + 1, n)]
 
-    def third(at, n):
-        d, g = diff[pl.ds(at, n)], grow[pl.ds(at, n)]
-        here = at - MARGIN
-        for i in range(POINTS // 2):
-            mid, slope = growth_of(fields.at[i], at, n, d, g)
-            put_rows(flat, 2 * i * rows, mid)
-            put_rows(flat, (2 * i + 1) * rows, mid + slope + core[pl.ds(odd_first + i * rows + here, n)])
-
-    over_rows(rows, 2, first)
-    over_rows(rows, 1, second)
-    over_rows(rows, 0, third)
-    for point in range(POINTS):
+    copies = []
+
+    def emit(point, value):
+        put_rows(flat, point * rows, value)
         for r in range(0, rows, 8):
             for c in range(depth):
                 start = (point * rows + r) * depth + c
-                out[point, pl.ds(r, 8), pl.ds(c * LANES, LANES)] = flat[
+                ready[point, pl.ds(r, 8), pl.ds(c * LANES, LANES)] = flat[
                     pl.ds(start, 8, stride=depth), :
                 ]
+        copy = pltpu.make_async_copy(ready.at[point], out.at[point], sems.at[point])
+        copy.start()
+        copies.append(copy)
+
+    def last(i):
+        at, n = MARGIN, rows
+        mid, slope = growth_of(fields.at[i], at, n, diff[pl.ds(at, n)], grow[pl.ds(at, n)])
+        emit(2 * i + 1, mid + slope + core[pl.ds(odd_first + i * rows, n)])
+
+    core_rows = pl.ds(MARGIN, rows)
+    emit(0, fields[0, core_rows])
+    over_rows(rows, 2, first)
+    emit(4, fields[2, core_rows])
+    over_rows(rows, 1, second)
+    emit(2, fields[1, core_rows])
+    emit(6, fields[3, core_rows])
+    for i in (0, 2, 1, 3):
+        last(i)
+    for copy in copies:
+        copy.wait()
 
 
 def moved(array, blocks, slabs):
@@ -709,7 +740,7 @@
         + [lines(rows)],
         raw + [lines(2 * EDGE * (len(STEPS_0) + len(STEPS_BEHIND_0))), lines(2 * rows)],
         initial, source, diffusivity, growth,
-        place=pltpu.HBM, sems=points // 2 + 3, mib=PACK_MIB,
+        place=pltpu.HBM, sems=points // 2 + 3,
     )
     apart = direct_windows(space)
     core, *windows = call(
@@ -736,7 +767,7 @@
         functools.partial(level0_kernel, tuple(apart)),
         [
             field(2 * rows), field(rim1 + extra), field(rim1), field(rimb), field(rimb),
-            field(rows), field(3 * rows), field(rows + 4), field(2 * (rows + 6)),
+            field(rows), field(3 * rows), field(rows + 4), field(2 * (rows + 4)),
             field(window_rows * space),
         ],
         [(len(CORES) + 2 + 3 * (POINTS // 2), wide, depth, LANES)] + buffers,
@@ -758,16 +789,18 @@
         functools.partial(sweep_kernel, share, rows),
         [(devices, held, LANES)],
         [(space * rows, LANES), (space * rows, LANES), (tm, space * rows, LANES)]
-        + [(LANES // share, 8 + space * rows + 2 * rows + held, LANES)]
-        + [(tm, 16 + space * rows, LANES)],
+        + [(LANES // share, 8 + space * rows + 2 * rows + held, LANES)],
         slots, windows.reshape(-1, LANES),
     )
     slots = lax.all_to_all(slots, ("tm", "space"), 0, 0, tiled=True)
     (out,) = call(
         functools.partial(up_kernel, share),
         [(points, rows, cols)],
-        [(6, wide, depth, LANES)] + buffers + [(points * rows * depth, LANES)],
+        [(6, wide, depth, LANES)]
+        + buffers
+        + [(points * rows * depth, LANES), (points, rows, cols)],
         slots.reshape(devices * held, LANES), next_forcing, late_a, late_b, core, coefs,
+        to=pltpu.HBM, sems=points,
     )
     return out
 

time: 73.1 us -> 70 us (0.958)
  Pallas kernels: 12.9 us -> 11.3 us
  local copies, waits for them, and re-layouts: 1.23 us -> 0 us
    pallas_call x6, Pallas kernels: 12.9 us -> 11.3 us  [call(): pl.pallas_call(kernel, out_shape=tuple((jax.ShapeDtypeStruct(shape, jnp.f...]
    unnamed x8 -> x0, local copies, waits for them, and re-layouts: 1.23 us -> none
  transfers between devices with their start and end apart: 11 -> 11, of which waited for: 5 -> 5; matrix products, arithmetic and copies ran while one was open for 0% -> 0% of each run, Pallas kernels for 2% -> 3%
where the time goes in v5:
time: 70 us; the launch traced here: 69.8 us
  blocking collectives  32.2 us (46%)
  starting transfers between devices  15.1 us (22%)
  Pallas kernels  11.3 us (16%)
  waiting for transfers between devices  11.2 us (16%)
    all_to_all x2, blocking collectives, body(): slots = lax.all_to_all(slots, ('tm', 'space'), 0, 0, tiled=True)  32.2 us
    ppermute x11, starting transfers between devices, moved(): return lax.ppermute(array, ('tm', 'space'), pairs)  15.1 us
    pallas_call x6, Pallas kernels, call(): pl.pallas_call(kernel, out_shape=tuple((jax.ShapeDtypeStruct(shape, jnp.f...  11.3 us
    ppermute x11, waiting for transfers between devices, moved(): return lax.ppermute(array, ('tm', 'space'), pairs)  11.2 us
  transfers between devices with their start and end apart: 11, of which 5 were waited for; matrix products, arithmetic and copies ran while one was open for 0% of the time, Pallas kernels for 3%

profile of v5, /device:TPU:0, one launch (start us, length us, event | category | flops | bytes accessed | tf_op | source)
XLA Modules:
  0.0 69.8 jit_solution(3858400659322497566)
XLA Ops:
  0.0 2.1 %shard_map.47 = (f32[512,128]{1,0:T(8,128)S(1)}, f32[480,128]{1,0:T(8,128)S(1)}, f32[512,128]{1,0:T(8,128)S(1)}, f32[80,128]{1,0:T(8,128)S(1)}, f32[80,128]{1,0:T(8,128)S(1)}, /*index=5*/f32[256,128]{1,0:T(8,128)S(1)}) custom-call(f32[8,16,2048]{2,1,0:T(8,128)} %initial_all.3, f32[8,16,2048]{2,1,0:T(8,128)} %source_all.3, f32[16,2048]{1,0:T(8,128)} %diffusivity_all.3, ...), custom_call_target="tpu_custom_call" | custom-call | tf_op jit(solution)/shard_map/pallas_call | solution.py:47
  2.1 0.5 collective-permute-start.2
  2.6 2.6 %collective-permute-start = (f32[32,16,128]{2,1,0:T(8,128)S(1)}, f32[32,16,128]{2,1,0:T(8,128)S(1)}, u32[]{:S(2)}, u32[]{:S(2)}) collective-permute-start(f32[32,16,128]{2,1,0:T(8,128)S(1)} %bitcast.16), channel_id=1, source_target_pairs={{0,1},{1,2},{2,3},{3,0},{4,5},{5,6},{6,7},{7,4},{8,9},{9,10},{10,1... | collective-permute-start | bytes 786440 | tf_op jit(solution)/shard_map/ppermute | solution.py:702
  5.2 1.0 %collective-permute-start.1 = (f32[30,16,128]{2,1,0:T(8,128)S(1)}, f32[30,16,128]{2,1,0:T(8,128)S(1)}, u32[]{:S(2)}, u32[]{:S(2)}) collective-permute-start(f32[30,16,128]{2,1,0:T(8,128)S(1)} %bitcast.18), channel_id=1, source_target_pairs={{0,3},{1,0},{2,1},{3,2},{4,7},{5,4},{6,5},{7,6},{8,11},{9,8},{10,9... | collective-permute-start | bytes 737288 | tf_op jit(solution)/shard_map/ppermute | solution.py:702
  6.2 4.5 %collective-permute-done.2.behind = f32[32,16,128]{2,1,0:T(8,128)S(1)} collective-permute-done((f32[32,16,128]{2,1,0:T(8,128)S(1)}, f32[32,16,128]{2,1,0:T(8,128)S(1)}, u32[]{:S(2)}, u32[]{:S(2)}) %collective-permute-start.2) | collective-permute-done | bytes 262176 | tf_op jit(solution)/shard_map/ppermute | solution.py:702
  10.7 0.0 collective-permute-start.5
  10.7 2.1 %collective-permute-start.3 = (f32[5,16,128]{2,1,0:T(8,128)S(1)}, f32[5,16,128]{2,1,0:T(8,128)S(1)}, u32[]{:S(2)}, u32[]{:S(2)}) collective-permute-start(f32[5,16,128]{2,1,0:T(8,128)S(1)} %bitcast.20), channel_id=1, source_target_pairs={{0,5},{1,6},{2,7},{3,4},{4,9},{5,10},{6,11},{7,8},{8,13},{9,14},{1... | collective-permute-start | bytes 122888 | tf_op jit(solution)/shard_map/ppermute | solution.py:702
  12.8 1.0 %collective-permute-start.4 = (f32[5,16,128]{2,1,0:T(8,128)S(1)}, f32[5,16,128]{2,1,0:T(8,128)S(1)}, u32[]{:S(2)}, u32[]{:S(2)}) collective-permute-start(f32[5,16,128]{2,1,0:T(8,128)S(1)} %bitcast.19), channel_id=1, source_target_pairs={{0,7},{1,4},{2,5},{3,6},{4,11},{5,8},{6,9},{7,10},{8,15},{9,12},{1... | collective-permute-start | bytes 122888 | tf_op jit(solution)/shard_map/ppermute | solution.py:702
  13.8 2.3 %shard_map.46 = (f32[3328,128]{1,0:T(8,128)S(1)}, f32[32,128]{1,0:T(8,128)S(1)}) custom-call(f32[8,16,2048]{2,1,0:T(8,128)} %initial_all.3, f32[8,16,2048]{2,1,0:T(8,128)} %source_all.3, f32[16,2048]{1,0:T(8,128)} %diffusivity_all.3, f32[16,2048]{1,0:T(8,128)} %growth_all.3), custom_call_target="tpu_custom_call" | custom-call | bytes 30000000 | tf_op jit(solution)/shard_map/pallas_call | solution.py:47
  16.1 2.1 %collective-permute-done.3.behind_above = f32[5,16,128]{2,1,0:T(8,128)S(1)} collective-permute-done((f32[5,16,128]{2,1,0:T(8,128)S(1)}, f32[5,16,128]{2,1,0:T(8,128)S(1)}, u32[]{:S(2)}, u32[]{:S(2)}) %collective-permute-start.3) | collective-permute-done | bytes 40992 | tf_op jit(solution)/shard_map/ppermute | solution.py:702
  18.1 0.8 %collective-permute-done.4.behind_below = f32[5,16,128]{2,1,0:T(8,128)S(1)} collective-permute-done((f32[5,16,128]{2,1,0:T(8,128)S(1)}, f32[5,16,128]{2,1,0:T(8,128)S(1)}, u32[]{:S(2)}, u32[]{:S(2)}) %collective-permute-start.4) | collective-permute-done | bytes 40992 | tf_op jit(solution)/shard_map/ppermute | solution.py:702
  19.0 0.4 collective-permute-done.1.below
  19.3 0.0 collective-permute-done.above
  19.3 0.0 collective-permute-done.5
  19.3 1.7 %shard_map.48 = (f32[32,16,128]{2,1,0:T(8,128)S(1)}, f32[9,16,128]{2,1,0:T(8,128)S(1)}, f32[7,16,128]{2,1,0:T(8,128)S(1)}, f32[5,16,128]{2,1,0:T(8,128)S(1)}, f3...) custom-call(f32[208,16,128]{2,1,0:T(8,128)S(1)} %bitcast.10, ...), custom_call_target="tpu_custom_call" | custom-call | tf_op jit(solution)/shard_map/pallas_call | solution.py:47
  21.1 1.4 %collective-permute-start.8 = (f32[32,16,128]{2,1,0:T(8,128)S(1)}, f32[32,16,128]{2,1,0:T(8,128)S(1)}, u32[]{:S(2)}, u32[]{:S(2)}) collective-permute-start(f32[32,16,128]{2,1,0:T(8,128)S(1)} %get-tuple-element.57.last_pair), channel_id=1, source_target_pairs={{0,4},{1,5},{2,6},{3,7},{4,8},{5,9},{6,10},{7,11},{8,12},{9,13},{1... | collective-permute-start | bytes 786440 | tf_op jit(solution)/shard_map/ppermute | solution.py:702
  22.5 1.5 %collective-permute-start.6 = (f32[9,16,128]{2,1,0:T(8,128)S(1)}, f32[9,16,128]{2,1,0:T(8,128)S(1)}, u32[]{:S(2)}, u32[]{:S(2)}) collective-permute-start(f32[9,16,128]{2,1,0:T(8,128)S(1)} %get-tuple-element.60), channel_id=1, source_target_pairs={{0,1},{1,2},{2,3},{3,0},{4,5},{5,6},{6,7},{7,4},{8,9},{9,10},{10,1... | collective-permute-start | bytes 221192 | tf_op jit(solution)/shard_map/ppermute | solution.py:702
  24.0 1.4 %collective-permute-start.7 = (f32[7,16,128]{2,1,0:T(8,128)S(1)}, f32[7,16,128]{2,1,0:T(8,128)S(1)}, u32[]{:S(2)}, u32[]{:S(2)}) collective-permute-start(f32[7,16,128]{2,1,0:T(8,128)S(1)} %get-tuple-element.61), channel_id=1, source_target_pairs={{0,3},{1,0},{2,1},{3,2},{4,7},{5,4},{6,5},{7,6},{8,11},{9,8},{10,9... | collective-permute-start | bytes 172040 | tf_op jit(solution)/shard_map/ppermute | solution.py:702
  25.4 0.0 collective-permute-start.9
  25.4 3.7 %collective-permute-start.10 = (f32[5,16,128]{2,1,0:T(8,128)S(1)}, f32[5,16,128]{2,1,0:T(8,128)S(1)}, u32[]{:S(2)}, u32[]{:S(2)}) collective-permute-start(f32[5,16,128]{2,1,0:T(8,128)S(1)} %get-tuple-element.63), channel_id=1, source_target_pairs={{0,7},{1,4},{2,5},{3,6},{4,11},{5,8},{6,9},{7,10},{8,15},{9,12},{1... | collective-permute-start | bytes 122888 | tf_op jit(solution)/shard_map/ppermute | solution.py:702
  29.1 3.4 %collective-permute-done.9.behind_above = f32[5,16,128]{2,1,0:T(8,128)S(1)} collective-permute-done((f32[5,16,128]{2,1,0:T(8,128)S(1)}, f32[5,16,128]{2,1,0:T(8,128)S(1)}, u32[]{:S(2)}, u32[]{:S(2)}) %collective-permute-start.9) | collective-permute-done | bytes 40992 | tf_op jit(solution)/shard_map/ppermute | solution.py:702
  32.4 0.0 collective-permute-done.10.behind_below
  32.4 0.0 collective-permute-done.7.below
  32.4 0.0 collective-permute-done.6.above
  32.4 0.0 collective-permute-done.8.behind
  32.5 1.1 %shard_map.49 = (f32[32,32,128]{2,1,0:T(8,128)S(1)}, f32[16,16,128]{2,1,0:T(8,128)S(1)}, f32[18,16,128]{2,1,0:T(8,128)S(1)}, f32[18,16,128]{2,1,0:T(8,128)S(1)}, f32[8,16,128]{2,1,0:T(8,128)S(1)}) custom-call(f32[16,16,128]{2,1,0:T(8,128)S(1)} %get-tuple-element.53.next_odd, f32[48,16,128]{2,1,0:T(8,128)S(1)} %get-tuple-element.54.forcing, ...), custom_call_target="tpu_custom_call" | custom-call | tf_op jit(solution)/shard_map/pallas_call | solution.py:47
  33.6 19.1 %all_to_all.10.arrived = f32[32,32,128]{2,1,0:T(8,128)S(1)} all-to-all(f32[32,32,128]{2,1,0:T(8,128)S(1)} %get-tuple-element.64), channel_id=1, replica_groups=mesh['tm'=8,'space'=4] {'tm','space'}, dimensions={0} | all-to-all | bytes 1048576 | tf_op jit(solution)/shard_map/all_to_all | solution.py:787
  52.6 2.2 %shard_map.50 = f32[32,16,128]{2,1,0:T(8,128)S(1)} custom-call(f32[32,32,128]{2,1,0:T(8,128)S(1)} %all_to_all.10.arrived, f32[128,128]{1,0:T(8,128)S(1)} %bitcast.14), custom_call_target="tpu_custom_call" | custom-call | tf_op jit(solution)/shard_map/pallas_call | solution.py:47
  54.8 13.1 %all_to_all.11 = f32[32,16,128]{2,1,0:T(8,128)S(1)} all-to-all(f32[32,16,128]{2,1,0:T(8,128)S(1)} %shard_map.50), channel_id=1, replica_groups=mesh['tm'=8,'space'=4] {'tm','space'}, dimensions={0} | all-to-all | bytes 524288 | tf_op jit(solution)/shard_map/all_to_all | solution.py:795
  67.9 1.9 %shard_map.51 = f32[8,16,2048]{2,1,0:T(8,128)} custom-call(f32[512,128]{1,0:T(8,128)S(1)} %bitcast.12, f32[16,16,128]{2,1,0:T(8,128)S(1)} %get-tuple-element.66.next_forcing, f32[18,16,128]{2,1,0:T(8,128)S(1)} %get-tuple-element.67.late_a, f32[18,16,128]{2,1,0:T(8,128)S(1)} %get-tuple-element.68.late_b, f32[208,16,128]{2,1,0:T(8,128)S(1)} %bitcast.11, ...), custom_call_target="tpu_custom_call" | custom-call | tf_op jit(solution)/shard_map/pallas_call | solution.py:47
Async XLA Ops:
  2.1 8.6 %collective-permute-start.2 = (f32[32,16,128]{2,1,0:T(8,128)S(1)}, f32[32,16,128]{2,1,0:T(8,128)S(1)}, u32[]{:S(2)}, u32[]{:S(2)}) collective-permute-start(f32[32,16,128]{2,1,0:T(8,128)S(1)} %bitcast.17), channel_id=1, source_target_pairs={{0,4},{1,5},{2,6},{3,7},{4,8},{5,9},{6,10},{7,11},{8,12},{9,13},{1... | collective-permute-start | bytes 786440 | tf_op jit(solution)/shard_map/ppermute | solution.py:702
  2.6 16.7 %collective-permute-start = (f32[32,16,128]{2,1,0:T(8,128)S(1)}, f32[32,16,128]{2,1,0:T(8,128)S(1)}, u32[]{:S(2)}, u32[]{:S(2)}) collective-permute-start(f32[32,16,128]{2,1,0:T(8,128)S(1)} %bitcast.16), channel_id=1, source_target_pairs={{0,1},{1,2},{2,3},{3,0},{4,5},{5,6},{6,7},{7,4},{8,9},{9,10},{10,1... | collective-permute-start | bytes 786440 | tf_op jit(solution)/shard_map/ppermute | solution.py:702
  5.2 14.2 %collective-permute-start.1 = (f32[30,16,128]{2,1,0:T(8,128)S(1)}, f32[30,16,128]{2,1,0:T(8,128)S(1)}, u32[]{:S(2)}, u32[]{:S(2)}) collective-permute-start(f32[30,16,128]{2,1,0:T(8,128)S(1)} %bitcast.18), channel_id=1, source_target_pairs={{0,3},{1,0},{2,1},{3,2},{4,7},{5,4},{6,5},{7,6},{8,11},{9,8},{10,9... | collective-permute-start | bytes 737288 | tf_op jit(solution)/shard_map/ppermute | solution.py:702
  10.7 8.6 %collective-permute-start.5 = (f32[256,128]{1,0:T(8,128)S(1)}, f32[256,128]{1,0:T(8,128)S(1)}, u32[]{:S(2)}, u32[]{:S(2)}) collective-permute-start(f32[256,128]{1,0:T(8,128)S(1)} %get-tuple-element.45), channel_id=1, source_target_pairs={{0,28},{1,29},{2,30},{3,31},{4,0},{5,1},{6,2},{7,3},{8,4},{9,5},{1... | collective-permute-start | bytes 393224 | tf_op jit(solution)/shard_map/ppermute | solution.py:702
  10.7 7.4 %collective-permute-start.3 = (f32[5,16,128]{2,1,0:T(8,128)S(1)}, f32[5,16,128]{2,1,0:T(8,128)S(1)}, u32[]{:S(2)}, u32[]{:S(2)}) collective-permute-start(f32[5,16,128]{2,1,0:T(8,128)S(1)} %bitcast.20), channel_id=1, source_target_pairs={{0,5},{1,6},{2,7},{3,4},{4,9},{5,10},{6,11},{7,8},{8,13},{9,14},{1... | collective-permute-start | bytes 122888 | tf_op jit(solution)/shard_map/ppermute | solution.py:702
  12.8 6.2 %collective-permute-start.4 = (f32[5,16,128]{2,1,0:T(8,128)S(1)}, f32[5,16,128]{2,1,0:T(8,128)S(1)}, u32[]{:S(2)}, u32[]{:S(2)}) collective-permute-start(f32[5,16,128]{2,1,0:T(8,128)S(1)} %bitcast.19), channel_id=1, source_target_pairs={{0,7},{1,4},{2,5},{3,6},{4,11},{5,8},{6,9},{7,10},{8,15},{9,12},{1... | collective-permute-start | bytes 122888 | tf_op jit(solution)/shard_map/ppermute | solution.py:702
  21.1 11.3 %collective-permute-start.8 = (f32[32,16,128]{2,1,0:T(8,128)S(1)}, f32[32,16,128]{2,1,0:T(8,128)S(1)}, u32[]{:S(2)}, u32[]{:S(2)}) collective-permute-start(f32[32,16,128]{2,1,0:T(8,128)S(1)} %get-tuple-element.57.last_pair), channel_id=1, source_target_pairs={{0,4},{1,5},{2,6},{3,7},{4,8},{5,9},{6,10},{7,11},{8,12},{9,13},{1... | collective-permute-start | bytes 786440 | tf_op jit(solution)/shard_map/ppermute | solution.py:702
  22.5 10.0 %collective-permute-start.6 = (f32[9,16,128]{2,1,0:T(8,128)S(1)}, f32[9,16,128]{2,1,0:T(8,128)S(1)}, u32[]{:S(2)}, u32[]{:S(2)}) collective-permute-start(f32[9,16,128]{2,1,0:T(8,128)S(1)} %get-tuple-element.60), channel_id=1, source_target_pairs={{0,1},{1,2},{2,3},{3,0},{4,5},{5,6},{6,7},{7,4},{8,9},{9,10},{10,1... | collective-permute-start | bytes 221192 | tf_op jit(solution)/shard_map/ppermute | solution.py:702
  24.0 8.5 %collective-permute-start.7 = (f32[7,16,128]{2,1,0:T(8,128)S(1)}, f32[7,16,128]{2,1,0:T(8,128)S(1)}, u32[]{:S(2)}, u32[]{:S(2)}) collective-permute-start(f32[7,16,128]{2,1,0:T(8,128)S(1)} %get-tuple-element.61), channel_id=1, source_target_pairs={{0,3},{1,0},{2,1},{3,2},{4,7},{5,4},{6,5},{7,6},{8,11},{9,8},{10,9... | collective-permute-start | bytes 172040 | tf_op jit(solution)/shard_map/ppermute | solution.py:702
  25.4 7.0 %collective-permute-start.9 = (f32[5,16,128]{2,1,0:T(8,128)S(1)}, f32[5,16,128]{2,1,0:T(8,128)S(1)}, u32[]{:S(2)}, u32[]{:S(2)}) collective-permute-start(f32[5,16,128]{2,1,0:T(8,128)S(1)} %get-tuple-element.62), channel_id=1, source_target_pairs={{0,5},{1,6},{2,7},{3,4},{4,9},{5,10},{6,11},{7,8},{8,13},{9,14},{1... | collective-permute-start | bytes 122888 | tf_op jit(solution)/shard_map/ppermute | solution.py:702
  25.4 7.0 %collective-permute-start.10 = (f32[5,16,128]{2,1,0:T(8,128)S(1)}, f32[5,16,128]{2,1,0:T(8,128)S(1)}, u32[]{:S(2)}, u32[]{:S(2)}) collective-permute-start(f32[5,16,128]{2,1,0:T(8,128)S(1)} %get-tuple-element.63), channel_id=1, source_target_pairs={{0,7},{1,4},{2,5},{3,6},{4,11},{5,8},{6,9},{7,10},{8,15},{9,12},{1... | collective-permute-start | bytes 122888 | tf_op jit(solution)/shard_map/ppermute | solution.py:702

commit v6 on v5

--- a/solution.py
+++ b/solution.py
@@ -11,28 +11,18 @@
 MARGIN = 4
 REACH = 32
 UP_RIM = 3
+POINTS = 8
 FIELDS = 3
 CORE_COST = 30_000_000
-POINTS = 8
 diffusion_number = 0.03
 time_step = 0.02
 
-RIMS_0 = (
-    ("e0", 2), ("e1", 2), ("e2", 2),
-    ("o0", 1), ("o1", 1), ("o2", 1), ("o3", 1),
-    ("s0", 2), ("s1", 2), ("s2", 2), ("s3", 2),
-    ("d", 2), ("g", 2),
-)
-BEHIND_0 = (("ep", 2), ("op", 1))
-STEPS_0 = (("e0", "o0"), ("e1", "o1"), ("e2", "o2"))
-STEPS_BEHIND_0 = (("ep", "op"),)
+CHAINS = POINTS // 2 - 1
+EDGE_0 = 4 * CHAINS + 7
+SLANT_0 = 4
+EDGE_1 = 5
+SLANT_1 = 3
 CORES = ("e0", "e1", "e2", "o0", "o1", "o2", "o3", "s0", "s1", "s2", "s3", "d", "g")
-RIMS_1 = (("next", 3), ("g1", 1), ("g3", 1), ("g2", 2))
-BEHIND = (("pair", 2), ("odd", 3))
-
-
-def count(rims):
-    return sum(rows for _, rows in rims)
 
 
 def params(mib):
@@ -90,10 +80,11 @@
     return low, high
 
 
-def set_rims(buffer, rows, rim, low_rows, high_rows, low, high, inner=0):
-    width = rim - inner
-    buffer[pl.ds(MARGIN - rim, width)] = low_rows * low
-    buffer[pl.ds(MARGIN + rows + inner, width)] = high_rows * high
+def rim_rows(rows, low, high):
+    return (
+        (lambda k: MARGIN - k, low),
+        (lambda k: MARGIN + rows - 1 + k, high),
+    )
 
 
 def pieces(name, evens, source, diffusivity, growth):
@@ -125,7 +116,7 @@
     return lax.axis_index("tm") * slabs + (lax.axis_index("space") + by) % slabs
 
 
-EDGE = 8
+SCRATCH = 10
 
 
 def pack_kernel(
@@ -145,25 +136,30 @@
             place = pl.ds(at * depth + c, count, stride=depth)
             ref[place, :] = get(pl.ds(first, count), pl.ds(c * LANES, LANES))
 
-    def rows_of(at, count):
-        return edge[pl.ds(at * depth, count * depth), :].reshape(count, depth, LANES)
-
-    def put_sides(early):
-        for rims, low, high in ((RIMS_0, down, up), (BEHIND_0, slant_down, slant_up)):
-            at = 0
-            for name, rim in rims:
-                if early == (name[0] not in "os"):
-                    put(low, at, name, rows - rim, rim)
-                    put(high, at, name, 0, rim)
-                at += rim
+    def rows_of(ref, at, count):
+        return ref[pl.ds(at * depth, count * depth), :].reshape(count, depth, LANES)
+
+    def coef_rows(which, first, count):
+        return rows_of(cells, which * rows + first, count)
+
+    chains = [(f"e{i}", f"o{i}", f"s{i + 1}", f"o{i + 1}") for i in range(CHAINS)]
+    chains.append(("ep", "op", None, None))
+    sides = ((down, slant_down, False), (up, slant_up, True))
+
+    def near(upward, count):
+        return 0 if upward else rows - count
 
     for wait in waits:
         wait.wait()
-    put_sides(True)
     for index, name in enumerate(("d", "g")):
         for r in range(0, rows, 8):
             put(cells, index * rows + r, name, r, 8)
-    end = (count(RIMS_0) + 2 * len(STEPS_0)) * depth
+    for side, (rim, slant, upward) in enumerate(sides):
+        for i, (start, _, _, _) in enumerate(chains):
+            put(edge, (2 * i + side) * SCRATCH, start, near(upward, 4), 4)
+        for which in range(2):
+            put_rows(rim, 4 * CHAINS + 3 + 2 * which, coef_rows(which, near(upward, 2), 2))
+    end = EDGE_0 * depth
     for ref, by, at in ((down, 1, end), (up, -1, end), (down, 2, end + 2 * rows)):
         if at < ref.shape[0]:
             for index in range(2):
@@ -171,36 +167,51 @@
                 ref[pl.ds(at + index * rows, rows), :] = window(
                     get, target_of(by) * share, depth
                 )
-    steps = [
-        (start, term, sides, at + 2 * i)
-        for group, sides, at in (
-            (STEPS_0, (down, up), count(RIMS_0)),
-            (STEPS_BEHIND_0, (slant_down, slant_up), count(BEHIND_0)),
-        )
-        for i, (start, term) in enumerate(group)
-    ]
-    for i, (start, _, _, _) in enumerate(steps):
-        put(edge, 2 * EDGE * i, start, rows - 4, 4)
-        put(edge, 2 * EDGE * i + EDGE, start, 0, 4)
     put(turn, 0, "ep", 0, 8)
     put(turn, 8, "ep", 8, 8)
     last.wait()
-    put_sides(False)
-    for i, (_, term, _, _) in enumerate(steps):
-        put(edge, 2 * EDGE * i + 4, term, rows - 3, 2)
-        put(edge, 2 * EDGE * i + EDGE + 4, term, 1, 2)
+    for side, (rim, slant, upward) in enumerate(sides):
+        for i, (_, term, after, after_odd) in enumerate(chains):
+            spot = (2 * i + side) * SCRATCH
+            put(edge, spot + 4, term, near(upward, 3), 3)
+            if after:
+                put(edge, spot + 7, after, near(upward, 2), 2)
+                put(edge, spot + 9, after_odd, near(upward, 1), 1)
+        put(rim, 4 * CHAINS, "s0", near(upward, 2), 2)
+        put(rim, 4 * CHAINS + 2, "o0", near(upward, 1), 1)
     for r in range(0, rows, 8):
         put(turn, rows + r, "op", r, 8)
         put(back, r, "s0", r, 8)
-    for side, first in enumerate((rows - 3, 1)):
-        diff, grow = (
-            cells[pl.ds((index * rows + first) * depth, 2 * depth), :].reshape(2, depth, LANES)
-            for index in range(2)
-        )
-        for i, (_, _, sides, at) in enumerate(steps):
-            spot = (2 * i + side) * EDGE
-            mid, slope = slope_of_rows(rows_of(spot, 4), diff, grow)
-            put_rows(sides[side], at, mid + slope + rows_of(spot + 4, 2))
+    for side, (rim, slant, upward) in enumerate(sides):
+        n0, n1, inner = (0, 1, 1) if upward else (rows - 1, rows - 2, rows - 3)
+        diff0, diff1, grow1 = coef_rows(0, n0, 1), coef_rows(0, n1, 1), coef_rows(1, n1, 1)
+        nothing = jnp.zeros_like(diff0)
+
+        def pick(value, k):
+            place = k if upward else value.shape[0] - 1 - k
+            return value[place : place + 1]
+
+        for i, (_, _, after, _) in enumerate(chains):
+            spot = (2 * i + side) * SCRATCH
+            start, term = rows_of(edge, spot, 4), rows_of(edge, spot + 4, 3)
+            mid, slope = slope_of_rows(start, coef_rows(0, inner, 2), coef_rows(1, inner, 2))
+            inner_term = term[1:] if upward else term[:-1]
+            odd = mid + slope + inner_term
+            wide = [nothing, odd] if upward else [odd, nothing]
+            mid, slope = slope_of_rows(jnp.concatenate(wide, axis=0), diff1, grow1)
+            part = mid + slope
+            odd1 = pick(odd, 0)
+            to, at = (rim, 4 * i) if after else (slant, 0)
+            put_rows(to, at, pick(start, 0))
+            put_rows(to, at + 1, pick(term, 0) + diff0 * pick(start, 1))
+            if after:
+                follow = rows_of(edge, spot + 7, 2)
+                put_rows(to, at + 2, pick(follow, 0) + diff0 * odd1)
+                part = part + pick(follow, 1)
+                put_rows(to, at + 3, rows_of(edge, spot + 9, 1) + diff0 * part)
+            else:
+                put_rows(to, at + 2, odd1)
+                put_rows(to, at + 3, part)
 
 
 def column_of(shape, offset):
@@ -250,14 +261,6 @@
 
 def direct_windows(slabs):
     return [0] if handed_on(slabs) else [0] + list(range(2, slabs - 1))
-
-
-def split(ref, rims):
-    at, out = 0, {}
-    for name, rim in rims:
-        out[name] = ref[pl.ds(at, rim)]
-        at += rim
-    return out
 
 
 def level0_kernel(
@@ -278,31 +281,39 @@
     odd = [extra + i for i in range(halves)]
     even = [extra + halves + i for i in range(halves)]
     image = [extra + 2 * halves + i for i in range(halves)]
-    for rims, steps, from_low, from_high in (
-        (RIMS_0, STEPS_0, above, below),
-        (BEHIND_0, STEPS_BEHIND_0, behind_above, behind_below),
+    nothing = jnp.zeros((1, depth, LANES), jnp.float32)
+    sides = rim_rows(rows, low, high)
+    for (at, flag), rim, slant in zip(
+        sides, (above, below), (behind_above, behind_below), strict=True
     ):
-        lows, highs = split(from_low, rims), split(from_high, rims)
-        for name, rim in rims:
-            if name in ("d", "g"):
-                buffer = diff if name == "d" else grow
-            else:
-                buffer = fields.at[spots[name]]
-            set_rims(buffer, rows, rim, lows[name], highs[name], low, high)
-        at = count(rims)
-        for start, _ in steps:
-            buffer = fields.at[odd[0 if start == "ep" else int(start[1]) + 1]]
-            set_rims(
-                buffer, rows, 3, from_low[pl.ds(at, 2)], from_high[pl.ds(at, 2)], low, high, 1
+
+        def put(name, k, ref, row):
+            fields[spots[name] if isinstance(name, str) else name, pl.ds(at(k), 1)] = (
+                ref[pl.ds(row, 1)] * flag
             )
-            at += 2
+
+        for i in range(CHAINS):
+            put(f"e{i}", 1, rim, 4 * i)
+            put(f"o{i}", 1, rim, 4 * i + 1)
+            put(f"s{i + 1}", 1, rim, 4 * i + 2)
+            fields[spots[f"e{i}"], pl.ds(at(2), 1)] = nothing
+            fields[odd[i + 1], pl.ds(at(2), 1)] = nothing
+        put("ep", 1, slant, 0)
+        put("op", 1, slant, 1)
+        put(odd[0], 2, slant, 2)
+        fields[spots["ep"], pl.ds(at(2), 1)] = nothing
+        first_row = min(at(1), at(2))
+        edge_at = 4 * CHAINS
+        fields[spots["s0"], pl.ds(first_row, 2)] = rim[pl.ds(edge_at, 2)] * flag
+        diff[pl.ds(first_row, 2)] = rim[pl.ds(edge_at + 3, 2)] * flag
+        grow[pl.ds(first_row, 2)] = rim[pl.ds(edge_at + 5, 2)] * flag
     for name in CORES:
         if name in ("d", "g"):
             buffer = diff if name == "d" else grow
         else:
             buffer = fields.at[spots[name]]
         buffer[pl.ds(MARGIN, rows)] = core[pl.ds(CORES.index(name) * rows, rows)]
-    for index, (name, _) in enumerate(BEHIND_0):
+    for index, name in enumerate(("ep", "op")):
         fields[spots[name], pl.ds(MARGIN, rows)] = behind[pl.ds(index * rows, rows)]
 
     def first(at, n):
@@ -342,48 +353,58 @@
                     turn[pl.ds(rows + here, n)] = fields[image[i], pl.ds(at, n)] + term
 
     over_rows(rows, 1, first)
-    over_rows(rows, 2, second)
+    over_rows(rows, 1, second)
+    for (at, flag), rim, slant in zip(
+        sides, (above, below), (behind_above, behind_below), strict=True
+    ):
+        near, far = pl.ds(at(1), 1), pl.ds(at(2), 1)
+        for i in range(halves):
+            place = 4 * CHAINS + 2 if i == 0 else 4 * i - 1
+            fields[spots[f"o{i}"], near] = rim[pl.ds(place, 1)] * flag
+            value = diff[far] * fields[odd[i], near]
+            if i == 0:
+                value = value + fields[spots["s0"], far] + slant[pl.ds(3, 1)] * flag
+            fields[even[i], far] = value
     over_rows(rows, 1, third)
     over_rows(rows, 0, fourth)
     first_forcing[...] = fields[spots["s0"], pl.ds(MARGIN - 2, rows + 4)]
     coefs[pl.ds(0, rows + 4)] = diff[pl.ds(MARGIN - 2, rows + 4)]
     coefs[pl.ds(rows + 4, rows + 4)] = grow[pl.ds(MARGIN - 2, rows + 4)]
-    send_behind(turn, slant_down, slant_up, rows)
-    at = 0
-    for (name, rim), (ref, first_row) in zip(
-        RIMS_1, ((next_odd, 0), (forcing, 0), (forcing, 2 * rows), (forcing, rows)), strict=True
-    ):
-        down[pl.ds(at, rim)] = ref[pl.ds(first_row + rows - rim, rim)]
-        up[pl.ds(at, rim)] = ref[pl.ds(first_row, rim)]
-        at += rim
+    for rim, slant, n0, n1 in ((down, slant_down, rows - 1, rows - 2), (up, slant_up, 0, 1)):
+
+        def row(ref, first, n):
+            return ref[pl.ds(first + n, 1)]
+
+        diff0 = 2.0 * row(diff, MARGIN, n0)
+        around = [
+            slope_of_rows(
+                ref[pl.ds(first + n1 - 1, 3)], row(diff, MARGIN, n1), row(grow, MARGIN, n1)
+            )
+            for ref, first in ((next_odd, 0), (turn, rows))
+        ]
+        (mid, slope), (mid_last, slope_last) = around
+        even1 = mid + 2.0 * slope + row(forcing, rows, n1)
+        g3 = row(forcing, 2 * rows, n0)
+        rim[pl.ds(0, 1)] = row(next_odd, 0, n0)
+        rim[pl.ds(1, 1)] = row(forcing, rows, n0) + diff0 * mid
+        rim[pl.ds(2, 1)] = g3 + diff0 * even1
+        rim[pl.ds(3, 1)] = g3
+        rim[pl.ds(4, 1)] = row(forcing, 0, n0)
+        slant[pl.ds(0, 1)] = row(turn, rows, n0)
+        slant[pl.ds(1, 1)] = row(turn, 0, n0) + diff0 * mid_last
+        slant[pl.ds(2, 1)] = row(turn, 0, n1) + mid_last + 2.0 * slope_last
+    at = EDGE_1
     extra_rows = down.shape[0] - at
     if extra_rows:
         down[pl.ds(at, extra_rows)] = above[pl.ds(above.shape[0] - extra_rows, extra_rows)]
     slab, slabs = lax.axis_index("space"), lax.axis_size("space")
     size = 2 * rows // depth
-    at = count(RIMS_0) + 2 * len(STEPS_0)
     for by, part in (
         *zip(apart, windows, strict=True),
-        (1, above.at[pl.ds(at, size)]),
-        (slabs - 1, below.at[pl.ds(at, size)]),
+        (1, above.at[pl.ds(EDGE_0, size)]),
+        (slabs - 1, below.at[pl.ds(EDGE_0, size)]),
     ):
         held[pl.ds((slab - by) % slabs * size, size)] = part[...]
-
-
-def send_behind(turn, slant_down, slant_up, rows):
-    at = 0
-    for index, (_, rim) in enumerate(BEHIND):
-        slant_down[pl.ds(at, rim)] = turn[pl.ds((index + 1) * rows - rim, rim)]
-        slant_up[pl.ds(at, rim)] = turn[pl.ds(index * rows, rim)]
-        at += rim
-
-
-def take_behind(rows, buffers, behind, behind_above, behind_below, low, high):
-    lows, highs = split(behind_above, BEHIND), split(behind_below, BEHIND)
-    for index, (name, rim) in enumerate(BEHIND):
-        buffer = buffers[index]
-        set_rims(buffer, rows, rim, lows[name], highs[name], low, high)
-        buffer[pl.ds(MARGIN, rows)] = behind[pl.ds(index * rows, rows)]
 
 
 def take_coefs(rows, coefs, diff, grow):
@@ -401,24 +422,31 @@
     low, high = flags()
     take_coefs(rows, coefs, diff, grow)
     windows[...] = held[...]
-    size = above.shape[0] - count(RIMS_1)
+    size = above.shape[0] - EDGE_1
     if size:
         slabs = lax.axis_size("space")
         slab = (lax.axis_index("space") - 2) % slabs
-        windows[pl.ds(slab * size, size)] = above[pl.ds(count(RIMS_1), size)]
-    g1, g3, g2, g0, pair, before, after, even0, even1, image0, image1, odd0, odd1 = range(13)
-    lows, highs = split(above, RIMS_1), split(below, RIMS_1)
-    for (name, rim), spot in zip(RIMS_1, (after, g1, g3, g2), strict=True):
-        set_rims(fields.at[spot], rows, rim, lows[name], highs[name], low, high)
+        windows[pl.ds(slab * size, size)] = above[pl.ds(EDGE_1, size)]
+    g1, g3, g2, g0, before, after, even0, even1, image0, image1, odd0, odd1 = range(12)
+    nothing = jnp.zeros((1, *forcing.shape[1:]), jnp.float32)
+    sides = rim_rows(rows, low, high)
     fields[after, pl.ds(MARGIN, rows)] = next_odd[...]
     for which, spot in enumerate((g1, g2, g3)):
         fields[spot, pl.ds(MARGIN, rows)] = forcing[pl.ds(which * rows, rows)]
-    take_behind(
-        rows, (fields.at[pair], fields.at[before]), behind, behind_above, behind_below, low, high
-    )
-    fields[g0, pl.ds(MARGIN - 2, rows + 4)] = (
-        first_forcing[...] + fields[pair, pl.ds(MARGIN - 2, rows + 4)]
-    )
+    fields[before, pl.ds(MARGIN, rows)] = behind[pl.ds(rows, rows)]
+    fields[g0, pl.ds(MARGIN, rows)] = first_forcing[pl.ds(2, rows)] + behind[pl.ds(0, rows)]
+    for (at, flag), rim, slant in zip(
+        sides, (above, below), (behind_above, behind_below), strict=True
+    ):
+        near, far = pl.ds(at(1), 1), pl.ds(at(2), 1)
+        for spot, row in ((after, 0), (g2, 1), (g3, 2), (g1, 4)):
+            fields[spot, near] = rim[pl.ds(row, 1)] * flag
+        own = [first_forcing[pl.ds(at(k) - MARGIN + 2, 1)] for k in (1, 2)]
+        fields[before, near] = slant[pl.ds(0, 1)] * flag
+        fields[g0, near] = own[0] + slant[pl.ds(1, 1)] * flag
+        fields[even0, far] = own[1] + slant[pl.ds(2, 1)] * flag
+        for spot in (after, before, even1):
+            fields[spot, far] = nothing
 
     def second(at, n):
         d, g = diff[pl.ds(at, n)], grow[pl.ds(at, n)]
@@ -446,11 +474,13 @@
         put_rows(flat, 2 * rows, term)
         put_rows(flat, 0, image + term)
 
-    over_rows(rows, 2, second)
+    over_rows(rows, 1, second)
     over_rows(rows, 1, third)
     over_rows(rows, 0, fourth)
     late_a[...] = fields[g1, pl.ds(MARGIN - 1, rows + 2)]
-    late_b[...] = fields[g3, pl.ds(MARGIN - 1, rows + 2)]
+    late_b[pl.ds(1, rows)] = fields[g3, pl.ds(MARGIN, rows)]
+    late_b[pl.ds(0, 1)] = above[pl.ds(3, 1)] * low
+    late_b[pl.ds(rows + 1, 1)] = below[pl.ds(3, 1)] * high
     depth = forcing.shape[1]
     if folded(rows, share, reach_of()):
         pack_folded(slots, flat, rows, depth, reach_of())
@@ -731,14 +761,13 @@
     window_rows = 2 * rows // depth
     assert window_rows * depth == 2 * rows
     raw = [(points // 2, rows, cols), source.shape, (2, rows, cols)]
-    sides = count(RIMS_0) + 2 * len(STEPS_0) + window_rows
-    behind = count(BEHIND_0) + 2 * len(STEPS_BEHIND_0)
+    sides = EDGE_0 + window_rows
     extra = window_rows if handed_on(space) else 0
     *sends, back = call(
         functools.partial(pack_kernel, share),
-        [lines(sides + extra), lines(sides), lines(2 * rows), lines(behind), lines(behind)]
+        [lines(sides + extra), lines(sides), lines(2 * rows), lines(SLANT_0), lines(SLANT_0)]
         + [lines(rows)],
-        raw + [lines(2 * EDGE * (len(STEPS_0) + len(STEPS_BEHIND_0))), lines(2 * rows)],
+        raw + [lines(2 * SCRATCH * (CHAINS + 1)), lines(2 * rows)],
         initial, source, diffusivity, growth,
         place=pltpu.HBM, sems=points // 2 + 3,
     )
@@ -762,11 +791,10 @@
     )
 
     buffers = [(wide, depth, LANES), (wide, depth, LANES)]
-    rim1, rimb = count(RIMS_1), count(BEHIND)
     turn, down, up, slant_down, slant_up, next_odd, forcing, first_forcing, coefs, held_windows = call(
         functools.partial(level0_kernel, tuple(apart)),
         [
-            field(2 * rows), field(rim1 + extra), field(rim1), field(rimb), field(rimb),
+            field(2 * rows), field(EDGE_1 + extra), field(EDGE_1), field(SLANT_1), field(SLANT_1),
             field(rows), field(3 * rows), field(rows + 4), field(2 * (rows + 4)),
             field(window_rows * space),
         ],
@@ -781,7 +809,7 @@
             (devices, held_rows, LANES),
             field(rows), field(rows + 2), field(rows + 2), field(window_rows * space),
         ],
-        [(13, wide, depth, LANES)] + buffers + [(FIELDS * rows * depth, LANES)],
+        [(12, wide, depth, LANES)] + buffers + [(FIELDS * rows * depth, LANES)],
         next_odd, forcing, first_forcing, coefs, turn, held_windows, ahead, *arrived,
     )
     slots = lax.all_to_all(slots, ("tm", "space"), 0, 0, tiled=True)

time: 70 us -> 68.9 us (0.984)
  starting transfers between devices: 15.1 us -> 12.1 us
  waiting for transfers between devices: 11.2 us -> 12.6 us
    ppermute x11, starting transfers between devices: 15.1 us -> 12.1 us  [moved(): return lax.ppermute(array, ('tm', 'space'), pairs)]
    ppermute x11, waiting for transfers between devices: 11.2 us -> 12.6 us  [moved(): return lax.ppermute(array, ('tm', 'space'), pairs)]
where the time goes in v6:
time: 68.9 us; the launch traced here: 68.7 us
  blocking collectives  32.8 us (48%)
  waiting for transfers between devices  12.6 us (18%)
  starting transfers between devices  12.1 us (18%)
  Pallas kernels  11.2 us (16%)
    all_to_all x2, blocking collectives, body(): slots = lax.all_to_all(slots, ('tm', 'space'), 0, 0, tiled=True)  32.8 us
    ppermute x11, waiting for transfers between devices, moved(): return lax.ppermute(array, ('tm', 'space'), pairs)  12.6 us
    ppermute x11, starting transfers between devices, moved(): return lax.ppermute(array, ('tm', 'space'), pairs)  12.1 us
    pallas_call x6, Pallas kernels, call(): pl.pallas_call(kernel, out_shape=tuple((jax.ShapeDtypeStruct(shape, jnp.f...  11.2 us
  transfers between devices with their start and end apart: 11, of which 5 were waited for; matrix products, arithmetic and copies ran while one was open for 0% of the time, Pallas kernels for 3%

profile of v6, /device:TPU:0, one launch (start us, length us, event | category | flops | bytes accessed | tf_op | source)
XLA Modules:
  0.0 68.7 jit_solution(2679433715360172657)
XLA Ops:
  0.0 2.1 %shard_map.47 = (f32[368,128]{1,0:T(8,128)S(1)}, f32[336,128]{1,0:T(8,128)S(1)}, f32[512,128]{1,0:T(8,128)S(1)}, f32[64,128]{1,0:T(8,128)S(1)}, f32[64,128]{1,0:T(8,128)S(1)}, /*index=5*/f32[256,128]{1,0:T(8,128)S(1)}) custom-call(f32[8,16,2048]{2,1,0:T(8,128)} %initial_all.3, f32[8,16,2048]{2,1,0:T(8,128)} %source_all.3, f32[16,2048]{1,0:T(8,128)} %diffusivity_all.3, ...), custom_call_target="tpu_custom_call" | custom-call | tf_op jit(solution)/shard_map/pallas_call | solution.py:37
  2.1 0.5 collective-permute-start.2
  2.6 2.6 %collective-permute-start = (f32[23,16,128]{2,1,0:T(8,128)S(1)}, f32[23,16,128]{2,1,0:T(8,128)S(1)}, u32[]{:S(2)}, u32[]{:S(2)}) collective-permute-start(f32[23,16,128]{2,1,0:T(8,128)S(1)} %bitcast.17), channel_id=1, source_target_pairs={{0,1},{1,2},{2,3},{3,0},{4,5},{5,6},{6,7},{7,4},{8,9},{9,10},{10,1... | collective-permute-start | bytes 565256 | tf_op jit(solution)/shard_map/ppermute | solution.py:732
  5.1 1.0 %collective-permute-start.1 = (f32[21,16,128]{2,1,0:T(8,128)S(1)}, f32[21,16,128]{2,1,0:T(8,128)S(1)}, u32[]{:S(2)}, u32[]{:S(2)}) collective-permute-start(f32[21,16,128]{2,1,0:T(8,128)S(1)} %bitcast.18), channel_id=1, source_target_pairs={{0,3},{1,0},{2,1},{3,2},{4,7},{5,4},{6,5},{7,6},{8,11},{9,8},{10,9... | collective-permute-start | bytes 516104 | tf_op jit(solution)/shard_map/ppermute | solution.py:732
  6.1 4.5 %collective-permute-done.2.behind = f32[32,16,128]{2,1,0:T(8,128)S(1)} collective-permute-done((f32[32,16,128]{2,1,0:T(8,128)S(1)}, f32[32,16,128]{2,1,0:T(8,128)S(1)}, u32[]{:S(2)}, u32[]{:S(2)}) %collective-permute-start.2) | collective-permute-done | bytes 262176 | tf_op jit(solution)/shard_map/ppermute | solution.py:732
  10.7 0.0 collective-permute-start.5
  10.7 2.1 %collective-permute-start.3 = (f32[4,16,128]{2,1,0:T(8,128)S(1)}, f32[4,16,128]{2,1,0:T(8,128)S(1)}, u32[]{:S(2)}, u32[]{:S(2)}) collective-permute-start(f32[4,16,128]{2,1,0:T(8,128)S(1)} %bitcast.20), channel_id=1, source_target_pairs={{0,5},{1,6},{2,7},{3,4},{4,9},{5,10},{6,11},{7,8},{8,13},{9,14},{1... | collective-permute-start | bytes 98312 | tf_op jit(solution)/shard_map/ppermute | solution.py:732
  12.8 1.0 %collective-permute-start.4 = (f32[4,16,128]{2,1,0:T(8,128)S(1)}, f32[4,16,128]{2,1,0:T(8,128)S(1)}, u32[]{:S(2)}, u32[]{:S(2)}) collective-permute-start(f32[4,16,128]{2,1,0:T(8,128)S(1)} %bitcast.19), channel_id=1, source_target_pairs={{0,7},{1,4},{2,5},{3,6},{4,11},{5,8},{6,9},{7,10},{8,15},{9,12},{1... | collective-permute-start | bytes 98312 | tf_op jit(solution)/shard_map/ppermute | solution.py:732
  13.7 2.3 %shard_map.46 = (f32[3328,128]{1,0:T(8,128)S(1)}, f32[32,128]{1,0:T(8,128)S(1)}) custom-call(f32[8,16,2048]{2,1,0:T(8,128)} %initial_all.3, f32[8,16,2048]{2,1,0:T(8,128)} %source_all.3, f32[16,2048]{1,0:T(8,128)} %diffusivity_all.3, f32[16,2048]{1,0:T(8,128)} %growth_all.3), custom_call_target="tpu_custom_call" | custom-call | bytes 30000000 | tf_op jit(solution)/shard_map/pallas_call | solution.py:37
  16.0 1.9 %collective-permute-done.3.behind_above = f32[4,16,128]{2,1,0:T(8,128)S(1)} collective-permute-done((f32[4,16,128]{2,1,0:T(8,128)S(1)}, f32[4,16,128]{2,1,0:T(8,128)S(1)}, u32[]{:S(2)}, u32[]{:S(2)}) %collective-permute-start.3) | collective-permute-done | bytes 32800 | tf_op jit(solution)/shard_map/ppermute | solution.py:732
  17.9 0.9 %collective-permute-done.4.behind_below = f32[4,16,128]{2,1,0:T(8,128)S(1)} collective-permute-done((f32[4,16,128]{2,1,0:T(8,128)S(1)}, f32[4,16,128]{2,1,0:T(8,128)S(1)}, u32[]{:S(2)}, u32[]{:S(2)}) %collective-permute-start.4) | collective-permute-done | bytes 32800 | tf_op jit(solution)/shard_map/ppermute | solution.py:732
  18.8 0.0 collective-permute-done.1.below
  18.8 0.0 collective-permute-done.above
  18.8 0.0 collective-permute-done.5
  18.8 1.7 %shard_map.48 = (f32[32,16,128]{2,1,0:T(8,128)S(1)}, f32[7,16,128]{2,1,0:T(8,128)S(1)}, f32[5,16,128]{2,1,0:T(8,128)S(1)}, f32[3,16,128]{2,1,0:T(8,128)S(1)}, f3...) custom-call(f32[208,16,128]{2,1,0:T(8,128)S(1)} %bitcast.10, ...), custom_call_target="tpu_custom_call" | custom-call | tf_op jit(solution)/shard_map/pallas_call | solution.py:37
  20.5 0.1 collective-permute-start.8
  20.6 2.4 %collective-permute-start.6 = (f32[7,16,128]{2,1,0:T(8,128)S(1)}, f32[7,16,128]{2,1,0:T(8,128)S(1)}, u32[]{:S(2)}, u32[]{:S(2)}) collective-permute-start(f32[7,16,128]{2,1,0:T(8,128)S(1)} %get-tuple-element.60), channel_id=1, source_target_pairs={{0,1},{1,2},{2,3},{3,0},{4,5},{5,6},{6,7},{7,4},{8,9},{9,10},{10,1... | collective-permute-start | bytes 172040 | tf_op jit(solution)/shard_map/ppermute | solution.py:732
  23.1 0.5 collective-permute-start.7
  23.6 0.0 collective-permute-start.9
  23.6 1.9 %collective-permute-start.10 = (f32[3,16,128]{2,1,0:T(8,128)S(1)}, f32[3,16,128]{2,1,0:T(8,128)S(1)}, u32[]{:S(2)}, u32[]{:S(2)}) collective-permute-start(f32[3,16,128]{2,1,0:T(8,128)S(1)} %get-tuple-element.63), channel_id=1, source_target_pairs={{0,7},{1,4},{2,5},{3,6},{4,11},{5,8},{6,9},{7,10},{8,15},{9,12},{1... | collective-permute-start | bytes 73736 | tf_op jit(solution)/shard_map/ppermute | solution.py:732
  25.5 5.0 %collective-permute-done.9.behind_above = f32[3,16,128]{2,1,0:T(8,128)S(1)} collective-permute-done((f32[3,16,128]{2,1,0:T(8,128)S(1)}, f32[3,16,128]{2,1,0:T(8,128)S(1)}, u32[]{:S(2)}, u32[]{:S(2)}) %collective-permute-start.9) | collective-permute-done | bytes 24608 | tf_op jit(solution)/shard_map/ppermute | solution.py:732
  30.4 0.3 collective-permute-done.10.behind_below
  30.8 0.0 collective-permute-done.7.below
  30.8 0.0 collective-permute-done.6.above
  30.8 0.0 collective-permute-done.8.behind
  30.8 1.1 %shard_map.49 = (f32[32,32,128]{2,1,0:T(8,128)S(1)}, f32[16,16,128]{2,1,0:T(8,128)S(1)}, f32[18,16,128]{2,1,0:T(8,128)S(1)}, f32[18,16,128]{2,1,0:T(8,128)S(1)}, f32[8,16,128]{2,1,0:T(8,128)S(1)}) custom-call(f32[16,16,128]{2,1,0:T(8,128)S(1)} %get-tuple-element.53.next_odd, f32[48,16,128]{2,1,0:T(8,128)S(1)} %get-tuple-element.54.forcing, ...), custom_call_target="tpu_custom_call" | custom-call | tf_op jit(solution)/shard_map/pallas_call | solution.py:37
  31.9 19.6 %all_to_all.10.arrived = f32[32,32,128]{2,1,0:T(8,128)S(1)} all-to-all(f32[32,32,128]{2,1,0:T(8,128)S(1)} %get-tuple-element.64), channel_id=1, replica_groups=mesh['tm'=8,'space'=4] {'tm','space'}, dimensions={0} | all-to-all | bytes 1048576 | tf_op jit(solution)/shard_map/all_to_all | solution.py:815
  51.5 2.1 %shard_map.50 = f32[32,16,128]{2,1,0:T(8,128)S(1)} custom-call(f32[32,32,128]{2,1,0:T(8,128)S(1)} %all_to_all.10.arrived, f32[128,128]{1,0:T(8,128)S(1)} %bitcast.14), custom_call_target="tpu_custom_call" | custom-call | tf_op jit(solution)/shard_map/pallas_call | solution.py:37
  53.7 13.1 %all_to_all.11 = f32[32,16,128]{2,1,0:T(8,128)S(1)} all-to-all(f32[32,16,128]{2,1,0:T(8,128)S(1)} %shard_map.50), channel_id=1, replica_groups=mesh['tm'=8,'space'=4] {'tm','space'}, dimensions={0} | all-to-all | bytes 524288 | tf_op jit(solution)/shard_map/all_to_all | solution.py:823
  66.8 1.9 %shard_map.51 = f32[8,16,2048]{2,1,0:T(8,128)} custom-call(f32[512,128]{1,0:T(8,128)S(1)} %bitcast.12, f32[16,16,128]{2,1,0:T(8,128)S(1)} %get-tuple-element.66.next_forcing, f32[18,16,128]{2,1,0:T(8,128)S(1)} %get-tuple-element.67.late_a, f32[18,16,128]{2,1,0:T(8,128)S(1)} %get-tuple-element.68.late_b, f32[208,16,128]{2,1,0:T(8,128)S(1)} %bitcast.11, ...), custom_call_target="tpu_custom_call" | custom-call | tf_op jit(solution)/shard_map/pallas_call | solution.py:37
Async XLA Ops:
  2.1 8.6 %collective-permute-start.2 = (f32[32,16,128]{2,1,0:T(8,128)S(1)}, f32[32,16,128]{2,1,0:T(8,128)S(1)}, u32[]{:S(2)}, u32[]{:S(2)}) collective-permute-start(f32[32,16,128]{2,1,0:T(8,128)S(1)} %bitcast.16), channel_id=1, source_target_pairs={{0,4},{1,5},{2,6},{3,7},{4,8},{5,9},{6,10},{7,11},{8,12},{9,13},{1... | collective-permute-start | bytes 786440 | tf_op jit(solution)/shard_map/ppermute | solution.py:732
  2.6 16.2 %collective-permute-start = (f32[23,16,128]{2,1,0:T(8,128)S(1)}, f32[23,16,128]{2,1,0:T(8,128)S(1)}, u32[]{:S(2)}, u32[]{:S(2)}) collective-permute-start(f32[23,16,128]{2,1,0:T(8,128)S(1)} %bitcast.17), channel_id=1, source_target_pairs={{0,1},{1,2},{2,3},{3,0},{4,5},{5,6},{6,7},{7,4},{8,9},{9,10},{10,1... | collective-permute-start | bytes 565256 | tf_op jit(solution)/shard_map/ppermute | solution.py:732
  5.1 13.7 %collective-permute-start.1 = (f32[21,16,128]{2,1,0:T(8,128)S(1)}, f32[21,16,128]{2,1,0:T(8,128)S(1)}, u32[]{:S(2)}, u32[]{:S(2)}) collective-permute-start(f32[21,16,128]{2,1,0:T(8,128)S(1)} %bitcast.18), channel_id=1, source_target_pairs={{0,3},{1,0},{2,1},{3,2},{4,7},{5,4},{6,5},{7,6},{8,11},{9,8},{10,9... | collective-permute-start | bytes 516104 | tf_op jit(solution)/shard_map/ppermute | solution.py:732
  10.7 8.1 %collective-permute-start.5 = (f32[256,128]{1,0:T(8,128)S(1)}, f32[256,128]{1,0:T(8,128)S(1)}, u32[]{:S(2)}, u32[]{:S(2)}) collective-permute-start(f32[256,128]{1,0:T(8,128)S(1)} %get-tuple-element.45), channel_id=1, source_target_pairs={{0,28},{1,29},{2,30},{3,31},{4,0},{5,1},{6,2},{7,3},{8,4},{9,5},{1... | collective-permute-start | bytes 393224 | tf_op jit(solution)/shard_map/ppermute | solution.py:732
  10.7 7.3 %collective-permute-start.3 = (f32[4,16,128]{2,1,0:T(8,128)S(1)}, f32[4,16,128]{2,1,0:T(8,128)S(1)}, u32[]{:S(2)}, u32[]{:S(2)}) collective-permute-start(f32[4,16,128]{2,1,0:T(8,128)S(1)} %bitcast.20), channel_id=1, source_target_pairs={{0,5},{1,6},{2,7},{3,4},{4,9},{5,10},{6,11},{7,8},{8,13},{9,14},{1... | collective-permute-start | bytes 98312 | tf_op jit(solution)/shard_map/ppermute | solution.py:732
  12.8 6.0 %collective-permute-start.4 = (f32[4,16,128]{2,1,0:T(8,128)S(1)}, f32[4,16,128]{2,1,0:T(8,128)S(1)}, u32[]{:S(2)}, u32[]{:S(2)}) collective-permute-start(f32[4,16,128]{2,1,0:T(8,128)S(1)} %bitcast.19), channel_id=1, source_target_pairs={{0,7},{1,4},{2,5},{3,6},{4,11},{5,8},{6,9},{7,10},{8,15},{9,12},{1... | collective-permute-start | bytes 98312 | tf_op jit(solution)/shard_map/ppermute | solution.py:732
  20.5 10.2 %collective-permute-start.8 = (f32[32,16,128]{2,1,0:T(8,128)S(1)}, f32[32,16,128]{2,1,0:T(8,128)S(1)}, u32[]{:S(2)}, u32[]{:S(2)}) collective-permute-start(f32[32,16,128]{2,1,0:T(8,128)S(1)} %get-tuple-element.57.last_pair), channel_id=1, source_target_pairs={{0,4},{1,5},{2,6},{3,7},{4,8},{5,9},{6,10},{7,11},{8,12},{9,13},{1... | collective-permute-start | bytes 786440 | tf_op jit(solution)/shard_map/ppermute | solution.py:732
  20.6 10.2 %collective-permute-start.6 = (f32[7,16,128]{2,1,0:T(8,128)S(1)}, f32[7,16,128]{2,1,0:T(8,128)S(1)}, u32[]{:S(2)}, u32[]{:S(2)}) collective-permute-start(f32[7,16,128]{2,1,0:T(8,128)S(1)} %get-tuple-element.60), channel_id=1, source_target_pairs={{0,1},{1,2},{2,3},{3,0},{4,5},{5,6},{6,7},{7,4},{8,9},{9,10},{10,1... | collective-permute-start | bytes 172040 | tf_op jit(solution)/shard_map/ppermute | solution.py:732
  23.1 7.7 %collective-permute-start.7 = (f32[5,16,128]{2,1,0:T(8,128)S(1)}, f32[5,16,128]{2,1,0:T(8,128)S(1)}, u32[]{:S(2)}, u32[]{:S(2)}) collective-permute-start(f32[5,16,128]{2,1,0:T(8,128)S(1)} %get-tuple-element.61), channel_id=1, source_target_pairs={{0,3},{1,0},{2,1},{3,2},{4,7},{5,4},{6,5},{7,6},{8,11},{9,8},{10,9... | collective-permute-start | bytes 122888 | tf_op jit(solution)/shard_map/ppermute | solution.py:732
  23.6 6.8 %collective-permute-start.9 = (f32[3,16,128]{2,1,0:T(8,128)S(1)}, f32[3,16,128]{2,1,0:T(8,128)S(1)}, u32[]{:S(2)}, u32[]{:S(2)}) collective-permute-start(f32[3,16,128]{2,1,0:T(8,128)S(1)} %get-tuple-element.62), channel_id=1, source_target_pairs={{0,5},{1,6},{2,7},{3,4},{4,9},{5,10},{6,11},{7,8},{8,13},{9,14},{1... | collective-permute-start | bytes 73736 | tf_op jit(solution)/shard_map/ppermute | solution.py:732
  23.6 7.2 %collective-permute-start.10 = (f32[3,16,128]{2,1,0:T(8,128)S(1)}, f32[3,16,128]{2,1,0:T(8,128)S(1)}, u32[]{:S(2)}, u32[]{:S(2)}) collective-permute-start(f32[3,16,128]{2,1,0:T(8,128)S(1)} %get-tuple-element.63), channel_id=1, source_target_pairs={{0,7},{1,4},{2,5},{3,6},{4,11},{5,8},{6,9},{7,10},{8,15},{9,12},{1... | collective-permute-start | bytes 73736 | tf_op jit(solution)/shard_map/ppermute | solution.py:732

commit v7 on v6

--- a/solution.py
+++ b/solution.py
@@ -20,6 +20,7 @@
 CHAINS = POINTS // 2 - 1
 EDGE_0 = 4 * CHAINS + 7
 SLANT_0 = 4
+TURN = 2
 EDGE_1 = 5
 SLANT_1 = 3
 CORES = ("e0", "e1", "e2", "o0", "o1", "o2", "o3", "s0", "s1", "s2", "s3", "d", "g")
@@ -121,7 +122,8 @@
 
 def pack_kernel(
     share, initial_all, source_all, diffusivity_all, growth_all,
-    down, up, turn, slant_down, slant_up, back, evens, source, coefs, edge, cells, sems,
+    down, up, slant_down, slant_up, inward, outward,
+    evens, source, coefs, edge, cells, turn, sems,
 ):
     waits, last = fetch(
         initial_all, source_all, diffusivity_all, growth_all, evens, source, coefs, sems
@@ -167,8 +169,10 @@
                 ref[pl.ds(at + index * rows, rows), :] = window(
                     get, target_of(by) * share, depth
                 )
-    put(turn, 0, "ep", 0, 8)
-    put(turn, 8, "ep", 8, 8)
+    put_rows(turn, 0, jnp.zeros((1, depth, LANES), jnp.float32))
+    for r in range(0, rows, 8):
+        put(turn, 1 + r, "ep", r, 8)
+    put_rows(turn, rows + 1, jnp.zeros((1, depth, LANES), jnp.float32))
     last.wait()
     for side, (rim, slant, upward) in enumerate(sides):
         for i, (_, term, after, after_odd) in enumerate(chains):
@@ -180,8 +184,18 @@
         put(rim, 4 * CHAINS, "s0", near(upward, 2), 2)
         put(rim, 4 * CHAINS + 2, "o0", near(upward, 1), 1)
     for r in range(0, rows, 8):
-        put(turn, rows + r, "op", r, 8)
-        put(back, r, "s0", r, 8)
+        put(turn, rows + 2 + r, "op", r, 8)
+        put(turn, 2 * rows + 2 + r, "s0", r, 8)
+    ahead = lax.axis_index("tm") % 2 == 0
+    wide = rows_of(turn, 0, rows + 2)
+    mid, slope = slope_of_rows(wide, coef_rows(0, 0, rows), coef_rows(1, 0, rows))
+    forward = mid + slope + rows_of(turn, rows + 2, rows)
+    backward = rows_of(turn, 2 * rows + 2, rows)
+    put_rows(inward, 0, jnp.where(ahead, forward, backward))
+    put_rows(outward, 0, jnp.where(ahead, backward, forward))
+    for i, row in enumerate((1, rows)):
+        for to in (inward, outward):
+            put_rows(to, rows + i, rows_of(turn, row, 1))
     for side, (rim, slant, upward) in enumerate(sides):
         n0, n1, inner = (0, 1, 1) if upward else (rows - 1, rows - 2, rows - 3)
         diff0, diff1, grow1 = coef_rows(0, n0, 1), coef_rows(0, n1, 1), coef_rows(1, n1, 1)
@@ -264,12 +278,12 @@
 
 
 def level0_kernel(
-    apart, core, above, below, behind, behind_above, behind_below, *refs
+    apart, core, above, below, behind_above, behind_below, inward, outward, *refs
 ):
     windows, refs = refs[: len(apart)], refs[len(apart) :]
     (
         turn, down, up, slant_down, slant_up, next_odd, forcing, first_forcing, coefs, held,
-        fields, diff, grow,
+        behind_part, fields, diff, grow,
     ) = refs
     rows = core.shape[0] // len(CORES)
     low, high = flags()
@@ -313,15 +327,26 @@
         else:
             buffer = fields.at[spots[name]]
         buffer[pl.ds(MARGIN, rows)] = core[pl.ds(CORES.index(name) * rows, rows)]
-    for index, name in enumerate(("ep", "op")):
-        fields[spots[name], pl.ds(MARGIN, rows)] = behind[pl.ds(index * rows, rows)]
+    even_block = lax.axis_index("tm") % 2 == 0
+    cells = pl.ds(0, rows)
+    from_behind = jnp.where(even_block, outward[cells], inward[cells])
+    ahead = jnp.where(even_block, inward[cells], outward[cells])
+    fields[odd[0], pl.ds(MARGIN, rows)] = from_behind
+    for (at, _), row, edge_row in zip(sides, (0, 1), (0, rows - 1), strict=True):
+        edge = pl.ds(rows + row, 1)
+        fields[spots["ep"], pl.ds(MARGIN + edge_row, 1)] = jnp.where(
+            even_block, outward[edge], inward[edge]
+        )
+        near, first = pl.ds(at(1), 1), pl.ds(MARGIN + edge_row, 1)
+        mid, slope = growth_of(fields.at[spots["ep"]], at(1), 1, diff[near], grow[near])
+        fields[odd[0], near] = mid + slope + fields[spots["op"], near]
+        fields[odd[0], first] = fields[odd[0], first] + diff[first] * mid
 
     def first(at, n):
         d, g = diff[pl.ds(at, n)], grow[pl.ds(at, n)]
-        for i in range(halves):
-            start, term = ("ep", "op") if i == 0 else (f"e{i - 1}", f"o{i - 1}")
-            mid, slope = growth_of(fields.at[spots[start]], at, n, d, g)
-            fields[odd[i], pl.ds(at, n)] = mid + slope + fields[spots[term], pl.ds(at, n)]
+        for i in range(CHAINS):
+            mid, slope = growth_of(fields.at[spots[f"e{i}"]], at, n, d, g)
+            fields[odd[i + 1], pl.ds(at, n)] = mid + slope + fields[spots[f"o{i}"], pl.ds(at, n)]
 
     def second(at, n):
         d, g = diff[pl.ds(at, n)], grow[pl.ds(at, n)]
@@ -344,6 +369,7 @@
             pair = mid + slope - fields[image[i], pl.ds(at, n)]
             if i == halves - 1:
                 turn[pl.ds(here, n)] = pair
+                behind_part[...] = ahead + pair
             else:
                 term = fields[spots[f"s{i + 1}"], pl.ds(at, n)] + pair
                 forcing[pl.ds(i * rows + here, n)] = term
@@ -413,7 +439,7 @@
 
 
 def level1_kernel(
-    share, next_odd, forcing, first_forcing, coefs, last_pair, held, ahead,
+    share, next_odd, forcing, first_forcing, coefs, behind_part, held,
     above, below, behind, behind_above, behind_below,
     slots, next_forcing, late_a, late_b, windows,
     fields, diff, grow, flat,
@@ -466,7 +492,7 @@
         here = at - MARGIN
         mid, slope = growth_of(fields.at[odd1], at, n, d, g)
         pair1 = mid + 2.0 * slope - fields[image1, pl.ds(at, n)]
-        put_rows(flat, rows, ahead[...] + last_pair[pl.ds(0, rows)] + pair1)
+        put_rows(flat, rows, behind_part[...] + pair1)
         mid, slope = growth_of(fields.at[odd0], at, n, d, g)
         image = fields[image0, pl.ds(at, n)]
         term = fields[g2, pl.ds(at, n)] + (mid + 2.0 * slope - image)
@@ -571,7 +597,7 @@
 def packing(rows, share):
     groups = LANES // share
     each = -(-(rows + 2 * UP_RIM) // groups)
-    return groups, each, -(-(each + -(-4 // groups)) // 8) * 8
+    return groups, each, each + -(-4 // groups)
 
 
 def sweep_kernel(share, rows, arrived, windows, slots, diff, grow, terms, padded):
@@ -585,7 +611,7 @@
         diff[pl.ds(slab * rows, rows), :] = windows[pl.ds(2 * slab * rows, rows), :]
         grow[pl.ds(slab * rows, rows), :] = windows[pl.ds((2 * slab + 1) * rows, rows), :]
     line = lax.broadcasted_iota(jnp.int32, (total, LANES), 0)
-    lane = lax.broadcasted_iota(jnp.int32, (held, LANES), 1)
+    lane = lax.broadcasted_iota(jnp.int32, (each, LANES), 1)
     padded[...] = jnp.zeros(padded.shape, jnp.float32)
 
     def block(field, index):
@@ -606,7 +632,7 @@
         return diff[...] * laplace + grow[...] * field / (1.0 + field * field)
 
     def put_late(index, slab):
-        to = slots.at[index * slabs + slab]
+        to = slots.at[pl.ds((index * slabs + slab) * held, held)]
         if folded(rows, share, reach):
             zero = jnp.zeros((2, LANES), jnp.float32)
             low = arrived[index * slabs + slab + 1, pl.ds(16, 2)] if slab < slabs - 1 else zero
@@ -645,11 +671,11 @@
             )
         for slab in range(slabs):
             start = 8 + slab * rows - UP_RIM
-            value = padded[0, pl.ds(start, held), :]
+            value = padded[0, pl.ds(start, each), :]
             for group in range(1, groups):
-                piece = padded[group, pl.ds(start + group * each, held), :]
+                piece = padded[group, pl.ds(start + group * each, each), :]
                 value = jnp.where(lane >= group * share, piece, value)
-            slots[index * slabs + slab] = value
+            slots[pl.ds((index * slabs + slab) * held, each), :] = value
             put_late(index, slab)
         if index < blocks - 1:
             field = field + 8.0 * slope_of(field) + terms[index]
@@ -732,14 +758,24 @@
     return lax.ppermute(array, ("tm", "space"), pairs)
 
 
-def exchange(down, up, turn, slant_down, slant_up):
+def swapped(array, offset):
+    tm, space = lax.axis_size("tm"), lax.axis_size("space")
+    pairs = [
+        (t * space + s, ((((t - offset) % tm) ^ 1) + offset) % tm * space + s)
+        for t in range(tm)
+        for s in range(space)
+    ]
+    return lax.ppermute(array, ("tm", "space"), pairs)
+
+
+def rims(down, up, slant_down, slant_up):
     slanted = moved(slant_down, 1, 1), moved(slant_up, 1, -1)
-    return moved(down, 0, 1), moved(up, 0, -1), moved(turn, 1, 0), *slanted
+    return moved(down, 0, 1), moved(up, 0, -1), *slanted
 
 
 def body(initial, source, diffusivity, growth):
     points, rows, cols = initial.shape
-    assert points == POINTS and rows % 8 == 0 and cols % LANES == 0
+    assert points == POINTS and lax.axis_size("tm") % 2 == 0 and rows % 8 == 0 and cols % LANES == 0
     depth = cols // LANES
     tm, space = lax.axis_size("tm"), lax.axis_size("space")
     devices = tm * space
@@ -763,11 +799,11 @@
     raw = [(points // 2, rows, cols), source.shape, (2, rows, cols)]
     sides = EDGE_0 + window_rows
     extra = window_rows if handed_on(space) else 0
-    *sends, back = call(
+    *sends, inward, outward = call(
         functools.partial(pack_kernel, share),
-        [lines(sides + extra), lines(sides), lines(2 * rows), lines(SLANT_0), lines(SLANT_0)]
-        + [lines(rows)],
-        raw + [lines(2 * SCRATCH * (CHAINS + 1)), lines(2 * rows)],
+        [lines(sides + extra), lines(sides), lines(SLANT_0), lines(SLANT_0)]
+        + [lines(rows + TURN)] * 2,
+        raw + [lines(2 * SCRATCH * (CHAINS + 1)), lines(2 * rows), lines(3 * rows + 2)],
         initial, source, diffusivity, growth,
         place=pltpu.HBM, sems=points // 2 + 3,
     )
@@ -780,28 +816,28 @@
         place=pltpu.HBM, sems=points // 2 + 3,
         cost=pl.CostEstimate(flops=0, transcendentals=0, bytes_accessed=CORE_COST),
     )
-    above, below, turned, *slanted = exchange(*(as_rows(part) for part in sends))
-    turned, back = lax.optimization_barrier((turned, back))
-    ahead = as_rows(moved(back, -1, 0))
+    sends, inward, outward = [as_rows(part) for part in sends], as_rows(inward), as_rows(outward)
+    inward = swapped(inward, 0)
+    inward, sends[2], sends[3] = lax.optimization_barrier((inward, sends[2], sends[3]))
+    arrived = [*rims(*sends), inward, swapped(outward, 1)]
     windows = [moved(part, 0, by) if by else part for by, part in zip(apart, windows, strict=True)]
     windows = [as_rows(part) for part in windows]
     core = as_rows(core)
-    above, below, turned, slanted, ahead, windows = lax.optimization_barrier(
-        (above, below, turned, slanted, ahead, windows)
-    )
+    arrived, windows = lax.optimization_barrier((arrived, windows))
 
     buffers = [(wide, depth, LANES), (wide, depth, LANES)]
-    turn, down, up, slant_down, slant_up, next_odd, forcing, first_forcing, coefs, held_windows = call(
+    turn, down, up, slant_down, slant_up, next_odd, forcing, first_forcing, coefs, held_windows, behind_part = call(
         functools.partial(level0_kernel, tuple(apart)),
         [
             field(2 * rows), field(EDGE_1 + extra), field(EDGE_1), field(SLANT_1), field(SLANT_1),
             field(rows), field(3 * rows), field(rows + 4), field(2 * (rows + 4)),
-            field(window_rows * space),
+            field(window_rows * space), field(rows),
         ],
         [(len(CORES) + 2 + 3 * (POINTS // 2), wide, depth, LANES)] + buffers,
-        core, above, below, turned, *slanted, *windows,
-    )
-    arrived = exchange(down, up, turn, slant_down, slant_up)
+        core, *arrived, *windows,
+    )
+    above, below, *slanted = rims(down, up, slant_down, slant_up)
+    arrived = above, below, moved(turn, 1, 0), *slanted
     held_rows = FIELDS * 8 + 8 if folded(rows, share, reach_of()) else FIELDS * rows
     slots, next_forcing, late_a, late_b, windows = call(
         functools.partial(level1_kernel, share),
@@ -810,16 +846,17 @@
             field(rows), field(rows + 2), field(rows + 2), field(window_rows * space),
         ],
         [(12, wide, depth, LANES)] + buffers + [(FIELDS * rows * depth, LANES)],
-        next_odd, forcing, first_forcing, coefs, turn, held_windows, ahead, *arrived,
+        next_odd, forcing, first_forcing, coefs, behind_part, held_windows, *arrived,
     )
     slots = lax.all_to_all(slots, ("tm", "space"), 0, 0, tiled=True)
     (slots,) = call(
         functools.partial(sweep_kernel, share, rows),
-        [(devices, held, LANES)],
+        [(devices * held, LANES)],
         [(space * rows, LANES), (space * rows, LANES), (tm, space * rows, LANES)]
         + [(LANES // share, 8 + space * rows + 2 * rows + held, LANES)],
         slots, windows.reshape(-1, LANES),
     )
+    slots = slots.reshape(devices, held, 1, LANES)
     slots = lax.all_to_all(slots, ("tm", "space"), 0, 0, tiled=True)
     (out,) = call(
         functools.partial(up_kernel, share),

time: 68.9 us -> 66.2 us (0.961)
  waiting for transfers between devices: 12.6 us -> 9.46 us
  starting transfers between devices: 12.1 us -> 13.3 us
  blocking collectives: 32.8 us -> 31.9 us
    ppermute x11 -> x9, waiting for transfers between devices: 12.6 us -> 8.29 us  [moved(): return lax.ppermute(array, ('tm', 'space'), pairs)]
    ppermute x0 -> x2, starting transfers between devices: none -> 3.77 us  [swapped(): return lax.ppermute(array, ('tm', 'space'), pairs)]
    ppermute x11 -> x9, starting transfers between devices: 12.1 us -> 9.56 us  [moved(): return lax.ppermute(array, ('tm', 'space'), pairs)]
    ppermute x0 -> x2, waiting for transfers between devices: none -> 1.17 us  [swapped(): return lax.ppermute(array, ('tm', 'space'), pairs)]
    all_to_all x2, blocking collectives: 32.8 us -> 31.9 us  [body(): slots = lax.all_to_all(slots, ('tm', 'space'), 0, 0, tiled=True)]
where the time goes in v7:
time: 66.2 us; the launch traced here: 65.9 us
  blocking collectives  31.9 us (48%)
  starting transfers between devices  13.3 us (20%)
  Pallas kernels  11.1 us (17%)
  waiting for transfers between devices  9.46 us (14%)
    all_to_all x2, blocking collectives, body(): slots = lax.all_to_all(slots, ('tm', 'space'), 0, 0, tiled=True)  31.9 us
    pallas_call x6, Pallas kernels, call(): pl.pallas_call(kernel, out_shape=tuple((jax.ShapeDtypeStruct(shape, jnp.f...  11.1 us
    ppermute x9, starting transfers between devices, moved(): return lax.ppermute(array, ('tm', 'space'), pairs)  9.56 us
    ppermute x9, waiting for transfers between devices, moved(): return lax.ppermute(array, ('tm', 'space'), pairs)  8.29 us
    ppermute x2, starting transfers between devices, swapped(): return lax.ppermute(array, ('tm', 'space'), pairs)  3.77 us
  transfers between devices with their start and end apart: 11, of which 5 were waited for; matrix products, arithmetic and copies ran while one was open for 0% of the time, Pallas kernels for 3%

profile of v7, /device:TPU:0, one launch (start us, length us, event | category | flops | bytes accessed | tf_op | source)
XLA Modules:
  0.0 65.9 jit_solution(16657964805143703135)
XLA Ops:
  0.0 2.1 %shard_map.47 = (f32[368,128]{1,0:T(8,128)S(1)}, f32[336,128]{1,0:T(8,128)S(1)}, f32[64,128]{1,0:T(8,128)S(1)}, f32[64,128]{1,0:T(8,128)S(1)}, f32[288,128]{1,0:T(8,128)S(1)}, /*index=5*/f32[288,128]{1,0:T(8,128)S(1)}) custom-call(f32[8,16,2048]{2,1,0:T(8,128)} %initial_all.3, f32[8,16,2048]{2,1,0:T(8,128)} %source_all.3, f32[16,2048]{1,0:T(8,128)} %diffusivity_all.3, ...), custom_call_target="tpu_custom_call" | custom-call | tf_op jit(solution)/shard_map/pallas_call | solution.py:38
  2.2 3.0 %collective-permute-start = (f32[23,16,128]{2,1,0:T(8,128)S(1)}, f32[23,16,128]{2,1,0:T(8,128)S(1)}, u32[]{:S(2)}, u32[]{:S(2)}) collective-permute-start(f32[23,16,128]{2,1,0:T(8,128)S(1)} %bitcast.17), channel_id=1, source_target_pairs={{0,1},{1,2},{2,3},{3,0},{4,5},{5,6},{6,7},{7,4},{8,9},{9,10},{10,1... | collective-permute-start | bytes 565256 | tf_op jit(solution)/shard_map/ppermute | solution.py:758
  5.1 0.0 collective-permute-start.2
  5.1 1.1 %collective-permute-start.1 = (f32[21,16,128]{2,1,0:T(8,128)S(1)}, f32[21,16,128]{2,1,0:T(8,128)S(1)}, u32[]{:S(2)}, u32[]{:S(2)}) collective-permute-start(f32[21,16,128]{2,1,0:T(8,128)S(1)} %bitcast.18), channel_id=1, source_target_pairs={{0,3},{1,0},{2,1},{3,2},{4,7},{5,4},{6,5},{7,6},{8,11},{9,8},{10,9... | collective-permute-start | bytes 516104 | tf_op jit(solution)/shard_map/ppermute | solution.py:758
  6.2 3.8 %collective-permute-start.5 = (f32[18,16,128]{2,1,0:T(8,128)S(1)}, f32[18,16,128]{2,1,0:T(8,128)S(1)}, u32[]{:S(2)}, u32[]{:S(2)}) collective-permute-start(f32[18,16,128]{2,1,0:T(8,128)S(1)} %bitcast.19), channel_id=1, source_target_pairs={{0,28},{1,29},{2,30},{3,31},{4,8},{5,9},{6,10},{7,11},{8,4},{9,5},... | collective-permute-start | bytes 442376 | tf_op jit(solution)/shard_map/ppermute | solution.py:768
  10.0 0.0 collective-permute-done.2.inward
  10.0 0.0 collective-permute-start.3
  10.0 0.2 collective-permute-start.4
  10.2 2.3 %shard_map.46 = (f32[3328,128]{1,0:T(8,128)S(1)}, f32[32,128]{1,0:T(8,128)S(1)}) custom-call(f32[8,16,2048]{2,1,0:T(8,128)} %initial_all.3, f32[8,16,2048]{2,1,0:T(8,128)} %source_all.3, f32[16,2048]{1,0:T(8,128)} %diffusivity_all.3, f32[16,2048]{1,0:T(8,128)} %growth_all.3), custom_call_target="tpu_custom_call" | custom-call | bytes 30000000 | tf_op jit(solution)/shard_map/pallas_call | solution.py:38
  12.5 1.2 %collective-permute-done.5.outward = f32[18,16,128]{2,1,0:T(8,128)S(1)} collective-permute-done((f32[18,16,128]{2,1,0:T(8,128)S(1)}, f32[18,16,128]{2,1,0:T(8,128)S(1)}, u32[]{:S(2)}, u32[]{:S(2)}) %collective-permute-start.5) | collective-permute-done | bytes 147488 | tf_op jit(solution)/shard_map/ppermute | solution.py:768
  13.7 1.0 %collective-permute-done.1.below = f32[21,16,128]{2,1,0:T(8,128)S(1)} collective-permute-done((f32[21,16,128]{2,1,0:T(8,128)S(1)}, f32[21,16,128]{2,1,0:T(8,128)S(1)}, u32[]{:S(2)}, u32[]{:S(2)}) %collective-permute-start.1) | collective-permute-done | bytes 172064 | tf_op jit(solution)/shard_map/ppermute | solution.py:758
  14.8 2.2 %collective-permute-done.3.behind_above = f32[4,16,128]{2,1,0:T(8,128)S(1)} collective-permute-done((f32[4,16,128]{2,1,0:T(8,128)S(1)}, f32[4,16,128]{2,1,0:T(8,128)S(1)}, u32[]{:S(2)}, u32[]{:S(2)}) %collective-permute-start.3) | collective-permute-done | bytes 32800 | tf_op jit(solution)/shard_map/ppermute | solution.py:758
  17.0 0.4 collective-permute-done.4.behind_below
  17.4 0.0 collective-permute-done.above
  17.4 1.7 %shard_map.48 = (f32[32,16,128]{2,1,0:T(8,128)S(1)}, f32[7,16,128]{2,1,0:T(8,128)S(1)}, f32[5,16,128]{2,1,0:T(8,128)S(1)}, f32[3,16,128]{2,1,0:T(8,128)S(1)}, f3...) custom-call(f32[208,16,128]{2,1,0:T(8,128)S(1)} %bitcast.11, ...), custom_call_target="tpu_custom_call" | custom-call | tf_op jit(solution)/shard_map/pallas_call | solution.py:38
  19.0 0.1 collective-permute-start.8
  19.1 0.6 collective-permute-start.6
  19.8 2.3 %collective-permute-start.7 = (f32[5,16,128]{2,1,0:T(8,128)S(1)}, f32[5,16,128]{2,1,0:T(8,128)S(1)}, u32[]{:S(2)}, u32[]{:S(2)}) collective-permute-start(f32[5,16,128]{2,1,0:T(8,128)S(1)} %get-tuple-element.64), channel_id=1, source_target_pairs={{0,3},{1,0},{2,1},{3,2},{4,7},{5,4},{6,5},{7,6},{8,11},{9,8},{10,9... | collective-permute-start | bytes 122888 | tf_op jit(solution)/shard_map/ppermute | solution.py:758
  22.1 0.0 collective-permute-start.9
  22.1 2.2 %collective-permute-start.10 = (f32[3,16,128]{2,1,0:T(8,128)S(1)}, f32[3,16,128]{2,1,0:T(8,128)S(1)}, u32[]{:S(2)}, u32[]{:S(2)}) collective-permute-start(f32[3,16,128]{2,1,0:T(8,128)S(1)} %get-tuple-element.67), channel_id=1, source_target_pairs={{0,7},{1,4},{2,5},{3,6},{4,11},{5,8},{6,9},{7,10},{8,15},{9,12},{1... | collective-permute-start | bytes 73736 | tf_op jit(solution)/shard_map/ppermute | solution.py:758
  24.3 4.6 %collective-permute-done.9.behind_above = f32[3,16,128]{2,1,0:T(8,128)S(1)} collective-permute-done((f32[3,16,128]{2,1,0:T(8,128)S(1)}, f32[3,16,128]{2,1,0:T(8,128)S(1)}, u32[]{:S(2)}, u32[]{:S(2)}) %collective-permute-start.9) | collective-permute-done | bytes 24608 | tf_op jit(solution)/shard_map/ppermute | solution.py:758
  28.9 0.0 collective-permute-done.10.behind_below
  28.9 0.0 collective-permute-done.7.below
  28.9 0.0 collective-permute-done.6.above
  28.9 0.0 collective-permute-done.8.behind
  29.0 1.1 %shard_map.49 = (f32[32,32,128]{2,1,0:T(8,128)S(1)}, f32[16,16,128]{2,1,0:T(8,128)S(1)}, f32[18,16,128]{2,1,0:T(8,128)S(1)}, f32[18,16,128]{2,1,0:T(8,128)S(1)}, f32[8,16,128]{2,1,0:T(8,128)S(1)}) custom-call(f32[16,16,128]{2,1,0:T(8,128)S(1)} %get-tuple-element.57.next_odd, f32[48,16,128]{2,1,0:T(8,128)S(1)} %get-tuple-element.58.forcing, ...), custom_call_target="tpu_custom_call" | custom-call | tf_op jit(solution)/shard_map/pallas_call | solution.py:38
  30.0 19.9 %all_to_all.10.arrived = f32[32,32,128]{2,1,0:T(8,128)S(1)} all-to-all(f32[32,32,128]{2,1,0:T(8,128)S(1)} %get-tuple-element.68), channel_id=1, replica_groups=mesh['tm'=8,'space'=4] {'tm','space'}, dimensions={0} | all-to-all | bytes 1048576 | tf_op jit(solution)/shard_map/all_to_all | solution.py:851
  49.9 2.2 %shard_map.50 = f32[416,128]{1,0:T(8,128)S(1)} custom-call(f32[32,32,128]{2,1,0:T(8,128)S(1)} %all_to_all.10.arrived, f32[128,128]{1,0:T(8,128)S(1)} %bitcast.15), custom_call_target="tpu_custom_call" | custom-call | tf_op jit(solution)/shard_map/pallas_call | solution.py:38
  52.1 12.1 %all_to_all.11 = f32[32,13,1,128]{3,2,1,0:T(1,128)S(1)} all-to-all(f32[32,13,1,128]{3,2,1,0:T(1,128)S(1)} %bitcast.14), channel_id=1, replica_groups=mesh['tm'=8,'space'=4] {'tm','space'}, dimensions={0} | all-to-all | bytes 425984 | tf_op jit(solution)/shard_map/all_to_all | solution.py:860
  64.2 1.8 %shard_map.51 = f32[8,16,2048]{2,1,0:T(8,128)} custom-call(f32[416,128]{1,0:T(8,128)S(1)} %bitcast.13, f32[16,16,128]{2,1,0:T(8,128)S(1)} %get-tuple-element.70.next_forcing, f32[18,16,128]{2,1,0:T(8,128)S(1)} %get-tuple-element.71.late_a, f32[18,16,128]{2,1,0:T(8,128)S(1)} %get-tuple-element.72.late_b, f32[208,16,128]{2,1,0:T(8,128)S(1)} %bitcast.12, ...), custom_call_target="tpu_custom_call" | custom-call | tf_op jit(solution)/shard_map/pallas_call | solution.py:38
Async XLA Ops:
  2.2 15.2 %collective-permute-start = (f32[23,16,128]{2,1,0:T(8,128)S(1)}, f32[23,16,128]{2,1,0:T(8,128)S(1)}, u32[]{:S(2)}, u32[]{:S(2)}) collective-permute-start(f32[23,16,128]{2,1,0:T(8,128)S(1)} %bitcast.17), channel_id=1, source_target_pairs={{0,1},{1,2},{2,3},{3,0},{4,5},{5,6},{6,7},{7,4},{8,9},{9,10},{10,1... | collective-permute-start | bytes 565256 | tf_op jit(solution)/shard_map/ppermute | solution.py:758
  5.1 4.9 %collective-permute-start.2 = (f32[18,16,128]{2,1,0:T(8,128)S(1)}, f32[18,16,128]{2,1,0:T(8,128)S(1)}, u32[]{:S(2)}, u32[]{:S(2)}) collective-permute-start(f32[18,16,128]{2,1,0:T(8,128)S(1)} %bitcast.20), channel_id=1, source_target_pairs={{0,4},{1,5},{2,6},{3,7},{4,0},{5,1},{6,2},{7,3},{8,12},{9,13},{10,... | collective-permute-start | bytes 442376 | tf_op jit(solution)/shard_map/ppermute | solution.py:768
  5.1 9.6 %collective-permute-start.1 = (f32[21,16,128]{2,1,0:T(8,128)S(1)}, f32[21,16,128]{2,1,0:T(8,128)S(1)}, u32[]{:S(2)}, u32[]{:S(2)}) collective-permute-start(f32[21,16,128]{2,1,0:T(8,128)S(1)} %bitcast.18), channel_id=1, source_target_pairs={{0,3},{1,0},{2,1},{3,2},{4,7},{5,4},{6,5},{7,6},{8,11},{9,8},{10,9... | collective-permute-start | bytes 516104 | tf_op jit(solution)/shard_map/ppermute | solution.py:758
  6.2 7.5 %collective-permute-start.5 = (f32[18,16,128]{2,1,0:T(8,128)S(1)}, f32[18,16,128]{2,1,0:T(8,128)S(1)}, u32[]{:S(2)}, u32[]{:S(2)}) collective-permute-start(f32[18,16,128]{2,1,0:T(8,128)S(1)} %bitcast.19), channel_id=1, source_target_pairs={{0,28},{1,29},{2,30},{3,31},{4,8},{5,9},{6,10},{7,11},{8,4},{9,5},... | collective-permute-start | bytes 442376 | tf_op jit(solution)/shard_map/ppermute | solution.py:768
  10.0 6.9 %collective-permute-start.3 = (f32[4,16,128]{2,1,0:T(8,128)S(1)}, f32[4,16,128]{2,1,0:T(8,128)S(1)}, u32[]{:S(2)}, u32[]{:S(2)}) collective-permute-start(f32[4,16,128]{2,1,0:T(8,128)S(1)} %bitcast.22), channel_id=1, source_target_pairs={{0,5},{1,6},{2,7},{3,4},{4,9},{5,10},{6,11},{7,8},{8,13},{9,14},{1... | collective-permute-start | bytes 98312 | tf_op jit(solution)/shard_map/ppermute | solution.py:758
  10.0 7.3 %collective-permute-start.4 = (f32[4,16,128]{2,1,0:T(8,128)S(1)}, f32[4,16,128]{2,1,0:T(8,128)S(1)}, u32[]{:S(2)}, u32[]{:S(2)}) collective-permute-start(f32[4,16,128]{2,1,0:T(8,128)S(1)} %bitcast.21), channel_id=1, source_target_pairs={{0,7},{1,4},{2,5},{3,6},{4,11},{5,8},{6,9},{7,10},{8,15},{9,12},{1... | collective-permute-start | bytes 98312 | tf_op jit(solution)/shard_map/ppermute | solution.py:758
  19.0 9.9 %collective-permute-start.8 = (f32[32,16,128]{2,1,0:T(8,128)S(1)}, f32[32,16,128]{2,1,0:T(8,128)S(1)}, u32[]{:S(2)}, u32[]{:S(2)}) collective-permute-start(f32[32,16,128]{2,1,0:T(8,128)S(1)} %get-tuple-element.65), channel_id=1, source_target_pairs={{0,4},{1,5},{2,6},{3,7},{4,8},{5,9},{6,10},{7,11},{8,12},{9,13},{1... | collective-permute-start | bytes 786440 | tf_op jit(solution)/shard_map/ppermute | solution.py:758
  19.1 9.8 %collective-permute-start.6 = (f32[7,16,128]{2,1,0:T(8,128)S(1)}, f32[7,16,128]{2,1,0:T(8,128)S(1)}, u32[]{:S(2)}, u32[]{:S(2)}) collective-permute-start(f32[7,16,128]{2,1,0:T(8,128)S(1)} %get-tuple-element.63), channel_id=1, source_target_pairs={{0,1},{1,2},{2,3},{3,0},{4,5},{5,6},{6,7},{7,4},{8,9},{9,10},{10,1... | collective-permute-start | bytes 172040 | tf_op jit(solution)/shard_map/ppermute | solution.py:758
  19.8 9.2 %collective-permute-start.7 = (f32[5,16,128]{2,1,0:T(8,128)S(1)}, f32[5,16,128]{2,1,0:T(8,128)S(1)}, u32[]{:S(2)}, u32[]{:S(2)}) collective-permute-start(f32[5,16,128]{2,1,0:T(8,128)S(1)} %get-tuple-element.64), channel_id=1, source_target_pairs={{0,3},{1,0},{2,1},{3,2},{4,7},{5,4},{6,5},{7,6},{8,11},{9,8},{10,9... | collective-permute-start | bytes 122888 | tf_op jit(solution)/shard_map/ppermute | solution.py:758
  22.1 6.8 %collective-permute-start.9 = (f32[3,16,128]{2,1,0:T(8,128)S(1)}, f32[3,16,128]{2,1,0:T(8,128)S(1)}, u32[]{:S(2)}, u32[]{:S(2)}) collective-permute-start(f32[3,16,128]{2,1,0:T(8,128)S(1)} %get-tuple-element.66), channel_id=1, source_target_pairs={{0,5},{1,6},{2,7},{3,4},{4,9},{5,10},{6,11},{7,8},{8,13},{9,14},{1... | collective-permute-start | bytes 73736 | tf_op jit(solution)/shard_map/ppermute | solution.py:758
  22.1 6.8 %collective-permute-start.10 = (f32[3,16,128]{2,1,0:T(8,128)S(1)}, f32[3,16,128]{2,1,0:T(8,128)S(1)}, u32[]{:S(2)}, u32[]{:S(2)}) collective-permute-start(f32[3,16,128]{2,1,0:T(8,128)S(1)} %get-tuple-element.67), channel_id=1, source_target_pairs={{0,7},{1,4},{2,5},{3,6},{4,11},{5,8},{6,9},{7,10},{8,15},{9,12},{1... | collective-permute-start | bytes 73736 | tf_op jit(solution)/shard_map/ppermute | solution.py:758

commit v8 on v7

--- a/solution.py
+++ b/solution.py
@@ -10,7 +10,7 @@
 LANES = 128
 MARGIN = 4
 REACH = 32
-UP_RIM = 3
+UP_RIM = 2
 POINTS = 8
 FIELDS = 3
 CORE_COST = 30_000_000
@@ -18,7 +18,7 @@
 time_step = 0.02
 
 CHAINS = POINTS // 2 - 1
-EDGE_0 = 4 * CHAINS + 7
+EDGE_0 = 4 * CHAINS + 6
 SLANT_0 = 4
 TURN = 2
 EDGE_1 = 5
@@ -159,16 +159,13 @@
     for side, (rim, slant, upward) in enumerate(sides):
         for i, (start, _, _, _) in enumerate(chains):
             put(edge, (2 * i + side) * SCRATCH, start, near(upward, 4), 4)
-        for which in range(2):
-            put_rows(rim, 4 * CHAINS + 3 + 2 * which, coef_rows(which, near(upward, 2), 2))
+        put_rows(rim, 4 * CHAINS + 3, coef_rows(0, near(upward, 2), 2))
+        put_rows(rim, 4 * CHAINS + 5, coef_rows(1, near(upward, 1), 1))
     end = EDGE_0 * depth
-    for ref, by, at in ((down, 1, end), (up, -1, end), (down, 2, end + 2 * rows)):
-        if at < ref.shape[0]:
-            for index in range(2):
-                get = lambda line: cells[pl.ds(index * rows * depth + line, rows, stride=depth), :]
-                ref[pl.ds(at + index * rows, rows), :] = window(
-                    get, target_of(by) * share, depth
-                )
+    if end < down.shape[0]:
+        for index in range(2):
+            get = lambda line: cells[pl.ds(index * rows * depth + line, rows, stride=depth), :]
+            down[pl.ds(end + index * rows, rows), :] = window(get, target_of(2) * share, depth)
     put_rows(turn, 0, jnp.zeros((1, depth, LANES), jnp.float32))
     for r in range(0, rows, 8):
         put(turn, 1 + r, "ep", r, 8)
@@ -262,7 +259,7 @@
             for r in range(0, rows, 8):
                 value = get(pl.ds(r, 8), pl.ds(c * LANES, LANES))
                 core[pl.ds((index * rows + r) * depth + c, 8, stride=depth), :] = value
-    for by, out in zip(direct_windows(lax.axis_size("space")), windows, strict=True):
+    for by, out in zip(sent_windows(lax.axis_size("space")), windows, strict=True):
         for which, name in enumerate(("d", "g")):
             start = CORES.index(name) * rows * depth
             get = lambda line: core[pl.ds(start + line, rows, stride=depth), :]
@@ -273,14 +270,20 @@
     return slabs == 4
 
 
-def direct_windows(slabs):
-    return [0] if handed_on(slabs) else [0] + list(range(2, slabs - 1))
+def far_windows(slabs):
+    return [] if handed_on(slabs) else list(range(2, slabs - 1))
+
+
+def sent_windows(slabs):
+    return [0, 1, slabs - 1] + far_windows(slabs)
 
 
 def level0_kernel(
-    apart, core, above, below, behind_above, behind_below, inward, outward, *refs
+    core, above, below, behind_above, behind_below, inward, outward, own, ahead_one, behind_one,
+    *refs,
 ):
-    windows, refs = refs[: len(apart)], refs[len(apart) :]
+    distant = far_windows(lax.axis_size("space"))
+    windows, refs = refs[: len(distant)], refs[len(distant) :]
     (
         turn, down, up, slant_down, slant_up, next_odd, forcing, first_forcing, coefs, held,
         behind_part, fields, diff, grow,
@@ -320,7 +323,8 @@
         edge_at = 4 * CHAINS
         fields[spots["s0"], pl.ds(first_row, 2)] = rim[pl.ds(edge_at, 2)] * flag
         diff[pl.ds(first_row, 2)] = rim[pl.ds(edge_at + 3, 2)] * flag
-        grow[pl.ds(first_row, 2)] = rim[pl.ds(edge_at + 5, 2)] * flag
+        grow[pl.ds(at(1), 1)] = rim[pl.ds(edge_at + 5, 1)] * flag
+        grow[pl.ds(at(2), 1)] = nothing
     for name in CORES:
         if name in ("d", "g"):
             buffer = diff if name == "d" else grow
@@ -419,17 +423,13 @@
         slant[pl.ds(0, 1)] = row(turn, rows, n0)
         slant[pl.ds(1, 1)] = row(turn, 0, n0) + diff0 * mid_last
         slant[pl.ds(2, 1)] = row(turn, 0, n1) + mid_last + 2.0 * slope_last
-    at = EDGE_1
-    extra_rows = down.shape[0] - at
-    if extra_rows:
-        down[pl.ds(at, extra_rows)] = above[pl.ds(above.shape[0] - extra_rows, extra_rows)]
     slab, slabs = lax.axis_index("space"), lax.axis_size("space")
     size = 2 * rows // depth
-    for by, part in (
-        *zip(apart, windows, strict=True),
-        (1, above.at[pl.ds(EDGE_0, size)]),
-        (slabs - 1, below.at[pl.ds(EDGE_0, size)]),
-    ):
+    down[pl.ds(EDGE_1, size)] = ahead_one[...]
+    up[pl.ds(EDGE_1, size)] = behind_one[...]
+    if handed_on(slabs):
+        down[pl.ds(EDGE_1 + size, size)] = above[pl.ds(EDGE_0, size)]
+    for by, part in zip([0] + distant, (own, *windows), strict=True):
         held[pl.ds((slab - by) % slabs * size, size)] = part[...]
 
 
@@ -448,11 +448,12 @@
     low, high = flags()
     take_coefs(rows, coefs, diff, grow)
     windows[...] = held[...]
-    size = above.shape[0] - EDGE_1
-    if size:
-        slabs = lax.axis_size("space")
-        slab = (lax.axis_index("space") - 2) % slabs
-        windows[pl.ds(slab * size, size)] = above[pl.ds(EDGE_1, size)]
+    slab, slabs = lax.axis_index("space"), lax.axis_size("space")
+    size = windows.shape[0] // slabs
+    windows[pl.ds((slab - 1) % slabs * size, size)] = above[pl.ds(EDGE_1, size)]
+    windows[pl.ds((slab + 1) % slabs * size, size)] = below[pl.ds(EDGE_1, size)]
+    if handed_on(slabs):
+        windows[pl.ds((slab - 2) % slabs * size, size)] = above[pl.ds(EDGE_1 + size, size)]
     g1, g3, g2, g0, before, after, even0, even1, image0, image1, odd0, odd1 = range(12)
     nothing = jnp.zeros((1, *forcing.shape[1:]), jnp.float32)
     sides = rim_rows(rows, low, high)
@@ -591,7 +592,7 @@
 
 
 def late_rows(rows):
-    return (rows, -2, rows + 1, -1)
+    return (("forcing", rows), ("forcing", -1), ("odd", rows + 1), ("odd", -2))
 
 
 def packing(rows, share):
@@ -600,7 +601,7 @@
     return groups, each, each + -(-4 // groups)
 
 
-def sweep_kernel(share, rows, arrived, windows, slots, diff, grow, terms, padded):
+def sweep_kernel(share, rows, arrived, windows, slots, diff, grow, terms, owns, padded, odds):
     slabs = lax.axis_size("space")
     devices = arrived.shape[0]
     blocks = devices // slabs
@@ -613,6 +614,7 @@
     line = lax.broadcasted_iota(jnp.int32, (total, LANES), 0)
     lane = lax.broadcasted_iota(jnp.int32, (each, LANES), 1)
     padded[...] = jnp.zeros(padded.shape, jnp.float32)
+    odds[...] = jnp.zeros(odds.shape, jnp.float32)
 
     def block(field, index):
         parts = []
@@ -634,15 +636,20 @@
     def put_late(index, slab):
         to = slots.at[pl.ds((index * slabs + slab) * held, held)]
         if folded(rows, share, reach):
-            zero = jnp.zeros((2, LANES), jnp.float32)
-            low = arrived[index * slabs + slab + 1, pl.ds(16, 2)] if slab < slabs - 1 else zero
-            high = arrived[index * slabs + slab - 1, pl.ds(22, 2)] if slab > 0 else zero
-            to[pl.ds(each, 2)] = jnp.where(lane[:2] < share, low, high)
+            zero = jnp.zeros((1, LANES), jnp.float32)
+            low = arrived[index * slabs + slab + 1, pl.ds(16, 1)] if slab < slabs - 1 else zero
+            high = arrived[index * slabs + slab - 1, pl.ds(23, 1)] if slab > 0 else zero
+            to[pl.ds(each, 1)] = jnp.where(lane[:1] < share, low, high)
+            low = odds[0, pl.ds(8 + slab * rows + rows + 1, 1)]
+            high = odds[1, pl.ds(8 + slab * rows - 2, 1)]
+            to[pl.ds(each + 1, 1)] = jnp.where(lane[:1] < share, low, high)
             return
-        for i, row in enumerate(late_rows(rows)):
+        for i, (what, row) in enumerate(late_rows(rows)):
             at, group = each + i // groups, i % groups
             beside_slab = slab + row // rows
-            if 0 <= beside_slab < slabs:
+            if what == "odd":
+                piece = odds[group, pl.ds(8 + slab * rows + row, 1)]
+            elif 0 <= beside_slab < slabs:
                 place = pl.ds(2 * rows + row % rows, 1)
                 piece = arrived[index * slabs + beside_slab, place]
                 piece = pltpu.roll(piece, group * share, 1)
@@ -658,17 +665,22 @@
         odd, term = block(0, behind), block(1, behind)
         even = odd + 4.0 * slope_of(odd) + term
         slope = slope_of(even)
-        odd = even + 4.0 * slope + block(2, index)
+        own = block(2, index)
+        owns[index] = own
+        odd = even + 4.0 * slope + own
         stepped = even + 8.0 * slope
         pair = odd + 4.0 * slope_of(odd) - stepped
         terms[index] = block(1, index) + pair
         if index == blocks - 1:
             field = stepped + terms[index]
     for index in range(blocks):
+        slope = slope_of(field)
+        odd = field + 4.0 * slope + owns[index]
         for group in range(groups):
-            padded[group, pl.ds(8, total), :] = (
-                pltpu.roll(field, group * share, 1) if group else field
-            )
+            for to, value in ((padded, field), (odds, odd)):
+                to[group, pl.ds(8, total), :] = (
+                    pltpu.roll(value, group * share, 1) if group else value
+                )
         for slab in range(slabs):
             start = 8 + slab * rows - UP_RIM
             value = padded[0, pl.ds(start, each), :]
@@ -678,7 +690,7 @@
             slots[pl.ds((index * slabs + slab) * held, each), :] = value
             put_late(index, slab)
         if index < blocks - 1:
-            field = field + 8.0 * slope_of(field) + terms[index]
+            field = field + 8.0 * slope + terms[index]
 
 
 def up_kernel(
@@ -701,8 +713,9 @@
 
     for row in range(rows + 2 * UP_RIM):
         fields[0, MARGIN - UP_RIM + row] = whole(row % each, row // each)
-    for i, row in enumerate(late_rows(rows)):
-        fields[5, MARGIN + row] = whole(each + i // groups, i % groups)
+    for i, (what, row) in enumerate(late_rows(rows)):
+        spot = 5 if what == "forcing" else 2
+        fields[spot, MARGIN + row] = whole(each + i // groups, i % groups)
     fields[5, pl.ds(MARGIN, rows)] = next_forcing[...]
     odd_first = CORES.index("o0") * rows
 
@@ -737,7 +750,7 @@
 
     core_rows = pl.ds(MARGIN, rows)
     emit(0, fields[0, core_rows])
-    over_rows(rows, 2, first)
+    over_rows(rows, 1, first)
     emit(4, fields[2, core_rows])
     over_rows(rows, 1, second)
     emit(2, fields[1, core_rows])
@@ -797,20 +810,18 @@
     window_rows = 2 * rows // depth
     assert window_rows * depth == 2 * rows
     raw = [(points // 2, rows, cols), source.shape, (2, rows, cols)]
-    sides = EDGE_0 + window_rows
     extra = window_rows if handed_on(space) else 0
     *sends, inward, outward = call(
         functools.partial(pack_kernel, share),
-        [lines(sides + extra), lines(sides), lines(SLANT_0), lines(SLANT_0)]
+        [lines(EDGE_0 + extra), lines(EDGE_0), lines(SLANT_0), lines(SLANT_0)]
         + [lines(rows + TURN)] * 2,
         raw + [lines(2 * SCRATCH * (CHAINS + 1)), lines(2 * rows), lines(3 * rows + 2)],
         initial, source, diffusivity, growth,
         place=pltpu.HBM, sems=points // 2 + 3,
     )
-    apart = direct_windows(space)
     core, *windows = call(
         functools.partial(core_kernel, share),
-        [lines(len(CORES) * rows)] + [(2 * rows, LANES)] * len(apart),
+        [lines(len(CORES) * rows)] + [(2 * rows, LANES)] * len(sent_windows(space)),
         raw,
         initial, source, diffusivity, growth,
         place=pltpu.HBM, sems=points // 2 + 3,
@@ -820,16 +831,18 @@
     inward = swapped(inward, 0)
     inward, sends[2], sends[3] = lax.optimization_barrier((inward, sends[2], sends[3]))
     arrived = [*rims(*sends), inward, swapped(outward, 1)]
-    windows = [moved(part, 0, by) if by else part for by, part in zip(apart, windows, strict=True)]
     windows = [as_rows(part) for part in windows]
+    for i, by in enumerate(far_windows(space), 3):
+        windows[i] = moved(windows[i], 0, by)
     core = as_rows(core)
     arrived, windows = lax.optimization_barrier((arrived, windows))
 
     buffers = [(wide, depth, LANES), (wide, depth, LANES)]
     turn, down, up, slant_down, slant_up, next_odd, forcing, first_forcing, coefs, held_windows, behind_part = call(
-        functools.partial(level0_kernel, tuple(apart)),
+        level0_kernel,
         [
-            field(2 * rows), field(EDGE_1 + extra), field(EDGE_1), field(SLANT_1), field(SLANT_1),
+            field(2 * rows), field(EDGE_1 + window_rows + extra), field(EDGE_1 + window_rows),
+            field(SLANT_1), field(SLANT_1),
             field(rows), field(3 * rows), field(rows + 4), field(2 * (rows + 4)),
             field(window_rows * space), field(rows),
         ],
@@ -852,8 +865,10 @@
     (slots,) = call(
         functools.partial(sweep_kernel, share, rows),
         [(devices * held, LANES)],
-        [(space * rows, LANES), (space * rows, LANES), (tm, space * rows, LANES)]
-        + [(LANES // share, 8 + space * rows + 2 * rows + held, LANES)],
+        [(space * rows, LANES)] * 2
+        + [(tm, space * rows, LANES)] * 2
+        + [(LANES // share, 8 + space * rows + 2 * rows + held, LANES)]
+        + [(LANES // share, 16 + space * rows, LANES)],
         slots, windows.reshape(-1, LANES),
     )
     slots = slots.reshape(devices, held, 1, LANES)

time: 66.2 us -> 65.6 us (level)
    ppermute x2, waiting for transfers between devices: 1.17 us -> 0.01 us  [swapped(): return lax.ppermute(array, ('tm', 'space'), pairs)]
    ppermute x9, waiting for transfers between devices: 8.29 us -> 9.15 us  [moved(): return lax.ppermute(array, ('tm', 'space'), pairs)]
  transfers between devices with their start and end apart: 11 -> 11, of which waited for: 5 -> 4; matrix products, arithmetic and copies ran while one was open for 0% -> 0% of each run, Pallas kernels for 3% -> 4%
where the time goes in v8:
time: 65.6 us; the launch traced here: 65.4 us
  blocking collectives  31.6 us (48%)
  starting transfers between devices  13.3 us (20%)
  Pallas kernels  11.3 us (17%)
  waiting for transfers between devices  9.15 us (14%)
    all_to_all x2, blocking collectives, body(): slots = lax.all_to_all(slots, ('tm', 'space'), 0, 0, tiled=True)  31.6 us
    pallas_call x6, Pallas kernels, call(): pl.pallas_call(kernel, out_shape=tuple((jax.ShapeDtypeStruct(shape, jnp.f...  11.3 us
    ppermute x9, starting transfers between devices, moved(): return lax.ppermute(array, ('tm', 'space'), pairs)  9.32 us
    ppermute x9, waiting for transfers between devices, moved(): return lax.ppermute(array, ('tm', 'space'), pairs)  9.15 us
    ppermute x2, starting transfers between devices, swapped(): return lax.ppermute(array, ('tm', 'space'), pairs)  4 us
  transfers between devices with their start and end apart: 11, of which 4 were waited for; matrix products, arithmetic and copies ran while one was open for 0% of the time, Pallas kernels for 4%

profile of v8, /device:TPU:0, one launch (start us, length us, event | category | flops | bytes accessed | tf_op | source)
XLA Modules:
  0.0 65.4 jit_solution(10950589921228693077)
XLA Ops:
  0.0 2.1 %shard_map.47 = (f32[320,128]{1,0:T(8,128)S(1)}, f32[288,128]{1,0:T(8,128)S(1)}, f32[64,128]{1,0:T(8,128)S(1)}, f32[64,128]{1,0:T(8,128)S(1)}, f32[288,128]{1,0:T(8,128)S(1)}, /*index=5*/f32[288,128]{1,0:T(8,128)S(1)}) custom-call(f32[8,16,2048]{2,1,0:T(8,128)} %initial_all.3, f32[8,16,2048]{2,1,0:T(8,128)} %source_all.3, f32[16,2048]{1,0:T(8,128)} %diffusivity_all.3, ...), custom_call_target="tpu_custom_call" | custom-call | tf_op jit(solution)/shard_map/pallas_call | solution.py:38
  2.2 0.5 collective-permute-start.2
  2.7 2.6 %collective-permute-start = (f32[20,16,128]{2,1,0:T(8,128)S(1)}, f32[20,16,128]{2,1,0:T(8,128)S(1)}, u32[]{:S(2)}, u32[]{:S(2)}) collective-permute-start(f32[20,16,128]{2,1,0:T(8,128)S(1)} %bitcast.21), channel_id=1, source_target_pairs={{0,1},{1,2},{2,3},{3,0},{4,5},{5,6},{6,7},{7,4},{8,9},{9,10},{10,1... | collective-permute-start | bytes 491528 | tf_op jit(solution)/shard_map/ppermute | solution.py:771
  5.2 1.0 %collective-permute-start.1 = (f32[18,16,128]{2,1,0:T(8,128)S(1)}, f32[18,16,128]{2,1,0:T(8,128)S(1)}, u32[]{:S(2)}, u32[]{:S(2)}) collective-permute-start(f32[18,16,128]{2,1,0:T(8,128)S(1)} %bitcast.23), channel_id=1, source_target_pairs={{0,3},{1,0},{2,1},{3,2},{4,7},{5,4},{6,5},{7,6},{8,11},{9,8},{10,9... | collective-permute-start | bytes 442376 | tf_op jit(solution)/shard_map/ppermute | solution.py:771
  6.3 3.5 %collective-permute-start.5 = (f32[18,16,128]{2,1,0:T(8,128)S(1)}, f32[18,16,128]{2,1,0:T(8,128)S(1)}, u32[]{:S(2)}, u32[]{:S(2)}) collective-permute-start(f32[18,16,128]{2,1,0:T(8,128)S(1)} %bitcast.22), channel_id=1, source_target_pairs={{0,28},{1,29},{2,30},{3,31},{4,8},{5,9},{6,10},{7,11},{8,4},{9,5},... | collective-permute-start | bytes 442376 | tf_op jit(solution)/shard_map/ppermute | solution.py:781
  9.7 0.0 collective-permute-done.2.inward
  9.8 0.0 collective-permute-start.3
  9.8 0.6 collective-permute-start.4
  10.3 2.3 %shard_map.46 = (f32[3328,128]{1,0:T(8,128)S(1)}, f32[32,128]{1,0:T(8,128)S(1)}, f32[32,128]{1,0:T(8,128)S(1)}, f32[32,128]{1,0:T(8,128)S(1)}) custom-call(f32[8,16,2048]{2,1,0:T(8,128)} %initial_all.3, f32[8,16,2048]{2,1,0:T(8,128)} %source_all.3, f32[16,2048]{1,0:T(8,128)} %diffusivity_all.3, f32[16,2048]{1,0:T(8,128)} %growth_all.3), custom_call_target="tpu_custom_call" | custom-call | bytes 30000000 | tf_op jit(solution)/shard_map/pallas_call | solution.py:38
  12.7 1.7 %collective-permute-done.1.below = f32[18,16,128]{2,1,0:T(8,128)S(1)} collective-permute-done((f32[18,16,128]{2,1,0:T(8,128)S(1)}, f32[18,16,128]{2,1,0:T(8,128)S(1)}, u32[]{:S(2)}, u32[]{:S(2)}) %collective-permute-start.1) | collective-permute-done | bytes 147488 | tf_op jit(solution)/shard_map/ppermute | solution.py:771
  14.4 0.0 collective-permute-done.5.outward
  14.4 0.0 collective-permute-done.above
  14.4 2.3 %collective-permute-done.3.behind_above = f32[4,16,128]{2,1,0:T(8,128)S(1)} collective-permute-done((f32[4,16,128]{2,1,0:T(8,128)S(1)}, f32[4,16,128]{2,1,0:T(8,128)S(1)}, u32[]{:S(2)}, u32[]{:S(2)}) %collective-permute-start.3) | collective-permute-done | bytes 32800 | tf_op jit(solution)/shard_map/ppermute | solution.py:771
  16.7 0.4 collective-permute-done.4.behind_below
  17.1 1.6 %shard_map.48 = (f32[32,16,128]{2,1,0:T(8,128)S(1)}, f32[9,16,128]{2,1,0:T(8,128)S(1)}, f32[7,16,128]{2,1,0:T(8,128)S(1)}, f32[3,16,128]{2,1,0:T(8,128)S(1)}, f3...) custom-call(f32[208,16,128]{2,1,0:T(8,128)S(1)} %bitcast.13, ...), custom_call_target="tpu_custom_call" | custom-call | tf_op jit(solution)/shard_map/pallas_call | solution.py:38
  18.8 0.1 collective-permute-start.8
  18.8 0.8 %collective-permute-start.6 = (f32[9,16,128]{2,1,0:T(8,128)S(1)}, f32[9,16,128]{2,1,0:T(8,128)S(1)}, u32[]{:S(2)}, u32[]{:S(2)}) collective-permute-start(f32[9,16,128]{2,1,0:T(8,128)S(1)} %get-tuple-element.71), channel_id=1, source_target_pairs={{0,1},{1,2},{2,3},{3,0},{4,5},{5,6},{6,7},{7,4},{8,9},{9,10},{10,1... | collective-permute-start | bytes 221192 | tf_op jit(solution)/shard_map/ppermute | solution.py:771
  19.7 2.1 %collective-permute-start.7 = (f32[7,16,128]{2,1,0:T(8,128)S(1)}, f32[7,16,128]{2,1,0:T(8,128)S(1)}, u32[]{:S(2)}, u32[]{:S(2)}) collective-permute-start(f32[7,16,128]{2,1,0:T(8,128)S(1)} %get-tuple-element.72), channel_id=1, source_target_pairs={{0,3},{1,0},{2,1},{3,2},{4,7},{5,4},{6,5},{7,6},{8,11},{9,8},{10,9... | collective-permute-start | bytes 172040 | tf_op jit(solution)/shard_map/ppermute | solution.py:771
  21.8 0.0 collective-permute-start.9
  21.8 2.1 %collective-permute-start.10 = (f32[3,16,128]{2,1,0:T(8,128)S(1)}, f32[3,16,128]{2,1,0:T(8,128)S(1)}, u32[]{:S(2)}, u32[]{:S(2)}) collective-permute-start(f32[3,16,128]{2,1,0:T(8,128)S(1)} %get-tuple-element.75), channel_id=1, source_target_pairs={{0,7},{1,4},{2,5},{3,6},{4,11},{5,8},{6,9},{7,10},{8,15},{9,12},{1... | collective-permute-start | bytes 73736 | tf_op jit(solution)/shard_map/ppermute | solution.py:771
  23.9 4.7 %collective-permute-done.9.behind_above = f32[3,16,128]{2,1,0:T(8,128)S(1)} collective-permute-done((f32[3,16,128]{2,1,0:T(8,128)S(1)}, f32[3,16,128]{2,1,0:T(8,128)S(1)}, u32[]{:S(2)}, u32[]{:S(2)}) %collective-permute-start.9) | collective-permute-done | bytes 24608 | tf_op jit(solution)/shard_map/ppermute | solution.py:771
  28.6 0.0 collective-permute-done.10.behind_below
  28.6 0.0 collective-permute-done.7.below
  28.7 0.0 collective-permute-done.6.above
  28.7 0.0 collective-permute-done.8.behind
  28.7 1.1 %shard_map.49 = (f32[32,32,128]{2,1,0:T(8,128)S(1)}, f32[16,16,128]{2,1,0:T(8,128)S(1)}, f32[18,16,128]{2,1,0:T(8,128)S(1)}, f32[18,16,128]{2,1,0:T(8,128)S(1)}, f32[8,16,128]{2,1,0:T(8,128)S(1)}) custom-call(f32[16,16,128]{2,1,0:T(8,128)S(1)} %get-tuple-element.65.next_odd, f32[48,16,128]{2,1,0:T(8,128)S(1)} %get-tuple-element.66.forcing, ...), custom_call_target="tpu_custom_call" | custom-call | tf_op jit(solution)/shard_map/pallas_call | solution.py:38
  29.8 19.9 %all_to_all.10.arrived = f32[32,32,128]{2,1,0:T(8,128)S(1)} all-to-all(f32[32,32,128]{2,1,0:T(8,128)S(1)} %get-tuple-element.76), channel_id=1, replica_groups=mesh['tm'=8,'space'=4] {'tm','space'}, dimensions={0} | all-to-all | bytes 1048576 | tf_op jit(solution)/shard_map/all_to_all | solution.py:864
  49.6 2.3 %shard_map.50 = f32[384,128]{1,0:T(8,128)S(1)} custom-call(f32[32,32,128]{2,1,0:T(8,128)S(1)} %all_to_all.10.arrived, f32[128,128]{1,0:T(8,128)S(1)} %bitcast.17), custom_call_target="tpu_custom_call" | custom-call | tf_op jit(solution)/shard_map/pallas_call | solution.py:38
  52.0 11.7 %all_to_all.11 = f32[32,12,1,128]{3,2,1,0:T(1,128)S(1)} all-to-all(f32[32,12,1,128]{3,2,1,0:T(1,128)S(1)} %bitcast.16), channel_id=1, replica_groups=mesh['tm'=8,'space'=4] {'tm','space'}, dimensions={0} | all-to-all | bytes 393216 | tf_op jit(solution)/shard_map/all_to_all | solution.py:875
  63.6 1.8 %shard_map.51 = f32[8,16,2048]{2,1,0:T(8,128)} custom-call(f32[384,128]{1,0:T(8,128)S(1)} %bitcast.15, f32[16,16,128]{2,1,0:T(8,128)S(1)} %get-tuple-element.78.next_forcing, f32[18,16,128]{2,1,0:T(8,128)S(1)} %get-tuple-element.79.late_a, f32[18,16,128]{2,1,0:T(8,128)S(1)} %get-tuple-element.80.late_b, f32[208,16,128]{2,1,0:T(8,128)S(1)} %bitcast.14, ...), custom_call_target="tpu_custom_call" | custom-call | tf_op jit(solution)/shard_map/pallas_call | solution.py:38
Async XLA Ops:
  2.2 7.6 %collective-permute-start.2 = (f32[18,16,128]{2,1,0:T(8,128)S(1)}, f32[18,16,128]{2,1,0:T(8,128)S(1)}, u32[]{:S(2)}, u32[]{:S(2)}) collective-permute-start(f32[18,16,128]{2,1,0:T(8,128)S(1)} %bitcast.24), channel_id=1, source_target_pairs={{0,4},{1,5},{2,6},{3,7},{4,0},{5,1},{6,2},{7,3},{8,12},{9,13},{10,... | collective-permute-start | bytes 442376 | tf_op jit(solution)/shard_map/ppermute | solution.py:781
  2.7 11.7 %collective-permute-start = (f32[20,16,128]{2,1,0:T(8,128)S(1)}, f32[20,16,128]{2,1,0:T(8,128)S(1)}, u32[]{:S(2)}, u32[]{:S(2)}) collective-permute-start(f32[20,16,128]{2,1,0:T(8,128)S(1)} %bitcast.21), channel_id=1, source_target_pairs={{0,1},{1,2},{2,3},{3,0},{4,5},{5,6},{6,7},{7,4},{8,9},{9,10},{10,1... | collective-permute-start | bytes 491528 | tf_op jit(solution)/shard_map/ppermute | solution.py:771
  5.2 9.2 %collective-permute-start.1 = (f32[18,16,128]{2,1,0:T(8,128)S(1)}, f32[18,16,128]{2,1,0:T(8,128)S(1)}, u32[]{:S(2)}, u32[]{:S(2)}) collective-permute-start(f32[18,16,128]{2,1,0:T(8,128)S(1)} %bitcast.23), channel_id=1, source_target_pairs={{0,3},{1,0},{2,1},{3,2},{4,7},{5,4},{6,5},{7,6},{8,11},{9,8},{10,9... | collective-permute-start | bytes 442376 | tf_op jit(solution)/shard_map/ppermute | solution.py:771
  6.3 8.1 %collective-permute-start.5 = (f32[18,16,128]{2,1,0:T(8,128)S(1)}, f32[18,16,128]{2,1,0:T(8,128)S(1)}, u32[]{:S(2)}, u32[]{:S(2)}) collective-permute-start(f32[18,16,128]{2,1,0:T(8,128)S(1)} %bitcast.22), channel_id=1, source_target_pairs={{0,28},{1,29},{2,30},{3,31},{4,8},{5,9},{6,10},{7,11},{8,4},{9,5},... | collective-permute-start | bytes 442376 | tf_op jit(solution)/shard_map/ppermute | solution.py:781
  9.8 6.9 %collective-permute-start.3 = (f32[4,16,128]{2,1,0:T(8,128)S(1)}, f32[4,16,128]{2,1,0:T(8,128)S(1)}, u32[]{:S(2)}, u32[]{:S(2)}) collective-permute-start(f32[4,16,128]{2,1,0:T(8,128)S(1)} %bitcast.26), channel_id=1, source_target_pairs={{0,5},{1,6},{2,7},{3,4},{4,9},{5,10},{6,11},{7,8},{8,13},{9,14},{1... | collective-permute-start | bytes 98312 | tf_op jit(solution)/shard_map/ppermute | solution.py:771
  9.8 7.3 %collective-permute-start.4 = (f32[4,16,128]{2,1,0:T(8,128)S(1)}, f32[4,16,128]{2,1,0:T(8,128)S(1)}, u32[]{:S(2)}, u32[]{:S(2)}) collective-permute-start(f32[4,16,128]{2,1,0:T(8,128)S(1)} %bitcast.25), channel_id=1, source_target_pairs={{0,7},{1,4},{2,5},{3,6},{4,11},{5,8},{6,9},{7,10},{8,15},{9,12},{1... | collective-permute-start | bytes 98312 | tf_op jit(solution)/shard_map/ppermute | solution.py:771
  18.8 9.9 %collective-permute-start.8 = (f32[32,16,128]{2,1,0:T(8,128)S(1)}, f32[32,16,128]{2,1,0:T(8,128)S(1)}, u32[]{:S(2)}, u32[]{:S(2)}) collective-permute-start(f32[32,16,128]{2,1,0:T(8,128)S(1)} %get-tuple-element.73), channel_id=1, source_target_pairs={{0,4},{1,5},{2,6},{3,7},{4,8},{5,9},{6,10},{7,11},{8,12},{9,13},{1... | collective-permute-start | bytes 786440 | tf_op jit(solution)/shard_map/ppermute | solution.py:771
  18.8 9.8 %collective-permute-start.6 = (f32[9,16,128]{2,1,0:T(8,128)S(1)}, f32[9,16,128]{2,1,0:T(8,128)S(1)}, u32[]{:S(2)}, u32[]{:S(2)}) collective-permute-start(f32[9,16,128]{2,1,0:T(8,128)S(1)} %get-tuple-element.71), channel_id=1, source_target_pairs={{0,1},{1,2},{2,3},{3,0},{4,5},{5,6},{6,7},{7,4},{8,9},{9,10},{10,1... | collective-permute-start | bytes 221192 | tf_op jit(solution)/shard_map/ppermute | solution.py:771
  19.7 9.0 %collective-permute-start.7 = (f32[7,16,128]{2,1,0:T(8,128)S(1)}, f32[7,16,128]{2,1,0:T(8,128)S(1)}, u32[]{:S(2)}, u32[]{:S(2)}) collective-permute-start(f32[7,16,128]{2,1,0:T(8,128)S(1)} %get-tuple-element.72), channel_id=1, source_target_pairs={{0,3},{1,0},{2,1},{3,2},{4,7},{5,4},{6,5},{7,6},{8,11},{9,8},{10,9... | collective-permute-start | bytes 172040 | tf_op jit(solution)/shard_map/ppermute | solution.py:771
  21.8 6.8 %collective-permute-start.9 = (f32[3,16,128]{2,1,0:T(8,128)S(1)}, f32[3,16,128]{2,1,0:T(8,128)S(1)}, u32[]{:S(2)}, u32[]{:S(2)}) collective-permute-start(f32[3,16,128]{2,1,0:T(8,128)S(1)} %get-tuple-element.74), channel_id=1, source_target_pairs={{0,5},{1,6},{2,7},{3,4},{4,9},{5,10},{6,11},{7,8},{8,13},{9,14},{1... | collective-permute-start | bytes 73736 | tf_op jit(solution)/shard_map/ppermute | solution.py:771
  21.8 6.8 %collective-permute-start.10 = (f32[3,16,128]{2,1,0:T(8,128)S(1)}, f32[3,16,128]{2,1,0:T(8,128)S(1)}, u32[]{:S(2)}, u32[]{:S(2)}) collective-permute-start(f32[3,16,128]{2,1,0:T(8,128)S(1)} %get-tuple-element.75), channel_id=1, source_target_pairs={{0,7},{1,4},{2,5},{3,6},{4,11},{5,8},{6,9},{7,10},{8,15},{9,12},{1... | collective-permute-start | bytes 73736 | tf_op jit(solution)/shard_map/ppermute | solution.py:771

commit v9 on v8

--- a/solution.py
+++ b/solution.py
@@ -21,8 +21,7 @@
 EDGE_0 = 4 * CHAINS + 6
 SLANT_0 = 4
 TURN = 2
-EDGE_1 = 5
-SLANT_1 = 3
+EDGE_1 = 8
 CORES = ("e0", "e1", "e2", "o0", "o1", "o2", "o3", "s0", "s1", "s2", "s3", "d", "g")
 
 
@@ -285,8 +284,8 @@
     distant = far_windows(lax.axis_size("space"))
     windows, refs = refs[: len(distant)], refs[len(distant) :]
     (
-        turn, down, up, slant_down, slant_up, next_odd, forcing, first_forcing, coefs, held,
-        behind_part, fields, diff, grow,
+        turn, down, up, next_odd, last_odd, forcing, coefs, held, next_first,
+        fields, diff, grow,
     ) = refs
     rows = core.shape[0] // len(CORES)
     low, high = flags()
@@ -372,15 +371,16 @@
             mid, slope = growth_of(fields.at[odd[i]], at, n, d, g)
             pair = mid + slope - fields[image[i], pl.ds(at, n)]
             if i == halves - 1:
-                turn[pl.ds(here, n)] = pair
-                behind_part[...] = ahead + pair
+                next_first[...] = ahead + pair
             else:
                 term = fields[spots[f"s{i + 1}"], pl.ds(at, n)] + pair
                 forcing[pl.ds(i * rows + here, n)] = term
+                if i < 2:
+                    turn[pl.ds(i * rows + here, n)] = term
                 if i == 0:
                     next_odd[...] = fields[image[0], pl.ds(at, n)] + term
                 if i == halves - 2:
-                    turn[pl.ds(rows + here, n)] = fields[image[i], pl.ds(at, n)] + term
+                    last_odd[...] = fields[image[i], pl.ds(at, n)] + term
 
     over_rows(rows, 1, first)
     over_rows(rows, 1, second)
@@ -397,10 +397,9 @@
             fields[even[i], far] = value
     over_rows(rows, 1, third)
     over_rows(rows, 0, fourth)
-    first_forcing[...] = fields[spots["s0"], pl.ds(MARGIN - 2, rows + 4)]
     coefs[pl.ds(0, rows + 4)] = diff[pl.ds(MARGIN - 2, rows + 4)]
     coefs[pl.ds(rows + 4, rows + 4)] = grow[pl.ds(MARGIN - 2, rows + 4)]
-    for rim, slant, n0, n1 in ((down, slant_down, rows - 1, rows - 2), (up, slant_up, 0, 1)):
+    for rim, n0, n1 in ((down, rows - 1, rows - 2), (up, 0, 1)):
 
         def row(ref, first, n):
             return ref[pl.ds(first + n, 1)]
@@ -410,7 +409,7 @@
             slope_of_rows(
                 ref[pl.ds(first + n1 - 1, 3)], row(diff, MARGIN, n1), row(grow, MARGIN, n1)
             )
-            for ref, first in ((next_odd, 0), (turn, rows))
+            for ref, first in ((next_odd, 0), (last_odd, 0))
         ]
         (mid, slope), (mid_last, slope_last) = around
         even1 = mid + 2.0 * slope + row(forcing, rows, n1)
@@ -420,9 +419,9 @@
         rim[pl.ds(2, 1)] = g3 + diff0 * even1
         rim[pl.ds(3, 1)] = g3
         rim[pl.ds(4, 1)] = row(forcing, 0, n0)
-        slant[pl.ds(0, 1)] = row(turn, rows, n0)
-        slant[pl.ds(1, 1)] = row(turn, 0, n0) + diff0 * mid_last
-        slant[pl.ds(2, 1)] = row(turn, 0, n1) + mid_last + 2.0 * slope_last
+        rim[pl.ds(5, 1)] = row(last_odd, 0, n0)
+        rim[pl.ds(6, 1)] = row(next_first, 0, n0) + diff0 * mid_last
+        rim[pl.ds(7, 1)] = row(next_first, 0, n1) + mid_last + 2.0 * slope_last
     slab, slabs = lax.axis_index("space"), lax.axis_size("space")
     size = 2 * rows // depth
     down[pl.ds(EDGE_1, size)] = ahead_one[...]
@@ -439,8 +438,7 @@
 
 
 def level1_kernel(
-    share, next_odd, forcing, first_forcing, coefs, behind_part, held,
-    above, below, behind, behind_above, behind_below,
+    share, next_odd, last_odd, forcing, coefs, next_first, held, above, below, ahead_terms,
     slots, next_forcing, late_a, late_b, windows,
     fields, diff, grow, flat,
 ):
@@ -457,21 +455,19 @@
     g1, g3, g2, g0, before, after, even0, even1, image0, image1, odd0, odd1 = range(12)
     nothing = jnp.zeros((1, *forcing.shape[1:]), jnp.float32)
     sides = rim_rows(rows, low, high)
-    fields[after, pl.ds(MARGIN, rows)] = next_odd[...]
-    for which, spot in enumerate((g1, g2, g3)):
-        fields[spot, pl.ds(MARGIN, rows)] = forcing[pl.ds(which * rows, rows)]
-    fields[before, pl.ds(MARGIN, rows)] = behind[pl.ds(rows, rows)]
-    fields[g0, pl.ds(MARGIN, rows)] = first_forcing[pl.ds(2, rows)] + behind[pl.ds(0, rows)]
-    for (at, flag), rim, slant in zip(
-        sides, (above, below), (behind_above, behind_below), strict=True
-    ):
+    core = pl.ds(MARGIN, rows)
+    fields[after, core] = next_odd[...]
+    fields[before, core] = last_odd[...]
+    fields[g0, core] = next_first[...]
+    fields[g1, core] = ahead_terms[pl.ds(0, rows)]
+    fields[g2, core] = forcing[pl.ds(rows, rows)]
+    fields[g3, core] = forcing[pl.ds(2 * rows, rows)]
+    for (at, flag), rim in zip(sides, (above, below), strict=True):
         near, far = pl.ds(at(1), 1), pl.ds(at(2), 1)
-        for spot, row in ((after, 0), (g2, 1), (g3, 2), (g1, 4)):
+        for spot, row in ((after, 0), (g2, 1), (g3, 2), (before, 5), (g0, 6)):
             fields[spot, near] = rim[pl.ds(row, 1)] * flag
-        own = [first_forcing[pl.ds(at(k) - MARGIN + 2, 1)] for k in (1, 2)]
-        fields[before, near] = slant[pl.ds(0, 1)] * flag
-        fields[g0, near] = own[0] + slant[pl.ds(1, 1)] * flag
-        fields[even0, far] = own[1] + slant[pl.ds(2, 1)] * flag
+        fields[even0, far] = rim[pl.ds(7, 1)] * flag
+        fields[g1, near] = nothing
         for spot in (after, before, even1):
             fields[spot, far] = nothing
 
@@ -493,10 +489,10 @@
         here = at - MARGIN
         mid, slope = growth_of(fields.at[odd1], at, n, d, g)
         pair1 = mid + 2.0 * slope - fields[image1, pl.ds(at, n)]
-        put_rows(flat, rows, behind_part[...] + pair1)
+        put_rows(flat, rows, next_first[...] + pair1)
         mid, slope = growth_of(fields.at[odd0], at, n, d, g)
         image = fields[image0, pl.ds(at, n)]
-        term = fields[g2, pl.ds(at, n)] + (mid + 2.0 * slope - image)
+        term = ahead_terms[pl.ds(rows, rows)] + (mid + 2.0 * slope - image)
         next_forcing[pl.ds(here, n)] = term
         put_rows(flat, 2 * rows, term)
         put_rows(flat, 0, image + term)
@@ -504,11 +500,13 @@
     over_rows(rows, 1, second)
     over_rows(rows, 1, third)
     over_rows(rows, 0, fourth)
-    late_a[...] = fields[g1, pl.ds(MARGIN - 1, rows + 2)]
-    late_b[pl.ds(1, rows)] = fields[g3, pl.ds(MARGIN, rows)]
-    late_b[pl.ds(0, 1)] = above[pl.ds(3, 1)] * low
-    late_b[pl.ds(rows + 1, 1)] = below[pl.ds(3, 1)] * high
+    for late, which, row in ((late_a, 0, 4), (late_b, 2, 3)):
+        late[pl.ds(1, rows)] = forcing[pl.ds(which * rows, rows)]
+        late[pl.ds(0, 1)] = above[pl.ds(row, 1)] * low
+        late[pl.ds(rows + 1, 1)] = below[pl.ds(row, 1)] * high
     depth = forcing.shape[1]
+    put_rows(flat, FIELDS * rows, ahead_terms[pl.ds(0, 1)])
+    put_rows(flat, FIELDS * rows + 1, ahead_terms[pl.ds(rows - 1, 1)])
     if folded(rows, share, reach_of()):
         pack_folded(slots, flat, rows, depth, reach_of())
     else:
@@ -525,12 +523,17 @@
     return lax.axis_size("tm") + 2
 
 
+def slot_lines(rows, share, reach):
+    return (FIELDS * 8 + 8 if folded(rows, share, reach) else FIELDS * rows) + 2
+
+
 def folded(rows, share, reach):
     return rows == 16 and 2 * share == LANES and FIELDS * 2 * reach <= share
 
 
 def pack_folded(slots, flat, rows, depth, reach):
-    devices = slots.shape[0]
+    lines = slot_lines(rows, LANES // 2, reach)
+    devices = slots.shape[0] // lines
     lane = lax.broadcasted_iota(jnp.int32, (8, LANES), 1)
     place = lane % (LANES // 2)
     rims = [None] * devices
@@ -543,7 +546,7 @@
             cells.append(jnp.where(lane < LANES // 2, top, pltpu.roll(low, LANES // 2, 1)))
             cells.append(jnp.where(lane < LANES // 2, pltpu.roll(top, LANES // 2, 1), low))
         for target in range(devices):
-            slots[target, pl.ds(field * 8, 8)] = cells[target]
+            slots[pl.ds(target * lines + field * 8, 8), :] = cells[target]
             left = cells[target - 1] if target > 0 else 0.0
             right = cells[target + 1] if target < devices - 1 else 0.0
             rim = jnp.where(
@@ -554,7 +557,21 @@
             else:
                 rims[target] = rims[target] + pltpu.roll(rim, 2 * reach * field, 1)
     for target in range(devices):
-        slots[target, pl.ds(FIELDS * 8, 8)] = rims[target]
+        slots[pl.ds(target * lines + FIELDS * 8, 8), :] = rims[target]
+    top = flat[pl.ds(FIELDS * rows * depth, depth), :]
+    low = flat[pl.ds((FIELDS * rows + 1) * depth, depth), :]
+    lane = lax.broadcasted_iota(jnp.int32, (depth, LANES), 1)
+    line = lax.broadcasted_iota(jnp.int32, (depth, LANES), 0)
+    place = lane % (LANES // 2)
+    evens = jnp.where(lane < LANES // 2, top, pltpu.roll(low, LANES // 2, 1))
+    odds = jnp.where(lane < LANES // 2, pltpu.roll(top, LANES // 2, 1), low)
+    before = jnp.where(line == 0, 0.0, pltpu.roll(odds, 1, 0))
+    after = jnp.where(line == depth - 1, 0.0, pltpu.roll(evens, depth - 1, 0))
+    for parity, cells, left, right in ((0, evens, before, odds), (1, odds, evens, after)):
+        rim = jnp.where(place >= LANES // 2 - reach, left, jnp.where(place < reach, right, 0.0))
+        for i, value in enumerate((cells, rim)):
+            start = parity * lines + lines - 2 + i
+            slots[pl.ds(start, depth, stride=2 * lines), :] = value
 
 
 def unfold(slot, field, reach):
@@ -573,22 +590,33 @@
     )
 
 
+def unfold_row(slot, which):
+    last = slot.shape[0] - 2
+    cells, rims = slot[pl.ds(last, 1)], slot[pl.ds(last + 1, 1)]
+    lane = lax.broadcasted_iota(jnp.int32, (1, LANES), 1)
+    half = LANES // 2
+    if which == 0:
+        return jnp.where(lane < half, cells, pltpu.roll(rims, half, 1))
+    return jnp.where(lane < half, pltpu.roll(cells, half, 1), rims)
+
+
 def pack_windows(slots, flat, rows, depth, share):
-    for field in range(FIELDS):
-        first = field * rows * depth
-        lines = [flat[pl.ds(first + line, rows, stride=depth), :] for line in range(depth)]
-        for target in range(slots.shape[0]):
+    lines = slot_lines(rows, share, reach_of())
+    for field in range(FIELDS + 1):
+        first, count = field * rows * depth, rows if field < FIELDS else 2
+        held = [flat[pl.ds(first + line, count, stride=depth), :] for line in range(depth)]
+        for target in range(slots.shape[0] // lines):
             line, offset = target * share // LANES, target * share % LANES
             shift = (LANES - offset) % LANES
-            place = column_of((rows, LANES), offset)
-            value = pltpu.roll(lines[line], shift, 1)
+            place = column_of((count, LANES), offset)
+            value = pltpu.roll(held[line], shift, 1)
             if offset < REACH:
-                before = pltpu.roll(lines[line - 1], shift, 1) if line > 0 else 0.0
+                before = pltpu.roll(held[line - 1], shift, 1) if line > 0 else 0.0
                 value = jnp.where(place < 0, before, value)
             if offset > REACH:
-                after = pltpu.roll(lines[line + 1], shift, 1) if line < depth - 1 else 0.0
+                after = pltpu.roll(held[line + 1], shift, 1) if line < depth - 1 else 0.0
                 value = jnp.where(place >= LANES, after, value)
-            slots[target, pl.ds(field * rows, rows)] = value
+            slots[pl.ds(target * lines + field * rows, count), :] = value
 
 
 def late_rows(rows):
@@ -601,12 +629,13 @@
     return groups, each, each + -(-4 // groups)
 
 
-def sweep_kernel(share, rows, arrived, windows, slots, diff, grow, terms, owns, padded, odds):
+def sweep_kernel(share, rows, arrived, windows, slots, diff, grow, terms, owns, adds, padded, odds):
     slabs = lax.axis_size("space")
-    devices = arrived.shape[0]
+    reach = reach_of()
+    lines = slot_lines(rows, share, reach)
+    devices = arrived.shape[0] // lines
     blocks = devices // slabs
     total = slabs * rows
-    reach = reach_of()
     groups, each, held = packing(rows, share)
     for slab in range(slabs):
         diff[pl.ds(slab * rows, rows), :] = windows[pl.ds(2 * slab * rows, rows), :]
@@ -619,12 +648,26 @@
     def block(field, index):
         parts = []
         for slab in range(slabs):
-            slot = arrived.at[index * slabs + slab]
+            slot = arrived.at[pl.ds((index * slabs + slab) * lines, lines)]
             if folded(rows, share, reach):
                 parts.append(unfold(slot, field, reach))
             else:
                 parts.append(slot[pl.ds(field * rows, rows)])
         return jnp.concatenate(parts, axis=0)
+
+    adds[...] = jnp.zeros(adds.shape, jnp.float32)
+
+    def beyond(index):
+        for slab in range(slabs):
+            slot = arrived.at[pl.ds((index * slabs + slab) * lines, lines)]
+            for which, at in ((0, slab * rows - 1), (1, (slab + 1) * rows)):
+                if not 0 <= at < total:
+                    continue
+                if folded(rows, share, reach):
+                    piece = unfold_row(slot, which)
+                else:
+                    piece = slot[pl.ds(FIELDS * rows + which, 1)]
+                adds[index, pl.ds(at, 1), :] = 2.0 * diff[pl.ds(at, 1), :] * piece
 
     def slope_of(field):
         north = jnp.where(line == 0, 0.0, pltpu.roll(field, 1, 0))
@@ -635,24 +678,14 @@
 
     def put_late(index, slab):
         to = slots.at[pl.ds((index * slabs + slab) * held, held)]
-        if folded(rows, share, reach):
-            zero = jnp.zeros((1, LANES), jnp.float32)
-            low = arrived[index * slabs + slab + 1, pl.ds(16, 1)] if slab < slabs - 1 else zero
-            high = arrived[index * slabs + slab - 1, pl.ds(23, 1)] if slab > 0 else zero
-            to[pl.ds(each, 1)] = jnp.where(lane[:1] < share, low, high)
-            low = odds[0, pl.ds(8 + slab * rows + rows + 1, 1)]
-            high = odds[1, pl.ds(8 + slab * rows - 2, 1)]
-            to[pl.ds(each + 1, 1)] = jnp.where(lane[:1] < share, low, high)
-            return
         for i, (what, row) in enumerate(late_rows(rows)):
             at, group = each + i // groups, i % groups
-            beside_slab = slab + row // rows
+            place = slab * rows + row
             if what == "odd":
-                piece = odds[group, pl.ds(8 + slab * rows + row, 1)]
-            elif 0 <= beside_slab < slabs:
-                place = pl.ds(2 * rows + row % rows, 1)
-                piece = arrived[index * slabs + beside_slab, place]
-                piece = pltpu.roll(piece, group * share, 1)
+                piece = odds[group, pl.ds(8 + place, 1)]
+            elif 0 <= place < total:
+                piece = owns[index, pl.ds(place, 1)]
+                piece = pltpu.roll(piece, group * share, 1) if group else piece
             else:
                 piece = jnp.zeros((1, LANES), jnp.float32)
             if group:
@@ -661,11 +694,13 @@
 
     field = None
     for index in range(blocks):
-        behind = (index - 1) % blocks
-        odd, term = block(0, behind), block(1, behind)
+        beyond(index)
+    for index in range(blocks):
+        behind, twice = (index - 1) % blocks, (index - 2) % blocks
+        odd, term = block(0, twice) + adds[twice], block(1, behind)
         even = odd + 4.0 * slope_of(odd) + term
         slope = slope_of(even)
-        own = block(2, index)
+        own = block(2, behind) + adds[behind]
         owns[index] = own
         odd = even + 4.0 * slope + own
         stepped = even + 8.0 * slope
@@ -717,6 +752,10 @@
         spot = 5 if what == "forcing" else 2
         fields[spot, MARGIN + row] = whole(each + i // groups, i % groups)
     fields[5, pl.ds(MARGIN, rows)] = next_forcing[...]
+    for row, rim in ((0, 0), (rows - 1, rows + 1)):
+        spot = pl.ds(MARGIN + row, 1)
+        added = 2.0 * diff[spot] * late_a[pl.ds(rim, 1)]
+        fields[5, spot] = next_forcing[pl.ds(row, 1)] + added
     odd_first = CORES.index("o0") * rows
 
     def first(at, n):
@@ -838,35 +877,36 @@
     arrived, windows = lax.optimization_barrier((arrived, windows))
 
     buffers = [(wide, depth, LANES), (wide, depth, LANES)]
-    turn, down, up, slant_down, slant_up, next_odd, forcing, first_forcing, coefs, held_windows, behind_part = call(
+    turn, down, up, next_odd, last_odd, forcing, coefs, held_windows, next_first = call(
         level0_kernel,
         [
             field(2 * rows), field(EDGE_1 + window_rows + extra), field(EDGE_1 + window_rows),
-            field(SLANT_1), field(SLANT_1),
-            field(rows), field(3 * rows), field(rows + 4), field(2 * (rows + 4)),
+            field(rows), field(rows), field(3 * rows), field(2 * (rows + 4)),
             field(window_rows * space), field(rows),
         ],
         [(len(CORES) + 2 + 3 * (POINTS // 2), wide, depth, LANES)] + buffers,
         core, *arrived, *windows,
     )
-    above, below, *slanted = rims(down, up, slant_down, slant_up)
-    arrived = above, below, moved(turn, 1, 0), *slanted
-    held_rows = FIELDS * 8 + 8 if folded(rows, share, reach_of()) else FIELDS * rows
+    above, below, ahead_terms = moved(down, 0, 1), moved(up, 0, -1), moved(turn, -1, 0)
+    slot_rows = slot_lines(rows, share, reach_of())
     slots, next_forcing, late_a, late_b, windows = call(
         functools.partial(level1_kernel, share),
         [
-            (devices, held_rows, LANES),
+            (devices * slot_rows, LANES),
             field(rows), field(rows + 2), field(rows + 2), field(window_rows * space),
         ],
-        [(12, wide, depth, LANES)] + buffers + [(FIELDS * rows * depth, LANES)],
-        next_odd, forcing, first_forcing, coefs, behind_part, held_windows, *arrived,
-    )
+        [(12, wide, depth, LANES)] + buffers + [((FIELDS * rows + 2) * depth, LANES)],
+        next_odd, last_odd, forcing, coefs, next_first, held_windows, above, below, ahead_terms,
+    )
+    next_forcing = moved(next_forcing, 1, 0)
+    slots = slots.reshape(devices, slot_rows, 1, LANES)
     slots = lax.all_to_all(slots, ("tm", "space"), 0, 0, tiled=True)
+    slots = slots.reshape(devices * slot_rows, LANES)
     (slots,) = call(
         functools.partial(sweep_kernel, share, rows),
         [(devices * held, LANES)],
         [(space * rows, LANES)] * 2
-        + [(tm, space * rows, LANES)] * 2
+        + [(tm, space * rows, LANES)] * 3
         + [(LANES // share, 8 + space * rows + 2 * rows + held, LANES)]
         + [(LANES // share, 16 + space * rows, LANES)],
         slots, windows.reshape(-1, LANES),

time: 65.6 us -> 65 us (level)
  blocking collectives: 31.6 us -> 19.8 us
  waiting for transfers between devices: 9.15 us -> 17.1 us
  starting transfers between devices: 13.3 us -> 15.6 us
  Pallas kernels: 11.3 us -> 12.3 us
    all_to_all x2 -> x1, blocking collectives: 31.6 us -> 19.8 us  [body(): slots = lax.all_to_all(slots, ('tm', 'space'), 0, 0, tiled=True)]
    ppermute x9 -> x8, waiting for transfers between devices: 9.15 us -> 16.7 us  [moved(): return lax.ppermute(array, ('tm', 'space'), pairs)]
    all_to_all x0 -> x1, starting transfers between devices: none -> 2.58 us  [body(): slots = lax.all_to_all(slots, ('tm', 'space'), 0, 0, tiled=True)]
    pallas_call x6, Pallas kernels: 11.3 us -> 12.3 us  [call(): pl.pallas_call(kernel, out_shape=tuple((jax.ShapeDtypeStruct(shape, jnp.f...]
    ppermute x9 -> x8, starting transfers between devices: 9.32 us -> 9.04 us  [moved(): return lax.ppermute(array, ('tm', 'space'), pairs)]
  transfers between devices with their start and end apart: 11 -> 11, of which waited for: 4 -> 6; matrix products, arithmetic and copies ran while one was open for 0% -> 0% of each run, Pallas kernels for 4% -> 4%
where the time goes in v9:
time: 65 us; the launch traced here: 64.8 us
  blocking collectives  19.8 us (30%)
  waiting for transfers between devices  17.1 us (26%)
  starting transfers between devices  15.6 us (24%)
  Pallas kernels  12.3 us (19%)
    all_to_all x1, blocking collectives, body(): slots = lax.all_to_all(slots, ('tm', 'space'), 0, 0, tiled=True)  19.8 us
    ppermute x8, waiting for transfers between devices, moved(): return lax.ppermute(array, ('tm', 'space'), pairs)  16.7 us
    pallas_call x6, Pallas kernels, call(): pl.pallas_call(kernel, out_shape=tuple((jax.ShapeDtypeStruct(shape, jnp.f...  12.3 us
    ppermute x8, starting transfers between devices, moved(): return lax.ppermute(array, ('tm', 'space'), pairs)  9.04 us
    ppermute x2, starting transfers between devices, swapped(): return lax.ppermute(array, ('tm', 'space'), pairs)  4 us
    all_to_all x1, starting transfers between devices, body(): slots = lax.all_to_all(slots, ('tm', 'space'), 0, 0, tiled=True)  2.58 us
  transfers between devices with their start and end apart: 11, of which 6 were waited for; matrix products, arithmetic and copies ran while one was open for 0% of the time, Pallas kernels for 4%

profile of v9, /device:TPU:0, one launch (start us, length us, event | category | flops | bytes accessed | tf_op | source)
XLA Modules:
  0.0 64.8 jit_solution(9234828128883979743)
XLA Ops:
  0.0 2.1 %shard_map.47 = (f32[320,128]{1,0:T(8,128)S(1)}, f32[288,128]{1,0:T(8,128)S(1)}, f32[64,128]{1,0:T(8,128)S(1)}, f32[64,128]{1,0:T(8,128)S(1)}, f32[288,128]{1,0:T(8,128)S(1)}, /*index=5*/f32[288,128]{1,0:T(8,128)S(1)}) custom-call(f32[8,16,2048]{2,1,0:T(8,128)} %initial_all.3, f32[8,16,2048]{2,1,0:T(8,128)} %source_all.3, f32[16,2048]{1,0:T(8,128)} %diffusivity_all.3, ...), custom_call_target="tpu_custom_call" | custom-call | tf_op jit(solution)/shard_map/pallas_call | solution.py:37
  2.2 0.5 collective-permute-start.2
  2.7 2.6 %collective-permute-start = (f32[20,16,128]{2,1,0:T(8,128)S(1)}, f32[20,16,128]{2,1,0:T(8,128)S(1)}, u32[]{:S(2)}, u32[]{:S(2)}) collective-permute-start(f32[20,16,128]{2,1,0:T(8,128)S(1)} %bitcast.24), channel_id=1, source_target_pairs={{0,1},{1,2},{2,3},{3,0},{4,5},{5,6},{6,7},{7,4},{8,9},{9,10},{10,1... | collective-permute-start | bytes 491528 | tf_op jit(solution)/shard_map/ppermute | solution.py:810
  5.2 1.0 %collective-permute-start.1 = (f32[18,16,128]{2,1,0:T(8,128)S(1)}, f32[18,16,128]{2,1,0:T(8,128)S(1)}, u32[]{:S(2)}, u32[]{:S(2)}) collective-permute-start(f32[18,16,128]{2,1,0:T(8,128)S(1)} %bitcast.26), channel_id=1, source_target_pairs={{0,3},{1,0},{2,1},{3,2},{4,7},{5,4},{6,5},{7,6},{8,11},{9,8},{10,9... | collective-permute-start | bytes 442376 | tf_op jit(solution)/shard_map/ppermute | solution.py:810
  6.3 3.5 %collective-permute-start.5 = (f32[18,16,128]{2,1,0:T(8,128)S(1)}, f32[18,16,128]{2,1,0:T(8,128)S(1)}, u32[]{:S(2)}, u32[]{:S(2)}) collective-permute-start(f32[18,16,128]{2,1,0:T(8,128)S(1)} %bitcast.25), channel_id=1, source_target_pairs={{0,28},{1,29},{2,30},{3,31},{4,8},{5,9},{6,10},{7,11},{8,4},{9,5},... | collective-permute-start | bytes 442376 | tf_op jit(solution)/shard_map/ppermute | solution.py:820
  9.7 0.0 collective-permute-done.2.inward
  9.8 0.0 collective-permute-start.3
  9.8 0.6 collective-permute-start.4
  10.3 2.3 %shard_map.46 = (f32[3328,128]{1,0:T(8,128)S(1)}, f32[32,128]{1,0:T(8,128)S(1)}, f32[32,128]{1,0:T(8,128)S(1)}, f32[32,128]{1,0:T(8,128)S(1)}) custom-call(f32[8,16,2048]{2,1,0:T(8,128)} %initial_all.3, f32[8,16,2048]{2,1,0:T(8,128)} %source_all.3, f32[16,2048]{1,0:T(8,128)} %diffusivity_all.3, f32[16,2048]{1,0:T(8,128)} %growth_all.3), custom_call_target="tpu_custom_call" | custom-call | bytes 30000000 | tf_op jit(solution)/shard_map/pallas_call | solution.py:37
  12.7 1.7 %collective-permute-done.1.below = f32[18,16,128]{2,1,0:T(8,128)S(1)} collective-permute-done((f32[18,16,128]{2,1,0:T(8,128)S(1)}, f32[18,16,128]{2,1,0:T(8,128)S(1)}, u32[]{:S(2)}, u32[]{:S(2)}) %collective-permute-start.1) | collective-permute-done | bytes 147488 | tf_op jit(solution)/shard_map/ppermute | solution.py:810
  14.4 0.0 collective-permute-done.5.outward
  14.4 0.0 collective-permute-done.above
  14.4 2.3 %collective-permute-done.3.behind_above = f32[4,16,128]{2,1,0:T(8,128)S(1)} collective-permute-done((f32[4,16,128]{2,1,0:T(8,128)S(1)}, f32[4,16,128]{2,1,0:T(8,128)S(1)}, u32[]{:S(2)}, u32[]{:S(2)}) %collective-permute-start.3) | collective-permute-done | bytes 32800 | tf_op jit(solution)/shard_map/ppermute | solution.py:810
  16.7 0.4 collective-permute-done.4.behind_below
  17.1 1.6 %shard_map.48 = (f32[32,16,128]{2,1,0:T(8,128)S(1)}, f32[12,16,128]{2,1,0:T(8,128)S(1)}, f32[10,16,128]{2,1,0:T(8,128)S(1)}, f32[16,16,128]{2,1,0:T(8,128)S(1)},...) custom-call(f32[208,16,128]{2,1,0:T(8,128)S(1)} %bitcast.15, ...), custom_call_target="tpu_custom_call" | custom-call | tf_op jit(solution)/shard_map/pallas_call | solution.py:37
  18.8 1.8 %collective-permute-start.8 = (f32[32,16,128]{2,1,0:T(8,128)S(1)}, f32[32,16,128]{2,1,0:T(8,128)S(1)}, u32[]{:S(2)}, u32[]{:S(2)}) collective-permute-start(f32[32,16,128]{2,1,0:T(8,128)S(1)} %get-tuple-element.71), channel_id=1, source_target_pairs={{0,28},{1,29},{2,30},{3,31},{4,0},{5,1},{6,2},{7,3},{8,4},{9,5},{1... | collective-permute-start | bytes 786440 | tf_op jit(solution)/shard_map/ppermute | solution.py:810
  20.5 1.5 %collective-permute-start.6 = (f32[12,16,128]{2,1,0:T(8,128)S(1)}, f32[12,16,128]{2,1,0:T(8,128)S(1)}, u32[]{:S(2)}, u32[]{:S(2)}) collective-permute-start(f32[12,16,128]{2,1,0:T(8,128)S(1)} %get-tuple-element.69), channel_id=1, source_target_pairs={{0,1},{1,2},{2,3},{3,0},{4,5},{5,6},{6,7},{7,4},{8,9},{9,10},{10,1... | collective-permute-start | bytes 294920 | tf_op jit(solution)/shard_map/ppermute | solution.py:810
  22.0 1.4 %collective-permute-start.7 = (f32[10,16,128]{2,1,0:T(8,128)S(1)}, f32[10,16,128]{2,1,0:T(8,128)S(1)}, u32[]{:S(2)}, u32[]{:S(2)}) collective-permute-start(f32[10,16,128]{2,1,0:T(8,128)S(1)} %get-tuple-element.70), channel_id=1, source_target_pairs={{0,3},{1,0},{2,1},{3,2},{4,7},{5,4},{6,5},{7,6},{8,11},{9,8},{10,9... | collective-permute-start | bytes 245768 | tf_op jit(solution)/shard_map/ppermute | solution.py:810
  23.5 3.1 %collective-permute-done.7.below = f32[10,16,128]{2,1,0:T(8,128)S(1)} collective-permute-done((f32[10,16,128]{2,1,0:T(8,128)S(1)}, f32[10,16,128]{2,1,0:T(8,128)S(1)}, u32[]{:S(2)}, u32[]{:S(2)}) %collective-permute-start.7) | collective-permute-done | bytes 81952 | tf_op jit(solution)/shard_map/ppermute | solution.py:810
  26.6 0.0 collective-permute-done.6.above
  26.6 0.0 collective-permute-done.8.ahead_terms
  26.6 1.1 %shard_map.49 = (f32[1088,128]{1,0:T(8,128)S(1)}, f32[16,16,128]{2,1,0:T(8,128)S(1)}, f32[18,16,128]{2,1,0:T(8,128)S(1)}, f32[18,16,128]{2,1,0:T(8,128)S(1)}, f32[8,16,128]{2,1,0:T(8,128)S(1)}) custom-call(f32[16,16,128]{2,1,0:T(8,128)S(1)} %get-tuple-element.63.next_odd, f32[16,16,128]{2,1,0:T(8,128)S(1)} %get-tuple-element.64.last_odd, ...), custom_call_target="tpu_custom_call" | custom-call | tf_op jit(solution)/shard_map/pallas_call | solution.py:37
  27.7 19.8 %all_to_all.10 = f32[32,34,1,128]{3,2,1,0:T(1,128)S(1)} all-to-all(f32[32,34,1,128]{3,2,1,0:T(1,128)S(1)} %bitcast.19), channel_id=1, replica_groups=mesh['tm'=8,'space'=4] {'tm','space'}, dimensions={0} | all-to-all | bytes 1114112 | tf_op jit(solution)/shard_map/all_to_all | solution.py:903
  47.4 3.3 %shard_map.50 = f32[384,128]{1,0:T(8,128)} custom-call(f32[1088,128]{1,0:T(8,128)S(1)} %bitcast.17, f32[128,128]{1,0:T(8,128)S(1)} %bitcast.20), custom_call_target="tpu_custom_call" | custom-call | tf_op jit(solution)/shard_map/pallas_call | solution.py:37
  50.7 2.6 %all-to-all-start.1 = ((f32[32,12,1,128]{3,2,1,0:T(1,128)}), f32[32,12,1,128]{3,2,1,0:T(1,128)S(1)}, u32[]{:S(2)}, u32[]{:S(2)}) async-start(f32[32,12,1,128]{3,2,1,0:T(1,128)} %bitcast.13), calls=%async_computation.1 | async-start | bytes 393216 | tf_op jit(solution)/shard_map/all_to_all | solution.py:915
  53.3 0.2 collective-permute-start.9
  53.5 9.1 %collective-permute-done.9.next_forcing = f32[16,16,128]{2,1,0:T(8,128)S(1)} collective-permute-done((f32[16,16,128]{2,1,0:T(8,128)S(1)}, f32[16,16,128]{2,1,0:T(8,128)S(1)}, u32[]{:S(2)}, u32[]{:S(2)}) %collective-permute-start.9) | collective-permute-done | bytes 131104 | tf_op jit(solution)/shard_map/ppermute | solution.py:810
  62.6 0.4 all-to-all-done.1
  63.0 1.8 %shard_map.51 = f32[8,16,2048]{2,1,0:T(8,128)} custom-call(f32[384,128]{1,0:T(8,128)S(1)} %bitcast.18, f32[16,16,128]{2,1,0:T(8,128)S(1)} %collective-permute-done.9.next_forcing, f32[18,16,128]{2,1,0:T(8,128)S(1)} %get-tuple-element.75.late_a, f32[18,16,128]{2,1,0:T(8,128)S(1)} %get-tuple-element.76.late_b, f32[208,16,128]{2,1,0:T(8,128)S(1)} %bitcast.16, ...), custom_call_target="tpu_custom_call" | custom-call | tf_op jit(solution)/shard_map/pallas_call | solution.py:37
Async XLA Ops:
  2.2 7.6 %collective-permute-start.2 = (f32[18,16,128]{2,1,0:T(8,128)S(1)}, f32[18,16,128]{2,1,0:T(8,128)S(1)}, u32[]{:S(2)}, u32[]{:S(2)}) collective-permute-start(f32[18,16,128]{2,1,0:T(8,128)S(1)} %bitcast.27), channel_id=1, source_target_pairs={{0,4},{1,5},{2,6},{3,7},{4,0},{5,1},{6,2},{7,3},{8,12},{9,13},{10,... | collective-permute-start | bytes 442376 | tf_op jit(solution)/shard_map/ppermute | solution.py:820
  2.7 11.7 %collective-permute-start = (f32[20,16,128]{2,1,0:T(8,128)S(1)}, f32[20,16,128]{2,1,0:T(8,128)S(1)}, u32[]{:S(2)}, u32[]{:S(2)}) collective-permute-start(f32[20,16,128]{2,1,0:T(8,128)S(1)} %bitcast.24), channel_id=1, source_target_pairs={{0,1},{1,2},{2,3},{3,0},{4,5},{5,6},{6,7},{7,4},{8,9},{9,10},{10,1... | collective-permute-start | bytes 491528 | tf_op jit(solution)/shard_map/ppermute | solution.py:810
  5.2 9.2 %collective-permute-start.1 = (f32[18,16,128]{2,1,0:T(8,128)S(1)}, f32[18,16,128]{2,1,0:T(8,128)S(1)}, u32[]{:S(2)}, u32[]{:S(2)}) collective-permute-start(f32[18,16,128]{2,1,0:T(8,128)S(1)} %bitcast.26), channel_id=1, source_target_pairs={{0,3},{1,0},{2,1},{3,2},{4,7},{5,4},{6,5},{7,6},{8,11},{9,8},{10,9... | collective-permute-start | bytes 442376 | tf_op jit(solution)/shard_map/ppermute | solution.py:810
  6.3 8.1 %collective-permute-start.5 = (f32[18,16,128]{2,1,0:T(8,128)S(1)}, f32[18,16,128]{2,1,0:T(8,128)S(1)}, u32[]{:S(2)}, u32[]{:S(2)}) collective-permute-start(f32[18,16,128]{2,1,0:T(8,128)S(1)} %bitcast.25), channel_id=1, source_target_pairs={{0,28},{1,29},{2,30},{3,31},{4,8},{5,9},{6,10},{7,11},{8,4},{9,5},... | collective-permute-start | bytes 442376 | tf_op jit(solution)/shard_map/ppermute | solution.py:820
  9.8 6.9 %collective-permute-start.3 = (f32[4,16,128]{2,1,0:T(8,128)S(1)}, f32[4,16,128]{2,1,0:T(8,128)S(1)}, u32[]{:S(2)}, u32[]{:S(2)}) collective-permute-start(f32[4,16,128]{2,1,0:T(8,128)S(1)} %bitcast.29), channel_id=1, source_target_pairs={{0,5},{1,6},{2,7},{3,4},{4,9},{5,10},{6,11},{7,8},{8,13},{9,14},{1... | collective-permute-start | bytes 98312 | tf_op jit(solution)/shard_map/ppermute | solution.py:810
  9.8 7.3 %collective-permute-start.4 = (f32[4,16,128]{2,1,0:T(8,128)S(1)}, f32[4,16,128]{2,1,0:T(8,128)S(1)}, u32[]{:S(2)}, u32[]{:S(2)}) collective-permute-start(f32[4,16,128]{2,1,0:T(8,128)S(1)} %bitcast.28), channel_id=1, source_target_pairs={{0,7},{1,4},{2,5},{3,6},{4,11},{5,8},{6,9},{7,10},{8,15},{9,12},{1... | collective-permute-start | bytes 98312 | tf_op jit(solution)/shard_map/ppermute | solution.py:810
  18.8 7.8 %collective-permute-start.8 = (f32[32,16,128]{2,1,0:T(8,128)S(1)}, f32[32,16,128]{2,1,0:T(8,128)S(1)}, u32[]{:S(2)}, u32[]{:S(2)}) collective-permute-start(f32[32,16,128]{2,1,0:T(8,128)S(1)} %get-tuple-element.71), channel_id=1, source_target_pairs={{0,28},{1,29},{2,30},{3,31},{4,0},{5,1},{6,2},{7,3},{8,4},{9,5},{1... | collective-permute-start | bytes 786440 | tf_op jit(solution)/shard_map/ppermute | solution.py:810
  20.5 6.0 %collective-permute-start.6 = (f32[12,16,128]{2,1,0:T(8,128)S(1)}, f32[12,16,128]{2,1,0:T(8,128)S(1)}, u32[]{:S(2)}, u32[]{:S(2)}) collective-permute-start(f32[12,16,128]{2,1,0:T(8,128)S(1)} %get-tuple-element.69), channel_id=1, source_target_pairs={{0,1},{1,2},{2,3},{3,0},{4,5},{5,6},{6,7},{7,4},{8,9},{9,10},{10,1... | collective-permute-start | bytes 294920 | tf_op jit(solution)/shard_map/ppermute | solution.py:810
  22.0 4.6 %collective-permute-start.7 = (f32[10,16,128]{2,1,0:T(8,128)S(1)}, f32[10,16,128]{2,1,0:T(8,128)S(1)}, u32[]{:S(2)}, u32[]{:S(2)}) collective-permute-start(f32[10,16,128]{2,1,0:T(8,128)S(1)} %get-tuple-element.70), channel_id=1, source_target_pairs={{0,3},{1,0},{2,1},{3,2},{4,7},{5,4},{6,5},{7,6},{8,11},{9,8},{10,9... | collective-permute-start | bytes 245768 | tf_op jit(solution)/shard_map/ppermute | solution.py:810
  50.7 12.3 %all-to-all-start.1 = ((f32[32,12,1,128]{3,2,1,0:T(1,128)}), f32[32,12,1,128]{3,2,1,0:T(1,128)S(1)}, u32[]{:S(2)}, u32[]{:S(2)}) async-start(f32[32,12,1,128]{3,2,1,0:T(1,128)} %bitcast.13), calls=%async_computation.1 | async-start | bytes 393216 | tf_op jit(solution)/shard_map/all_to_all | solution.py:915
  53.3 9.3 %collective-permute-start.9 = (f32[16,16,128]{2,1,0:T(8,128)S(1)}, f32[16,16,128]{2,1,0:T(8,128)S(1)}, u32[]{:S(2)}, u32[]{:S(2)}) collective-permute-start(f32[16,16,128]{2,1,0:T(8,128)S(1)} %get-tuple-element.74), channel_id=1, source_target_pairs={{0,4},{1,5},{2,6},{3,7},{4,8},{5,9},{6,10},{7,11},{8,12},{9,13},{1... | collective-permute-start | bytes 393224 | tf_op jit(solution)/shard_map/ppermute | solution.py:810

commit v10 on v9

--- a/solution.py
+++ b/solution.py
@@ -241,15 +241,7 @@
     return jnp.where(source < 0, before, jnp.where(source >= LANES, after, here))
 
 
-def core_kernel(
-    share, initial_all, source_all, diffusivity_all, growth_all, core, *refs
-):
-    *windows, evens, source, coefs, sems = refs
-    waits, last = fetch(
-        initial_all, source_all, diffusivity_all, growth_all, evens, source, coefs, sems
-    )
-    for wait in (*waits, last):
-        wait.wait()
+def core_kernel(share, evens, source, coefs, core, *windows):
     _, rows, cols = coefs.shape
     depth = cols // LANES
     for index, name in enumerate(CORES):
@@ -850,20 +842,20 @@
     assert window_rows * depth == 2 * rows
     raw = [(points // 2, rows, cols), source.shape, (2, rows, cols)]
     extra = window_rows if handed_on(space) else 0
-    *sends, inward, outward = call(
+    *sends, inward, outward, evens, terms, rates = call(
         functools.partial(pack_kernel, share),
         [lines(EDGE_0 + extra), lines(EDGE_0), lines(SLANT_0), lines(SLANT_0)]
-        + [lines(rows + TURN)] * 2,
-        raw + [lines(2 * SCRATCH * (CHAINS + 1)), lines(2 * rows), lines(3 * rows + 2)],
+        + [lines(rows + TURN)] * 2
+        + raw,
+        [lines(2 * SCRATCH * (CHAINS + 1)), lines(2 * rows), lines(3 * rows + 2)],
         initial, source, diffusivity, growth,
         place=pltpu.HBM, sems=points // 2 + 3,
     )
     core, *windows = call(
         functools.partial(core_kernel, share),
         [lines(len(CORES) * rows)] + [(2 * rows, LANES)] * len(sent_windows(space)),
-        raw,
-        initial, source, diffusivity, growth,
-        place=pltpu.HBM, sems=points // 2 + 3,
+        [],
+        evens, terms, rates,
         cost=pl.CostEstimate(flops=0, transcendentals=0, bytes_accessed=CORE_COST),
     )
     sends, inward, outward = [as_rows(part) for part in sends], as_rows(inward), as_rows(outward)

time: 65 us -> 65 us (level)
  Pallas kernels: 12.3 us -> 10.7 us
  waiting for transfers between devices: 17.1 us -> 18.7 us
    ppermute x8, waiting for transfers between devices: 16.7 us -> 18.3 us  [moved(): return lax.ppermute(array, ('tm', 'space'), pairs)]
    pallas_call x6, Pallas kernels: 12.3 us -> 10.7 us  [call(): pl.pallas_call(kernel, out_shape=tuple((jax.ShapeDtypeStruct(shape, jnp.f...]
  transfers between devices with their start and end apart: 11 -> 11, of which waited for: 6 -> 6; matrix products, arithmetic and copies ran while one was open for 0% -> 0% of each run, Pallas kernels for 4% -> 1%
where the time goes in v10:
time: 65 us; the launch traced here: 64.8 us
  blocking collectives  19.8 us (30%)
  waiting for transfers between devices  18.7 us (29%)
  starting transfers between devices  15.6 us (24%)
  Pallas kernels  10.7 us (16%)
    all_to_all x1, blocking collectives, body(): slots = lax.all_to_all(slots, ('tm', 'space'), 0, 0, tiled=True)  19.8 us
    ppermute x8, waiting for transfers between devices, moved(): return lax.ppermute(array, ('tm', 'space'), pairs)  18.3 us
    pallas_call x6, Pallas kernels, call(): pl.pallas_call(kernel, out_shape=tuple((jax.ShapeDtypeStruct(shape, jnp.f...  10.7 us
    ppermute x8, starting transfers between devices, moved(): return lax.ppermute(array, ('tm', 'space'), pairs)  9.04 us
    ppermute x2, starting transfers between devices, swapped(): return lax.ppermute(array, ('tm', 'space'), pairs)  4 us
    all_to_all x1, starting transfers between devices, body(): slots = lax.all_to_all(slots, ('tm', 'space'), 0, 0, tiled=True)  2.58 us
  transfers between devices with their start and end apart: 11, of which 6 were waited for; matrix products, arithmetic and copies ran while one was open for 0% of the time, Pallas kernels for 1%

profile of v10, /device:TPU:0, one launch (start us, length us, event | category | flops | bytes accessed | tf_op | source)
XLA Modules:
  0.0 64.8 jit_solution(5979642037880697149)
XLA Ops:
  0.0 2.1 %shard_map.46 = (f32[320,128]{1,0:T(8,128)S(1)}, f32[288,128]{1,0:T(8,128)S(1)}, f32[64,128]{1,0:T(8,128)S(1)}, f32[64,128]{1,0:T(8,128)S(1)}, f32[288,128]{1,0:...) custom-call(f32[8,16,2048]{2,1,0:T(8,128)} %initial_all.1, ...), custom_call_target="tpu_custom_call" | custom-call | tf_op jit(solution)/shard_map/pallas_call | solution.py:37
  2.2 0.5 collective-permute-start.2
  2.7 2.6 %collective-permute-start = (f32[20,16,128]{2,1,0:T(8,128)S(1)}, f32[20,16,128]{2,1,0:T(8,128)S(1)}, u32[]{:S(2)}, u32[]{:S(2)}) collective-permute-start(f32[20,16,128]{2,1,0:T(8,128)S(1)} %bitcast.24), channel_id=1, source_target_pairs={{0,1},{1,2},{2,3},{3,0},{4,5},{5,6},{6,7},{7,4},{8,9},{9,10},{10,1... | collective-permute-start | bytes 491528 | tf_op jit(solution)/shard_map/ppermute | solution.py:802
  5.2 1.0 %collective-permute-start.1 = (f32[18,16,128]{2,1,0:T(8,128)S(1)}, f32[18,16,128]{2,1,0:T(8,128)S(1)}, u32[]{:S(2)}, u32[]{:S(2)}) collective-permute-start(f32[18,16,128]{2,1,0:T(8,128)S(1)} %bitcast.26), channel_id=1, source_target_pairs={{0,3},{1,0},{2,1},{3,2},{4,7},{5,4},{6,5},{7,6},{8,11},{9,8},{10,9... | collective-permute-start | bytes 442376 | tf_op jit(solution)/shard_map/ppermute | solution.py:802
  6.3 3.5 %collective-permute-start.5 = (f32[18,16,128]{2,1,0:T(8,128)S(1)}, f32[18,16,128]{2,1,0:T(8,128)S(1)}, u32[]{:S(2)}, u32[]{:S(2)}) collective-permute-start(f32[18,16,128]{2,1,0:T(8,128)S(1)} %bitcast.25), channel_id=1, source_target_pairs={{0,28},{1,29},{2,30},{3,31},{4,8},{5,9},{6,10},{7,11},{8,4},{9,5},... | collective-permute-start | bytes 442376 | tf_op jit(solution)/shard_map/ppermute | solution.py:812
  9.7 0.0 collective-permute-done.2.inward
  9.8 0.0 collective-permute-start.3
  9.8 0.6 collective-permute-start.4
  10.3 0.7 %shard_map.47 = (f32[3328,128]{1,0:T(8,128)S(1)}, f32[32,128]{1,0:T(8,128)S(1)}, f32[32,128]{1,0:T(8,128)S(1)}, f32[32,128]{1,0:T(8,128)S(1)}) custom-call(f32[4,16,2048]{2,1,0:T(8,128)S(1)} %get-tuple-element.44.evens, f32[8,16,2048]{2,1,0:T(8,128)S(1)} %get-tuple-element.45.source, f32[2,16,2048]{2,1,0:T(8,128)S(1)} %get-tuple-element.46.coefs), custom_call_target="tpu_custom_call" | custom-call | bytes 30000000 | tf_op jit(solution)/shard_map/pallas_call | solution.py:37
  11.0 3.4 %collective-permute-done.1.below = f32[18,16,128]{2,1,0:T(8,128)S(1)} collective-permute-done((f32[18,16,128]{2,1,0:T(8,128)S(1)}, f32[18,16,128]{2,1,0:T(8,128)S(1)}, u32[]{:S(2)}, u32[]{:S(2)}) %collective-permute-start.1) | collective-permute-done | bytes 147488 | tf_op jit(solution)/shard_map/ppermute | solution.py:802
  14.4 0.0 collective-permute-done.5.outward
  14.4 0.0 collective-permute-done.above
  14.4 2.3 %collective-permute-done.3.behind_above = f32[4,16,128]{2,1,0:T(8,128)S(1)} collective-permute-done((f32[4,16,128]{2,1,0:T(8,128)S(1)}, f32[4,16,128]{2,1,0:T(8,128)S(1)}, u32[]{:S(2)}, u32[]{:S(2)}) %collective-permute-start.3) | collective-permute-done | bytes 32800 | tf_op jit(solution)/shard_map/ppermute | solution.py:802
  16.7 0.4 collective-permute-done.4.behind_below
  17.1 1.6 %shard_map.48 = (f32[32,16,128]{2,1,0:T(8,128)S(1)}, f32[12,16,128]{2,1,0:T(8,128)S(1)}, f32[10,16,128]{2,1,0:T(8,128)S(1)}, f32[16,16,128]{2,1,0:T(8,128)S(1)},...) custom-call(f32[208,16,128]{2,1,0:T(8,128)S(1)} %bitcast.15, ...), custom_call_target="tpu_custom_call" | custom-call | tf_op jit(solution)/shard_map/pallas_call | solution.py:37
  18.8 1.8 %collective-permute-start.8 = (f32[32,16,128]{2,1,0:T(8,128)S(1)}, f32[32,16,128]{2,1,0:T(8,128)S(1)}, u32[]{:S(2)}, u32[]{:S(2)}) collective-permute-start(f32[32,16,128]{2,1,0:T(8,128)S(1)} %get-tuple-element.77), channel_id=1, source_target_pairs={{0,28},{1,29},{2,30},{3,31},{4,0},{5,1},{6,2},{7,3},{8,4},{9,5},{1... | collective-permute-start | bytes 786440 | tf_op jit(solution)/shard_map/ppermute | solution.py:802
  20.5 1.5 %collective-permute-start.6 = (f32[12,16,128]{2,1,0:T(8,128)S(1)}, f32[12,16,128]{2,1,0:T(8,128)S(1)}, u32[]{:S(2)}, u32[]{:S(2)}) collective-permute-start(f32[12,16,128]{2,1,0:T(8,128)S(1)} %get-tuple-element.75), channel_id=1, source_target_pairs={{0,1},{1,2},{2,3},{3,0},{4,5},{5,6},{6,7},{7,4},{8,9},{9,10},{10,1... | collective-permute-start | bytes 294920 | tf_op jit(solution)/shard_map/ppermute | solution.py:802
  22.0 1.4 %collective-permute-start.7 = (f32[10,16,128]{2,1,0:T(8,128)S(1)}, f32[10,16,128]{2,1,0:T(8,128)S(1)}, u32[]{:S(2)}, u32[]{:S(2)}) collective-permute-start(f32[10,16,128]{2,1,0:T(8,128)S(1)} %get-tuple-element.76), channel_id=1, source_target_pairs={{0,3},{1,0},{2,1},{3,2},{4,7},{5,4},{6,5},{7,6},{8,11},{9,8},{10,9... | collective-permute-start | bytes 245768 | tf_op jit(solution)/shard_map/ppermute | solution.py:802
  23.5 3.1 %collective-permute-done.7.below = f32[10,16,128]{2,1,0:T(8,128)S(1)} collective-permute-done((f32[10,16,128]{2,1,0:T(8,128)S(1)}, f32[10,16,128]{2,1,0:T(8,128)S(1)}, u32[]{:S(2)}, u32[]{:S(2)}) %collective-permute-start.7) | collective-permute-done | bytes 81952 | tf_op jit(solution)/shard_map/ppermute | solution.py:802
  26.6 0.0 collective-permute-done.6.above
  26.6 0.0 collective-permute-done.8.ahead_terms
  26.6 1.1 %shard_map.49 = (f32[1088,128]{1,0:T(8,128)S(1)}, f32[16,16,128]{2,1,0:T(8,128)S(1)}, f32[18,16,128]{2,1,0:T(8,128)S(1)}, f32[18,16,128]{2,1,0:T(8,128)S(1)}, f32[8,16,128]{2,1,0:T(8,128)S(1)}) custom-call(f32[16,16,128]{2,1,0:T(8,128)S(1)} %get-tuple-element.69.next_odd, f32[16,16,128]{2,1,0:T(8,128)S(1)} %get-tuple-element.70.last_odd, ...), custom_call_target="tpu_custom_call" | custom-call | tf_op jit(solution)/shard_map/pallas_call | solution.py:37
  27.7 19.8 %all_to_all.10 = f32[32,34,1,128]{3,2,1,0:T(1,128)S(1)} all-to-all(f32[32,34,1,128]{3,2,1,0:T(1,128)S(1)} %bitcast.19), channel_id=1, replica_groups=mesh['tm'=8,'space'=4] {'tm','space'}, dimensions={0} | all-to-all | bytes 1114112 | tf_op jit(solution)/shard_map/all_to_all | solution.py:895
  47.4 3.3 %shard_map.50 = f32[384,128]{1,0:T(8,128)} custom-call(f32[1088,128]{1,0:T(8,128)S(1)} %bitcast.17, f32[128,128]{1,0:T(8,128)S(1)} %bitcast.20), custom_call_target="tpu_custom_call" | custom-call | tf_op jit(solution)/shard_map/pallas_call | solution.py:37
  50.7 2.6 %all-to-all-start.1 = ((f32[32,12,1,128]{3,2,1,0:T(1,128)}), f32[32,12,1,128]{3,2,1,0:T(1,128)S(1)}, u32[]{:S(2)}, u32[]{:S(2)}) async-start(f32[32,12,1,128]{3,2,1,0:T(1,128)} %bitcast.13), calls=%async_computation.1 | async-start | bytes 393216 | tf_op jit(solution)/shard_map/all_to_all | solution.py:907
  53.3 0.2 collective-permute-start.9
  53.5 9.1 %collective-permute-done.9.next_forcing = f32[16,16,128]{2,1,0:T(8,128)S(1)} collective-permute-done((f32[16,16,128]{2,1,0:T(8,128)S(1)}, f32[16,16,128]{2,1,0:T(8,128)S(1)}, u32[]{:S(2)}, u32[]{:S(2)}) %collective-permute-start.9) | collective-permute-done | bytes 131104 | tf_op jit(solution)/shard_map/ppermute | solution.py:802
  62.6 0.4 all-to-all-done.1
  63.0 1.8 %shard_map.51 = f32[8,16,2048]{2,1,0:T(8,128)} custom-call(f32[384,128]{1,0:T(8,128)S(1)} %bitcast.18, f32[16,16,128]{2,1,0:T(8,128)S(1)} %collective-permute-done.9.next_forcing, f32[18,16,128]{2,1,0:T(8,128)S(1)} %get-tuple-element.81.late_a, f32[18,16,128]{2,1,0:T(8,128)S(1)} %get-tuple-element.82.late_b, f32[208,16,128]{2,1,0:T(8,128)S(1)} %bitcast.16, ...), custom_call_target="tpu_custom_call" | custom-call | tf_op jit(solution)/shard_map/pallas_call | solution.py:37
Async XLA Ops:
  2.2 7.6 %collective-permute-start.2 = (f32[18,16,128]{2,1,0:T(8,128)S(1)}, f32[18,16,128]{2,1,0:T(8,128)S(1)}, u32[]{:S(2)}, u32[]{:S(2)}) collective-permute-start(f32[18,16,128]{2,1,0:T(8,128)S(1)} %bitcast.27), channel_id=1, source_target_pairs={{0,4},{1,5},{2,6},{3,7},{4,0},{5,1},{6,2},{7,3},{8,12},{9,13},{10,... | collective-permute-start | bytes 442376 | tf_op jit(solution)/shard_map/ppermute | solution.py:812
  2.7 11.7 %collective-permute-start = (f32[20,16,128]{2,1,0:T(8,128)S(1)}, f32[20,16,128]{2,1,0:T(8,128)S(1)}, u32[]{:S(2)}, u32[]{:S(2)}) collective-permute-start(f32[20,16,128]{2,1,0:T(8,128)S(1)} %bitcast.24), channel_id=1, source_target_pairs={{0,1},{1,2},{2,3},{3,0},{4,5},{5,6},{6,7},{7,4},{8,9},{9,10},{10,1... | collective-permute-start | bytes 491528 | tf_op jit(solution)/shard_map/ppermute | solution.py:802
  5.2 9.2 %collective-permute-start.1 = (f32[18,16,128]{2,1,0:T(8,128)S(1)}, f32[18,16,128]{2,1,0:T(8,128)S(1)}, u32[]{:S(2)}, u32[]{:S(2)}) collective-permute-start(f32[18,16,128]{2,1,0:T(8,128)S(1)} %bitcast.26), channel_id=1, source_target_pairs={{0,3},{1,0},{2,1},{3,2},{4,7},{5,4},{6,5},{7,6},{8,11},{9,8},{10,9... | collective-permute-start | bytes 442376 | tf_op jit(solution)/shard_map/ppermute | solution.py:802
  6.3 8.1 %collective-permute-start.5 = (f32[18,16,128]{2,1,0:T(8,128)S(1)}, f32[18,16,128]{2,1,0:T(8,128)S(1)}, u32[]{:S(2)}, u32[]{:S(2)}) collective-permute-start(f32[18,16,128]{2,1,0:T(8,128)S(1)} %bitcast.25), channel_id=1, source_target_pairs={{0,28},{1,29},{2,30},{3,31},{4,8},{5,9},{6,10},{7,11},{8,4},{9,5},... | collective-permute-start | bytes 442376 | tf_op jit(solution)/shard_map/ppermute | solution.py:812
  9.8 6.9 %collective-permute-start.3 = (f32[4,16,128]{2,1,0:T(8,128)S(1)}, f32[4,16,128]{2,1,0:T(8,128)S(1)}, u32[]{:S(2)}, u32[]{:S(2)}) collective-permute-start(f32[4,16,128]{2,1,0:T(8,128)S(1)} %bitcast.29), channel_id=1, source_target_pairs={{0,5},{1,6},{2,7},{3,4},{4,9},{5,10},{6,11},{7,8},{8,13},{9,14},{1... | collective-permute-start | bytes 98312 | tf_op jit(solution)/shard_map/ppermute | solution.py:802
  9.8 7.3 %collective-permute-start.4 = (f32[4,16,128]{2,1,0:T(8,128)S(1)}, f32[4,16,128]{2,1,0:T(8,128)S(1)}, u32[]{:S(2)}, u32[]{:S(2)}) collective-permute-start(f32[4,16,128]{2,1,0:T(8,128)S(1)} %bitcast.28), channel_id=1, source_target_pairs={{0,7},{1,4},{2,5},{3,6},{4,11},{5,8},{6,9},{7,10},{8,15},{9,12},{1... | collective-permute-start | bytes 98312 | tf_op jit(solution)/shard_map/ppermute | solution.py:802
  18.8 7.8 %collective-permute-start.8 = (f32[32,16,128]{2,1,0:T(8,128)S(1)}, f32[32,16,128]{2,1,0:T(8,128)S(1)}, u32[]{:S(2)}, u32[]{:S(2)}) collective-permute-start(f32[32,16,128]{2,1,0:T(8,128)S(1)} %get-tuple-element.77), channel_id=1, source_target_pairs={{0,28},{1,29},{2,30},{3,31},{4,0},{5,1},{6,2},{7,3},{8,4},{9,5},{1... | collective-permute-start | bytes 786440 | tf_op jit(solution)/shard_map/ppermute | solution.py:802
  20.5 6.0 %collective-permute-start.6 = (f32[12,16,128]{2,1,0:T(8,128)S(1)}, f32[12,16,128]{2,1,0:T(8,128)S(1)}, u32[]{:S(2)}, u32[]{:S(2)}) collective-permute-start(f32[12,16,128]{2,1,0:T(8,128)S(1)} %get-tuple-element.75), channel_id=1, source_target_pairs={{0,1},{1,2},{2,3},{3,0},{4,5},{5,6},{6,7},{7,4},{8,9},{9,10},{10,1... | collective-permute-start | bytes 294920 | tf_op jit(solution)/shard_map/ppermute | solution.py:802
  22.0 4.6 %collective-permute-start.7 = (f32[10,16,128]{2,1,0:T(8,128)S(1)}, f32[10,16,128]{2,1,0:T(8,128)S(1)}, u32[]{:S(2)}, u32[]{:S(2)}) collective-permute-start(f32[10,16,128]{2,1,0:T(8,128)S(1)} %get-tuple-element.76), channel_id=1, source_target_pairs={{0,3},{1,0},{2,1},{3,2},{4,7},{5,4},{6,5},{7,6},{8,11},{9,8},{10,9... | collective-permute-start | bytes 245768 | tf_op jit(solution)/shard_map/ppermute | solution.py:802
  50.7 12.3 %all-to-all-start.1 = ((f32[32,12,1,128]{3,2,1,0:T(1,128)}), f32[32,12,1,128]{3,2,1,0:T(1,128)S(1)}, u32[]{:S(2)}, u32[]{:S(2)}) async-start(f32[32,12,1,128]{3,2,1,0:T(1,128)} %bitcast.13), calls=%async_computation.1 | async-start | bytes 393216 | tf_op jit(solution)/shard_map/all_to_all | solution.py:907
  53.3 9.3 %collective-permute-start.9 = (f32[16,16,128]{2,1,0:T(8,128)S(1)}, f32[16,16,128]{2,1,0:T(8,128)S(1)}, u32[]{:S(2)}, u32[]{:S(2)}) collective-permute-start(f32[16,16,128]{2,1,0:T(8,128)S(1)} %get-tuple-element.80), channel_id=1, source_target_pairs={{0,4},{1,5},{2,6},{3,7},{4,8},{5,9},{6,10},{7,11},{8,12},{9,13},{1... | collective-permute-start | bytes 393224 | tf_op jit(solution)/shard_map/ppermute | solution.py:802

commit v11 on v9

--- a/solution.py
+++ b/solution.py
@@ -695,9 +695,10 @@
     field = None
     for index in range(blocks):
         beyond(index)
+    last_term = block(1, blocks - 1)
     for index in range(blocks):
         behind, twice = (index - 1) % blocks, (index - 2) % blocks
-        odd, term = block(0, twice) + adds[twice], block(1, behind)
+        odd, term = block(0, twice) + adds[twice], last_term if index == 0 else next_term
         even = odd + 4.0 * slope_of(odd) + term
         slope = slope_of(even)
         own = block(2, behind) + adds[behind]
@@ -705,7 +706,8 @@
         odd = even + 4.0 * slope + own
         stepped = even + 8.0 * slope
         pair = odd + 4.0 * slope_of(odd) - stepped
-        terms[index] = block(1, index) + pair
+        next_term = block(1, index) if index < blocks - 1 else last_term
+        terms[index] = next_term + pair
         if index == blocks - 1:
             field = stepped + terms[index]
     for index in range(blocks):

time: 65 us -> 65 us (level)
  no operation moved by 1% of the time
where the time goes in v11:
time: 65 us; the launch traced here: 64.7 us
  blocking collectives  19.8 us (30%)
  waiting for transfers between devices  17.1 us (26%)
  starting transfers between devices  15.6 us (24%)
  Pallas kernels  12.2 us (19%)
    all_to_all x1, blocking collectives, body(): slots = lax.all_to_all(slots, ('tm', 'space'), 0, 0, tiled=True)  19.8 us
    ppermute x8, waiting for transfers between devices, moved(): return lax.ppermute(array, ('tm', 'space'), pairs)  16.7 us
    pallas_call x6, Pallas kernels, call(): pl.pallas_call(kernel, out_shape=tuple((jax.ShapeDtypeStruct(shape, jnp.f...  12.2 us
    ppermute x8, starting transfers between devices, moved(): return lax.ppermute(array, ('tm', 'space'), pairs)  9.04 us
    ppermute x2, starting transfers between devices, swapped(): return lax.ppermute(array, ('tm', 'space'), pairs)  4 us
    all_to_all x1, starting transfers between devices, body(): slots = lax.all_to_all(slots, ('tm', 'space'), 0, 0, tiled=True)  2.58 us
  transfers between devices with their start and end apart: 11, of which 6 were waited for; matrix products, arithmetic and copies ran while one was open for 0% of the time, Pallas kernels for 4%

profile of v11, /device:TPU:0, one launch (start us, length us, event | category | flops | bytes accessed | tf_op | source)
XLA Modules:
  0.0 64.7 jit_solution(3126047897738669478)
XLA Ops:
  0.0 2.1 %shard_map.47 = (f32[320,128]{1,0:T(8,128)S(1)}, f32[288,128]{1,0:T(8,128)S(1)}, f32[64,128]{1,0:T(8,128)S(1)}, f32[64,128]{1,0:T(8,128)S(1)}, f32[288,128]{1,0:T(8,128)S(1)}, /*index=5*/f32[288,128]{1,0:T(8,128)S(1)}) custom-call(f32[8,16,2048]{2,1,0:T(8,128)} %initial_all.3, f32[8,16,2048]{2,1,0:T(8,128)} %source_all.3, f32[16,2048]{1,0:T(8,128)} %diffusivity_all.3, ...), custom_call_target="tpu_custom_call" | custom-call | tf_op jit(solution)/shard_map/pallas_call | solution.py:37
  2.2 0.5 collective-permute-start.2
  2.7 2.6 %collective-permute-start = (f32[20,16,128]{2,1,0:T(8,128)S(1)}, f32[20,16,128]{2,1,0:T(8,128)S(1)}, u32[]{:S(2)}, u32[]{:S(2)}) collective-permute-start(f32[20,16,128]{2,1,0:T(8,128)S(1)} %bitcast.24), channel_id=1, source_target_pairs={{0,1},{1,2},{2,3},{3,0},{4,5},{5,6},{6,7},{7,4},{8,9},{9,10},{10,1... | collective-permute-start | bytes 491528 | tf_op jit(solution)/shard_map/ppermute | solution.py:812
  5.2 1.0 %collective-permute-start.1 = (f32[18,16,128]{2,1,0:T(8,128)S(1)}, f32[18,16,128]{2,1,0:T(8,128)S(1)}, u32[]{:S(2)}, u32[]{:S(2)}) collective-permute-start(f32[18,16,128]{2,1,0:T(8,128)S(1)} %bitcast.26), channel_id=1, source_target_pairs={{0,3},{1,0},{2,1},{3,2},{4,7},{5,4},{6,5},{7,6},{8,11},{9,8},{10,9... | collective-permute-start | bytes 442376 | tf_op jit(solution)/shard_map/ppermute | solution.py:812
  6.3 3.5 %collective-permute-start.5 = (f32[18,16,128]{2,1,0:T(8,128)S(1)}, f32[18,16,128]{2,1,0:T(8,128)S(1)}, u32[]{:S(2)}, u32[]{:S(2)}) collective-permute-start(f32[18,16,128]{2,1,0:T(8,128)S(1)} %bitcast.25), channel_id=1, source_target_pairs={{0,28},{1,29},{2,30},{3,31},{4,8},{5,9},{6,10},{7,11},{8,4},{9,5},... | collective-permute-start | bytes 442376 | tf_op jit(solution)/shard_map/ppermute | solution.py:822
  9.7 0.0 collective-permute-done.2.inward
  9.8 0.0 collective-permute-start.3
  9.8 0.6 collective-permute-start.4
  10.3 2.3 %shard_map.46 = (f32[3328,128]{1,0:T(8,128)S(1)}, f32[32,128]{1,0:T(8,128)S(1)}, f32[32,128]{1,0:T(8,128)S(1)}, f32[32,128]{1,0:T(8,128)S(1)}) custom-call(f32[8,16,2048]{2,1,0:T(8,128)} %initial_all.3, f32[8,16,2048]{2,1,0:T(8,128)} %source_all.3, f32[16,2048]{1,0:T(8,128)} %diffusivity_all.3, f32[16,2048]{1,0:T(8,128)} %growth_all.3), custom_call_target="tpu_custom_call" | custom-call | bytes 30000000 | tf_op jit(solution)/shard_map/pallas_call | solution.py:37
  12.7 1.7 %collective-permute-done.1.below = f32[18,16,128]{2,1,0:T(8,128)S(1)} collective-permute-done((f32[18,16,128]{2,1,0:T(8,128)S(1)}, f32[18,16,128]{2,1,0:T(8,128)S(1)}, u32[]{:S(2)}, u32[]{:S(2)}) %collective-permute-start.1) | collective-permute-done | bytes 147488 | tf_op jit(solution)/shard_map/ppermute | solution.py:812
  14.4 0.0 collective-permute-done.5.outward
  14.4 0.0 collective-permute-done.above
  14.4 2.3 %collective-permute-done.3.behind_above = f32[4,16,128]{2,1,0:T(8,128)S(1)} collective-permute-done((f32[4,16,128]{2,1,0:T(8,128)S(1)}, f32[4,16,128]{2,1,0:T(8,128)S(1)}, u32[]{:S(2)}, u32[]{:S(2)}) %collective-permute-start.3) | collective-permute-done | bytes 32800 | tf_op jit(solution)/shard_map/ppermute | solution.py:812
  16.7 0.4 collective-permute-done.4.behind_below
  17.1 1.6 %shard_map.48 = (f32[32,16,128]{2,1,0:T(8,128)S(1)}, f32[12,16,128]{2,1,0:T(8,128)S(1)}, f32[10,16,128]{2,1,0:T(8,128)S(1)}, f32[16,16,128]{2,1,0:T(8,128)S(1)},...) custom-call(f32[208,16,128]{2,1,0:T(8,128)S(1)} %bitcast.15, ...), custom_call_target="tpu_custom_call" | custom-call | tf_op jit(solution)/shard_map/pallas_call | solution.py:37
  18.8 1.8 %collective-permute-start.8 = (f32[32,16,128]{2,1,0:T(8,128)S(1)}, f32[32,16,128]{2,1,0:T(8,128)S(1)}, u32[]{:S(2)}, u32[]{:S(2)}) collective-permute-start(f32[32,16,128]{2,1,0:T(8,128)S(1)} %get-tuple-element.71), channel_id=1, source_target_pairs={{0,28},{1,29},{2,30},{3,31},{4,0},{5,1},{6,2},{7,3},{8,4},{9,5},{1... | collective-permute-start | bytes 786440 | tf_op jit(solution)/shard_map/ppermute | solution.py:812
  20.5 1.5 %collective-permute-start.6 = (f32[12,16,128]{2,1,0:T(8,128)S(1)}, f32[12,16,128]{2,1,0:T(8,128)S(1)}, u32[]{:S(2)}, u32[]{:S(2)}) collective-permute-start(f32[12,16,128]{2,1,0:T(8,128)S(1)} %get-tuple-element.69), channel_id=1, source_target_pairs={{0,1},{1,2},{2,3},{3,0},{4,5},{5,6},{6,7},{7,4},{8,9},{9,10},{10,1... | collective-permute-start | bytes 294920 | tf_op jit(solution)/shard_map/ppermute | solution.py:812
  22.0 1.4 %collective-permute-start.7 = (f32[10,16,128]{2,1,0:T(8,128)S(1)}, f32[10,16,128]{2,1,0:T(8,128)S(1)}, u32[]{:S(2)}, u32[]{:S(2)}) collective-permute-start(f32[10,16,128]{2,1,0:T(8,128)S(1)} %get-tuple-element.70), channel_id=1, source_target_pairs={{0,3},{1,0},{2,1},{3,2},{4,7},{5,4},{6,5},{7,6},{8,11},{9,8},{10,9... | collective-permute-start | bytes 245768 | tf_op jit(solution)/shard_map/ppermute | solution.py:812
  23.5 3.1 %collective-permute-done.7.below = f32[10,16,128]{2,1,0:T(8,128)S(1)} collective-permute-done((f32[10,16,128]{2,1,0:T(8,128)S(1)}, f32[10,16,128]{2,1,0:T(8,128)S(1)}, u32[]{:S(2)}, u32[]{:S(2)}) %collective-permute-start.7) | collective-permute-done | bytes 81952 | tf_op jit(solution)/shard_map/ppermute | solution.py:812
  26.6 0.0 collective-permute-done.6.above
  26.6 0.0 collective-permute-done.8.ahead_terms
  26.6 1.1 %shard_map.49 = (f32[1088,128]{1,0:T(8,128)S(1)}, f32[16,16,128]{2,1,0:T(8,128)S(1)}, f32[18,16,128]{2,1,0:T(8,128)S(1)}, f32[18,16,128]{2,1,0:T(8,128)S(1)}, f32[8,16,128]{2,1,0:T(8,128)S(1)}) custom-call(f32[16,16,128]{2,1,0:T(8,128)S(1)} %get-tuple-element.63.next_odd, f32[16,16,128]{2,1,0:T(8,128)S(1)} %get-tuple-element.64.last_odd, ...), custom_call_target="tpu_custom_call" | custom-call | tf_op jit(solution)/shard_map/pallas_call | solution.py:37
  27.7 19.8 %all_to_all.10 = f32[32,34,1,128]{3,2,1,0:T(1,128)S(1)} all-to-all(f32[32,34,1,128]{3,2,1,0:T(1,128)S(1)} %bitcast.19), channel_id=1, replica_groups=mesh['tm'=8,'space'=4] {'tm','space'}, dimensions={0} | all-to-all | bytes 1114112 | tf_op jit(solution)/shard_map/all_to_all | solution.py:905
  47.4 3.2 %shard_map.50 = f32[384,128]{1,0:T(8,128)} custom-call(f32[1088,128]{1,0:T(8,128)S(1)} %bitcast.17, f32[128,128]{1,0:T(8,128)S(1)} %bitcast.20), custom_call_target="tpu_custom_call" | custom-call | tf_op jit(solution)/shard_map/pallas_call | solution.py:37
  50.7 2.6 %all-to-all-start.1 = ((f32[32,12,1,128]{3,2,1,0:T(1,128)}), f32[32,12,1,128]{3,2,1,0:T(1,128)S(1)}, u32[]{:S(2)}, u32[]{:S(2)}) async-start(f32[32,12,1,128]{3,2,1,0:T(1,128)} %bitcast.13), calls=%async_computation.1 | async-start | bytes 393216 | tf_op jit(solution)/shard_map/all_to_all | solution.py:917
  53.2 0.2 collective-permute-start.9
  53.4 9.1 %collective-permute-done.9.next_forcing = f32[16,16,128]{2,1,0:T(8,128)S(1)} collective-permute-done((f32[16,16,128]{2,1,0:T(8,128)S(1)}, f32[16,16,128]{2,1,0:T(8,128)S(1)}, u32[]{:S(2)}, u32[]{:S(2)}) %collective-permute-start.9) | collective-permute-done | bytes 131104 | tf_op jit(solution)/shard_map/ppermute | solution.py:812
  62.5 0.4 all-to-all-done.1
  63.0 1.8 %shard_map.51 = f32[8,16,2048]{2,1,0:T(8,128)} custom-call(f32[384,128]{1,0:T(8,128)S(1)} %bitcast.18, f32[16,16,128]{2,1,0:T(8,128)S(1)} %collective-permute-done.9.next_forcing, f32[18,16,128]{2,1,0:T(8,128)S(1)} %get-tuple-element.75.late_a, f32[18,16,128]{2,1,0:T(8,128)S(1)} %get-tuple-element.76.late_b, f32[208,16,128]{2,1,0:T(8,128)S(1)} %bitcast.16, ...), custom_call_target="tpu_custom_call" | custom-call | tf_op jit(solution)/shard_map/pallas_call | solution.py:37
Async XLA Ops:
  2.2 7.6 %collective-permute-start.2 = (f32[18,16,128]{2,1,0:T(8,128)S(1)}, f32[18,16,128]{2,1,0:T(8,128)S(1)}, u32[]{:S(2)}, u32[]{:S(2)}) collective-permute-start(f32[18,16,128]{2,1,0:T(8,128)S(1)} %bitcast.27), channel_id=1, source_target_pairs={{0,4},{1,5},{2,6},{3,7},{4,0},{5,1},{6,2},{7,3},{8,12},{9,13},{10,... | collective-permute-start | bytes 442376 | tf_op jit(solution)/shard_map/ppermute | solution.py:822
  2.7 11.7 %collective-permute-start = (f32[20,16,128]{2,1,0:T(8,128)S(1)}, f32[20,16,128]{2,1,0:T(8,128)S(1)}, u32[]{:S(2)}, u32[]{:S(2)}) collective-permute-start(f32[20,16,128]{2,1,0:T(8,128)S(1)} %bitcast.24), channel_id=1, source_target_pairs={{0,1},{1,2},{2,3},{3,0},{4,5},{5,6},{6,7},{7,4},{8,9},{9,10},{10,1... | collective-permute-start | bytes 491528 | tf_op jit(solution)/shard_map/ppermute | solution.py:812
  5.2 9.2 %collective-permute-start.1 = (f32[18,16,128]{2,1,0:T(8,128)S(1)}, f32[18,16,128]{2,1,0:T(8,128)S(1)}, u32[]{:S(2)}, u32[]{:S(2)}) collective-permute-start(f32[18,16,128]{2,1,0:T(8,128)S(1)} %bitcast.26), channel_id=1, source_target_pairs={{0,3},{1,0},{2,1},{3,2},{4,7},{5,4},{6,5},{7,6},{8,11},{9,8},{10,9... | collective-permute-start | bytes 442376 | tf_op jit(solution)/shard_map/ppermute | solution.py:812
  6.3 8.1 %collective-permute-start.5 = (f32[18,16,128]{2,1,0:T(8,128)S(1)}, f32[18,16,128]{2,1,0:T(8,128)S(1)}, u32[]{:S(2)}, u32[]{:S(2)}) collective-permute-start(f32[18,16,128]{2,1,0:T(8,128)S(1)} %bitcast.25), channel_id=1, source_target_pairs={{0,28},{1,29},{2,30},{3,31},{4,8},{5,9},{6,10},{7,11},{8,4},{9,5},... | collective-permute-start | bytes 442376 | tf_op jit(solution)/shard_map/ppermute | solution.py:822
  9.8 6.9 %collective-permute-start.3 = (f32[4,16,128]{2,1,0:T(8,128)S(1)}, f32[4,16,128]{2,1,0:T(8,128)S(1)}, u32[]{:S(2)}, u32[]{:S(2)}) collective-permute-start(f32[4,16,128]{2,1,0:T(8,128)S(1)} %bitcast.29), channel_id=1, source_target_pairs={{0,5},{1,6},{2,7},{3,4},{4,9},{5,10},{6,11},{7,8},{8,13},{9,14},{1... | collective-permute-start | bytes 98312 | tf_op jit(solution)/shard_map/ppermute | solution.py:812
  9.8 7.3 %collective-permute-start.4 = (f32[4,16,128]{2,1,0:T(8,128)S(1)}, f32[4,16,128]{2,1,0:T(8,128)S(1)}, u32[]{:S(2)}, u32[]{:S(2)}) collective-permute-start(f32[4,16,128]{2,1,0:T(8,128)S(1)} %bitcast.28), channel_id=1, source_target_pairs={{0,7},{1,4},{2,5},{3,6},{4,11},{5,8},{6,9},{7,10},{8,15},{9,12},{1... | collective-permute-start | bytes 98312 | tf_op jit(solution)/shard_map/ppermute | solution.py:812
  18.8 7.8 %collective-permute-start.8 = (f32[32,16,128]{2,1,0:T(8,128)S(1)}, f32[32,16,128]{2,1,0:T(8,128)S(1)}, u32[]{:S(2)}, u32[]{:S(2)}) collective-permute-start(f32[32,16,128]{2,1,0:T(8,128)S(1)} %get-tuple-element.71), channel_id=1, source_target_pairs={{0,28},{1,29},{2,30},{3,31},{4,0},{5,1},{6,2},{7,3},{8,4},{9,5},{1... | collective-permute-start | bytes 786440 | tf_op jit(solution)/shard_map/ppermute | solution.py:812
  20.5 6.0 %collective-permute-start.6 = (f32[12,16,128]{2,1,0:T(8,128)S(1)}, f32[12,16,128]{2,1,0:T(8,128)S(1)}, u32[]{:S(2)}, u32[]{:S(2)}) collective-permute-start(f32[12,16,128]{2,1,0:T(8,128)S(1)} %get-tuple-element.69), channel_id=1, source_target_pairs={{0,1},{1,2},{2,3},{3,0},{4,5},{5,6},{6,7},{7,4},{8,9},{9,10},{10,1... | collective-permute-start | bytes 294920 | tf_op jit(solution)/shard_map/ppermute | solution.py:812
  22.0 4.6 %collective-permute-start.7 = (f32[10,16,128]{2,1,0:T(8,128)S(1)}, f32[10,16,128]{2,1,0:T(8,128)S(1)}, u32[]{:S(2)}, u32[]{:S(2)}) collective-permute-start(f32[10,16,128]{2,1,0:T(8,128)S(1)} %get-tuple-element.70), channel_id=1, source_target_pairs={{0,3},{1,0},{2,1},{3,2},{4,7},{5,4},{6,5},{7,6},{8,11},{9,8},{10,9... | collective-permute-start | bytes 245768 | tf_op jit(solution)/shard_map/ppermute | solution.py:812
  50.7 12.3 %all-to-all-start.1 = ((f32[32,12,1,128]{3,2,1,0:T(1,128)}), f32[32,12,1,128]{3,2,1,0:T(1,128)S(1)}, u32[]{:S(2)}, u32[]{:S(2)}) async-start(f32[32,12,1,128]{3,2,1,0:T(1,128)} %bitcast.13), calls=%async_computation.1 | async-start | bytes 393216 | tf_op jit(solution)/shard_map/all_to_all | solution.py:917
  53.2 9.3 %collective-permute-start.9 = (f32[16,16,128]{2,1,0:T(8,128)S(1)}, f32[16,16,128]{2,1,0:T(8,128)S(1)}, u32[]{:S(2)}, u32[]{:S(2)}) collective-permute-start(f32[16,16,128]{2,1,0:T(8,128)S(1)} %get-tuple-element.74), channel_id=1, source_target_pairs={{0,4},{1,5},{2,6},{3,7},{4,8},{5,9},{6,10},{7,11},{8,12},{9,13},{1... | collective-permute-start | bytes 393224 | tf_op jit(solution)/shard_map/ppermute | solution.py:812
